TPU v7x, 512 devices: a whole 4x8x8 slice. The times are simulated.
512 devices in a mesh: seq: 8 (over x, core), dp: 64 (over y, z).
Axes of the slice: x: 4, y: 8, z: 8, core: 2. Of those that a mesh axis runs over, the one named last changes fastest.
Arguments:
- hidden: bfloat16 [64, 1024, 4096], P('dp', 'seq'), may hold values from -16 to 16
- query: bfloat16 [64, 1024, 4096], P('dp', 'seq'), may hold values from -5 to 5
- key: bfloat16 [64, 1024, 1024], P('dp', 'seq'), may hold values from -5 to 5
- grad_out: bfloat16 [64, 1024, 4096], P('dp', 'seq'), may hold values from -6 to 6
- doc_lens: int32 [64, 8], P('dp'), may hold values from 1 to 384, 1024 in all within a row
- master: float32 [4096, 1024], P('dp', 'seq'), may hold values from -6 to 6
- m_code: bfloat16 [4096, 1024], P('dp', 'seq'), may hold values from -1 to 1
- m_scale: float32 [2048, 8], P('dp', 'seq'), may hold values from 0.02 to 0.2
- v_code: bfloat16 [4096, 1024], P('dp', 'seq'), may hold values from 0.049804688 to 1
- v_scale: float32 [2048, 8], P('dp', 'seq'), may hold values from 0.5 to 5
Outputs:
- grad_query: bfloat16 [64, 1024, 4096], P('dp', 'seq')
- grad_key: bfloat16 [64, 1024, 1024], P('dp', 'seq')
- new_master: float32 [4096, 1024], P('dp', 'seq')
- new_m_code: bfloat16 [4096, 1024], P('dp', 'seq')
- new_m_scale: float32 [2048, 8], P('dp', 'seq')
- new_v_code: bfloat16 [4096, 1024], P('dp', 'seq')
- new_v_scale: float32 [2048, 8], P('dp', 'seq')
Inputs may be any that keep to these rules, and one draw needn't show every extreme that they name: `doc_lens`: row g lists the lengths of the documents packed in order into sequence g; they sum to 1024 and the largest is exactly 384.
All inputs are finite; a program needn't handle non-finite values. Where the computation divides by a largest or mean magnitude, that divisor is 1e-20 or more.
Results may differ from a plain program's by a relative error of at most 0.027.
Values may be sent and summed in bfloat16 or wider, within the bound.
No kernel may reach another device: no remote copies, remote signals or barrier semaphores. Data moves between devices by JAX's collectives and lax.ppermute only.
A program may use at most 128 MiB of HBM per device.

v0:
```python
import math

import jax
import jax.numpy as jnp
from jax import lax
from jax.sharding import PartitionSpec as P

D = 4096
HD = 128
DOCS = 8
STEP = 1000


def doc_tables(doc_lens, length):
    lengths = doc_lens[0]
    ends = jnp.cumsum(lengths)
    position = jnp.arange(length)
    after = position[:, None] >= ends[None, :]
    doc_ids = jnp.sum(after.astype(jnp.int32), axis=1)
    starts = jnp.sum(jnp.where(after, lengths[None, :], 0), axis=1)
    return (doc_ids, starts)


def block_terms(query_rows, cot_rows, key_heads, value_heads, doc_ids, first, lower, upper):
    count = query_rows.shape[0]
    kv_local = key_heads.shape[1] // HD
    group_size = query_rows.shape[1] // (kv_local * HD)
    scale = 1.0 / math.sqrt(HD)
    queries = query_rows.reshape(count, kv_local, group_size, HD)
    cotangent = cot_rows.reshape(count, kv_local, group_size, HD)
    key_tile = key_heads[lower:upper].reshape(upper - lower, kv_local, HD)
    value_tile = value_heads[lower:upper].reshape(upper - lower, kv_local, HD)
    scores = (
        jnp.einsum("qhgd,khd->hgqk", queries, key_tile, preferred_element_type=jnp.float32) * scale
    )
    query_pos = first + jnp.arange(count)
    key_pos = lower + jnp.arange(upper - lower)
    same_doc = doc_ids[first : first + count][:, None] == doc_ids[lower:upper][None, :]
    allowed = (key_pos[None, :] <= query_pos[:, None]) & same_doc
    scores = jnp.where(allowed, scores, -jnp.inf)
    highest = jnp.max(scores, axis=3, keepdims=True)
    weights = jnp.exp(scores - highest)
    probabilities = (weights / jnp.sum(weights, axis=3, keepdims=True)).astype(jnp.bfloat16)
    attended = jnp.einsum(
        "hgqk,khd->qhgd", probabilities, value_tile, preferred_element_type=jnp.float32
    ).astype(jnp.bfloat16)
    delta = jnp.einsum("qhgd,qhgd->hgq", attended, cotangent, preferred_element_type=jnp.float32)
    prob_grad = jnp.einsum(
        "qhgd,khd->hgqk", cotangent, value_tile, preferred_element_type=jnp.float32
    )
    score_grad = (probabilities.astype(jnp.float32) * (prob_grad - delta[..., None])).astype(
        jnp.bfloat16
    )
    grad_rows = (
        jnp.einsum("hgqk,khd->qhgd", score_grad, key_tile, preferred_element_type=jnp.float32)
        * scale
    )
    grad_rows = grad_rows.astype(jnp.bfloat16).reshape(count, kv_local * group_size * HD)
    key_part = (
        jnp.einsum("hgqk,qhgd->khd", score_grad, queries, preferred_element_type=jnp.float32)
        * scale
    )
    value_part = jnp.einsum(
        "hgqk,qhgd->khd", probabilities, cotangent, preferred_element_type=jnp.float32
    )
    total_rows = key_heads.shape[0]
    padding = ((lower, total_rows - upper), (0, 0), (0, 0))
    return (grad_rows, jnp.pad(key_part, padding), jnp.pad(value_part, padding))


def adam_update(grad_w, master, m_code, m_scale, v_code, v_scale):
    shape4 = (grad_w.shape[0] // 2, 2, m_scale.shape[1], HD)
    grad4 = grad_w.reshape(shape4)
    m_old = m_code.astype(jnp.float32).reshape(shape4) * m_scale[:, None, :, None]
    v_old = v_code.astype(jnp.float32).reshape(shape4) * v_scale[:, None, :, None]
    m_new = 0.9 * m_old + 0.1 * grad4
    v_new = 0.999 * v_old + 0.001 * grad4 * grad4
    first_fix = 1.0 - 0.9**STEP
    second_fix = 1.0 - 0.999**STEP
    update = m_new / first_fix / (jnp.sqrt(v_new / second_fix) + 1e-08)
    new_master = master - 0.01 * update.reshape(master.shape)
    m_top = jnp.max(jnp.abs(m_new), axis=(1, 3))
    v_top = jnp.max(jnp.abs(v_new), axis=(1, 3))
    new_m_code = (
        (m_new / (m_top[:, None, :, None] + 1e-06)).astype(jnp.bfloat16).reshape(master.shape)
    )
    new_v_code = (
        (v_new / (v_top[:, None, :, None] + 1e-06)).astype(jnp.bfloat16).reshape(master.shape)
    )
    return (new_master, new_m_code, m_top, new_v_code, v_top)


def shards(hidden, query, key, grad_out, doc_lens, master, m_code, m_scale, v_code, v_scale):
    inv_width = 1.0 / math.sqrt(D)
    weight = lax.all_gather(master.astype(jnp.bfloat16), "dp", axis=0, tiled=True)
    whole = lax.all_gather(hidden, "seq", axis=1, tiled=True)[0]
    values = (jnp.dot(whole, weight, preferred_element_type=jnp.float32) * inv_width).astype(
        jnp.bfloat16
    )
    query_heads, key_heads = (
        lax.all_to_all(query, "seq", split_axis=2, concat_axis=1, tiled=True),
        lax.all_to_all(key, "seq", split_axis=2, concat_axis=1, tiled=True),
    )
    cot_heads = lax.all_to_all(grad_out, "seq", split_axis=2, concat_axis=1, tiled=True)
    query_heads = query_heads[0]
    key_heads = key_heads[0]
    cot_heads = cot_heads[0]
    length = whole.shape[0]
    kv_local = key_heads.shape[1] // HD
    doc_ids, starts = doc_tables(doc_lens, length)
    block = min(128, length)
    longest = 3 * length // DOCS
    window = min(length, (longest + 2 * block - 2) // block * block)
    grad_pieces = []
    key_sum = jnp.zeros((length, kv_local, HD), jnp.float32)
    value_sum = jnp.zeros((length, kv_local, HD), jnp.float32)
    for index in range(length // block):
        first = index * block
        upper = first + block
        query_rows = query_heads[first:upper]
        cot_rows = cot_heads[first:upper]
        outputs = block_terms(
            query_rows, cot_rows, key_heads, values, doc_ids, first, max(0, upper - window), upper
        )
        grad_pieces.append(outputs[0])
        key_sum = key_sum + outputs[1]
        value_sum = value_sum + outputs[2]
    grad_query_heads = jnp.concatenate(grad_pieces, axis=0)[None]
    grad_key_heads = key_sum.reshape(length, kv_local * HD).astype(jnp.bfloat16)[None]
    grad_values = value_sum.reshape(length, kv_local * HD).astype(jnp.bfloat16)
    grad_query, grad_key = (
        lax.all_to_all(grad_query_heads, "seq", split_axis=1, concat_axis=2, tiled=True),
        lax.all_to_all(grad_key_heads, "seq", split_axis=1, concat_axis=2, tiled=True),
    )
    term = (
        lax.dot_general(
            whole, grad_values, (((0,), (0,)), ((), ())), preferred_element_type=jnp.float32
        )
        * inv_width
    )
    grad_w = lax.psum_scatter(term, "dp", scatter_dimension=0, tiled=True)
    new_master, new_m_code, new_m_scale, new_v_code, new_v_scale = adam_update(
        grad_w, master, m_code, m_scale, v_code, v_scale
    )
    return (grad_query, grad_key, new_master, new_m_code, new_m_scale, new_v_code, new_v_scale)


def solution(mesh):
    return jax.shard_map(
        shards,
        mesh=mesh,
        in_specs=(
            P("dp", "seq", None),
            P("dp", "seq", None),
            P("dp", "seq", None),
            P("dp", "seq", None),
            P("dp", None),
            P("dp", "seq"),
            P("dp", "seq"),
            P("dp", "seq"),
            P("dp", "seq"),
            P("dp", "seq"),
        ),
        out_specs=(
            P("dp", "seq", None),
            P("dp", "seq", None),
            P("dp", "seq"),
            P("dp", "seq"),
            P("dp", "seq"),
            P("dp", "seq"),
            P("dp", "seq"),
        ),
        check_vma=False,
    )
```

profile of v0, /device:TPU:1, one launch (start us, length us, event | category | flops | bytes accessed | tf_op | source)
XLA Modules:
  0.0 528.2 jit_solution(1171744129633130919)
XLA Ops:
  7.2 0.7 all-gather.3.cloned.1.call-update
  7.9 1.3 copy.478
  9.2 0.5 broadcast.368
  9.7 2.2 reduce.40
  11.9 0.8 reshape.946
  12.7 10.2 %all-to-all-start = ((bf16[8,2,8192]{2,1,0:T(2,128)(2,1)}), bf16[8,2,8192]{2,1,0:T(2,128)(2,1)S(1)}, u32[]{:S(2)}, u32[]{:S(2)}) async-start(bf16[8,2,8192]{2,1,0:T(2,128)(2,1)} %reshape.946), calls=%async_computation | async-start | bytes 524288 | tf_op jit(solution)/shard_map/all_to_all | solution.py:102
  23.2 2.8 copy.480
  26.1 22.4 %reduce.39 = bf16[4096,128]{1,0:T(8,128)(2,1)S(1)} reduce(bf16[4096,1,128]{2,1,0:T(2,128)(2,1)S(1)} %bitcast.762, bf16[]{:T(256)} %broadcast.368), dimensions={1}, to_apply=%bitcast.681.reduce_sub_computation | reduce | bytes 2097154
  48.5 1.1 reshape.944
  49.6 5.2 all-to-all-start.1
  54.8 5.0 copy.482
  59.8 23.4 %reduce.38 = bf16[4096,128]{1,0:T(8,128)(2,1)} reduce(bf16[4096,1,128]{2,1,0:T(2,128)(2,1)S(1)} %bitcast.763, bf16[]{:T(256)} %broadcast.368), dimensions={1}, to_apply=%bitcast.679.reduce_sub_computation | reduce | bytes 2097154
  83.2 2.2 reshape.942
  85.4 0.7 fusion.148
  86.1 0.7 fusion.145
  86.9 0.8 compare_and_fusion.3
  87.7 4.8 all-to-all-start.2
  92.5 0.5 reduce-scatter.4.cloned.1.call-start
  93.2 0.9 fusion.142
  94.1 1.0 compare_and_fusion.1
  95.6 0.7 slice.217
  96.3 0.6 slice.221
  96.9 0.9 fusion.154
  97.8 1.0 reshape.945
  99.0 8.7 %all-to-all-done.2 = bf16[8,2,32768]{2,1,0:T(2,128)(2,1)} async-done(((bf16[8,2,32768]{2,1,0:T(2,128)(2,1)}), bf16[8,2,32768]{2,1,0:T(2,128)(2,1)}, u32[]{:S(2)}, u32[]{:S(2)}) %all-to-all-start.2) | async-done | bytes 1048608 | tf_op jit(solution)/shard_map/all_to_all | solution.py:104
  107.7 4.3 reshape.943
  112.7 0.4 copy-done.56
  113.8 0.3 fusion.162
  117.0 0.5 copy-done.21
  117.5 0.8 convolution_bitcast_fusion.22
  118.4 0.7 copy-done.7
  119.1 0.9 convolution_bitcast_fusion.20
  120.1 0.9 convolution_bitcast_fusion.18
  121.3 1.0 convolution_bitcast_fusion.11
  122.5 1.0 convolution_bitcast_fusion.9
  123.7 1.0 convolution_bitcast_fusion.8
  125.0 1.0 convolution_bitcast_fusion.7
  126.2 0.8 copy-done
  127.0 1.0 convolution_bitcast_fusion.10
  128.0 5.2 fusion.7
  133.2 1.9 copy.699
  135.3 0.4 copy-done.76
  136.1 238.2 %reduce-scatter.4.cloned.1.call-done = f32[64,128]{1,0:T(8,128)} async-done(((f32[4096,128]{1,0:T(8,128)}), f32[64,128]{1,0:T(8,128)}) %reduce-scatter.4.cloned.1.call-update) | async-done | bytes 32784 | tf_op jit(solution)/shard_map/reduce_scatter | solution.py:141
  374.3 2.1 abs_reduce_fusion
  376.4 81.2 %all-gather.5.cloned.1.call-done = bf16[4096,128]{1,0:T(8,128)(2,1)} async-done(((bf16[64,128]{1,0:T(8,128)(2,1)}), bf16[4096,128]{1,0:T(8,128)(2,1)}) %all-gather.5.cloned.1.call-update) | async-done | bytes 1048592 | tf_op jit(solution)/shard_map/all_gather | solution.py:95
  457.7 5.9 %fusion.51 = bf16[1024,128]{1,0:T(8,128)(2,1)S(1)} fusion(bf16[4096,128]{1,0:T(8,128)(2,1)} %all-gather.5.cloned.1.call-done, bf16[1,1024,4096]{2,1,0:T(8,128)(2,1)} %all-gather.3.cloned.1.call-done), kind=kOutput, calls=%fused_computation.59 | convolution fusion | flops 1074003968 | bytes 9699328 | tf_op jit(solution)/shard_map/dot_general | solution.py:97
  467.0 0.3 fusion.62
  468.2 0.3 fusion.64
  469.4 0.3 fusion.66
  472.8 1.0 fusion.72
  473.9 0.4 copy.709
  474.3 2.2 reduce.42
  476.5 0.8 reshape.950
  477.3 9.5 %all-to-all-start.4 = ((bf16[8,2,8192]{2,1,0:T(2,128)(2,1)}), bf16[8,2,8192]{2,1,0:T(2,128)(2,1)S(1)}, u32[]{:S(2)}, u32[]{:S(2)}) async-start(bf16[8,2,8192]{2,1,0:T(2,128)(2,1)} %reshape.950), calls=%async_computation.4 | async-start | bytes 524288 | tf_op jit(solution)/shard_map/all_to_all | solution.py:133
  487.9 1.6 copy.708
  489.5 7.0 %reduce.41 = bf16[1024,512]{1,0:T(8,128)(2,1)S(1)} reduce(bf16[1024,1,512]{2,1,0:T(2,128)(2,1)S(1)} %bitcast.761, bf16[]{:T(256)} %broadcast.368), dimensions={1}, to_apply=%bitcast.756.reduce_sub_computation | reduce | bytes 2097154
  496.6 1.6 reshape.948
  498.2 4.8 all-to-all-start.3
  503.9 0.7 divide_convert_fusion.8
  505.1 0.9 copy.562
  506.0 12.1 %all-to-all-done.3 = bf16[8,2,32768]{2,1,0:T(2,128)(2,1)S(1)} async-done(((bf16[8,2,32768]{2,1,0:T(2,128)(2,1)}), bf16[8,2,32768]{2,1,0:T(2,128)(2,1)S(1)}, u32[]{:S(2)}, u32[]{:S(2)}) %all-to-all-start.3) | async-done | bytes 1048608 | tf_op jit(solution)/shard_map/all_to_all | solution.py:132
  518.1 1.0 reshape.949
  519.5 0.7 copy.539
  520.1 1.3 copy.561
  (276 shorter events, 17.1 us)
Async XLA Ops:
  7.2 15.7 %copy-start.80 = (s32[1,8]{1,0:T(1,128)S(1)}, s32[1,8]{1,0:T(1,128)}, u32[]{:S(2)}) copy-start(s32[1,8]{1,0:T(1,128)} %param.14) | copy-start | bytes 100
  7.2 16.1 %copy-start.53 = (bf16[1,128,4096]{2,1,0:T(8,128)(2,1)S(1)}, bf16[1,128,4096]{2,1,0:T(8,128)(2,1)}, u32[]{:S(2)}) copy-start(bf16[1,128,4096]{2,1,0:T(8,128)(2,1)} %param.11) | copy-start | bytes 3145732
  7.2 120.8 %all-gather.3.cloned.1.call-start = ((), (), s32[]{:S(2)}) async-start(), calls=%async_computation.6 | async-start | bytes 9437184 | tf_op jit(solution)/shard_map/all_gather | solution.py:96
  12.7 36.9 %all-to-all-start = ((bf16[8,2,8192]{2,1,0:T(2,128)(2,1)}), bf16[8,2,8192]{2,1,0:T(2,128)(2,1)S(1)}, u32[]{:S(2)}, u32[]{:S(2)}) async-start(bf16[8,2,8192]{2,1,0:T(2,128)(2,1)} %reshape.946), calls=%async_computation | async-start | bytes 524288 | tf_op jit(solution)/shard_map/all_to_all | solution.py:102
  49.6 38.1 %all-to-all-start.1 = ((bf16[8,2,32768]{2,1,0:T(2,128)(2,1)}), bf16[8,2,32768]{2,1,0:T(2,128)(2,1)S(1)}, u32[]{:S(2)}, u32[]{:S(2)}) async-start(bf16[8,2,32768]{2,1,0:T(2,128)(2,1)} %reshape.944), calls=%async_computation.1 | async-start | bytes 2097152 | tf_op jit(solution)/shard_map/all_to_all | solution.py:101
  87.7 20.0 %all-to-all-start.2 = ((bf16[8,2,32768]{2,1,0:T(2,128)(2,1)}), bf16[8,2,32768]{2,1,0:T(2,128)(2,1)}, u32[]{:S(2)}, u32[]{:S(2)}) async-start(bf16[8,2,32768]{2,1,0:T(2,128)(2,1)} %reshape.942), calls=%async_computation.2 | async-start | bytes 2097152 | tf_op jit(solution)/shard_map/all_to_all | solution.py:104
  92.5 281.7 %reduce-scatter.4.cloned.1.call-start = ((), (), s32[]{:S(2)}) async-start(), calls=%async_computation.8 | async-start | bytes 2129920 | tf_op jit(solution)/shard_map/reduce_scatter | solution.py:141
  95.6 16.9 %copy-start.6 = (bf16[1,128,8,128]{3,1,2,0:T(8,128)(2,1)}, bf16[1,128,8,128]{3,1,2,0:T(8,128)(2,1)S(1)}, u32[]{:S(2)}) copy-start(bf16[1,128,8,128]{3,1,2,0:T(8,128)(2,1)S(1)} %copy.479) | copy-start | bytes 786436
  112.3 1.8 copy-start.27
  112.3 1.8 copy-start.31
  112.4 1.8 copy-start.45
  112.4 2.0 copy-start.35
  112.4 2.5 copy-start.37
  112.4 3.2 copy-start.39
  112.4 3.7 copy-start.33
  112.4 1.4 copy-start.41
  112.4 1.4 copy-start.60
  116.9 1.5 copy-start.23
  117.0 4.3 copy-start.9
  117.0 4.3 copy-start.25
  117.0 4.3 copy-start.11
  117.0 5.5 %copy-start.15 = (bf16[1,1,128,512]{2,3,1,0:T(8,128)(2,1)}, bf16[1,1,128,512]{2,3,1,0:T(8,128)(2,1)S(1)}, u32[]{:S(2)}) copy-start(bf16[1,1,128,512]{2,3,1,0:T(8,128)(2,1)S(1)} %get-tuple-element.68) | copy-start | bytes 393220
  117.0 6.7 %copy-start.17 = (bf16[1,1,128,512]{2,3,1,0:T(8,128)(2,1)}, bf16[1,1,128,512]{2,3,1,0:T(8,128)(2,1)S(1)}, u32[]{:S(2)}) copy-start(bf16[1,1,128,512]{2,3,1,0:T(8,128)(2,1)S(1)} %get-tuple-element.67) | copy-start | bytes 393220
  117.0 7.9 %copy-start.19 = (bf16[1,1,128,512]{2,3,1,0:T(8,128)(2,1)}, bf16[1,1,128,512]{2,3,1,0:T(8,128)(2,1)S(1)}, u32[]{:S(2)}) copy-start(bf16[1,1,128,512]{2,3,1,0:T(8,128)(2,1)S(1)} %get-tuple-element.66) | copy-start | bytes 393220
  117.0 9.2 %copy-start.13 = (bf16[1,1,128,512]{2,3,1,0:T(8,128)(2,1)}, bf16[1,1,128,512]{2,3,1,0:T(8,128)(2,1)S(1)}, u32[]{:S(2)}) copy-start(bf16[1,1,128,512]{2,3,1,0:T(8,128)(2,1)S(1)} %get-tuple-element.69) | copy-start | bytes 393220
  123.7 1.2 copy-start.2
  124.9 1.2 copy-start.4
  135.1 239.2 %copy-start.66 = (bf16[64,128]{1,0:T(8,128)(2,1)S(1)}, bf16[64,128]{1,0:T(8,128)(2,1)}, u32[]{:S(2)}) copy-start(bf16[64,128]{1,0:T(8,128)(2,1)} %param.18) | copy-start | bytes 49156
  135.1 239.2 %copy-start.67 = (bf16[64,128]{1,0:T(8,128)(2,1)S(1)}, bf16[64,128]{1,0:T(8,128)(2,1)}, u32[]{:S(2)}) copy-start(bf16[64,128]{1,0:T(8,128)(2,1)} %param.16) | copy-start | bytes 49156
  135.1 239.2 %copy-start.69 = (f32[64,128]{1,0:T(8,128)S(1)}, f32[64,128]{1,0:T(8,128)}, u32[]{:S(2)}) copy-start(f32[64,128]{1,0:T(8,128)} %param.15) | copy-start | bytes 98308
  135.1 322.6 %all-gather.5.cloned.1.call-start = ((), (), s32[]{:S(2)}) async-start(), calls=%async_computation.7 | async-start | bytes 1064960 | tf_op jit(solution)/shard_map/all_gather | solution.py:95
  135.9 240.5 %copy-start.70 = (f32[64]{0:T(128)}, f32[64]{0:T(128)S(1)}, u32[]{:S(2)}) copy-start(f32[64]{0:T(128)S(1)} %mul.465) | copy-start | bytes 772
  136.1 240.3 %copy-start.72 = (f32[64]{0:T(128)}, f32[64]{0:T(128)S(1)}, u32[]{:S(2)}) copy-start(f32[64]{0:T(128)S(1)} %mul.477) | copy-start | bytes 772
  376.4 87.2 %copy-start.5 = (bf16[1,4,128,512]{2,3,1,0:T(8,128)(2,1)S(1)}, bf16[1,4,128,512]{2,3,1,0:T(8,128)(2,1)}, u32[]{:S(2)}) copy-start(bf16[1,4,128,512]{2,3,1,0:T(8,128)(2,1)} %copy-done.4) | copy-start | bytes 1572868
  376.4 87.2 %copy-start.20 = (bf16[1,1,128,512]{2,3,1,0:T(8,128)(2,1)S(1)}, bf16[1,1,128,512]{2,3,1,0:T(8,128)(2,1)}, u32[]{:S(2)}) copy-start(bf16[1,1,128,512]{2,3,1,0:T(8,128)(2,1)} %copy-done.19) | copy-start | bytes 393220
  463.6 1.5 copy-start.3
  463.7 1.5 copy-start.18
  465.1 1.2 copy-start.16
  465.7 1.2 copy-start.36
  466.1 1.2 copy-start.48
  466.3 1.2 copy-start.1
  466.4 1.2 copy-start.14
  467.3 1.2 copy-start.44
  467.6 1.2 copy-start.12
  468.8 1.2 copy-start.26
  469.1 1.5 copy-start.46
  469.4 1.5 copy-start.55
  469.7 1.5 copy-start.8
  469.7 1.5 copy-start.24
  470.0 1.6 copy-start.30
  470.3 1.6 copy-start.57
  470.3 1.8 copy-start.10
  470.3 1.8 copy-start.22
  470.6 2.0 copy-start.28
  477.3 21.0 %all-to-all-start.4 = ((bf16[8,2,8192]{2,1,0:T(2,128)(2,1)}), bf16[8,2,8192]{2,1,0:T(2,128)(2,1)S(1)}, u32[]{:S(2)}, u32[]{:S(2)}) async-start(bf16[8,2,8192]{2,1,0:T(2,128)(2,1)} %reshape.950), calls=%async_computation.4 | async-start | bytes 524288 | tf_op jit(solution)/shard_map/all_to_all | solution.py:133
  496.6 6.5 %copy-start.75 = (f32[64]{0:T(128)S(1)}, f32[64]{0:T(128)}, u32[]{:S(2)}) copy-start(f32[64]{0:T(128)} %get-tuple-element.57) | copy-start | bytes 772
  496.6 6.9 %copy-start.74 = (f32[64]{0:T(128)S(1)}, f32[64]{0:T(128)}, u32[]{:S(2)}) copy-start(f32[64]{0:T(128)} %get-tuple-element.56) | copy-start | bytes 772
  496.6 7.3 %copy-start.65 = (f32[64,128]{1,0:T(8,128)S(1)}, f32[64,128]{1,0:T(8,128)}, u32[]{:S(2)}) copy-start(f32[64,128]{1,0:T(8,128)} %reduce-scatter.4.cloned.1.call-done) | copy-start | bytes 98308
  496.6 7.3 %copy-start.68 = (bf16[64,128]{1,0:T(8,128)(2,1)S(1)}, bf16[64,128]{1,0:T(8,128)(2,1)}, u32[]{:S(2)}) copy-start(bf16[64,128]{1,0:T(8,128)(2,1)} %param.16) | copy-start | bytes 49156
  496.6 7.3 %copy-start.71 = (f32[64]{0:T(128)S(1)}, f32[64]{0:T(128)}, u32[]{:S(2)}) copy-start(f32[64]{0:T(128)} %copy-done.70) | copy-start | bytes 772
  496.6 7.3 %copy-start.73 = (f32[64]{0:T(128)S(1)}, f32[64]{0:T(128)}, u32[]{:S(2)}) copy-start(f32[64]{0:T(128)} %copy-done.72) | copy-start | bytes 772
  498.2 19.9 %all-to-all-start.3 = ((bf16[8,2,32768]{2,1,0:T(2,128)(2,1)}), bf16[8,2,32768]{2,1,0:T(2,128)(2,1)S(1)}, u32[]{:S(2)}, u32[]{:S(2)}) async-start(bf16[8,2,32768]{2,1,0:T(2,128)(2,1)} %reshape.948), calls=%async_computation.3 | async-start | bytes 2097152 | tf_op jit(solution)/shard_map/all_to_all | solution.py:132
  503.2 15.9 %copy-start.78 = (f32[32]{0:T(128)}, f32[32]{0:T(128)S(1)}, u32[]{:S(2)}) copy-start(f32[32]{0:T(128)S(1)} %reduce_max.118) | copy-start | bytes 388
  503.7 15.5 %copy-start.79 = (f32[32]{0:T(128)}, f32[32]{0:T(128)S(1)}, u32[]{:S(2)}) copy-start(f32[32]{0:T(128)S(1)} %reduce_max.122) | copy-start | bytes 388
  (25 other events, 24.3 us)
Sparse Core Ops, SparseCore 0:
  10.2 71.2 all-gather.2
  135.2 239.0 reduce-scatter.3
  378.3 79.3 all-gather.4
where the time goes:
time: 535 us; the launch traced here: 528 us
  waiting for transfers between devices  341 us (64%)
  other arithmetic  67.2 us (13%)
  local copies, waits for them, and re-layouts  38.7 us (7%)
  starting transfers between devices  35.3 us (7%)
  matrix products  30.2 us (6%)
  between operations  15.8 us (3%)
    reduce_scatter x1, waiting for transfers between devices, shards(): grad_w = lax.psum_scatter(term, 'dp', scatter_dimension=0, tiled=True)  238 us
    all_gather x1, waiting for transfers between devices, shards(): lax.all_gather(master.astype(jnp.bfloat16), 'dp', axis=0, tiled=True)  81.2 us
    unnamed x5, other arithmetic  57.2 us
    unnamed x191, local copies, waits for them, and re-layouts  31.5 us
    all_to_all x1, waiting for transfers between devices, shards(): lax.all_to_all(grad_query_heads, 'seq', split_axis=1, concat_axis=2, tile...  12.1 us
  transfers between devices with their start and end apart: 8, of which 4 were waited for; matrix products, arithmetic and copies ran while one was open for 19% of the time, Pallas kernels for 0%

commit v1 on v0

v1 whole, which is shorter than its diff:
```python
import functools
import math

import jax
import jax.numpy as jnp
from jax import lax
from jax.experimental import pallas as pl
from jax.experimental.pallas import tpu as pltpu
from jax.sharding import PartitionSpec as P

D = 4096
HD = 128
DOCS = 8
STEP = 1000
SEQ = 1024
GROUP = 4
QW = GROUP * HD
ROWS = 128
BLOCKS = SEQ // ROWS
MOST = 4
NEG = -1e30
INV_WIDTH = 1.0 / math.sqrt(D)
SCALE = 1.0 / math.sqrt(HD)
VMEM_LIMIT = 48 * 1024 * 1024
F32 = jnp.float32
BF16 = jnp.bfloat16


def dot(a, b):
    return jnp.dot(a, b, preferred_element_type=F32)


def stacked(block):
    return jnp.concatenate([block[:, a * HD : (a + 1) * HD] for a in range(GROUP)], axis=0)


def params():
    return pltpu.CompilerParams(vmem_limit_bytes=VMEM_LIMIT)


def pack_kernel(q_ref, c_ref, k_ref, out_ref):
    out_ref[0, :, 0:QW] = q_ref[...]
    out_ref[0, :, QW : 2 * QW] = c_ref[...]
    out_ref[0, :, 2 * QW :] = k_ref[...]


def pack(query, cot, key):
    tokens = query.shape[0]
    return pl.pallas_call(
        pack_kernel,
        grid=(8,),
        in_specs=[
            pl.BlockSpec((tokens, QW), lambda j: (0, j)),
            pl.BlockSpec((tokens, QW), lambda j: (0, j)),
            pl.BlockSpec((tokens, HD), lambda j: (0, j)),
        ],
        out_specs=pl.BlockSpec((1, tokens, 2 * QW + HD), lambda j: (j, 0, 0)),
        out_shape=jax.ShapeDtypeStruct((8, tokens, 2 * QW + HD), BF16),
        compiler_params=params(),
    )(query, cot, key)


def by_window(i, body):
    for count in range(1, MOST + 1):
        chosen = (i == count - 1) if count < MOST else (i >= MOST - 1)
        pl.when(chosen)(functools.partial(body, count))


def probs_kernel(lens_ref, r_ref, pt_ref, gv_ref, acc_ref):
    i = pl.program_id(0)

    @pl.when(i == 0)
    def _():
        acc_ref[...] = jnp.zeros_like(acc_ref)

    first = pl.multiple_of(i * ROWS, ROWS)

    def body(count):
        lower = pl.multiple_of((i + 1 - count) * ROWS, ROWS)
        queries = stacked(r_ref[pl.ds(first, ROWS), 0:QW])
        cot = stacked(r_ref[pl.ds(first, ROWS), QW : 2 * QW])
        lane = lax.broadcasted_iota(jnp.int32, (1, GROUP * ROWS), 1)
        position = first + jnp.bitwise_and(lane, ROWS - 1)
        start = jnp.zeros_like(position)
        end = jnp.int32(0)
        for k in range(DOCS):
            length = lens_ref[0, k]
            end = end + length
            start = start + jnp.where(position >= end, length, 0)
        row = lax.broadcasted_iota(jnp.int32, (ROWS, GROUP * ROWS), 0)
        first_row = start - lower
        last_row = position - lower
        scores = []
        highest = None
        for b in range(count):
            keys = r_ref[pl.ds(lower + b * ROWS, ROWS), 2 * QW :]
            tile = lax.dot_general(
                keys, queries, (((1,), (1,)), ((), ())), preferred_element_type=F32
            )
            allowed = row >= first_row - b * ROWS
            if b == count - 1:
                allowed = allowed & (row <= last_row - b * ROWS)
            tile = jnp.where(allowed, tile, NEG)
            top = jnp.max(tile, axis=0, keepdims=True)
            highest = top if highest is None else jnp.maximum(highest, top)
            scores.append(tile)
        total = None
        weights = []
        for tile in scores:
            weight = jnp.exp2((tile - highest) * (SCALE * math.log2(math.e)))
            part = jnp.sum(weight, axis=0, keepdims=True)
            total = part if total is None else total + part
            weights.append(weight)
        inverse = 1.0 / total
        for b in range(count):
            probs = (weights[b] * inverse).astype(BF16)
            pt_ref[0, b * ROWS : (b + 1) * ROWS, :] = probs
            rows = pl.ds(lower + b * ROWS, ROWS)
            acc_ref[rows, :] = acc_ref[rows, :] + dot(probs, cot)

    by_window(i, body)

    @pl.when(i == BLOCKS - 1)
    def _():
        gv_ref[...] = acc_ref[...].astype(BF16)


def probs_call(doc_lens, packed):
    width = 2 * QW + HD
    return pl.pallas_call(
        probs_kernel,
        grid=(BLOCKS,),
        in_specs=[
            pl.BlockSpec(memory_space=pltpu.SMEM),
            pl.BlockSpec((SEQ, width), lambda i: (0, 0)),
        ],
        out_specs=[
            pl.BlockSpec((1, MOST * ROWS, GROUP * ROWS), lambda i: (i, 0, 0)),
            pl.BlockSpec((SEQ, HD), lambda i: (0, 0)),
        ],
        out_shape=[
            jax.ShapeDtypeStruct((BLOCKS, MOST * ROWS, GROUP * ROWS), BF16),
            jax.ShapeDtypeStruct((SEQ, HD), BF16),
        ],
        scratch_shapes=[pltpu.VMEM((SEQ, HD), F32)],
        compiler_params=params(),
    )(doc_lens, packed)


def project_kernel(h_ref, w_ref, gv_ref, val_ref, term_ref, acc_ref, gvt_ref):
    j = pl.program_id(0)

    @pl.when(j == 0)
    def _():
        acc_ref[...] = jnp.zeros_like(acc_ref)
        gvt_ref[...] = gv_ref[...].T

    hidden = h_ref[...]
    term = dot(gvt_ref[...], hidden)
    term_ref[...] = (term.T * INV_WIDTH).astype(BF16)
    acc_ref[...] = acc_ref[...] + dot(hidden, w_ref[...])

    @pl.when(j == pl.num_programs(0) - 1)
    def _():
        val_ref[...] = (acc_ref[...] * INV_WIDTH).astype(BF16)


def project_call(whole, weight, grad_values):
    step = 512
    return pl.pallas_call(
        project_kernel,
        grid=(D // step,),
        in_specs=[
            pl.BlockSpec((SEQ, step), lambda j: (0, j)),
            pl.BlockSpec((step, HD), lambda j: (j, 0)),
            pl.BlockSpec((SEQ, HD), lambda j: (0, 0)),
        ],
        out_specs=[
            pl.BlockSpec((SEQ, HD), lambda j: (0, 0)),
            pl.BlockSpec((step, HD), lambda j: (j, 0)),
        ],
        out_shape=[
            jax.ShapeDtypeStruct((SEQ, HD), BF16),
            jax.ShapeDtypeStruct((D, HD), BF16),
        ],
        scratch_shapes=[pltpu.VMEM((SEQ, HD), F32), pltpu.VMEM((HD, SEQ), BF16)],
        compiler_params=params(),
    )(whole, weight, grad_values)


def grads_kernel(r_ref, pt_ref, val_ref, out_ref, acc_ref, kt_ref, vt_ref):
    i = pl.program_id(0)

    @pl.when(i == 0)
    def _():
        acc_ref[...] = jnp.zeros_like(acc_ref)
        kt_ref[...] = r_ref[:, 2 * QW :].T
        vt_ref[...] = val_ref[...].T

    first = pl.multiple_of(i * ROWS, ROWS)

    def body(count):
        lower = pl.multiple_of((i + 1 - count) * ROWS, ROWS)
        size = count * ROWS
        queries = stacked(r_ref[pl.ds(first, ROWS), 0:QW])
        cot_t = stacked(r_ref[pl.ds(first, ROWS), QW : 2 * QW]).T
        attn_t = dot(vt_ref[:, pl.ds(lower, size)], pt_ref[0, 0:size, :]).astype(BF16)
        delta = jnp.sum(attn_t.astype(F32) * cot_t.astype(F32), axis=0, keepdims=True)
        grads = []
        for b in range(count):
            rows = pl.ds(lower + b * ROWS, ROWS)
            prob_grad = dot(val_ref[rows, :], cot_t)
            probs = pt_ref[0, b * ROWS : (b + 1) * ROWS, :].astype(F32)
            score_grad = (probs * (prob_grad - delta)).astype(BF16)
            acc_ref[rows, :] = acc_ref[rows, :] + dot(score_grad, queries)
            grads.append(score_grad)
        grad_t = dot(kt_ref[:, pl.ds(lower, size)], jnp.concatenate(grads, axis=0)) * SCALE
        grad = grad_t.T.astype(BF16)
        for a in range(GROUP):
            out_ref[pl.ds(first, ROWS), a * HD : (a + 1) * HD] = grad[a * ROWS : (a + 1) * ROWS, :]

    by_window(i, body)

    @pl.when(i == BLOCKS - 1)
    def _():
        out_ref[:, QW:] = (acc_ref[...] * SCALE).astype(BF16)


def grads_call(packed, probs, values):
    width = 2 * QW + HD
    return pl.pallas_call(
        grads_kernel,
        grid=(BLOCKS,),
        in_specs=[
            pl.BlockSpec((SEQ, width), lambda i: (0, 0)),
            pl.BlockSpec((1, MOST * ROWS, GROUP * ROWS), lambda i: (i, 0, 0)),
            pl.BlockSpec((SEQ, HD), lambda i: (0, 0)),
        ],
        out_specs=pl.BlockSpec((SEQ, QW + HD), lambda i: (0, 0)),
        out_shape=jax.ShapeDtypeStruct((SEQ, QW + HD), BF16),
        scratch_shapes=[
            pltpu.VMEM((SEQ, HD), F32),
            pltpu.VMEM((HD, SEQ), BF16),
            pltpu.VMEM((HD, SEQ), BF16),
        ],
        compiler_params=params(),
    )(packed, probs, values)


def unpack_kernel(in_ref, q_ref, k_ref):
    q_ref[...] = in_ref[0, :, 0:QW]
    k_ref[...] = in_ref[0, :, QW:]


def unpack(back):
    tokens = back.shape[1]
    return pl.pallas_call(
        unpack_kernel,
        grid=(8,),
        in_specs=[pl.BlockSpec((1, tokens, QW + HD), lambda j: (j, 0, 0))],
        out_specs=[
            pl.BlockSpec((tokens, QW), lambda j: (0, j)),
            pl.BlockSpec((tokens, HD), lambda j: (0, j)),
        ],
        out_shape=[
            jax.ShapeDtypeStruct((tokens, 8 * QW), BF16),
            jax.ShapeDtypeStruct((tokens, 8 * HD), BF16),
        ],
        compiler_params=params(),
    )(back)


def adam_kernel(
    parts_ref,
    master_ref,
    mc_ref,
    ms_ref,
    vc_ref,
    vs_ref,
    master_out,
    mc_out,
    ms_out,
    vc_out,
    vs_out,
    grad_ref,
    mold_ref,
    vold_ref,
    step_ref,
    mcode_ref,
    vcode_ref,
):
    total = jnp.zeros(grad_ref.shape, F32)
    for g in range(parts_ref.shape[0]):
        total = total + parts_ref[g].astype(F32)
    grad_ref[...] = total
    mold_ref[...] = mc_ref[...].astype(F32)
    vold_ref[...] = vc_ref[...].astype(F32)
    half = grad_ref.shape[0] // 2
    first_fix = 1.0 - 0.9**STEP
    second_fix = 1.0 - 0.999**STEP
    news = []
    for odd in range(2):
        rows = pl.ds(odd, half, stride=2)
        grad = grad_ref[rows, :]
        m_new = 0.9 * (mold_ref[rows, :] * ms_ref[...]) + 0.1 * grad
        v_new = 0.999 * (vold_ref[rows, :] * vs_ref[...]) + 0.001 * grad * grad
        step_ref[rows, :] = m_new / first_fix / (jnp.sqrt(v_new / second_fix) + 1e-08)
        news.append((m_new, v_new))
    m_top = jnp.maximum(
        jnp.max(jnp.abs(news[0][0]), axis=1, keepdims=True),
        jnp.max(jnp.abs(news[1][0]), axis=1, keepdims=True),
    )
    v_top = jnp.maximum(
        jnp.max(jnp.abs(news[0][1]), axis=1, keepdims=True),
        jnp.max(jnp.abs(news[1][1]), axis=1, keepdims=True),
    )
    ms_out[...] = m_top
    vs_out[...] = v_top
    for odd in range(2):
        rows = pl.ds(odd, half, stride=2)
        mcode_ref[rows, :] = news[odd][0] / (m_top + 1e-06)
        vcode_ref[rows, :] = news[odd][1] / (v_top + 1e-06)
    mc_out[...] = mcode_ref[...].astype(BF16)
    vc_out[...] = vcode_ref[...].astype(BF16)
    master_out[...] = master_ref[...] - 0.01 * step_ref[...]


def adam_call(parts, master, m_code, m_scale, v_code, v_scale):
    shape = master.shape
    return pl.pallas_call(
        adam_kernel,
        out_shape=[
            jax.ShapeDtypeStruct(shape, F32),
            jax.ShapeDtypeStruct(shape, BF16),
            jax.ShapeDtypeStruct(m_scale.shape, F32),
            jax.ShapeDtypeStruct(shape, BF16),
            jax.ShapeDtypeStruct(v_scale.shape, F32),
        ],
        scratch_shapes=[pltpu.VMEM(shape, F32) for _ in range(6)],
        compiler_params=params(),
    )(parts, master, m_code, m_scale, v_code, v_scale)


def shards(hidden, query, key, grad_out, doc_lens, master, m_code, m_scale, v_code, v_scale):
    n_dp = lax.axis_size("dp")
    packed = pack(query[0], grad_out[0], key[0])
    packed = lax.all_to_all(packed, "seq", split_axis=0, concat_axis=0, tiled=True)
    packed = packed.reshape(SEQ, 2 * QW + HD)
    whole = lax.all_gather(hidden[0], "seq", axis=0, tiled=True)
    copies = jnp.broadcast_to(master.astype(BF16)[None], (n_dp,) + master.shape)
    weight = lax.all_to_all(copies, "dp", split_axis=0, concat_axis=0, tiled=True)
    weight = weight.reshape(D, HD)
    probs, grad_values = probs_call(doc_lens, packed)
    values, term = project_call(whole, weight, grad_values)
    parts = lax.all_to_all(
        term.reshape((n_dp,) + master.shape), "dp", split_axis=0, concat_axis=0, tiled=True
    )
    grads = grads_call(packed, probs, values)
    back = lax.all_to_all(
        grads.reshape(8, ROWS, QW + HD), "seq", split_axis=0, concat_axis=0, tiled=True
    )
    grad_query, grad_key = unpack(back)
    state = adam_call(parts, master, m_code, m_scale, v_code, v_scale)
    return (grad_query[None], grad_key[None]) + tuple(state)


def solution(mesh):
    return jax.shard_map(
        shards,
        mesh=mesh,
        in_specs=(
            P("dp", "seq", None),
            P("dp", "seq", None),
            P("dp", "seq", None),
            P("dp", "seq", None),
            P("dp", None),
            P("dp", "seq"),
            P("dp", "seq"),
            P("dp", "seq"),
            P("dp", "seq"),
            P("dp", "seq"),
        ),
        out_specs=(
            P("dp", "seq", None),
            P("dp", "seq", None),
            P("dp", "seq"),
            P("dp", "seq"),
            P("dp", "seq"),
            P("dp", "seq"),
            P("dp", "seq"),
        ),
        check_vma=False,
    )
```

time: 535 us -> 201 us (0.38)
  the two profiles are of different devices: /device:TPU:1 before, /device:TPU:16 now
where the time goes in v1:
time: 201 us; the launch traced here: 200 us
  waiting for transfers between devices  92.2 us (46%)
  starting transfers between devices  32.2 us (16%)
  Pallas kernels  30.7 us (15%)
  blocking collectives  21.4 us (11%)
  between operations  14.1 us (7%)
  local copies, waits for them, and re-layouts  9.11 us (5%)
    all_to_all x1, waiting for transfers between devices, shards(): lax.all_to_all(packed, 'seq', split_axis=0, concat_axis=0, tiled=True)  43.7 us
    all_to_all x1, waiting for transfers between devices, shards(): lax.all_to_all(term.reshape((n_dp,) + master.shape), 'dp', split_axis=0,...  27.2 us
    all_to_all x1, starting transfers between devices, shards(): lax.all_to_all(copies, 'dp', split_axis=0, concat_axis=0, tiled=True)  21.7 us
    all_to_all x1, blocking collectives, shards(): lax.all_to_all(grads.reshape(8, ROWS, QW + HD), 'seq', split_axis=0, conc...  21.4 us
    all_to_all x1, waiting for transfers between devices, shards(): lax.all_to_all(copies, 'dp', split_axis=0, concat_axis=0, tiled=True)  20.6 us
    pallas_call x1, Pallas kernels, grads_call(): pl.pallas_call(grads_kernel, grid=(BLOCKS,), in_specs=[pl.BlockSpec((SEQ,...  9.43 us
    pallas_call x1, Pallas kernels, project_call(): pl.pallas_call(project_kernel, grid=(D // step,), in_specs=[pl.BlockSpec(...  9.08 us
    pallas_call x1, Pallas kernels, probs_call(): pl.pallas_call(probs_kernel, grid=(BLOCKS,), in_specs=[pl.BlockSpec(memor...  7.96 us
  transfers between devices with their start and end apart: 4, of which 3 were waited for; matrix products, arithmetic and copies ran while one was open for 1% of the time, Pallas kernels for 6%

profile of v1, /device:TPU:16, one launch (start us, length us, event | category | flops | bytes accessed | tf_op | source)
XLA Modules:
  0.0 199.7 jit_solution(9192690278728170552)
XLA Ops:
  7.2 0.0 all-gather.3.cloned.1.call-start
  7.2 0.7 all-gather.3.cloned.1.call-update
  7.9 0.0 copy-start.1
  7.9 1.2 copy-done.1
  9.1 0.0 copy-start.2
  9.1 1.2 copy-done.2
  10.4 0.0 copy-start.3
  10.4 0.9 copy-done.3
  11.3 0.6 shard_map.153
  11.9 0.0 copy-start
  11.9 1.5 copy-done
  13.4 0.0 copy-start.6
  13.4 4.4 %all-to-all-start = ((bf16[8,128,1152]{2,1,0:T(8,128)(2,1)}), bf16[8,128,1152]{2,1,0:T(8,128)(2,1)S(1)}, u32[]{:S(2)}, u32[]{:S(2)}) async-start(bf16[8,128,1152]{2,1,0:T(8,128)(2,1)} %copy-done), calls=%async_computation | async-start | bytes 4718592 | tf_op jit(solution)/shard_map/all_to_all | solution.py:347
  17.8 0.0 copy-done.6
  17.8 0.0 copy-start.9
  17.8 43.7 %all-to-all-done = bf16[8,128,1152]{2,1,0:T(8,128)(2,1)S(1)} async-done(((bf16[8,128,1152]{2,1,0:T(8,128)(2,1)}), bf16[8,128,1152]{2,1,0:T(8,128)(2,1)S(1)}, u32[]{:S(2)}, u32[]{:S(2)}) %all-to-all-start) | async-done | bytes 2359328 | tf_op jit(solution)/shard_map/all_to_all | solution.py:347
  61.5 1.2 broadcast_in_dim.12
  62.8 21.7 %all-to-all-start.1 = ((bf16[64,64,128]{2,1,0:T(8,128)(2,1)}), bf16[64,64,128]{2,1,0:T(8,128)(2,1)S(1)}, u32[]{:S(2)}, u32[]{:S(2)}) async-start(bf16[64,64,128]{2,1,0:T(8,128)(2,1)} %broadcast_in_dim.12), calls=%async_computation.1 | async-start | bytes 2097152 | tf_op jit(solution)/shard_map/all_to_all | solution.py:351
  84.5 0.0 copy-done.9
  84.5 8.0 %shard_map.154 = (bf16[8,512,512]{2,1,0:T(8,128)(2,1)}, bf16[1024,128]{1,0:T(8,128)(2,1)S(1)}) custom-call(s32[1,8]{1,0:T(1,128)S(1)} %copy-done.9, bf16[1024,1152]{1,0:T(8,128)(2,1)S(1)} %bitcast.10), custom_call_target="tpu_custom_call" | custom-call | tf_op jit(solution)/shard_map/pallas_call | solution.py:130
  92.5 0.0 copy-start.4
  92.5 0.7 copy-done.4
  93.2 20.6 %all-to-all-done.1 = bf16[64,64,128]{2,1,0:T(8,128)(2,1)S(1)} async-done(((bf16[64,64,128]{2,1,0:T(8,128)(2,1)}), bf16[64,64,128]{2,1,0:T(8,128)(2,1)S(1)}, u32[]{:S(2)}, u32[]{:S(2)}) %all-to-all-start.1) | async-done | bytes 1048608 | tf_op jit(solution)/shard_map/all_to_all | solution.py:351
  113.8 0.0 all-gather.3.cloned.1.call-done
  113.8 0.0 copy-start.5
  113.8 0.9 copy-done.5
  114.8 9.1 %shard_map.155 = (bf16[1024,128]{1,0:T(8,128)(2,1)S(1)}, bf16[4096,128]{1,0:T(8,128)(2,1)}) custom-call(bf16[1024,4096]{1,0:T(8,128)(2,1)} %bitcast.17, bf16[4096,128]{1,0:T(8,128)(2,1)S(1)} %bitcast.13, bf16[1024,128]{1,0:T(8,128)(2,1)S(1)} %copy-done.5), custom_call_target="tpu_custom_call" | custom-call | tf_op jit(solution)/shard_map/pallas_call | solution.py:170
  123.8 9.4 %shard_map.156 = bf16[1024,640]{1,0:T(8,128)(2,1)S(1)} custom-call(bf16[1024,1152]{1,0:T(8,128)(2,1)S(1)} %bitcast.11, bf16[8,512,512]{2,1,0:T(8,128)(2,1)} %get-tuple-element.18.pt_ref, bf16[1024,128]{1,0:T(8,128)(2,1)S(1)} %get-tuple-element.20.val_ref), custom_call_target="tpu_custom_call" | custom-call | tf_op jit(solution)/shard_map/pallas_call | solution.py:231
  133.3 0.0 copy-start.10
  133.3 0.0 copy-start.11
  133.3 21.4 %all_to_all.20.in_ref = bf16[8,128,640]{2,1,0:T(8,128)(2,1)S(1)} all-to-all(bf16[8,128,640]{2,1,0:T(8,128)(2,1)S(1)} %bitcast.12), channel_id=1, replica_groups=mesh['seq'=8,'dp'=64] {'seq'}, dimensions={0} | all-to-all | bytes 2621440 | tf_op jit(solution)/shard_map/all_to_all | solution.py:359
  154.7 0.0 copy-start.7
  154.7 0.0 copy-start.8
  154.7 6.0 %all-to-all-start.3 = ((bf16[64,64,128]{2,1,0:T(8,128)(2,1)}), bf16[64,64,128]{2,1,0:T(8,128)(2,1)S(1)}, u32[]{:S(2)}, u32[]{:S(2)}) async-start(bf16[64,64,128]{2,1,0:T(8,128)(2,1)} %bitcast.9), calls=%async_computation.3 | async-start | bytes 2097152 | tf_op jit(solution)/shard_map/all_to_all | solution.py:355
  160.7 0.0 copy-done.10
  160.7 0.1 copy.17.ms_ref
  160.8 0.0 copy-done.11
  160.8 0.1 copy.18.vs_ref
  160.9 2.7 %shard_map.157 = (bf16[128,4096]{1,0:T(8,128)(2,1)}, bf16[128,1024]{1,0:T(8,128)(2,1)}) custom-call(bf16[8,128,640]{2,1,0:T(8,128)(2,1)S(1)} %all_to_all.20.in_ref), custom_call_target="tpu_custom_call" | custom-call | tf_op jit(solution)/shard_map/pallas_call | solution.py:257
  163.6 27.2 %all-to-all-done.3.parts_ref = bf16[64,64,128]{2,1,0:T(8,128)(2,1)S(1)} async-done(((bf16[64,64,128]{2,1,0:T(8,128)(2,1)}), bf16[64,64,128]{2,1,0:T(8,128)(2,1)S(1)}, u32[]{:S(2)}, u32[]{:S(2)}) %all-to-all-start.3) | async-done | bytes 1048608 | tf_op jit(solution)/shard_map/all_to_all | solution.py:355
  190.8 0.0 copy-done.7
  190.8 0.0 copy-done.8
  190.8 0.9 shard_map.158
  191.7 0.6 copy.19
  192.3 0.6 copy.20
  (1 shorter events, 0.0 us)
Async XLA Ops:
  7.2 106.6 %all-gather.3.cloned.1.call-start = ((), (), s32[]{:S(2)}) async-start(), calls=%async_computation.4 | async-start | bytes 9437184 | tf_op jit(solution)/shard_map/all_gather | solution.py:349
  7.9 1.2 copy-start.1
  9.1 1.2 copy-start.2
  10.4 0.9 copy-start.3
  11.9 1.5 copy-start
  13.4 4.4 %copy-start.6 = (f32[64,128]{1,0:T(8,128)S(1)}, f32[64,128]{1,0:T(8,128)}, u32[]{:S(2)}) copy-start(f32[64,128]{1,0:T(8,128)} %master_ref.1) | copy-start | bytes 98308
  13.4 48.2 %all-to-all-start = ((bf16[8,128,1152]{2,1,0:T(8,128)(2,1)}), bf16[8,128,1152]{2,1,0:T(8,128)(2,1)S(1)}, u32[]{:S(2)}, u32[]{:S(2)}) async-start(bf16[8,128,1152]{2,1,0:T(8,128)(2,1)} %copy-done), calls=%async_computation | async-start | bytes 4718592 | tf_op jit(solution)/shard_map/all_to_all | solution.py:347
  17.8 66.7 %copy-start.9 = (s32[1,8]{1,0:T(1,128)S(1)}, s32[1,8]{1,0:T(1,128)}, u32[]{:S(2)}) copy-start(s32[1,8]{1,0:T(1,128)} %lens_ref.1) | copy-start | bytes 100
  62.8 51.0 %all-to-all-start.1 = ((bf16[64,64,128]{2,1,0:T(8,128)(2,1)}), bf16[64,64,128]{2,1,0:T(8,128)(2,1)S(1)}, u32[]{:S(2)}, u32[]{:S(2)}) async-start(bf16[64,64,128]{2,1,0:T(8,128)(2,1)} %broadcast_in_dim.12), calls=%async_computation.1 | async-start | bytes 2097152 | tf_op jit(solution)/shard_map/all_to_all | solution.py:351
  92.5 0.7 copy-start.4
  113.8 1.0 copy-start.5
  133.3 27.4 %copy-start.10 = (f32[32,1]{0,1:T(1,128)S(1)}, f32[32,1]{0,1:T(1,128)}, u32[]{:S(2)}) copy-start(f32[32,1]{0,1:T(1,128)} %param.17) | copy-start | bytes 388
  133.3 27.5 %copy-start.11 = (f32[32,1]{0,1:T(1,128)S(1)}, f32[32,1]{0,1:T(1,128)}, u32[]{:S(2)}) copy-start(f32[32,1]{0,1:T(1,128)} %param.19) | copy-start | bytes 388
  154.7 36.1 %copy-start.7 = (bf16[64,128]{1,0:T(8,128)(2,1)S(1)}, bf16[64,128]{1,0:T(8,128)(2,1)}, u32[]{:S(2)}) copy-start(bf16[64,128]{1,0:T(8,128)(2,1)} %mc_ref.1) | copy-start | bytes 49156
  154.7 36.1 %copy-start.8 = (bf16[64,128]{1,0:T(8,128)(2,1)S(1)}, bf16[64,128]{1,0:T(8,128)(2,1)}, u32[]{:S(2)}) copy-start(bf16[64,128]{1,0:T(8,128)(2,1)} %vc_ref.1) | copy-start | bytes 49156
  154.7 36.1 %all-to-all-start.3 = ((bf16[64,64,128]{2,1,0:T(8,128)(2,1)}), bf16[64,64,128]{2,1,0:T(8,128)(2,1)S(1)}, u32[]{:S(2)}, u32[]{:S(2)}) async-start(bf16[64,64,128]{2,1,0:T(8,128)(2,1)} %bitcast.9), calls=%async_computation.3 | async-start | bytes 2097152 | tf_op jit(solution)/shard_map/all_to_all | solution.py:355
Sparse Core Ops, SparseCore 0:
  10.2 72.8 all-gather.2

commit v2 on v1

--- a/solution.py
+++ b/solution.py
@@ -38,26 +38,78 @@
     return pltpu.CompilerParams(vmem_limit_bytes=VMEM_LIMIT)
 
 
-def pack_kernel(q_ref, c_ref, k_ref, out_ref):
-    out_ref[0, :, 0:QW] = q_ref[...]
-    out_ref[0, :, QW : 2 * QW] = c_ref[...]
-    out_ref[0, :, 2 * QW :] = k_ref[...]
-
-
-def pack(query, cot, key):
+XS = 4
+HOPS = [(0, 0), (0, 1), (1, 0), (3, 0), (1, 1), (3, 1), (2, 0), (2, 1)]
+
+
+def hop(value, k):
+    dx, dc = HOPS[k]
+    return lax.rem(lax.div(value, 2) + dx, XS) * 2 + jnp.bitwise_xor(lax.rem(value, 2), dc)
+
+
+def perm(k):
+    dx, dc = HOPS[k]
+    return [(s, ((s // 2 + dx) % XS) * 2 + ((s % 2) ^ dc)) for s in range(2 * XS)]
+
+
+def send(array, k):
+    return lax.ppermute(array, "seq", perm(k))
+
+
+ANYWHERE = pl.BlockSpec(memory_space=pl.ANY)
+SCALARS = pl.BlockSpec(memory_space=pltpu.SMEM)
+
+
+def run_copies(copies):
+    for copy in copies:
+        copy.start()
+    for copy in copies:
+        copy.wait()
+
+
+def pack_kernel(to_ref, q_ref, c_ref, k_ref, *refs):
+    outs, sems = refs[:-1], refs[-1]
+    copies = []
+    for r, out in enumerate(outs):
+        j = to_ref[r]
+        wide = pl.ds(pl.multiple_of(j * QW, QW), QW)
+        thin = pl.ds(pl.multiple_of(j * HD, HD), HD)
+        for n, (src, lanes, place) in enumerate(
+            [
+                (q_ref, wide, pl.ds(0, QW)),
+                (c_ref, wide, pl.ds(QW, QW)),
+                (k_ref, thin, pl.ds(2 * QW, HD)),
+            ]
+        ):
+            copies.append(
+                pltpu.make_async_copy(src.at[:, lanes], out.at[:, place], sems.at[3 * r + n])
+            )
+    run_copies(copies)
+
+
+def pack(to, query, cot, key):
     tokens = query.shape[0]
     return pl.pallas_call(
         pack_kernel,
-        grid=(8,),
-        in_specs=[
-            pl.BlockSpec((tokens, QW), lambda j: (0, j)),
-            pl.BlockSpec((tokens, QW), lambda j: (0, j)),
-            pl.BlockSpec((tokens, HD), lambda j: (0, j)),
-        ],
-        out_specs=pl.BlockSpec((1, tokens, 2 * QW + HD), lambda j: (j, 0, 0)),
-        out_shape=jax.ShapeDtypeStruct((8, tokens, 2 * QW + HD), BF16),
+        in_specs=[SCALARS, ANYWHERE, ANYWHERE, ANYWHERE],
+        out_specs=[ANYWHERE] * 8,
+        out_shape=[jax.ShapeDtypeStruct((tokens, 2 * QW + HD), BF16)] * 8,
+        scratch_shapes=[pltpu.SemaphoreType.DMA((24,))],
         compiler_params=params(),
-    )(query, cot, key)
+    )(to, query, cot, key)
+
+
+def gather_pieces(from_ref, piece_refs, whole_ref, sems):
+    run_copies(
+        [
+            pltpu.make_async_copy(
+                piece,
+                whole_ref.at[pl.ds(pl.multiple_of(from_ref[r] * ROWS, ROWS), ROWS), :],
+                sems.at[r],
+            )
+            for r, piece in enumerate(piece_refs)
+        ]
+    )
 
 
 def by_window(i, body):
@@ -66,11 +118,13 @@
         pl.when(chosen)(functools.partial(body, count))
 
 
-def probs_kernel(lens_ref, r_ref, pt_ref, gv_ref, acc_ref):
+def probs_kernel(lens_ref, from_ref, *refs):
+    pieces, (pt_ref, gv_ref, r_ref, acc_ref, sems) = refs[:8], refs[8:]
     i = pl.program_id(0)
 
     @pl.when(i == 0)
     def _():
+        gather_pieces(from_ref, pieces, r_ref, sems)
         acc_ref[...] = jnp.zeros_like(acc_ref)
 
     first = pl.multiple_of(i * ROWS, ROWS)
@@ -125,15 +179,12 @@
         gv_ref[...] = acc_ref[...].astype(BF16)
 
 
-def probs_call(doc_lens, packed):
+def probs_call(doc_lens, origin, pieces):
     width = 2 * QW + HD
     return pl.pallas_call(
         probs_kernel,
         grid=(BLOCKS,),
-        in_specs=[
-            pl.BlockSpec(memory_space=pltpu.SMEM),
-            pl.BlockSpec((SEQ, width), lambda i: (0, 0)),
-        ],
+        in_specs=[SCALARS, SCALARS] + [ANYWHERE] * 8,
         out_specs=[
             pl.BlockSpec((1, MOST * ROWS, GROUP * ROWS), lambda i: (i, 0, 0)),
             pl.BlockSpec((SEQ, HD), lambda i: (0, 0)),
@@ -142,36 +193,47 @@
             jax.ShapeDtypeStruct((BLOCKS, MOST * ROWS, GROUP * ROWS), BF16),
             jax.ShapeDtypeStruct((SEQ, HD), BF16),
         ],
-        scratch_shapes=[pltpu.VMEM((SEQ, HD), F32)],
+        scratch_shapes=[
+            pltpu.VMEM((SEQ, width), BF16),
+            pltpu.VMEM((SEQ, HD), F32),
+            pltpu.SemaphoreType.DMA((8,)),
+        ],
         compiler_params=params(),
-    )(doc_lens, packed)
-
-
-def project_kernel(h_ref, w_ref, gv_ref, val_ref, term_ref, acc_ref, gvt_ref):
+    )(doc_lens, origin, *pieces)
+
+
+def project_kernel(from_ref, *refs):
+    hidden_refs, (w_ref, gv_ref, val_ref, term_ref, acc_ref, gvt_ref) = refs[:10], refs[10:]
     j = pl.program_id(0)
 
     @pl.when(j == 0)
     def _():
         acc_ref[...] = jnp.zeros_like(acc_ref)
-        gvt_ref[...] = gv_ref[...].T
-
-    hidden = h_ref[...]
+        for r in range(8):
+            rows = pl.ds(pl.multiple_of(from_ref[r] * ROWS, ROWS), ROWS)
+            gvt_ref[:, r * ROWS : (r + 1) * ROWS] = gv_ref[rows, :].T
+
+    hidden = jnp.concatenate([ref[...] for ref in hidden_refs], axis=0)
     term = dot(gvt_ref[...], hidden)
     term_ref[...] = (term.T * INV_WIDTH).astype(BF16)
     acc_ref[...] = acc_ref[...] + dot(hidden, w_ref[...])
 
     @pl.when(j == pl.num_programs(0) - 1)
     def _():
-        val_ref[...] = (acc_ref[...] * INV_WIDTH).astype(BF16)
-
-
-def project_call(whole, weight, grad_values):
+        for r in range(8):
+            rows = pl.ds(pl.multiple_of(from_ref[r] * ROWS, ROWS), ROWS)
+            part = acc_ref[r * ROWS : (r + 1) * ROWS, :]
+            val_ref[rows, :] = (part * INV_WIDTH).astype(BF16)
+
+
+def project_call(origin, pieces, weight, grad_values):
     step = 512
     return pl.pallas_call(
         project_kernel,
         grid=(D // step,),
-        in_specs=[
-            pl.BlockSpec((SEQ, step), lambda j: (0, j)),
+        in_specs=[SCALARS]
+        + [pl.BlockSpec((piece.shape[0], step), lambda j: (0, j)) for piece in pieces]
+        + [
             pl.BlockSpec((step, HD), lambda j: (j, 0)),
             pl.BlockSpec((SEQ, HD), lambda j: (0, 0)),
         ],
@@ -185,14 +247,17 @@
         ],
         scratch_shapes=[pltpu.VMEM((SEQ, HD), F32), pltpu.VMEM((HD, SEQ), BF16)],
         compiler_params=params(),
-    )(whole, weight, grad_values)
-
-
-def grads_kernel(r_ref, pt_ref, val_ref, out_ref, acc_ref, kt_ref, vt_ref):
+    )(origin, *pieces, weight, grad_values)
+
+
+def grads_kernel(from_ref, to_ref, *refs):
+    pieces, (pt_ref, val_ref), outs = refs[:8], refs[8:10], refs[10:18]
+    r_ref, out_ref, acc_ref, kt_ref, vt_ref, sems = refs[18:]
     i = pl.program_id(0)
 
     @pl.when(i == 0)
     def _():
+        gather_pieces(from_ref, pieces, r_ref, sems)
         acc_ref[...] = jnp.zeros_like(acc_ref)
         kt_ref[...] = r_ref[:, 2 * QW :].T
         vt_ref[...] = val_ref[...].T
@@ -224,50 +289,71 @@
     @pl.when(i == BLOCKS - 1)
     def _():
         out_ref[:, QW:] = (acc_ref[...] * SCALE).astype(BF16)
-
-
-def grads_call(packed, probs, values):
+        run_copies(
+            [
+                pltpu.make_async_copy(
+                    out_ref.at[pl.ds(pl.multiple_of(to_ref[r] * ROWS, ROWS), ROWS), :],
+                    out,
+                    sems.at[r],
+                )
+                for r, out in enumerate(outs)
+            ]
+        )
+
+
+def grads_call(origin, to, pieces, probs, values):
     width = 2 * QW + HD
     return pl.pallas_call(
         grads_kernel,
         grid=(BLOCKS,),
-        in_specs=[
-            pl.BlockSpec((SEQ, width), lambda i: (0, 0)),
+        in_specs=[SCALARS, SCALARS]
+        + [ANYWHERE] * 8
+        + [
             pl.BlockSpec((1, MOST * ROWS, GROUP * ROWS), lambda i: (i, 0, 0)),
             pl.BlockSpec((SEQ, HD), lambda i: (0, 0)),
         ],
-        out_specs=pl.BlockSpec((SEQ, QW + HD), lambda i: (0, 0)),
-        out_shape=jax.ShapeDtypeStruct((SEQ, QW + HD), BF16),
+        out_specs=[ANYWHERE] * 8,
+        out_shape=[jax.ShapeDtypeStruct((ROWS, QW + HD), BF16)] * 8,
         scratch_shapes=[
+            pltpu.VMEM((SEQ, width), BF16),
+            pltpu.VMEM((SEQ, QW + HD), BF16),
             pltpu.VMEM((SEQ, HD), F32),
             pltpu.VMEM((HD, SEQ), BF16),
             pltpu.VMEM((HD, SEQ), BF16),
+            pltpu.SemaphoreType.DMA((8,)),
         ],
         compiler_params=params(),
-    )(packed, probs, values)
-
-
-def unpack_kernel(in_ref, q_ref, k_ref):
-    q_ref[...] = in_ref[0, :, 0:QW]
-    k_ref[...] = in_ref[0, :, QW:]
-
-
-def unpack(back):
-    tokens = back.shape[1]
+    )(origin, to, *pieces, probs, values)
+
+
+def unpack_kernel(from_ref, *refs):
+    pieces, (q_ref, k_ref, sems) = refs[:8], refs[8:]
+    copies = []
+    for r, piece in enumerate(pieces):
+        j = from_ref[r]
+        wide = pl.ds(pl.multiple_of(j * QW, QW), QW)
+        thin = pl.ds(pl.multiple_of(j * HD, HD), HD)
+        copies.append(
+            pltpu.make_async_copy(piece.at[:, pl.ds(0, QW)], q_ref.at[:, wide], sems.at[2 * r])
+        )
+        copies.append(
+            pltpu.make_async_copy(piece.at[:, pl.ds(QW, HD)], k_ref.at[:, thin], sems.at[2 * r + 1])
+        )
+    run_copies(copies)
+
+
+def unpack(origin, pieces):
     return pl.pallas_call(
         unpack_kernel,
-        grid=(8,),
-        in_specs=[pl.BlockSpec((1, tokens, QW + HD), lambda j: (j, 0, 0))],
-        out_specs=[
-            pl.BlockSpec((tokens, QW), lambda j: (0, j)),
-            pl.BlockSpec((tokens, HD), lambda j: (0, j)),
-        ],
+        in_specs=[SCALARS] + [ANYWHERE] * 8,
+        out_specs=[ANYWHERE] * 2,
         out_shape=[
-            jax.ShapeDtypeStruct((tokens, 8 * QW), BF16),
-            jax.ShapeDtypeStruct((tokens, 8 * HD), BF16),
-        ],
+            jax.ShapeDtypeStruct((ROWS, 8 * QW), BF16),
+            jax.ShapeDtypeStruct((ROWS, 8 * HD), BF16),
+        ],
+        scratch_shapes=[pltpu.SemaphoreType.DMA((16,))],
         compiler_params=params(),
-    )(back)
+    )(origin, *pieces)
 
 
 def adam_kernel(
@@ -341,25 +427,46 @@
     )(parts, master, m_code, m_scale, v_code, v_scale)
 
 
+def exchange(pieces):
+    return [pieces[0]] + [send(pieces[r], r) for r in range(1, 8)]
+
+
+def spread(own):
+    right, left, core = send(own, 2), send(own, 3), send(own, 1)
+    half = own.shape[0] // 2
+    far_lo, far_hi = send(right[:half], 2), send(left[half:], 3)
+    return [
+        own,
+        core,
+        right,
+        left,
+        send(right, 1),
+        send(left, 1),
+        far_lo,
+        far_hi,
+        send(far_lo, 1),
+        send(far_hi, 1),
+    ]
+
+
 def shards(hidden, query, key, grad_out, doc_lens, master, m_code, m_scale, v_code, v_scale):
     n_dp = lax.axis_size("dp")
-    packed = pack(query[0], grad_out[0], key[0])
-    packed = lax.all_to_all(packed, "seq", split_axis=0, concat_axis=0, tiled=True)
-    packed = packed.reshape(SEQ, 2 * QW + HD)
-    whole = lax.all_gather(hidden[0], "seq", axis=0, tiled=True)
+    me = lax.axis_index("seq")
+    to = jnp.stack([hop(me, r) for r in range(8)])
+    back = [0, 1, 3, 2, 5, 4, 6, 7]
+    origin = jnp.stack([hop(me, back[r]) for r in range(8)])
+    hiddens = spread(hidden[0])
+    pieces = exchange(pack(to, query[0], grad_out[0], key[0]))
     copies = jnp.broadcast_to(master.astype(BF16)[None], (n_dp,) + master.shape)
     weight = lax.all_to_all(copies, "dp", split_axis=0, concat_axis=0, tiled=True)
     weight = weight.reshape(D, HD)
-    probs, grad_values = probs_call(doc_lens, packed)
-    values, term = project_call(whole, weight, grad_values)
+    probs, grad_values = probs_call(doc_lens, origin, pieces)
+    values, term = project_call(origin, hiddens, weight, grad_values)
     parts = lax.all_to_all(
         term.reshape((n_dp,) + master.shape), "dp", split_axis=0, concat_axis=0, tiled=True
     )
-    grads = grads_call(packed, probs, values)
-    back = lax.all_to_all(
-        grads.reshape(8, ROWS, QW + HD), "seq", split_axis=0, concat_axis=0, tiled=True
-    )
-    grad_query, grad_key = unpack(back)
+    grads = grads_call(origin, to, pieces, probs, values)
+    grad_query, grad_key = unpack(origin, exchange(grads))
     state = adam_call(parts, master, m_code, m_scale, v_code, v_scale)
     return (grad_query[None], grad_key[None]) + tuple(state)
 

time: 201 us -> 171 us (0.85)
  the two profiles are of different devices: /device:TPU:16 before, /device:TPU:1 now
where the time goes in v2:
time: 171 us; the launch traced here: 170 us
  starting transfers between devices  104 us (61%)
  Pallas kernels  32.8 us (19%)
  waiting for transfers between devices  17.3 us (10%)
  local copies, waits for them, and re-layouts  14.2 us (8%)
    ppermute x23, starting transfers between devices, send(): return lax.ppermute(array, 'seq', perm(k))  74.4 us
    ppermute x23, waiting for transfers between devices, send(): return lax.ppermute(array, 'seq', perm(k))  17.3 us
    all_to_all x1, starting transfers between devices, shards(): lax.all_to_all(copies, 'dp', split_axis=0, concat_axis=0, tiled=True)  16.8 us
    all_to_all x1, starting transfers between devices, shards(): lax.all_to_all(term.reshape((n_dp,) + master.shape), 'dp', split_axis=0,...  12.5 us
    pallas_call x1, Pallas kernels, grads_call(): pl.pallas_call(grads_kernel, grid=(BLOCKS,), in_specs=[SCALARS, SCALARS]...  11.8 us
    unnamed x38, local copies, waits for them, and re-layouts  10.6 us
    pallas_call x1, Pallas kernels, probs_call(): pl.pallas_call(probs_kernel, grid=(BLOCKS,), in_specs=[SCALARS, SCALARS]...  8.67 us
    pallas_call x1, Pallas kernels, project_call(): pl.pallas_call(project_kernel, grid=(D // step,), in_specs=[SCALARS] + [p...  8.49 us
  transfers between devices with their start and end apart: 25, of which 5 were waited for; matrix products, arithmetic and copies ran while one was open for 3% of the time, Pallas kernels for 14%

profile of v2, /device:TPU:1, one launch (start us, length us, event | category | flops | bytes accessed | tf_op | source)
XLA Modules:
  0.0 169.9 jit_solution(13642240207265025971)
XLA Ops:
  0.7 4.1 %collective-permute-start.8 = (bf16[128,4096]{1,0:T(8,128)(2,1)}, bf16[128,4096]{1,0:T(8,128)(2,1)}, u32[]{:S(2)}, u32[]{:S(2)}) collective-permute-start(bf16[128,4096]{1,0:T(8,128)(2,1)} %bitcast.16), channel_id=1, source_target_pairs={{0,128},{64,192},{128,256},{192,320},{256,384},{320,448},{384,0},{... | collective-permute-start | bytes 3145736 | tf_op jit(solution)/shard_map/ppermute | solution.py:56
  4.7 3.2 %collective-permute-start.9 = (bf16[128,4096]{1,0:T(8,128)(2,1)}, bf16[128,4096]{1,0:T(8,128)(2,1)}, u32[]{:S(2)}, u32[]{:S(2)}) collective-permute-start(bf16[128,4096]{1,0:T(8,128)(2,1)} %bitcast.17), channel_id=1, source_target_pairs={{0,384},{64,448},{128,0},{192,64},{256,128},{320,192},{384,256},{4... | collective-permute-start | bytes 3145736 | tf_op jit(solution)/shard_map/ppermute | solution.py:56
  7.9 0.8 convert_element_type.3
  8.7 1.2 broadcast_in_dim.12
  9.9 16.8 %all-to-all-start = ((bf16[64,64,128]{2,1,0:T(8,128)(2,1)}), bf16[64,64,128]{2,1,0:T(8,128)(2,1)}, u32[]{:S(2)}, u32[]{:S(2)}) async-start(bf16[64,64,128]{2,1,0:T(8,128)(2,1)} %broadcast_in_dim.12), calls=%async_computation | async-start | bytes 2097152 | tf_op jit(solution)/shard_map/all_to_all | solution.py:461
  26.7 0.1 stack.47.to_ref
  26.8 1.2 copy-done.1
  28.1 1.2 copy-done.2
  29.3 0.9 copy-done.4
  30.2 1.2 shard_map.153
  31.5 3.4 %collective-permute-start = (bf16[128,1152]{1,0:T(8,128)(2,1)S(1)}, bf16[128,1152]{1,0:T(8,128)(2,1)S(1)}, u32[]{:S(2)}, u32[]{:S(2)}) collective-permute-start(bf16[128,1152]{1,0:T(8,128)(2,1)S(1)} %get-tuple-element.35), channel_id=1, source_target_pairs={{0,64},{64,0},{128,192},{192,128},{256,320},{320,256},{384,448},{4... | collective-permute-start | bytes 884744 | tf_op jit(solution)/shard_map/ppermute | solution.py:56
  34.9 1.9 %collective-permute-start.1 = (bf16[128,1152]{1,0:T(8,128)(2,1)S(1)}, bf16[128,1152]{1,0:T(8,128)(2,1)S(1)}, u32[]{:S(2)}, u32[]{:S(2)}) collective-permute-start(bf16[128,1152]{1,0:T(8,128)(2,1)S(1)} %get-tuple-element.36), channel_id=1, source_target_pairs={{0,128},{64,192},{128,256},{192,320},{256,384},{320,448},{384,0},{... | collective-permute-start | bytes 884744 | tf_op jit(solution)/shard_map/ppermute | solution.py:56
  36.8 4.6 %collective-permute-start.2 = (bf16[128,1152]{1,0:T(8,128)(2,1)S(1)}, bf16[128,1152]{1,0:T(8,128)(2,1)S(1)}, u32[]{:S(2)}, u32[]{:S(2)}) collective-permute-start(bf16[128,1152]{1,0:T(8,128)(2,1)S(1)} %get-tuple-element.37), channel_id=1, source_target_pairs={{0,384},{64,448},{128,0},{192,64},{256,128},{320,192},{384,256},{4... | collective-permute-start | bytes 884744 | tf_op jit(solution)/shard_map/ppermute | solution.py:56
  41.4 0.0 collective-permute-done.refs_1_
  41.4 1.9 %collective-permute-start.3 = (bf16[128,1152]{1,0:T(8,128)(2,1)S(1)}, bf16[128,1152]{1,0:T(8,128)(2,1)S(1)}, u32[]{:S(2)}, u32[]{:S(2)}) collective-permute-start(bf16[128,1152]{1,0:T(8,128)(2,1)S(1)} %get-tuple-element.38), channel_id=1, source_target_pairs={{0,192},{64,128},{128,320},{192,256},{256,448},{320,384},{384,64},... | collective-permute-start | bytes 884744 | tf_op jit(solution)/shard_map/ppermute | solution.py:56
  43.3 3.4 %collective-permute-done.1.refs_2_ = bf16[128,1152]{1,0:T(8,128)(2,1)S(1)} collective-permute-done((bf16[128,1152]{1,0:T(8,128)(2,1)S(1)}, bf16[128,1152]{1,0:T(8,128)(2,1)S(1)}, u32[]{:S(2)}, u32[]{:S(2)}) %collective-permute-start.1) | collective-permute-done | bytes 294944 | tf_op jit(solution)/shard_map/ppermute | solution.py:56
  46.7 2.9 %collective-permute-start.4 = (bf16[128,1152]{1,0:T(8,128)(2,1)S(1)}, bf16[128,1152]{1,0:T(8,128)(2,1)S(1)}, u32[]{:S(2)}, u32[]{:S(2)}) collective-permute-start(bf16[128,1152]{1,0:T(8,128)(2,1)S(1)} %get-tuple-element.39), channel_id=1, source_target_pairs={{0,448},{64,384},{128,64},{192,0},{256,192},{320,128},{384,320},{4... | collective-permute-start | bytes 884744 | tf_op jit(solution)/shard_map/ppermute | solution.py:56
  49.7 0.0 collective-permute-done.8.refs_2_
  49.7 2.0 %collective-permute-start.5 = (bf16[128,1152]{1,0:T(8,128)(2,1)S(1)}, bf16[128,1152]{1,0:T(8,128)(2,1)S(1)}, u32[]{:S(2)}, u32[]{:S(2)}) collective-permute-start(bf16[128,1152]{1,0:T(8,128)(2,1)S(1)} %get-tuple-element.40), channel_id=1, source_target_pairs={{0,256},{64,320},{128,384},{192,448},{256,0},{320,64},{384,128},{4... | collective-permute-start | bytes 884744 | tf_op jit(solution)/shard_map/ppermute | solution.py:56
  51.7 0.0 collective-permute-done.9.refs_3_
  51.7 4.6 %collective-permute-start.6 = (bf16[128,1152]{1,0:T(8,128)(2,1)S(1)}, bf16[128,1152]{1,0:T(8,128)(2,1)S(1)}, u32[]{:S(2)}, u32[]{:S(2)}) collective-permute-start(bf16[128,1152]{1,0:T(8,128)(2,1)S(1)} %get-tuple-element.41), channel_id=1, source_target_pairs={{0,320},{64,256},{128,448},{192,384},{256,64},{320,0},{384,192},{4... | collective-permute-start | bytes 884744 | tf_op jit(solution)/shard_map/ppermute | solution.py:56
  56.3 1.1 slice.8
  57.4 1.1 slice.9
  58.5 0.0 collective-permute-done.2.refs_3_
  58.5 2.5 %collective-permute-start.7 = (bf16[128,4096]{1,0:T(8,128)(2,1)S(1)}, bf16[128,4096]{1,0:T(8,128)(2,1)}, u32[]{:S(2)}, u32[]{:S(2)}) collective-permute-start(bf16[128,4096]{1,0:T(8,128)(2,1)S(1)} %bitcast.18), channel_id=1, source_target_pairs={{0,64},{64,0},{128,192},{192,128},{256,320},{320,256},{384,448},{4... | collective-permute-start | bytes 3145736 | tf_op jit(solution)/shard_map/ppermute | solution.py:56
  61.0 3.0 %collective-permute-start.12 = (bf16[64,4096]{1,0:T(8,128)(2,1)S(1)}, bf16[64,4096]{1,0:T(8,128)(2,1)}, u32[]{:S(2)}, u32[]{:S(2)}) collective-permute-start(bf16[64,4096]{1,0:T(8,128)(2,1)S(1)} %slice.8), channel_id=1, source_target_pairs={{0,128},{64,192},{128,256},{192,320},{256,384},{320,448},{384,0},{... | collective-permute-start | bytes 1572872 | tf_op jit(solution)/shard_map/ppermute | solution.py:56
  64.0 2.3 %collective-permute-start.10 = (bf16[128,4096]{1,0:T(8,128)(2,1)}, bf16[128,4096]{1,0:T(8,128)(2,1)}, u32[]{:S(2)}, u32[]{:S(2)}) collective-permute-start(bf16[128,4096]{1,0:T(8,128)(2,1)} %collective-permute-done.8.refs_2_), channel_id=1, source_target_pairs={{0,64},{64,0},{128,192},{192,128},{256,320},{320,256},{384,448},{4... | collective-permute-start | bytes 3145736 | tf_op jit(solution)/shard_map/ppermute | solution.py:56
  66.2 2.1 %collective-permute-start.11 = (bf16[128,4096]{1,0:T(8,128)(2,1)}, bf16[128,4096]{1,0:T(8,128)(2,1)}, u32[]{:S(2)}, u32[]{:S(2)}) collective-permute-start(bf16[128,4096]{1,0:T(8,128)(2,1)} %collective-permute-done.9.refs_3_), channel_id=1, source_target_pairs={{0,64},{64,0},{128,192},{192,128},{256,320},{320,256},{384,448},{4... | collective-permute-start | bytes 3145736 | tf_op jit(solution)/shard_map/ppermute | solution.py:56
  68.3 6.8 %collective-permute-start.13 = (bf16[64,4096]{1,0:T(8,128)(2,1)S(1)}, bf16[64,4096]{1,0:T(8,128)(2,1)}, u32[]{:S(2)}, u32[]{:S(2)}) collective-permute-start(bf16[64,4096]{1,0:T(8,128)(2,1)S(1)} %slice.9), channel_id=1, source_target_pairs={{0,384},{64,448},{128,0},{192,64},{256,128},{320,192},{384,256},{4... | collective-permute-start | bytes 1572872 | tf_op jit(solution)/shard_map/ppermute | solution.py:56
  75.1 4.6 %collective-permute-done.12.refs_6_ = bf16[64,4096]{1,0:T(8,128)(2,1)} collective-permute-done((bf16[64,4096]{1,0:T(8,128)(2,1)S(1)}, bf16[64,4096]{1,0:T(8,128)(2,1)}, u32[]{:S(2)}, u32[]{:S(2)}) %collective-permute-start.12) | collective-permute-done | bytes 524320 | tf_op jit(solution)/shard_map/ppermute | solution.py:56
  79.7 2.3 %collective-permute-start.14 = (bf16[64,4096]{1,0:T(8,128)(2,1)}, bf16[64,4096]{1,0:T(8,128)(2,1)}, u32[]{:S(2)}, u32[]{:S(2)}) collective-permute-start(bf16[64,4096]{1,0:T(8,128)(2,1)} %collective-permute-done.12.refs_6_), channel_id=1, source_target_pairs={{0,64},{64,0},{128,192},{192,128},{256,320},{320,256},{384,448},{4... | collective-permute-start | bytes 1572872 | tf_op jit(solution)/shard_map/ppermute | solution.py:56
  82.1 4.0 %collective-permute-done.13.refs_7_ = bf16[64,4096]{1,0:T(8,128)(2,1)} collective-permute-done((bf16[64,4096]{1,0:T(8,128)(2,1)S(1)}, bf16[64,4096]{1,0:T(8,128)(2,1)}, u32[]{:S(2)}, u32[]{:S(2)}) %collective-permute-start.13) | collective-permute-done | bytes 524320 | tf_op jit(solution)/shard_map/ppermute | solution.py:56
  86.0 3.1 %collective-permute-start.15 = (bf16[64,4096]{1,0:T(8,128)(2,1)}, bf16[64,4096]{1,0:T(8,128)(2,1)}, u32[]{:S(2)}, u32[]{:S(2)}) collective-permute-start(bf16[64,4096]{1,0:T(8,128)(2,1)} %collective-permute-done.13.refs_7_), channel_id=1, source_target_pairs={{0,64},{64,0},{128,192},{192,128},{256,320},{320,256},{384,448},{4... | collective-permute-start | bytes 1572872 | tf_op jit(solution)/shard_map/ppermute | solution.py:56
  89.2 0.1 stack.46.from_ref
  89.3 8.7 %shard_map.154 = (bf16[8,512,512]{2,1,0:T(8,128)(2,1)}, bf16[1024,128]{1,0:T(8,128)(2,1)S(1)}) custom-call(s32[1,8]{1,0:T(1,128)S(1)} %copy-done.14, s32[8]{0:T(128)S(1)} %stack.46.from_ref, bf16[128,1152]{1,0:T(8,128)(2,1)S(1)} %get-tuple-element.34.refs_0_, bf16[128,1152]{1,0:T(8,128)(2,1)S(1)} %collective-permute-done.refs_1_, ...), custom_call_target="tpu_custom_call" | custom-call | tf_op jit(solution)/shard_map/pallas_call | solution.py:184
  97.9 0.0 copy-start.7
  97.9 0.7 copy-done.7
  98.7 0.0 copy-start.8
  98.7 0.9 copy-done.8
  99.6 8.5 %shard_map.155 = (bf16[1024,128]{1,0:T(8,128)(2,1)S(1)}, bf16[4096,128]{1,0:T(8,128)(2,1)S(1)}) custom-call(s32[8]{0:T(128)S(1)} %stack.46.from_ref, bf16[128,4096]{1,0:T(8,128)(2,1)S(1)} %bitcast.19, bf16[128,4096]{1,0:T(8,128)(2,1)} %collective-permute-done.7.refs_1_, bf16[128,4096]{1,0:T(8,128)(2,1)} %collective-permute-done.8.refs_2_, ...), custom_call_target="tpu_custom_call" | custom-call | tf_op jit(solution)/shard_map/pallas_call | solution.py:231
  108.1 1.0 copy-done.3
  109.1 0.7 copy-done.5
  109.8 0.0 copy-start.13
  109.9 12.5 %all-to-all-start.1 = ((bf16[64,64,128]{2,1,0:T(8,128)(2,1)}), bf16[64,64,128]{2,1,0:T(8,128)(2,1)S(1)}, u32[]{:S(2)}, u32[]{:S(2)}) async-start(bf16[64,64,128]{2,1,0:T(8,128)(2,1)} %bitcast.22), calls=%async_computation.1 | async-start | bytes 2097152 | tf_op jit(solution)/shard_map/all_to_all | solution.py:465
  122.4 0.0 copy-start.6
  122.4 0.9 copy-done.6
  123.3 11.8 %shard_map.156 = (bf16[128,640]{1,0:T(8,128)(2,1)S(1)}, bf16[128,640]{1,0:T(8,128)(2,1)S(1)}, bf16[128,640]{1,0:T(8,128)(2,1)S(1)}, bf16[128,640]{1,0:T(8,128)(2...) custom-call(s32[8]{0:T(128)S(1)} %stack.46.from_ref, ...), custom_call_target="tpu_custom_call" | custom-call | tf_op jit(solution)/shard_map/pallas_call | solution.py:306
  135.1 0.7 copy-done.9
  135.8 2.2 %collective-permute-start.16 = (bf16[128,640]{1,0:T(8,128)(2,1)S(1)}, bf16[128,640]{1,0:T(8,128)(2,1)S(1)}, u32[]{:S(2)}, u32[]{:S(2)}) collective-permute-start(bf16[128,640]{1,0:T(8,128)(2,1)S(1)} %get-tuple-element.46), channel_id=1, source_target_pairs={{0,64},{64,0},{128,192},{192,128},{256,320},{320,256},{384,448},{4... | collective-permute-start | bytes 491528 | tf_op jit(solution)/shard_map/ppermute | solution.py:56
  138.0 1.9 %collective-permute-start.17 = (bf16[128,640]{1,0:T(8,128)(2,1)S(1)}, bf16[128,640]{1,0:T(8,128)(2,1)S(1)}, u32[]{:S(2)}, u32[]{:S(2)}) collective-permute-start(bf16[128,640]{1,0:T(8,128)(2,1)S(1)} %get-tuple-element.47), channel_id=1, source_target_pairs={{0,128},{64,192},{128,256},{192,320},{256,384},{320,448},{384,0},{... | collective-permute-start | bytes 491528 | tf_op jit(solution)/shard_map/ppermute | solution.py:56
  139.9 5.4 %collective-permute-start.18 = (bf16[128,640]{1,0:T(8,128)(2,1)}, bf16[128,640]{1,0:T(8,128)(2,1)S(1)}, u32[]{:S(2)}, u32[]{:S(2)}) collective-permute-start(bf16[128,640]{1,0:T(8,128)(2,1)} %get-tuple-element.48), channel_id=1, source_target_pairs={{0,384},{64,448},{128,0},{192,64},{256,128},{320,192},{384,256},{4... | collective-permute-start | bytes 491528 | tf_op jit(solution)/shard_map/ppermute | solution.py:56
  145.3 1.9 %collective-permute-start.19 = (bf16[128,640]{1,0:T(8,128)(2,1)}, bf16[128,640]{1,0:T(8,128)(2,1)S(1)}, u32[]{:S(2)}, u32[]{:S(2)}) collective-permute-start(bf16[128,640]{1,0:T(8,128)(2,1)} %get-tuple-element.49), channel_id=1, source_target_pairs={{0,192},{64,128},{128,320},{192,256},{256,448},{320,384},{384,64},... | collective-permute-start | bytes 491528 | tf_op jit(solution)/shard_map/ppermute | solution.py:56
  147.3 4.9 %collective-permute-start.20 = (bf16[128,640]{1,0:T(8,128)(2,1)}, bf16[128,640]{1,0:T(8,128)(2,1)S(1)}, u32[]{:S(2)}, u32[]{:S(2)}) collective-permute-start(bf16[128,640]{1,0:T(8,128)(2,1)} %get-tuple-element.50), channel_id=1, source_target_pairs={{0,448},{64,384},{128,64},{192,0},{256,192},{320,128},{384,320},{4... | collective-permute-start | bytes 491528 | tf_op jit(solution)/shard_map/ppermute | solution.py:56
  152.1 2.3 %collective-permute-start.21 = (bf16[128,640]{1,0:T(8,128)(2,1)}, bf16[128,640]{1,0:T(8,128)(2,1)S(1)}, u32[]{:S(2)}, u32[]{:S(2)}) collective-permute-start(bf16[128,640]{1,0:T(8,128)(2,1)} %get-tuple-element.51), channel_id=1, source_target_pairs={{0,256},{64,320},{128,384},{192,448},{256,0},{320,64},{384,128},{4... | collective-permute-start | bytes 491528 | tf_op jit(solution)/shard_map/ppermute | solution.py:56
  154.4 5.2 %collective-permute-start.22 = (bf16[128,640]{1,0:T(8,128)(2,1)}, bf16[128,640]{1,0:T(8,128)(2,1)S(1)}, u32[]{:S(2)}, u32[]{:S(2)}) collective-permute-start(bf16[128,640]{1,0:T(8,128)(2,1)} %get-tuple-element.52), channel_id=1, source_target_pairs={{0,320},{64,256},{128,448},{192,384},{256,64},{320,0},{384,192},{4... | collective-permute-start | bytes 491528 | tf_op jit(solution)/shard_map/ppermute | solution.py:56
  159.6 0.1 copy.17.ms_ref
  159.7 0.1 copy.18.vs_ref
  159.8 1.2 collective-permute-done.21.refs_6_
  161.0 4.2 %collective-permute-done.22.refs_7_ = bf16[128,640]{1,0:T(8,128)(2,1)S(1)} collective-permute-done((bf16[128,640]{1,0:T(8,128)(2,1)}, bf16[128,640]{1,0:T(8,128)(2,1)S(1)}, u32[]{:S(2)}, u32[]{:S(2)}) %collective-permute-start.22) | collective-permute-done | bytes 163872 | tf_op jit(solution)/shard_map/ppermute | solution.py:56
  165.2 0.9 copy-done.10
  166.1 1.7 %shard_map.157 = (bf16[128,4096]{1,0:T(8,128)(2,1)}, bf16[128,1024]{1,0:T(8,128)(2,1)}) custom-call(s32[8]{0:T(128)S(1)} %stack.46.from_ref, bf16[128,640]{1,0:T(8,128)(2,1)S(1)} %copy-done.10, bf16[128,640]{1,0:T(8,128)(2,1)S(1)} %collective-permute-done.16.refs_1_, bf16[128,640]{1,0:T(8,128)(2,1)S(1)} %collective-permute-done.17.refs_2_, ...), custom_call_target="tpu_custom_call" | custom-call | tf_op jit(solution)/shard_map/pallas_call | solution.py:346
  167.9 0.9 shard_map.158
  168.8 0.6 copy.19
  169.3 0.6 copy.20
  (36 shorter events, 0.1 us)
Async XLA Ops:
  0.6 57.9 %copy-start = (bf16[1,128,4096]{2,1,0:T(8,128)(2,1)S(1)}, bf16[1,128,4096]{2,1,0:T(8,128)(2,1)}, u32[]{:S(2)}) copy-start(bf16[1,128,4096]{2,1,0:T(8,128)(2,1)} %param.10) | copy-start | bytes 3145732
  0.6 88.6 %copy-start.14 = (s32[1,8]{1,0:T(1,128)S(1)}, s32[1,8]{1,0:T(1,128)}, u32[]{:S(2)}) copy-start(s32[1,8]{1,0:T(1,128)} %lens_ref.1) | copy-start | bytes 100
  0.7 49.0 %collective-permute-start.8 = (bf16[128,4096]{1,0:T(8,128)(2,1)}, bf16[128,4096]{1,0:T(8,128)(2,1)}, u32[]{:S(2)}, u32[]{:S(2)}) collective-permute-start(bf16[128,4096]{1,0:T(8,128)(2,1)} %bitcast.16), channel_id=1, source_target_pairs={{0,128},{64,192},{128,256},{192,320},{256,384},{320,448},{384,0},{... | collective-permute-start | bytes 3145736 | tf_op jit(solution)/shard_map/ppermute | solution.py:56
  4.7 47.0 %collective-permute-start.9 = (bf16[128,4096]{1,0:T(8,128)(2,1)}, bf16[128,4096]{1,0:T(8,128)(2,1)}, u32[]{:S(2)}, u32[]{:S(2)}) collective-permute-start(bf16[128,4096]{1,0:T(8,128)(2,1)} %bitcast.17), channel_id=1, source_target_pairs={{0,384},{64,448},{128,0},{192,64},{256,128},{320,192},{384,256},{4... | collective-permute-start | bytes 3145736 | tf_op jit(solution)/shard_map/ppermute | solution.py:56
  9.9 88.7 %all-to-all-start = ((bf16[64,64,128]{2,1,0:T(8,128)(2,1)}), bf16[64,64,128]{2,1,0:T(8,128)(2,1)}, u32[]{:S(2)}, u32[]{:S(2)}) async-start(bf16[64,64,128]{2,1,0:T(8,128)(2,1)} %broadcast_in_dim.12), calls=%async_computation | async-start | bytes 2097152 | tf_op jit(solution)/shard_map/all_to_all | solution.py:461
  26.8 1.2 copy-start.1
  28.1 1.2 copy-start.2
  29.3 0.9 copy-start.4
  31.5 9.9 %collective-permute-start = (bf16[128,1152]{1,0:T(8,128)(2,1)S(1)}, bf16[128,1152]{1,0:T(8,128)(2,1)S(1)}, u32[]{:S(2)}, u32[]{:S(2)}) collective-permute-start(bf16[128,1152]{1,0:T(8,128)(2,1)S(1)} %get-tuple-element.35), channel_id=1, source_target_pairs={{0,64},{64,0},{128,192},{192,128},{256,320},{320,256},{384,448},{4... | collective-permute-start | bytes 884744 | tf_op jit(solution)/shard_map/ppermute | solution.py:56
  34.9 11.8 %collective-permute-start.1 = (bf16[128,1152]{1,0:T(8,128)(2,1)S(1)}, bf16[128,1152]{1,0:T(8,128)(2,1)S(1)}, u32[]{:S(2)}, u32[]{:S(2)}) collective-permute-start(bf16[128,1152]{1,0:T(8,128)(2,1)S(1)} %get-tuple-element.36), channel_id=1, source_target_pairs={{0,128},{64,192},{128,256},{192,320},{256,384},{320,448},{384,0},{... | collective-permute-start | bytes 884744 | tf_op jit(solution)/shard_map/ppermute | solution.py:56
  36.8 21.7 %collective-permute-start.2 = (bf16[128,1152]{1,0:T(8,128)(2,1)S(1)}, bf16[128,1152]{1,0:T(8,128)(2,1)S(1)}, u32[]{:S(2)}, u32[]{:S(2)}) collective-permute-start(bf16[128,1152]{1,0:T(8,128)(2,1)S(1)} %get-tuple-element.37), channel_id=1, source_target_pairs={{0,384},{64,448},{128,0},{192,64},{256,128},{320,192},{384,256},{4... | collective-permute-start | bytes 884744 | tf_op jit(solution)/shard_map/ppermute | solution.py:56
  41.4 19.6 %collective-permute-start.3 = (bf16[128,1152]{1,0:T(8,128)(2,1)S(1)}, bf16[128,1152]{1,0:T(8,128)(2,1)S(1)}, u32[]{:S(2)}, u32[]{:S(2)}) collective-permute-start(bf16[128,1152]{1,0:T(8,128)(2,1)S(1)} %get-tuple-element.38), channel_id=1, source_target_pairs={{0,192},{64,128},{128,320},{192,256},{256,448},{320,384},{384,64},... | collective-permute-start | bytes 884744 | tf_op jit(solution)/shard_map/ppermute | solution.py:56
  46.7 17.2 %collective-permute-start.4 = (bf16[128,1152]{1,0:T(8,128)(2,1)S(1)}, bf16[128,1152]{1,0:T(8,128)(2,1)S(1)}, u32[]{:S(2)}, u32[]{:S(2)}) collective-permute-start(bf16[128,1152]{1,0:T(8,128)(2,1)S(1)} %get-tuple-element.39), channel_id=1, source_target_pairs={{0,448},{64,384},{128,64},{192,0},{256,192},{320,128},{384,320},{4... | collective-permute-start | bytes 884744 | tf_op jit(solution)/shard_map/ppermute | solution.py:56
  49.7 16.6 %collective-permute-start.5 = (bf16[128,1152]{1,0:T(8,128)(2,1)S(1)}, bf16[128,1152]{1,0:T(8,128)(2,1)S(1)}, u32[]{:S(2)}, u32[]{:S(2)}) collective-permute-start(bf16[128,1152]{1,0:T(8,128)(2,1)S(1)} %get-tuple-element.40), channel_id=1, source_target_pairs={{0,256},{64,320},{128,384},{192,448},{256,0},{320,64},{384,128},{4... | collective-permute-start | bytes 884744 | tf_op jit(solution)/shard_map/ppermute | solution.py:56
  51.7 16.6 %collective-permute-start.6 = (bf16[128,1152]{1,0:T(8,128)(2,1)S(1)}, bf16[128,1152]{1,0:T(8,128)(2,1)S(1)}, u32[]{:S(2)}, u32[]{:S(2)}) collective-permute-start(bf16[128,1152]{1,0:T(8,128)(2,1)S(1)} %get-tuple-element.41), channel_id=1, source_target_pairs={{0,320},{64,256},{128,448},{192,384},{256,64},{320,0},{384,192},{4... | collective-permute-start | bytes 884744 | tf_op jit(solution)/shard_map/ppermute | solution.py:56
  58.5 40.1 %collective-permute-start.7 = (bf16[128,4096]{1,0:T(8,128)(2,1)S(1)}, bf16[128,4096]{1,0:T(8,128)(2,1)}, u32[]{:S(2)}, u32[]{:S(2)}) collective-permute-start(bf16[128,4096]{1,0:T(8,128)(2,1)S(1)} %bitcast.18), channel_id=1, source_target_pairs={{0,64},{64,0},{128,192},{192,128},{256,320},{320,256},{384,448},{4... | collective-permute-start | bytes 3145736 | tf_op jit(solution)/shard_map/ppermute | solution.py:56
  61.0 18.7 %collective-permute-start.12 = (bf16[64,4096]{1,0:T(8,128)(2,1)S(1)}, bf16[64,4096]{1,0:T(8,128)(2,1)}, u32[]{:S(2)}, u32[]{:S(2)}) collective-permute-start(bf16[64,4096]{1,0:T(8,128)(2,1)S(1)} %slice.8), channel_id=1, source_target_pairs={{0,128},{64,192},{128,256},{192,320},{256,384},{320,448},{384,0},{... | collective-permute-start | bytes 1572872 | tf_op jit(solution)/shard_map/ppermute | solution.py:56
  64.0 34.7 %collective-permute-start.10 = (bf16[128,4096]{1,0:T(8,128)(2,1)}, bf16[128,4096]{1,0:T(8,128)(2,1)}, u32[]{:S(2)}, u32[]{:S(2)}) collective-permute-start(bf16[128,4096]{1,0:T(8,128)(2,1)} %collective-permute-done.8.refs_2_), channel_id=1, source_target_pairs={{0,64},{64,0},{128,192},{192,128},{256,320},{320,256},{384,448},{4... | collective-permute-start | bytes 3145736 | tf_op jit(solution)/shard_map/ppermute | solution.py:56
  66.2 32.4 %collective-permute-start.11 = (bf16[128,4096]{1,0:T(8,128)(2,1)}, bf16[128,4096]{1,0:T(8,128)(2,1)}, u32[]{:S(2)}, u32[]{:S(2)}) collective-permute-start(bf16[128,4096]{1,0:T(8,128)(2,1)} %collective-permute-done.9.refs_3_), channel_id=1, source_target_pairs={{0,64},{64,0},{128,192},{192,128},{256,320},{320,256},{384,448},{4... | collective-permute-start | bytes 3145736 | tf_op jit(solution)/shard_map/ppermute | solution.py:56
  68.3 17.7 %collective-permute-start.13 = (bf16[64,4096]{1,0:T(8,128)(2,1)S(1)}, bf16[64,4096]{1,0:T(8,128)(2,1)}, u32[]{:S(2)}, u32[]{:S(2)}) collective-permute-start(bf16[64,4096]{1,0:T(8,128)(2,1)S(1)} %slice.9), channel_id=1, source_target_pairs={{0,384},{64,448},{128,0},{192,64},{256,128},{320,192},{384,256},{4... | collective-permute-start | bytes 1572872 | tf_op jit(solution)/shard_map/ppermute | solution.py:56
  79.7 18.9 %collective-permute-start.14 = (bf16[64,4096]{1,0:T(8,128)(2,1)}, bf16[64,4096]{1,0:T(8,128)(2,1)}, u32[]{:S(2)}, u32[]{:S(2)}) collective-permute-start(bf16[64,4096]{1,0:T(8,128)(2,1)} %collective-permute-done.12.refs_6_), channel_id=1, source_target_pairs={{0,64},{64,0},{128,192},{192,128},{256,320},{320,256},{384,448},{4... | collective-permute-start | bytes 1572872 | tf_op jit(solution)/shard_map/ppermute | solution.py:56
  86.0 12.6 %collective-permute-start.15 = (bf16[64,4096]{1,0:T(8,128)(2,1)}, bf16[64,4096]{1,0:T(8,128)(2,1)}, u32[]{:S(2)}, u32[]{:S(2)}) collective-permute-start(bf16[64,4096]{1,0:T(8,128)(2,1)} %collective-permute-done.13.refs_7_), channel_id=1, source_target_pairs={{0,64},{64,0},{128,192},{192,128},{256,320},{320,256},{384,448},{4... | collective-permute-start | bytes 1572872 | tf_op jit(solution)/shard_map/ppermute | solution.py:56
  97.9 0.7 copy-start.7
  98.7 1.0 copy-start.8
  108.1 1.0 copy-start.3
  109.1 0.7 copy-start.5
  109.8 49.8 %copy-start.15 = (f32[32,1]{0,1:T(1,128)S(1)}, f32[32,1]{0,1:T(1,128)}, u32[]{:S(2)}) copy-start(f32[32,1]{0,1:T(1,128)} %param.17) | copy-start | bytes 388
  109.8 49.9 %copy-start.16 = (f32[32,1]{0,1:T(1,128)S(1)}, f32[32,1]{0,1:T(1,128)}, u32[]{:S(2)}) copy-start(f32[32,1]{0,1:T(1,128)} %param.19) | copy-start | bytes 388
  109.8 58.0 %copy-start.11 = (f32[64,128]{1,0:T(8,128)S(1)}, f32[64,128]{1,0:T(8,128)}, u32[]{:S(2)}) copy-start(f32[64,128]{1,0:T(8,128)} %master_ref.1) | copy-start | bytes 98308
  109.8 58.0 %copy-start.12 = (bf16[64,128]{1,0:T(8,128)(2,1)S(1)}, bf16[64,128]{1,0:T(8,128)(2,1)}, u32[]{:S(2)}) copy-start(bf16[64,128]{1,0:T(8,128)(2,1)} %mc_ref.1) | copy-start | bytes 49156
  109.8 58.0 %copy-start.13 = (bf16[64,128]{1,0:T(8,128)(2,1)S(1)}, bf16[64,128]{1,0:T(8,128)(2,1)}, u32[]{:S(2)}) copy-start(bf16[64,128]{1,0:T(8,128)(2,1)} %vc_ref.1) | copy-start | bytes 49156
  109.9 58.0 %all-to-all-start.1 = ((bf16[64,64,128]{2,1,0:T(8,128)(2,1)}), bf16[64,64,128]{2,1,0:T(8,128)(2,1)S(1)}, u32[]{:S(2)}, u32[]{:S(2)}) async-start(bf16[64,64,128]{2,1,0:T(8,128)(2,1)} %bitcast.22), calls=%async_computation.1 | async-start | bytes 2097152 | tf_op jit(solution)/shard_map/all_to_all | solution.py:465
  122.4 1.0 copy-start.6
  135.1 0.7 copy-start.9
  135.8 16.3 %collective-permute-start.16 = (bf16[128,640]{1,0:T(8,128)(2,1)S(1)}, bf16[128,640]{1,0:T(8,128)(2,1)S(1)}, u32[]{:S(2)}, u32[]{:S(2)}) collective-permute-start(bf16[128,640]{1,0:T(8,128)(2,1)S(1)} %get-tuple-element.46), channel_id=1, source_target_pairs={{0,64},{64,0},{128,192},{192,128},{256,320},{320,256},{384,448},{4... | collective-permute-start | bytes 491528 | tf_op jit(solution)/shard_map/ppermute | solution.py:56
  138.0 16.5 %collective-permute-start.17 = (bf16[128,640]{1,0:T(8,128)(2,1)S(1)}, bf16[128,640]{1,0:T(8,128)(2,1)S(1)}, u32[]{:S(2)}, u32[]{:S(2)}) collective-permute-start(bf16[128,640]{1,0:T(8,128)(2,1)S(1)} %get-tuple-element.47), channel_id=1, source_target_pairs={{0,128},{64,192},{128,256},{192,320},{256,384},{320,448},{384,0},{... | collective-permute-start | bytes 491528 | tf_op jit(solution)/shard_map/ppermute | solution.py:56
  139.9 19.9 %collective-permute-start.18 = (bf16[128,640]{1,0:T(8,128)(2,1)}, bf16[128,640]{1,0:T(8,128)(2,1)S(1)}, u32[]{:S(2)}, u32[]{:S(2)}) collective-permute-start(bf16[128,640]{1,0:T(8,128)(2,1)} %get-tuple-element.48), channel_id=1, source_target_pairs={{0,384},{64,448},{128,0},{192,64},{256,128},{320,192},{384,256},{4... | collective-permute-start | bytes 491528 | tf_op jit(solution)/shard_map/ppermute | solution.py:56
  145.3 14.5 %collective-permute-start.19 = (bf16[128,640]{1,0:T(8,128)(2,1)}, bf16[128,640]{1,0:T(8,128)(2,1)S(1)}, u32[]{:S(2)}, u32[]{:S(2)}) collective-permute-start(bf16[128,640]{1,0:T(8,128)(2,1)} %get-tuple-element.49), channel_id=1, source_target_pairs={{0,192},{64,128},{128,320},{192,256},{256,448},{320,384},{384,64},... | collective-permute-start | bytes 491528 | tf_op jit(solution)/shard_map/ppermute | solution.py:56
  147.3 12.5 %collective-permute-start.20 = (bf16[128,640]{1,0:T(8,128)(2,1)}, bf16[128,640]{1,0:T(8,128)(2,1)S(1)}, u32[]{:S(2)}, u32[]{:S(2)}) collective-permute-start(bf16[128,640]{1,0:T(8,128)(2,1)} %get-tuple-element.50), channel_id=1, source_target_pairs={{0,448},{64,384},{128,64},{192,0},{256,192},{320,128},{384,320},{4... | collective-permute-start | bytes 491528 | tf_op jit(solution)/shard_map/ppermute | solution.py:56
  152.1 8.9 %collective-permute-start.21 = (bf16[128,640]{1,0:T(8,128)(2,1)}, bf16[128,640]{1,0:T(8,128)(2,1)S(1)}, u32[]{:S(2)}, u32[]{:S(2)}) collective-permute-start(bf16[128,640]{1,0:T(8,128)(2,1)} %get-tuple-element.51), channel_id=1, source_target_pairs={{0,256},{64,320},{128,384},{192,448},{256,0},{320,64},{384,128},{4... | collective-permute-start | bytes 491528 | tf_op jit(solution)/shard_map/ppermute | solution.py:56
  154.4 10.7 %collective-permute-start.22 = (bf16[128,640]{1,0:T(8,128)(2,1)}, bf16[128,640]{1,0:T(8,128)(2,1)S(1)}, u32[]{:S(2)}, u32[]{:S(2)}) collective-permute-start(bf16[128,640]{1,0:T(8,128)(2,1)} %get-tuple-element.52), channel_id=1, source_target_pairs={{0,320},{64,256},{128,448},{192,384},{256,64},{320,0},{384,192},{4... | collective-permute-start | bytes 491528 | tf_op jit(solution)/shard_map/ppermute | solution.py:56
  165.2 0.9 copy-start.10

commit v3 on v2

v3 whole, which is shorter than its diff:
```python
import functools
import math

import jax
import jax.numpy as jnp
from jax import lax
from jax.experimental import pallas as pl
from jax.experimental.pallas import tpu as pltpu
from jax.sharding import PartitionSpec as P

D = 4096
HD = 128
DOCS = 8
STEP = 1000
SEQ = 1024
GROUP = 4
QW = GROUP * HD
ROWS = 128
BLOCKS = SEQ // ROWS
MOST = 4
NEG = -1e30
INV_WIDTH = 1.0 / math.sqrt(D)
SCALE = 1.0 / math.sqrt(HD)
F32 = jnp.float32
BF16 = jnp.bfloat16


def dot(a, b):
    return jnp.dot(a, b, preferred_element_type=F32)


def stacked(block):
    return jnp.concatenate([block[:, a * HD : (a + 1) * HD] for a in range(GROUP)], axis=0)


def params(mebibytes=24):
    return pltpu.CompilerParams(vmem_limit_bytes=mebibytes * 1024 * 1024)


XS = 4


def place(value, dx, dc):
    chip = lax.rem(lax.div(value, 2) + dx, XS)
    return chip * 2 + jnp.bitwise_xor(lax.rem(value, 2), dc)


def send(array, dx, dc):
    pairs = [(s, ((s // 2 + dx) % XS) * 2 + ((s % 2) ^ dc)) for s in range(2 * XS)]
    return lax.ppermute(array, "seq", pairs)


ANYWHERE = pl.BlockSpec(memory_space=pl.ANY)
SCALARS = pl.BlockSpec(memory_space=pltpu.SMEM)


def run_copies(copies):
    for copy in copies:
        copy.start()
    for copy in copies:
        copy.wait()


def pack_kernel(to_ref, q_ref, c_ref, k_ref, *refs):
    outs, sems = refs[:-1], refs[-1]
    copies = []
    for r in range(8):
        out = outs[r // 2].at[r % 2]
        j = to_ref[r]
        wide = pl.ds(pl.multiple_of(j * QW, QW), QW)
        thin = pl.ds(pl.multiple_of(j * HD, HD), HD)
        for n, (src, lanes, into) in enumerate(
            [
                (q_ref, wide, pl.ds(0, QW)),
                (c_ref, wide, pl.ds(QW, QW)),
                (k_ref, thin, pl.ds(2 * QW, HD)),
            ]
        ):
            copies.append(
                pltpu.make_async_copy(src.at[:, lanes], out.at[:, into], sems.at[3 * r + n])
            )
    run_copies(copies)


def pack(to, query, cot, key):
    tokens = query.shape[0]
    return pl.pallas_call(
        pack_kernel,
        in_specs=[SCALARS, ANYWHERE, ANYWHERE, ANYWHERE],
        out_specs=[ANYWHERE] * XS,
        out_shape=[jax.ShapeDtypeStruct((2, tokens, 2 * QW + HD), BF16)] * XS,
        scratch_shapes=[pltpu.SemaphoreType.DMA((24,))],
        compiler_params=params(60),
    )(to, query, cot, key)


def merge_kernel(*refs):
    pairs, out, sems = refs[:XS], refs[XS], refs[XS + 1]
    run_copies(
        [pltpu.make_async_copy(pair.at[1], out.at[r], sems.at[r]) for r, pair in enumerate(pairs)]
    )


def merge(pairs):
    return pl.pallas_call(
        merge_kernel,
        in_specs=[ANYWHERE] * XS,
        out_specs=ANYWHERE,
        out_shape=jax.ShapeDtypeStruct((XS,) + pairs[0].shape[1:], BF16),
        scratch_shapes=[pltpu.SemaphoreType.DMA((XS,))],
        compiler_params=params(4),
    )(*pairs)


def exchange(pairs):
    got = [pairs[0]] + [send(pairs[dx], dx, 0) for dx in (1, 3, 2)]
    got = [got[0], got[1], got[3], got[2]]
    return got + [send(merge(got), 0, 1)]


def arrived(refs):
    return [refs[r // 2].at[0] if r % 2 == 0 else refs[XS].at[r // 2] for r in range(8)]


def gather_pieces(from_ref, piece_refs, whole_ref, sems):
    run_copies(
        [
            pltpu.make_async_copy(
                piece,
                whole_ref.at[pl.ds(pl.multiple_of(from_ref[r] * ROWS, ROWS), ROWS), :],
                sems.at[r],
            )
            for r, piece in enumerate(arrived(piece_refs))
        ]
    )


def by_step(i, body):
    for v in range(BLOCKS // 2):
        pl.when(i == v)(functools.partial(body, v))


def window(block):
    count = min(block + 1, MOST)
    return count, (block + 1 - count) * ROWS


def block_probs(block, lens_ref, r_ref, pt_ref):
    first = block * ROWS
    count, lower = window(block)
    queries = stacked(r_ref[first : first + ROWS, 0:QW])
    lane = lax.broadcasted_iota(jnp.int32, (1, GROUP * ROWS), 1)
    position = first + jnp.bitwise_and(lane, ROWS - 1)
    start = jnp.zeros_like(position)
    end = jnp.int32(0)
    for k in range(DOCS):
        length = lens_ref[0, k]
        end = end + length
        start = start + jnp.where(position >= end, length, 0)
    row = lax.broadcasted_iota(jnp.int32, (ROWS, GROUP * ROWS), 0)
    first_row = start - lower
    last_row = position - lower
    scores = []
    highest = None
    for b in range(count):
        keys = r_ref[lower + b * ROWS : lower + (b + 1) * ROWS, 2 * QW :]
        tile = lax.dot_general(keys, queries, (((1,), (1,)), ((), ())), preferred_element_type=F32)
        allowed = row >= first_row - b * ROWS
        if b == count - 1:
            allowed = allowed & (row <= last_row - b * ROWS)
        tile = jnp.where(allowed, tile, NEG)
        top = jnp.max(tile, axis=0, keepdims=True)
        highest = top if highest is None else jnp.maximum(highest, top)
        scores.append(tile)
    total = None
    weights = []
    for tile in scores:
        weight = jnp.exp2((tile - highest) * (SCALE * math.log2(math.e)))
        part = jnp.sum(weight, axis=0, keepdims=True)
        total = part if total is None else total + part
        weights.append(weight)
    inverse = 1.0 / total
    for b in range(count):
        pt_ref[b * ROWS : (b + 1) * ROWS, :] = (weights[b] * inverse).astype(BF16)


def probs_kernel(lens_ref, from_ref, *refs):
    pieces, (pt_ref, gv_ref, r_ref, acc_ref, sems) = refs[:5], refs[5:]
    i = pl.program_id(0)

    @pl.when(i == 0)
    def _():
        gather_pieces(from_ref, pieces, r_ref, sems)
        acc_ref[...] = jnp.zeros_like(acc_ref)

    def body(v):
        for n, block in enumerate((v, v + MOST)):
            block_probs(block, lens_ref, r_ref, pt_ref.at[0, n])
        for n, block in enumerate((v, v + MOST)):
            count, lower = window(block)
            cot = stacked(r_ref[block * ROWS : (block + 1) * ROWS, QW : 2 * QW])
            size = count * ROWS
            acc_ref[lower : lower + size, :] += dot(pt_ref[0, n, 0:size, :], cot)

    by_step(i, body)

    @pl.when(i == BLOCKS // 2 - 1)
    def _():
        gv_ref[...] = acc_ref[...].astype(BF16)


PROBS_SHAPE = (BLOCKS // 2, 2, MOST * ROWS, GROUP * ROWS)
PROBS_SPEC = pl.BlockSpec((1,) + PROBS_SHAPE[1:], lambda i: (i, 0, 0, 0))


def probs_call(doc_lens, origin, pieces):
    width = 2 * QW + HD
    return pl.pallas_call(
        probs_kernel,
        grid=(BLOCKS // 2,),
        in_specs=[SCALARS, SCALARS] + [ANYWHERE] * 5,
        out_specs=[PROBS_SPEC, pl.BlockSpec((SEQ, HD), lambda i: (0, 0))],
        out_shape=[
            jax.ShapeDtypeStruct(PROBS_SHAPE, BF16),
            jax.ShapeDtypeStruct((SEQ, HD), BF16),
        ],
        scratch_shapes=[
            pltpu.VMEM((SEQ, width), BF16),
            pltpu.VMEM((SEQ, HD), F32),
            pltpu.SemaphoreType.DMA((8,)),
        ],
        compiler_params=params(),
    )(doc_lens, origin, *pieces)


def join(refs):
    return jnp.concatenate([ref[...] for ref in refs], axis=0)


def term_kernel(from_ref, *refs):
    hidden_refs, (gv_ref, term_ref, gvt_ref) = refs[:10], refs[10:]

    @pl.when(pl.program_id(0) == 0)
    def _():
        for r in range(8):
            rows = pl.ds(pl.multiple_of(from_ref[r] * ROWS, ROWS), ROWS)
            gvt_ref[:, r * ROWS : (r + 1) * ROWS] = gv_ref[rows, :].T

    term = dot(gvt_ref[...], join(hidden_refs))
    term_ref[...] = (term.T * INV_WIDTH).astype(BF16)


def values_kernel(from_ref, *refs):
    hidden_refs, (w_ref, val_ref, acc_ref) = refs[:10], refs[10:]
    j = pl.program_id(0)

    @pl.when(j == 0)
    def _():
        acc_ref[...] = jnp.zeros_like(acc_ref)

    acc_ref[...] += dot(join(hidden_refs), w_ref[...])

    @pl.when(j == pl.num_programs(0) - 1)
    def _():
        for r in range(8):
            rows = pl.ds(pl.multiple_of(from_ref[r] * ROWS, ROWS), ROWS)
            part = acc_ref[r * ROWS : (r + 1) * ROWS, :]
            val_ref[rows, :] = (part * INV_WIDTH).astype(BF16)


STRIPE = 1024


def hidden_specs(pieces):
    return [pl.BlockSpec((piece.shape[0], STRIPE), lambda j: (0, j)) for piece in pieces]


def term_call(origin, pieces, grad_values):
    return pl.pallas_call(
        term_kernel,
        grid=(D // STRIPE,),
        in_specs=[SCALARS]
        + hidden_specs(pieces)
        + [pl.BlockSpec((SEQ, HD), lambda j: (0, 0))],
        out_specs=pl.BlockSpec((STRIPE, HD), lambda j: (j, 0)),
        out_shape=jax.ShapeDtypeStruct((D, HD), BF16),
        scratch_shapes=[pltpu.VMEM((HD, SEQ), BF16)],
        compiler_params=params(),
    )(origin, *pieces, grad_values)


def values_call(origin, pieces, weight):
    return pl.pallas_call(
        values_kernel,
        grid=(D // STRIPE,),
        in_specs=[SCALARS]
        + hidden_specs(pieces)
        + [pl.BlockSpec((STRIPE, HD), lambda j: (j, 0))],
        out_specs=pl.BlockSpec((SEQ, HD), lambda j: (0, 0)),
        out_shape=jax.ShapeDtypeStruct((SEQ, HD), BF16),
        scratch_shapes=[pltpu.VMEM((SEQ, HD), F32)],
        compiler_params=params(),
    )(origin, *pieces, weight)


def block_grads(block, r_ref, pt_ref, val_ref, out_ref, acc_ref, kt_ref, vt_ref):
    first = block * ROWS
    count, lower = window(block)
    size = count * ROWS
    queries = stacked(r_ref[first : first + ROWS, 0:QW])
    cot_t = stacked(r_ref[first : first + ROWS, QW : 2 * QW]).T
    attn_t = dot(vt_ref[:, lower : lower + size], pt_ref[0:size, :]).astype(BF16)
    delta = jnp.sum(attn_t.astype(F32) * cot_t.astype(F32), axis=0, keepdims=True)
    prob_grad = dot(val_ref[lower : lower + size, :], cot_t)
    probs = pt_ref[0:size, :].astype(F32)
    score_grad = (probs * (prob_grad - delta)).astype(BF16)
    acc_ref[lower : lower + size, :] += dot(score_grad, queries)
    grad_t = dot(kt_ref[:, lower : lower + size], score_grad) * SCALE
    grad = grad_t.T.astype(BF16)
    for a in range(GROUP):
        out_ref[first : first + ROWS, a * HD : (a + 1) * HD] = grad[a * ROWS : (a + 1) * ROWS, :]


def grads_kernel(from_ref, to_ref, *refs):
    pieces, (pt_ref, val_ref), outs = refs[:5], refs[5:7], refs[7 : 7 + XS]
    r_ref, out_ref, acc_ref, kt_ref, vt_ref, sems = refs[7 + XS :]
    i = pl.program_id(0)

    @pl.when(i == 0)
    def _():
        gather_pieces(from_ref, pieces, r_ref, sems)
        acc_ref[...] = jnp.zeros_like(acc_ref)
        kt_ref[...] = r_ref[:, 2 * QW :].T
        vt_ref[...] = val_ref[...].T

    def body(v):
        for n, block in enumerate((v, v + MOST)):
            block_grads(block, r_ref, pt_ref.at[0, n], val_ref, out_ref, acc_ref, kt_ref, vt_ref)

    by_step(i, body)

    @pl.when(i == BLOCKS // 2 - 1)
    def _():
        out_ref[:, QW:] = (acc_ref[...] * SCALE).astype(BF16)
        run_copies(
            [
                pltpu.make_async_copy(
                    out_ref.at[pl.ds(pl.multiple_of(to_ref[r] * ROWS, ROWS), ROWS), :],
                    outs[r // 2].at[r % 2],
                    sems.at[r],
                )
                for r in range(8)
            ]
        )


def grads_call(origin, to, pieces, probs, values):
    width = 2 * QW + HD
    return pl.pallas_call(
        grads_kernel,
        grid=(BLOCKS // 2,),
        in_specs=[SCALARS, SCALARS]
        + [ANYWHERE] * 5
        + [PROBS_SPEC, pl.BlockSpec((SEQ, HD), lambda i: (0, 0))],
        out_specs=[ANYWHERE] * XS,
        out_shape=[jax.ShapeDtypeStruct((2, ROWS, QW + HD), BF16)] * XS,
        scratch_shapes=[
            pltpu.VMEM((SEQ, width), BF16),
            pltpu.VMEM((SEQ, QW + HD), BF16),
            pltpu.VMEM((SEQ, HD), F32),
            pltpu.VMEM((HD, SEQ), BF16),
            pltpu.VMEM((HD, SEQ), BF16),
            pltpu.SemaphoreType.DMA((8,)),
        ],
        compiler_params=params(),
    )(origin, to, *pieces, probs, values)


def unpack_kernel(from_ref, *refs):
    pieces, (q_ref, k_ref, sems) = refs[:5], refs[5:]
    copies = []
    for r, piece in enumerate(arrived(pieces)):
        j = from_ref[r]
        wide = pl.ds(pl.multiple_of(j * QW, QW), QW)
        thin = pl.ds(pl.multiple_of(j * HD, HD), HD)
        copies.append(
            pltpu.make_async_copy(piece.at[:, pl.ds(0, QW)], q_ref.at[:, wide], sems.at[2 * r])
        )
        copies.append(
            pltpu.make_async_copy(piece.at[:, pl.ds(QW, HD)], k_ref.at[:, thin], sems.at[2 * r + 1])
        )
    run_copies(copies)


def unpack(origin, pieces):
    return pl.pallas_call(
        unpack_kernel,
        in_specs=[SCALARS] + [ANYWHERE] * 5,
        out_specs=[ANYWHERE] * 2,
        out_shape=[
            jax.ShapeDtypeStruct((ROWS, 8 * QW), BF16),
            jax.ShapeDtypeStruct((ROWS, 8 * HD), BF16),
        ],
        scratch_shapes=[pltpu.SemaphoreType.DMA((16,))],
        compiler_params=params(4),
    )(origin, *pieces)


def adam_kernel(
    parts_ref,
    master_ref,
    mc_ref,
    ms_ref,
    vc_ref,
    vs_ref,
    master_out,
    mc_out,
    ms_out,
    vc_out,
    vs_out,
    grad_ref,
    mold_ref,
    vold_ref,
    step_ref,
    mcode_ref,
    vcode_ref,
):
    total = jnp.zeros(grad_ref.shape, F32)
    for g in range(parts_ref.shape[0]):
        total = total + parts_ref[g].astype(F32)
    grad_ref[...] = total
    mold_ref[...] = mc_ref[...].astype(F32)
    vold_ref[...] = vc_ref[...].astype(F32)
    half = grad_ref.shape[0] // 2
    first_fix = 1.0 - 0.9**STEP
    second_fix = 1.0 - 0.999**STEP
    news = []
    for odd in range(2):
        rows = pl.ds(odd, half, stride=2)
        grad = grad_ref[rows, :]
        m_new = 0.9 * (mold_ref[rows, :] * ms_ref[...]) + 0.1 * grad
        v_new = 0.999 * (vold_ref[rows, :] * vs_ref[...]) + 0.001 * grad * grad
        step_ref[rows, :] = m_new / first_fix / (jnp.sqrt(v_new / second_fix) + 1e-08)
        news.append((m_new, v_new))
    m_top = jnp.maximum(
        jnp.max(jnp.abs(news[0][0]), axis=1, keepdims=True),
        jnp.max(jnp.abs(news[1][0]), axis=1, keepdims=True),
    )
    v_top = jnp.maximum(
        jnp.max(jnp.abs(news[0][1]), axis=1, keepdims=True),
        jnp.max(jnp.abs(news[1][1]), axis=1, keepdims=True),
    )
    ms_out[...] = m_top
    vs_out[...] = v_top
    for odd in range(2):
        rows = pl.ds(odd, half, stride=2)
        mcode_ref[rows, :] = news[odd][0] / (m_top + 1e-06)
        vcode_ref[rows, :] = news[odd][1] / (v_top + 1e-06)
    mc_out[...] = mcode_ref[...].astype(BF16)
    vc_out[...] = vcode_ref[...].astype(BF16)
    master_out[...] = master_ref[...] - 0.01 * step_ref[...]


def adam_call(parts, master, m_code, m_scale, v_code, v_scale):
    shape = master.shape
    return pl.pallas_call(
        adam_kernel,
        out_shape=[
            jax.ShapeDtypeStruct(shape, F32),
            jax.ShapeDtypeStruct(shape, BF16),
            jax.ShapeDtypeStruct(m_scale.shape, F32),
            jax.ShapeDtypeStruct(shape, BF16),
            jax.ShapeDtypeStruct(v_scale.shape, F32),
        ],
        scratch_shapes=[pltpu.VMEM(shape, F32) for _ in range(6)],
        compiler_params=params(16),
    )(parts, master, m_code, m_scale, v_code, v_scale)


def shards(hidden, query, key, grad_out, doc_lens, master, m_code, m_scale, v_code, v_scale):
    n_dp = lax.axis_size("dp")
    me = lax.axis_index("seq")
    to = jnp.stack([place(me, r // 2, r % 2) for r in range(8)])
    origin = jnp.stack([place(me, (XS - r // 2) % XS, r % 2) for r in range(8)])
    around = jnp.stack([place(me, dx, dc) for dx in (0, 3, 1, 2) for dc in (0, 1)])
    own = hidden[0]
    half = own.shape[0] // 2
    left, right = send(own, 1, 0), send(own, 3, 0)
    pairs = pack(to, query[0], grad_out[0], key[0])
    pieces = exchange(pairs)
    master_bf, _ = lax.optimization_barrier((master.astype(BF16), pairs[0]))
    copies = jnp.broadcast_to(master_bf[None], (n_dp,) + master.shape)
    weight = lax.all_to_all(copies, "dp", split_axis=0, concat_axis=0, tiled=True)
    weight = weight.reshape(D, HD)
    far_lo, far_hi = send(left[:half], 1, 0), send(right[half:], 3, 0)
    own_core, left_core, right_core = send(own, 0, 1), send(left, 0, 1), send(right, 0, 1)
    probs, grad_values = probs_call(doc_lens, origin, pieces)
    far_lo, far_hi, grad_values = lax.optimization_barrier((far_lo, far_hi, grad_values))
    far_core = [send(far_lo, 0, 1), send(far_hi, 0, 1)]
    hiddens = [own, own_core, left, left_core, right, right_core, far_lo, far_hi] + far_core
    term = term_call(around, hiddens, grad_values)
    parts = lax.all_to_all(
        term.reshape((n_dp,) + master.shape), "dp", split_axis=0, concat_axis=0, tiled=True
    )
    values = values_call(around, hiddens, weight)
    grads = grads_call(origin, to, pieces, probs, values)
    grad_query, grad_key = unpack(origin, exchange(grads))
    state = adam_call(parts, master, m_code, m_scale, v_code, v_scale)
    return (grad_query[None], grad_key[None]) + tuple(state)


def solution(mesh):
    return jax.shard_map(
        shards,
        mesh=mesh,
        in_specs=(
            P("dp", "seq", None),
            P("dp", "seq", None),
            P("dp", "seq", None),
            P("dp", "seq", None),
            P("dp", None),
            P("dp", "seq"),
            P("dp", "seq"),
            P("dp", "seq"),
            P("dp", "seq"),
            P("dp", "seq"),
        ),
        out_specs=(
            P("dp", "seq", None),
            P("dp", "seq", None),
            P("dp", "seq"),
            P("dp", "seq"),
            P("dp", "seq"),
            P("dp", "seq"),
            P("dp", "seq"),
        ),
        check_vma=False,
    )
```

time: 171 us -> 245 us (1.43)
  Pallas kernels: 32.8 us -> 105 us
  waiting for transfers between devices: 17.3 us -> 39.2 us
  starting transfers between devices: 104 us -> 87.3 us
  local copies, waits for them, and re-layouts: 14.2 us -> 11.6 us
    pallas_call x1, Pallas kernels: 1.22 us -> 73.5 us  [pack(): pl.pallas_call(pack_kernel, in_specs=[SCALARS, ANYWHERE, ANYWHERE, ANYWHE...]
    ppermute x23 -> x17, waiting for transfers between devices: 17.3 us -> 39.2 us  [send(): return lax.ppermute(array, 'seq', pairs)]
    ppermute x23 -> x17, starting transfers between devices: 74.4 us -> 53.6 us  [send(): return lax.ppermute(array, 'seq', pairs)]
    all_to_all x1, starting transfers between devices: 12.5 us -> 16.9 us  [shards(): lax.all_to_all(term.reshape((n_dp,) + master.shape), 'dp', split_axis=0,...]
    unnamed x38 -> x42, local copies, waits for them, and re-layouts: 10.6 us -> 7.93 us
    pallas_call x4 -> x7, Pallas kernels: 30.7 us -> 29.4 us  [the longest x1 8.21 us: grads_call(): pl.pallas_call(grads_kernel, grid=(BLOCKS // 2,), in_specs=[SCALARS, SCAL...]
  transfers between devices with their start and end apart: 25 -> 19, of which waited for: 5 -> 8; matrix products, arithmetic and copies ran while one was open for 3% -> 1% of each run, Pallas kernels for 14% -> 12%
where the time goes in v3:
time: 245 us; the launch traced here: 244 us
  Pallas kernels  105 us (43%)
  starting transfers between devices  87.3 us (36%)
  waiting for transfers between devices  39.2 us (16%)
  local copies, waits for them, and re-layouts  11.6 us (5%)
    pallas_call x1, Pallas kernels, pack(): pl.pallas_call(pack_kernel, in_specs=[SCALARS, ANYWHERE, ANYWHERE, ANYWHE...  73.5 us
    ppermute x17, starting transfers between devices, send(): return lax.ppermute(array, 'seq', pairs)  53.6 us
    ppermute x17, waiting for transfers between devices, send(): return lax.ppermute(array, 'seq', pairs)  39.2 us
    all_to_all x1, starting transfers between devices, shards(): lax.all_to_all(term.reshape((n_dp,) + master.shape), 'dp', split_axis=0,...  16.9 us
    all_to_all x1, starting transfers between devices, shards(): lax.all_to_all(copies, 'dp', split_axis=0, concat_axis=0, tiled=True)  16.8 us
    pallas_call x1, Pallas kernels, grads_call(): pl.pallas_call(grads_kernel, grid=(BLOCKS // 2,), in_specs=[SCALARS, SCAL...  8.21 us
    unnamed x42, local copies, waits for them, and re-layouts  7.93 us
    pallas_call x1, Pallas kernels, probs_call(): pl.pallas_call(probs_kernel, grid=(BLOCKS // 2,), in_specs=[SCALARS, SCAL...  7.2 us
  transfers between devices with their start and end apart: 19, of which 8 were waited for; matrix products, arithmetic and copies ran while one was open for 1% of the time, Pallas kernels for 12%

profile of v3, /device:TPU:1, one launch (start us, length us, event | category | flops | bytes accessed | tf_op | source)
XLA Modules:
  0.0 244.2 jit_solution(14342333739875004026)
XLA Ops:
  0.7 0.6 stack.58.to_ref
  1.3 73.5 %shard_map.153 = (bf16[2,128,1152]{2,1,0:T(8,128)(2,1)}, bf16[2,128,1152]{2,1,0:T(8,128)(2,1)}, bf16[2,128,1152]{2,1,0:T(8,128)(2,1)}, bf16[2,128,1152]{2,1,0:T(8,128)(2,1)}) custom-call(s32[8]{0:T(128)} %stack.58.to_ref, bf16[128,4096]{1,0:T(8,128)(2,1)} %bitcast.17, bf16[128,4096]{1,0:T(8,128)(2,1)} %bitcast.18, bf16[128,1024]{1,0:T(8,128)(2,1)} %bitcast.19), custom_call_target="tpu_custom_call" | custom-call | tf_op jit(solution)/shard_map/pallas_call | solution.py:87
  74.8 3.9 %collective-permute-start = (bf16[2,128,1152]{2,1,0:T(8,128)(2,1)}, bf16[2,128,1152]{2,1,0:T(8,128)(2,1)S(1)}, u32[]{:S(2)}, u32[]{:S(2)}) collective-permute-start(bf16[2,128,1152]{2,1,0:T(8,128)(2,1)} %get-tuple-element.29), channel_id=1, source_target_pairs={{0,128},{64,192},{128,256},{192,320},{256,384},{320,448},{384,0},{... | collective-permute-start | bytes 1769480 | tf_op jit(solution)/shard_map/ppermute | solution.py:50
  78.7 4.4 %collective-permute-start.1 = (bf16[2,128,1152]{2,1,0:T(8,128)(2,1)}, bf16[2,128,1152]{2,1,0:T(8,128)(2,1)S(1)}, u32[]{:S(2)}, u32[]{:S(2)}) collective-permute-start(bf16[2,128,1152]{2,1,0:T(8,128)(2,1)} %get-tuple-element.30), channel_id=1, source_target_pairs={{0,256},{64,320},{128,384},{192,448},{256,0},{320,64},{384,128},{4... | collective-permute-start | bytes 1769480 | tf_op jit(solution)/shard_map/ppermute | solution.py:50
  83.1 3.1 %collective-permute-start.2 = (bf16[2,128,1152]{2,1,0:T(8,128)(2,1)}, bf16[2,128,1152]{2,1,0:T(8,128)(2,1)S(1)}, u32[]{:S(2)}, u32[]{:S(2)}) collective-permute-start(bf16[2,128,1152]{2,1,0:T(8,128)(2,1)} %get-tuple-element.31), channel_id=1, source_target_pairs={{0,384},{64,448},{128,0},{192,64},{256,128},{320,192},{384,256},{4... | collective-permute-start | bytes 1769480 | tf_op jit(solution)/shard_map/ppermute | solution.py:50
  86.2 1.3 collective-permute-done.refs_1_
  87.5 19.3 %collective-permute-done.1.refs_2_ = bf16[2,128,1152]{2,1,0:T(8,128)(2,1)S(1)} collective-permute-done((bf16[2,128,1152]{2,1,0:T(8,128)(2,1)}, bf16[2,128,1152]{2,1,0:T(8,128)(2,1)S(1)}, u32[]{:S(2)}, u32[]{:S(2)}) %collective-permute-start.1) | collective-permute-done | bytes 589856 | tf_op jit(solution)/shard_map/ppermute | solution.py:50
  106.7 0.0 collective-permute-done.2.refs_3_
  106.8 1.5 copy-done
  108.2 1.1 shard_map.154
  109.3 4.6 %collective-permute-start.3 = (bf16[4,128,1152]{2,1,0:T(8,128)(2,1)}, bf16[4,128,1152]{2,1,0:T(8,128)(2,1)}, u32[]{:S(2)}, u32[]{:S(2)}) collective-permute-start(bf16[4,128,1152]{2,1,0:T(8,128)(2,1)} %shard_map.154), channel_id=1, source_target_pairs={{0,64},{64,0},{128,192},{192,128},{256,320},{320,256},{384,448},{4... | collective-permute-start | bytes 3538952 | tf_op jit(solution)/shard_map/ppermute | solution.py:50
  114.0 4.3 %collective-permute-start.7 = (bf16[128,4096]{1,0:T(8,128)(2,1)}, bf16[128,4096]{1,0:T(8,128)(2,1)S(1)}, u32[]{:S(2)}, u32[]{:S(2)}) collective-permute-start(bf16[128,4096]{1,0:T(8,128)(2,1)} %bitcast.11.refs_0_), channel_id=1, source_target_pairs={{0,384},{64,448},{128,0},{192,64},{256,128},{320,192},{384,256},{4... | collective-permute-start | bytes 3145736 | tf_op jit(solution)/shard_map/ppermute | solution.py:50
  118.2 1.9 collective-permute-start.5
  120.2 1.2 broadcast_in_dim.12
  121.4 16.8 %all-to-all-start = ((bf16[64,64,128]{2,1,0:T(8,128)(2,1)}), bf16[64,64,128]{2,1,0:T(8,128)(2,1)}, u32[]{:S(2)}, u32[]{:S(2)}) async-start(bf16[64,64,128]{2,1,0:T(8,128)(2,1)} %broadcast_in_dim.12), calls=%async_computation | async-start | bytes 2097152 | tf_op jit(solution)/shard_map/all_to_all | solution.py:493
  138.2 0.0 copy-start.16
  138.2 3.7 %collective-permute-done.7.refs_4_ = bf16[128,4096]{1,0:T(8,128)(2,1)S(1)} collective-permute-done((bf16[128,4096]{1,0:T(8,128)(2,1)}, bf16[128,4096]{1,0:T(8,128)(2,1)S(1)}, u32[]{:S(2)}, u32[]{:S(2)}) %collective-permute-start.7) | collective-permute-done | bytes 1048608 | tf_op jit(solution)/shard_map/ppermute | solution.py:50
  141.9 0.8 slice.9
  142.7 4.4 %collective-permute-start.10 = (bf16[64,4096]{1,0:T(8,128)(2,1)}, bf16[64,4096]{1,0:T(8,128)(2,1)}, u32[]{:S(2)}, u32[]{:S(2)}) collective-permute-start(bf16[64,4096]{1,0:T(8,128)(2,1)} %slice.9), channel_id=1, source_target_pairs={{0,384},{64,448},{128,0},{192,64},{256,128},{320,192},{384,256},{4... | collective-permute-start | bytes 1572872 | tf_op jit(solution)/shard_map/ppermute | solution.py:50
  147.1 0.0 collective-permute-done.5.refs_2_
  147.2 0.8 slice.8
  148.0 1.9 collective-permute-start.9
  149.9 3.0 %collective-permute-start.4 = (bf16[128,4096]{1,0:T(8,128)(2,1)}, bf16[128,4096]{1,0:T(8,128)(2,1)}, u32[]{:S(2)}, u32[]{:S(2)}) collective-permute-start(bf16[128,4096]{1,0:T(8,128)(2,1)} %bitcast.11.refs_0_), channel_id=1, source_target_pairs={{0,64},{64,0},{128,192},{192,128},{256,320},{320,256},{384,448},{4... | collective-permute-start | bytes 3145736 | tf_op jit(solution)/shard_map/ppermute | solution.py:50
  152.9 1.9 collective-permute-start.8
  154.8 0.0 collective-permute-done.3.refs_4_
  154.8 2.4 collective-permute-start.6
  157.3 0.1 stack.57.from_ref
  157.4 1.1 copy-done.3
  158.4 1.1 copy-done.6
  159.5 7.2 %shard_map.155 = (bf16[4,2,512,512]{3,2,1,0:T(8,128)(2,1)S(1)}, bf16[1024,128]{1,0:T(8,128)(2,1)S(1)}) custom-call(s32[1,8]{1,0:T(1,128)S(1)} %copy-done.16, s32[8]{0:T(128)S(1)} %stack.57.from_ref, bf16[2,128,1152]{2,1,0:T(8,128)(2,1)S(1)} %copy-done.1, bf16[2,128,1152]{2,1,0:T(8,128)(2,1)S(1)} %collective-permute-done.refs_1_, ...), custom_call_target="tpu_custom_call" | custom-call | tf_op jit(solution)/shard_map/pallas_call | solution.py:218
  166.7 2.0 copy-done.9
  168.7 0.0 collective-permute-done.10.refs_7_
  168.7 1.9 collective-permute-start.11
  170.6 2.4 collective-permute-start.12
  173.0 0.1 stack.59.from_ref
  173.1 0.0 collective-permute-done.11.refs_8_
  173.1 1.7 collective-permute-done.12.refs_9_
  174.9 4.8 %shard_map.160 = bf16[4096,128]{1,0:T(8,128)(2,1)S(1)} custom-call(s32[8]{0:T(128)S(1)} %stack.59.from_ref, bf16[128,4096]{1,0:T(8,128)(2,1)} %bitcast.11.refs_0_, bf16[128,4096]{1,0:T(8,128)(2,1)} %collective-permute-done.4.refs_1_, bf16[128,4096]{1,0:T(8,128)(2,1)S(1)} %collective-permute-done.5.refs_2_, bf16[128,4096]{1,0:T(8,128)(2,1)} %collective-permute-done.6.refs_3_, ...), custom_call_target="tpu_custom_call" | custom-call | tf_op jit(solution)/shard_map/pallas_call | solution.py:279
  179.6 0.9 copy-done.8
  180.6 0.0 all-to-all-done
  180.6 16.9 %all-to-all-start.1 = ((bf16[64,64,128]{2,1,0:T(8,128)(2,1)}), bf16[64,64,128]{2,1,0:T(8,128)(2,1)}, u32[]{:S(2)}, u32[]{:S(2)}) async-start(bf16[64,64,128]{2,1,0:T(8,128)(2,1)} %bitcast.16), calls=%async_computation.1 | async-start | bytes 2097152 | tf_op jit(solution)/shard_map/all_to_all | solution.py:502
  197.6 5.6 %shard_map.156.refs_6_ = bf16[1024,128]{1,0:T(8,128)(2,1)S(1)} custom-call(s32[8]{0:T(128)S(1)} %stack.59.from_ref, bf16[128,4096]{1,0:T(8,128)(2,1)} %bitcast.11.refs_0_, bf16[128,4096]{1,0:T(8,128)(2,1)} %collective-permute-done.4.refs_1_, bf16[128,4096]{1,0:T(8,128)(2,1)S(1)} %collective-permute-done.5.refs_2_, ...), custom_call_target="tpu_custom_call" | custom-call | tf_op jit(solution)/shard_map/pallas_call | solution.py:293
  203.2 8.2 %shard_map.157 = (bf16[2,128,640]{2,1,0:T(8,128)(2,1)S(1)}, bf16[2,128,640]{2,1,0:T(8,128)(2,1)S(1)}, bf16[2,128,640]{2,1,0:T(8,128)(2,1)S(1)}, bf16[2,128,640]{2,1,0:T(8,128)(2,1)S(1)}) custom-call(s32[8]{0:T(128)S(1)} %stack.57.from_ref, s32[8]{0:T(128)S(1)} %copy-done.15, bf16[2,128,1152]{2,1,0:T(8,128)(2,1)S(1)} %copy-done.1, ...), custom_call_target="tpu_custom_call" | custom-call | tf_op jit(solution)/shard_map/pallas_call | solution.py:359
  211.5 0.0 copy-start.17
  211.5 0.0 copy-start.18
  211.5 2.2 collective-permute-start.13
  213.7 5.8 %collective-permute-start.14 = (bf16[2,128,640]{2,1,0:T(8,128)(2,1)S(1)}, bf16[2,128,640]{2,1,0:T(8,128)(2,1)S(1)}, u32[]{:S(2)}, u32[]{:S(2)}) collective-permute-start(bf16[2,128,640]{2,1,0:T(8,128)(2,1)S(1)} %get-tuple-element.39), channel_id=1, source_target_pairs={{0,256},{64,320},{128,384},{192,448},{256,0},{320,64},{384,128},{4... | collective-permute-start | bytes 983048 | tf_op jit(solution)/shard_map/ppermute | solution.py:50
  219.4 1.9 collective-permute-start.15
  221.4 2.5 %collective-permute-done.13.refs_1_ = bf16[2,128,640]{2,1,0:T(8,128)(2,1)S(1)} collective-permute-done((bf16[2,128,640]{2,1,0:T(8,128)(2,1)S(1)}, bf16[2,128,640]{2,1,0:T(8,128)(2,1)S(1)}, u32[]{:S(2)}, u32[]{:S(2)}) %collective-permute-start.13) | collective-permute-done | bytes 327712 | tf_op jit(solution)/shard_map/ppermute | solution.py:50
  223.9 7.8 %collective-permute-done.14.refs_2_ = bf16[2,128,640]{2,1,0:T(8,128)(2,1)S(1)} collective-permute-done((bf16[2,128,640]{2,1,0:T(8,128)(2,1)S(1)}, bf16[2,128,640]{2,1,0:T(8,128)(2,1)S(1)}, u32[]{:S(2)}, u32[]{:S(2)}) %collective-permute-start.14) | collective-permute-done | bytes 327712 | tf_op jit(solution)/shard_map/ppermute | solution.py:50
  231.6 1.4 collective-permute-done.15.refs_3_
  233.0 0.9 shard_map.158
  233.9 0.0 copy-start.12
  233.9 0.0 copy-start.13
  233.9 0.0 copy-start.14
  233.9 3.6 %collective-permute-start.16 = (bf16[4,128,640]{2,1,0:T(8,128)(2,1)S(1)}, bf16[4,128,640]{2,1,0:T(8,128)(2,1)S(1)}, u32[]{:S(2)}, u32[]{:S(2)}) collective-permute-start(bf16[4,128,640]{2,1,0:T(8,128)(2,1)S(1)} %shard_map.158), channel_id=1, source_target_pairs={{0,64},{64,0},{128,192},{192,128},{256,320},{320,256},{384,448},{4... | collective-permute-start | bytes 1966088 | tf_op jit(solution)/shard_map/ppermute | solution.py:50
  237.5 0.1 copy.17.ms_ref
  237.6 0.1 copy.18.vs_ref
  237.7 1.5 collective-permute-done.16.refs_4_
  239.2 1.7 shard_map.159
  240.9 0.0 all-to-all-done.1.parts_ref
  241.0 2.1 shard_map.161
  243.1 0.6 copy.19
  243.7 0.6 copy.20
  (32 shorter events, 0.1 us)
Async XLA Ops:
  74.8 12.7 %collective-permute-start = (bf16[2,128,1152]{2,1,0:T(8,128)(2,1)}, bf16[2,128,1152]{2,1,0:T(8,128)(2,1)S(1)}, u32[]{:S(2)}, u32[]{:S(2)}) collective-permute-start(bf16[2,128,1152]{2,1,0:T(8,128)(2,1)} %get-tuple-element.29), channel_id=1, source_target_pairs={{0,128},{64,192},{128,256},{192,320},{256,384},{320,448},{384,0},{... | collective-permute-start | bytes 1769480 | tf_op jit(solution)/shard_map/ppermute | solution.py:50
  78.7 28.0 %collective-permute-start.1 = (bf16[2,128,1152]{2,1,0:T(8,128)(2,1)}, bf16[2,128,1152]{2,1,0:T(8,128)(2,1)S(1)}, u32[]{:S(2)}, u32[]{:S(2)}) collective-permute-start(bf16[2,128,1152]{2,1,0:T(8,128)(2,1)} %get-tuple-element.30), channel_id=1, source_target_pairs={{0,256},{64,320},{128,384},{192,448},{256,0},{320,64},{384,128},{4... | collective-permute-start | bytes 1769480 | tf_op jit(solution)/shard_map/ppermute | solution.py:50
  83.1 23.6 %collective-permute-start.2 = (bf16[2,128,1152]{2,1,0:T(8,128)(2,1)}, bf16[2,128,1152]{2,1,0:T(8,128)(2,1)S(1)}, u32[]{:S(2)}, u32[]{:S(2)}) collective-permute-start(bf16[2,128,1152]{2,1,0:T(8,128)(2,1)} %get-tuple-element.31), channel_id=1, source_target_pairs={{0,384},{64,448},{128,0},{192,64},{256,128},{320,192},{384,256},{4... | collective-permute-start | bytes 1769480 | tf_op jit(solution)/shard_map/ppermute | solution.py:50
  106.7 2.6 %copy-start.2 = (bf16[2,128,1152]{2,1,0:T(8,128)(2,1)}, bf16[2,128,1152]{2,1,0:T(8,128)(2,1)S(1)}, u32[]{:S(2)}) copy-start(bf16[2,128,1152]{2,1,0:T(8,128)(2,1)S(1)} %collective-permute-done.1.refs_2_) | copy-start | bytes 1769476
  106.7 2.6 %copy-start.5 = (bf16[2,128,1152]{2,1,0:T(8,128)(2,1)}, bf16[2,128,1152]{2,1,0:T(8,128)(2,1)S(1)}, u32[]{:S(2)}) copy-start(bf16[2,128,1152]{2,1,0:T(8,128)(2,1)S(1)} %collective-permute-done.2.refs_3_) | copy-start | bytes 1769476
  106.8 1.5 copy-start
  108.2 11.9 %copy-start.11 = (f32[64,128]{1,0:T(8,128)S(1)}, f32[64,128]{1,0:T(8,128)}, u32[]{:S(2)}) copy-start(f32[64,128]{1,0:T(8,128)} %master_ref.1) | copy-start | bytes 98308
  109.3 45.5 %collective-permute-start.3 = (bf16[4,128,1152]{2,1,0:T(8,128)(2,1)}, bf16[4,128,1152]{2,1,0:T(8,128)(2,1)}, u32[]{:S(2)}, u32[]{:S(2)}) collective-permute-start(bf16[4,128,1152]{2,1,0:T(8,128)(2,1)} %shard_map.154), channel_id=1, source_target_pairs={{0,64},{64,0},{128,192},{192,128},{256,320},{320,256},{384,448},{4... | collective-permute-start | bytes 3538952 | tf_op jit(solution)/shard_map/ppermute | solution.py:50
  114.0 27.9 %collective-permute-start.7 = (bf16[128,4096]{1,0:T(8,128)(2,1)}, bf16[128,4096]{1,0:T(8,128)(2,1)S(1)}, u32[]{:S(2)}, u32[]{:S(2)}) collective-permute-start(bf16[128,4096]{1,0:T(8,128)(2,1)} %bitcast.11.refs_0_), channel_id=1, source_target_pairs={{0,384},{64,448},{128,0},{192,64},{256,128},{320,192},{384,256},{4... | collective-permute-start | bytes 3145736 | tf_op jit(solution)/shard_map/ppermute | solution.py:50
  118.2 28.9 %collective-permute-start.5 = (bf16[128,4096]{1,0:T(8,128)(2,1)}, bf16[128,4096]{1,0:T(8,128)(2,1)S(1)}, u32[]{:S(2)}, u32[]{:S(2)}) collective-permute-start(bf16[128,4096]{1,0:T(8,128)(2,1)} %bitcast.11.refs_0_), channel_id=1, source_target_pairs={{0,128},{64,192},{128,256},{192,320},{256,384},{320,448},{384,0},{... | collective-permute-start | bytes 3145736 | tf_op jit(solution)/shard_map/ppermute | solution.py:50
  121.4 59.2 %all-to-all-start = ((bf16[64,64,128]{2,1,0:T(8,128)(2,1)}), bf16[64,64,128]{2,1,0:T(8,128)(2,1)}, u32[]{:S(2)}, u32[]{:S(2)}) async-start(bf16[64,64,128]{2,1,0:T(8,128)(2,1)} %broadcast_in_dim.12), calls=%async_computation | async-start | bytes 2097152 | tf_op jit(solution)/shard_map/all_to_all | solution.py:493
  138.2 19.2 %copy-start.1 = (bf16[2,128,1152]{2,1,0:T(8,128)(2,1)S(1)}, bf16[2,128,1152]{2,1,0:T(8,128)(2,1)}, u32[]{:S(2)}) copy-start(bf16[2,128,1152]{2,1,0:T(8,128)(2,1)} %get-tuple-element.28.refs_0_) | copy-start | bytes 1769476
  138.2 19.2 %copy-start.16 = (s32[1,8]{1,0:T(1,128)S(1)}, s32[1,8]{1,0:T(1,128)}, u32[]{:S(2)}) copy-start(s32[1,8]{1,0:T(1,128)} %lens_ref.1) | copy-start | bytes 100
  142.7 26.0 %collective-permute-start.10 = (bf16[64,4096]{1,0:T(8,128)(2,1)}, bf16[64,4096]{1,0:T(8,128)(2,1)}, u32[]{:S(2)}, u32[]{:S(2)}) collective-permute-start(bf16[64,4096]{1,0:T(8,128)(2,1)} %slice.9), channel_id=1, source_target_pairs={{0,384},{64,448},{128,0},{192,64},{256,128},{320,192},{384,256},{4... | collective-permute-start | bytes 1572872 | tf_op jit(solution)/shard_map/ppermute | solution.py:50
  148.0 20.7 %collective-permute-start.9 = (bf16[64,4096]{1,0:T(8,128)(2,1)}, bf16[64,4096]{1,0:T(8,128)(2,1)}, u32[]{:S(2)}, u32[]{:S(2)}) collective-permute-start(bf16[64,4096]{1,0:T(8,128)(2,1)} %slice.8), channel_id=1, source_target_pairs={{0,128},{64,192},{128,256},{192,320},{256,384},{320,448},{384,0},{... | collective-permute-start | bytes 1572872 | tf_op jit(solution)/shard_map/ppermute | solution.py:50
  149.9 23.2 %collective-permute-start.4 = (bf16[128,4096]{1,0:T(8,128)(2,1)}, bf16[128,4096]{1,0:T(8,128)(2,1)}, u32[]{:S(2)}, u32[]{:S(2)}) collective-permute-start(bf16[128,4096]{1,0:T(8,128)(2,1)} %bitcast.11.refs_0_), channel_id=1, source_target_pairs={{0,64},{64,0},{128,192},{192,128},{256,320},{320,256},{384,448},{4... | collective-permute-start | bytes 3145736 | tf_op jit(solution)/shard_map/ppermute | solution.py:50
  152.9 20.2 %collective-permute-start.8 = (bf16[128,4096]{1,0:T(8,128)(2,1)S(1)}, bf16[128,4096]{1,0:T(8,128)(2,1)}, u32[]{:S(2)}, u32[]{:S(2)}) collective-permute-start(bf16[128,4096]{1,0:T(8,128)(2,1)S(1)} %collective-permute-done.7.refs_4_), channel_id=1, source_target_pairs={{0,64},{64,0},{128,192},{192,128},{256,320},{320,256},{384,448},{4... | collective-permute-start | bytes 3145736 | tf_op jit(solution)/shard_map/ppermute | solution.py:50
  154.8 18.3 %collective-permute-start.6 = (bf16[128,4096]{1,0:T(8,128)(2,1)S(1)}, bf16[128,4096]{1,0:T(8,128)(2,1)}, u32[]{:S(2)}, u32[]{:S(2)}) collective-permute-start(bf16[128,4096]{1,0:T(8,128)(2,1)S(1)} %collective-permute-done.5.refs_2_), channel_id=1, source_target_pairs={{0,64},{64,0},{128,192},{192,128},{256,320},{320,256},{384,448},{4... | collective-permute-start | bytes 3145736 | tf_op jit(solution)/shard_map/ppermute | solution.py:50
  157.3 1.1 copy-start.3
  158.4 1.1 copy-start.6
  166.7 2.0 copy-start.9
  168.7 4.5 %collective-permute-start.11 = (bf16[64,4096]{1,0:T(8,128)(2,1)}, bf16[64,4096]{1,0:T(8,128)(2,1)}, u32[]{:S(2)}, u32[]{:S(2)}) collective-permute-start(bf16[64,4096]{1,0:T(8,128)(2,1)} %collective-permute-done.9.refs_6_), channel_id=1, source_target_pairs={{0,64},{64,0},{128,192},{192,128},{256,320},{320,256},{384,448},{4... | collective-permute-start | bytes 1572872 | tf_op jit(solution)/shard_map/ppermute | solution.py:50
  170.6 4.3 %collective-permute-start.12 = (bf16[64,4096]{1,0:T(8,128)(2,1)}, bf16[64,4096]{1,0:T(8,128)(2,1)}, u32[]{:S(2)}, u32[]{:S(2)}) collective-permute-start(bf16[64,4096]{1,0:T(8,128)(2,1)} %collective-permute-done.10.refs_7_), channel_id=1, source_target_pairs={{0,64},{64,0},{128,192},{192,128},{256,320},{320,256},{384,448},{4... | collective-permute-start | bytes 1572872 | tf_op jit(solution)/shard_map/ppermute | solution.py:50
  179.6 1.0 copy-start.8
  180.6 60.3 %all-to-all-start.1 = ((bf16[64,64,128]{2,1,0:T(8,128)(2,1)}), bf16[64,64,128]{2,1,0:T(8,128)(2,1)}, u32[]{:S(2)}, u32[]{:S(2)}) async-start(bf16[64,64,128]{2,1,0:T(8,128)(2,1)} %bitcast.16), calls=%async_computation.1 | async-start | bytes 2097152 | tf_op jit(solution)/shard_map/all_to_all | solution.py:502
  197.5 5.7 %copy-start.4 = (bf16[2,128,1152]{2,1,0:T(8,128)(2,1)S(1)}, bf16[2,128,1152]{2,1,0:T(8,128)(2,1)}, u32[]{:S(2)}) copy-start(bf16[2,128,1152]{2,1,0:T(8,128)(2,1)} %copy-done.2) | copy-start | bytes 1769476
  197.6 5.7 %copy-start.7 = (bf16[2,128,1152]{2,1,0:T(8,128)(2,1)S(1)}, bf16[2,128,1152]{2,1,0:T(8,128)(2,1)}, u32[]{:S(2)}) copy-start(bf16[2,128,1152]{2,1,0:T(8,128)(2,1)} %copy-done.5) | copy-start | bytes 1769476
  197.6 5.7 %copy-start.10 = (bf16[4,2,512,512]{3,2,1,0:T(8,128)(2,1)S(1)}, bf16[4,2,512,512]{3,2,1,0:T(8,128)(2,1)}, u32[]{:S(2)}) copy-start(bf16[4,2,512,512]{3,2,1,0:T(8,128)(2,1)} %copy-done.9) | copy-start | bytes 12582916
  197.6 5.7 %copy-start.15 = (s32[8]{0:T(128)S(1)}, s32[8]{0:T(128)}, u32[]{:S(2)}) copy-start(s32[8]{0:T(128)} %stack.58.to_ref) | copy-start | bytes 100
  211.5 26.0 %copy-start.17 = (f32[32,1]{0,1:T(1,128)S(1)}, f32[32,1]{0,1:T(1,128)}, u32[]{:S(2)}) copy-start(f32[32,1]{0,1:T(1,128)} %param.17) | copy-start | bytes 388
  211.5 26.1 %copy-start.18 = (f32[32,1]{0,1:T(1,128)S(1)}, f32[32,1]{0,1:T(1,128)}, u32[]{:S(2)}) copy-start(f32[32,1]{0,1:T(1,128)} %param.19) | copy-start | bytes 388
  211.5 12.4 %collective-permute-start.13 = (bf16[2,128,640]{2,1,0:T(8,128)(2,1)S(1)}, bf16[2,128,640]{2,1,0:T(8,128)(2,1)S(1)}, u32[]{:S(2)}, u32[]{:S(2)}) collective-permute-start(bf16[2,128,640]{2,1,0:T(8,128)(2,1)S(1)} %get-tuple-element.38), channel_id=1, source_target_pairs={{0,128},{64,192},{128,256},{192,320},{256,384},{320,448},{384,0},{... | collective-permute-start | bytes 983048 | tf_op jit(solution)/shard_map/ppermute | solution.py:50
  213.7 18.0 %collective-permute-start.14 = (bf16[2,128,640]{2,1,0:T(8,128)(2,1)S(1)}, bf16[2,128,640]{2,1,0:T(8,128)(2,1)S(1)}, u32[]{:S(2)}, u32[]{:S(2)}) collective-permute-start(bf16[2,128,640]{2,1,0:T(8,128)(2,1)S(1)} %get-tuple-element.39), channel_id=1, source_target_pairs={{0,256},{64,320},{128,384},{192,448},{256,0},{320,64},{384,128},{4... | collective-permute-start | bytes 983048 | tf_op jit(solution)/shard_map/ppermute | solution.py:50
  219.4 13.6 %collective-permute-start.15 = (bf16[2,128,640]{2,1,0:T(8,128)(2,1)S(1)}, bf16[2,128,640]{2,1,0:T(8,128)(2,1)S(1)}, u32[]{:S(2)}, u32[]{:S(2)}) collective-permute-start(bf16[2,128,640]{2,1,0:T(8,128)(2,1)S(1)} %get-tuple-element.40), channel_id=1, source_target_pairs={{0,384},{64,448},{128,0},{192,64},{256,128},{320,192},{384,256},{4... | collective-permute-start | bytes 983048 | tf_op jit(solution)/shard_map/ppermute | solution.py:50
  233.9 7.1 %copy-start.12 = (f32[64,128]{1,0:T(8,128)S(1)}, f32[64,128]{1,0:T(8,128)}, u32[]{:S(2)}) copy-start(f32[64,128]{1,0:T(8,128)} %master_ref.1) | copy-start | bytes 98308
  233.9 7.1 %copy-start.13 = (bf16[64,128]{1,0:T(8,128)(2,1)S(1)}, bf16[64,128]{1,0:T(8,128)(2,1)}, u32[]{:S(2)}) copy-start(bf16[64,128]{1,0:T(8,128)(2,1)} %mc_ref.1) | copy-start | bytes 49156
  233.9 7.1 %copy-start.14 = (bf16[64,128]{1,0:T(8,128)(2,1)S(1)}, bf16[64,128]{1,0:T(8,128)(2,1)}, u32[]{:S(2)}) copy-start(bf16[64,128]{1,0:T(8,128)(2,1)} %vc_ref.1) | copy-start | bytes 49156
  233.9 5.3 %collective-permute-start.16 = (bf16[4,128,640]{2,1,0:T(8,128)(2,1)S(1)}, bf16[4,128,640]{2,1,0:T(8,128)(2,1)S(1)}, u32[]{:S(2)}, u32[]{:S(2)}) collective-permute-start(bf16[4,128,640]{2,1,0:T(8,128)(2,1)S(1)} %shard_map.158), channel_id=1, source_target_pairs={{0,64},{64,0},{128,192},{192,128},{256,320},{320,256},{384,448},{4... | collective-permute-start | bytes 1966088 | tf_op jit(solution)/shard_map/ppermute | solution.py:50

commit v4 on v3

--- a/solution.py
+++ b/solution.py
@@ -86,7 +86,7 @@
     tokens = query.shape[0]
     return pl.pallas_call(
         pack_kernel,
-        in_specs=[SCALARS, ANYWHERE, ANYWHERE, ANYWHERE],
+        in_specs=[SCALARS] + [pl.BlockSpec(memory_space=pltpu.VMEM)] * 3,
         out_specs=[ANYWHERE] * XS,
         out_shape=[jax.ShapeDtypeStruct((2, tokens, 2 * QW + HD), BF16)] * XS,
         scratch_shapes=[pltpu.SemaphoreType.DMA((24,))],
@@ -495,7 +495,7 @@
     far_lo, far_hi = send(left[:half], 1, 0), send(right[half:], 3, 0)
     own_core, left_core, right_core = send(own, 0, 1), send(left, 0, 1), send(right, 0, 1)
     probs, grad_values = probs_call(doc_lens, origin, pieces)
-    far_lo, far_hi, grad_values = lax.optimization_barrier((far_lo, far_hi, grad_values))
+
     far_core = [send(far_lo, 0, 1), send(far_hi, 0, 1)]
     hiddens = [own, own_core, left, left_core, right, right_core, far_lo, far_hi] + far_core
     term = term_call(around, hiddens, grad_values)

time: 245 us -> 166 us (0.68)
  Pallas kernels: 105 us -> 34.9 us
  waiting for transfers between devices: 39.2 us -> 33.2 us
  local copies, waits for them, and re-layouts: 11.6 us -> 8.82 us
    pallas_call x1, Pallas kernels: 73.5 us -> 3.28 us  [pack(): pl.pallas_call(pack_kernel, in_specs=[SCALARS] + [pl.BlockSpec(memory_spa...]
    ppermute x17, waiting for transfers between devices: 39.2 us -> 33.2 us  [send(): return lax.ppermute(array, 'seq', pairs)]
    unnamed x42 -> x32, local copies, waits for them, and re-layouts: 7.93 us -> 6.74 us
  transfers between devices with their start and end apart: 19 -> 19, of which waited for: 8 -> 8; matrix products, arithmetic and copies ran while one was open for 1% -> 1% of each run, Pallas kernels for 12% -> 20%
where the time goes in v4:
time: 166 us; the launch traced here: 165 us
  starting transfers between devices  87.3 us (53%)
  Pallas kernels  34.9 us (21%)
  waiting for transfers between devices  33.2 us (20%)
  local copies, waits for them, and re-layouts  8.82 us (5%)
    ppermute x17, starting transfers between devices, send(): return lax.ppermute(array, 'seq', pairs)  53.8 us
    ppermute x17, waiting for transfers between devices, send(): return lax.ppermute(array, 'seq', pairs)  33.2 us
    all_to_all x1, starting transfers between devices, shards(): lax.all_to_all(term.reshape((n_dp,) + master.shape), 'dp', split_axis=0,...  16.8 us
    all_to_all x1, starting transfers between devices, shards(): lax.all_to_all(copies, 'dp', split_axis=0, concat_axis=0, tiled=True)  16.7 us
    pallas_call x1, Pallas kernels, grads_call(): pl.pallas_call(grads_kernel, grid=(BLOCKS // 2,), in_specs=[SCALARS, SCAL...  8.19 us
    pallas_call x1, Pallas kernels, probs_call(): pl.pallas_call(probs_kernel, grid=(BLOCKS // 2,), in_specs=[SCALARS, SCAL...  7.19 us
    unnamed x32, local copies, waits for them, and re-layouts  6.74 us
    pallas_call x1, Pallas kernels, values_call(): pl.pallas_call(values_kernel, grid=(D // STRIPE,), in_specs=[SCALARS] + h...  5.62 us
  transfers between devices with their start and end apart: 19, of which 8 were waited for; matrix products, arithmetic and copies ran while one was open for 1% of the time, Pallas kernels for 20%

profile of v4, /device:TPU:1, one launch (start us, length us, event | category | flops | bytes accessed | tf_op | source)
XLA Modules:
  0.0 165.4 jit_solution(5182086972426419086)
XLA Ops:
  0.6 5.2 %collective-permute-start.7 = (bf16[128,4096]{1,0:T(8,128)(2,1)}, bf16[128,4096]{1,0:T(8,128)(2,1)S(1)}, u32[]{:S(2)}, u32[]{:S(2)}) collective-permute-start(bf16[128,4096]{1,0:T(8,128)(2,1)} %bitcast.11.refs_0_), channel_id=1, source_target_pairs={{0,384},{64,448},{128,0},{192,64},{256,128},{320,192},{384,256},{4... | collective-permute-start | bytes 3145736 | tf_op jit(solution)/shard_map/ppermute | solution.py:50
  5.9 0.6 stack.58.to_ref
  6.5 3.3 %shard_map.153 = (bf16[2,128,1152]{2,1,0:T(8,128)(2,1)}, bf16[2,128,1152]{2,1,0:T(8,128)(2,1)}, bf16[2,128,1152]{2,1,0:T(8,128)(2,1)}, bf16[2,128,1152]{2,1,0:T(8,128)(2,1)}) custom-call(s32[8]{0:T(128)} %stack.58.to_ref, bf16[128,4096]{1,0:T(8,128)(2,1)} %bitcast.17, bf16[128,4096]{1,0:T(8,128)(2,1)} %bitcast.18, bf16[128,1024]{1,0:T(8,128)(2,1)} %bitcast.19), custom_call_target="tpu_custom_call" | custom-call | tf_op jit(solution)/shard_map/pallas_call | solution.py:87
  9.8 1.9 %collective-permute-start = (bf16[2,128,1152]{2,1,0:T(8,128)(2,1)}, bf16[2,128,1152]{2,1,0:T(8,128)(2,1)S(1)}, u32[]{:S(2)}, u32[]{:S(2)}) collective-permute-start(bf16[2,128,1152]{2,1,0:T(8,128)(2,1)} %get-tuple-element.26), channel_id=1, source_target_pairs={{0,128},{64,192},{128,256},{192,320},{256,384},{320,448},{384,0},{... | collective-permute-start | bytes 1769480 | tf_op jit(solution)/shard_map/ppermute | solution.py:50
  11.7 3.6 %collective-permute-start.1 = (bf16[2,128,1152]{2,1,0:T(8,128)(2,1)}, bf16[2,128,1152]{2,1,0:T(8,128)(2,1)}, u32[]{:S(2)}, u32[]{:S(2)}) collective-permute-start(bf16[2,128,1152]{2,1,0:T(8,128)(2,1)} %get-tuple-element.27), channel_id=1, source_target_pairs={{0,256},{64,320},{128,384},{192,448},{256,0},{320,64},{384,128},{4... | collective-permute-start | bytes 1769480 | tf_op jit(solution)/shard_map/ppermute | solution.py:50
  15.4 2.9 %collective-permute-start.2 = (bf16[2,128,1152]{2,1,0:T(8,128)(2,1)}, bf16[2,128,1152]{2,1,0:T(8,128)(2,1)}, u32[]{:S(2)}, u32[]{:S(2)}) collective-permute-start(bf16[2,128,1152]{2,1,0:T(8,128)(2,1)} %get-tuple-element.28), channel_id=1, source_target_pairs={{0,384},{64,448},{128,0},{192,64},{256,128},{320,192},{384,256},{4... | collective-permute-start | bytes 1769480 | tf_op jit(solution)/shard_map/ppermute | solution.py:50
  18.2 2.5 %collective-permute-start.5 = (bf16[128,4096]{1,0:T(8,128)(2,1)}, bf16[128,4096]{1,0:T(8,128)(2,1)S(1)}, u32[]{:S(2)}, u32[]{:S(2)}) collective-permute-start(bf16[128,4096]{1,0:T(8,128)(2,1)} %bitcast.11.refs_0_), channel_id=1, source_target_pairs={{0,128},{64,192},{128,256},{192,320},{256,384},{320,448},{384,0},{... | collective-permute-start | bytes 3145736 | tf_op jit(solution)/shard_map/ppermute | solution.py:50
  20.8 1.2 broadcast_in_dim.12
  22.0 16.7 %all-to-all-start = ((bf16[64,64,128]{2,1,0:T(8,128)(2,1)}), bf16[64,64,128]{2,1,0:T(8,128)(2,1)}, u32[]{:S(2)}, u32[]{:S(2)}) async-start(bf16[64,64,128]{2,1,0:T(8,128)(2,1)} %broadcast_in_dim.12), calls=%async_computation | async-start | bytes 2097152 | tf_op jit(solution)/shard_map/all_to_all | solution.py:493
  38.7 0.0 collective-permute-done.refs_1_
  38.7 0.1 collective-permute-done.1.refs_2_
  38.8 11.7 %collective-permute-done.2.refs_3_ = bf16[2,128,1152]{2,1,0:T(8,128)(2,1)} collective-permute-done((bf16[2,128,1152]{2,1,0:T(8,128)(2,1)}, bf16[2,128,1152]{2,1,0:T(8,128)(2,1)}, u32[]{:S(2)}, u32[]{:S(2)}) %collective-permute-start.2) | collective-permute-done | bytes 589856 | tf_op jit(solution)/shard_map/ppermute | solution.py:50
  50.6 1.2 shard_map.154
  51.8 0.0 copy-start.11
  51.8 6.1 %collective-permute-start.3 = (bf16[4,128,1152]{2,1,0:T(8,128)(2,1)S(1)}, bf16[4,128,1152]{2,1,0:T(8,128)(2,1)S(1)}, u32[]{:S(2)}, u32[]{:S(2)}) collective-permute-start(bf16[4,128,1152]{2,1,0:T(8,128)(2,1)S(1)} %shard_map.154), channel_id=1, source_target_pairs={{0,64},{64,0},{128,192},{192,128},{256,320},{320,256},{384,448},{4... | collective-permute-start | bytes 3538952 | tf_op jit(solution)/shard_map/ppermute | solution.py:50
  57.9 0.0 collective-permute-done.7.refs_4_
  58.0 5.3 %collective-permute-start.10 = (bf16[64,4096]{1,0:T(8,128)(2,1)S(1)}, bf16[64,4096]{1,0:T(8,128)(2,1)}, u32[]{:S(2)}, u32[]{:S(2)}) collective-permute-start(bf16[64,4096]{1,0:T(8,128)(2,1)S(1)} %slice.9), channel_id=1, source_target_pairs={{0,384},{64,448},{128,0},{192,64},{256,128},{320,192},{384,256},{4... | collective-permute-start | bytes 1572872 | tf_op jit(solution)/shard_map/ppermute | solution.py:50
  63.3 0.0 collective-permute-done.5.refs_2_
  63.4 1.9 %collective-permute-start.9 = (bf16[64,4096]{1,0:T(8,128)(2,1)S(1)}, bf16[64,4096]{1,0:T(8,128)(2,1)}, u32[]{:S(2)}, u32[]{:S(2)}) collective-permute-start(bf16[64,4096]{1,0:T(8,128)(2,1)S(1)} %slice.8), channel_id=1, source_target_pairs={{0,128},{64,192},{128,256},{192,320},{256,384},{320,448},{384,0},{... | collective-permute-start | bytes 1572872 | tf_op jit(solution)/shard_map/ppermute | solution.py:50
  65.3 2.5 %collective-permute-start.4 = (bf16[128,4096]{1,0:T(8,128)(2,1)}, bf16[128,4096]{1,0:T(8,128)(2,1)}, u32[]{:S(2)}, u32[]{:S(2)}) collective-permute-start(bf16[128,4096]{1,0:T(8,128)(2,1)} %bitcast.11.refs_0_), channel_id=1, source_target_pairs={{0,64},{64,0},{128,192},{192,128},{256,320},{320,256},{384,448},{4... | collective-permute-start | bytes 3145736 | tf_op jit(solution)/shard_map/ppermute | solution.py:50
  67.9 1.9 %collective-permute-start.8 = (bf16[128,4096]{1,0:T(8,128)(2,1)S(1)}, bf16[128,4096]{1,0:T(8,128)(2,1)}, u32[]{:S(2)}, u32[]{:S(2)}) collective-permute-start(bf16[128,4096]{1,0:T(8,128)(2,1)S(1)} %collective-permute-done.7.refs_4_), channel_id=1, source_target_pairs={{0,64},{64,0},{128,192},{192,128},{256,320},{320,256},{384,448},{4... | collective-permute-start | bytes 3145736 | tf_op jit(solution)/shard_map/ppermute | solution.py:50
  69.8 4.9 %collective-permute-done.10.refs_7_ = bf16[64,4096]{1,0:T(8,128)(2,1)} collective-permute-done((bf16[64,4096]{1,0:T(8,128)(2,1)S(1)}, bf16[64,4096]{1,0:T(8,128)(2,1)}, u32[]{:S(2)}, u32[]{:S(2)}) %collective-permute-start.10) | collective-permute-done | bytes 524320 | tf_op jit(solution)/shard_map/ppermute | solution.py:50
  74.6 2.7 %collective-permute-start.6 = (bf16[128,4096]{1,0:T(8,128)(2,1)S(1)}, bf16[128,4096]{1,0:T(8,128)(2,1)}, u32[]{:S(2)}, u32[]{:S(2)}) collective-permute-start(bf16[128,4096]{1,0:T(8,128)(2,1)S(1)} %collective-permute-done.5.refs_2_), channel_id=1, source_target_pairs={{0,64},{64,0},{128,192},{192,128},{256,320},{320,256},{384,448},{4... | collective-permute-start | bytes 3145736 | tf_op jit(solution)/shard_map/ppermute | solution.py:50
  77.3 2.1 %collective-permute-done.9.refs_6_ = bf16[64,4096]{1,0:T(8,128)(2,1)} collective-permute-done((bf16[64,4096]{1,0:T(8,128)(2,1)S(1)}, bf16[64,4096]{1,0:T(8,128)(2,1)}, u32[]{:S(2)}, u32[]{:S(2)}) %collective-permute-start.9) | collective-permute-done | bytes 524320 | tf_op jit(solution)/shard_map/ppermute | solution.py:50
  79.4 3.4 %collective-permute-start.12 = (bf16[64,4096]{1,0:T(8,128)(2,1)}, bf16[64,4096]{1,0:T(8,128)(2,1)}, u32[]{:S(2)}, u32[]{:S(2)}) collective-permute-start(bf16[64,4096]{1,0:T(8,128)(2,1)} %collective-permute-done.10.refs_7_), channel_id=1, source_target_pairs={{0,64},{64,0},{128,192},{192,128},{256,320},{320,256},{384,448},{4... | collective-permute-start | bytes 1572872 | tf_op jit(solution)/shard_map/ppermute | solution.py:50
  82.8 0.0 collective-permute-done.3.refs_4_
  82.9 1.1 copy-done.1
  83.9 1.9 %collective-permute-start.11 = (bf16[64,4096]{1,0:T(8,128)(2,1)}, bf16[64,4096]{1,0:T(8,128)(2,1)}, u32[]{:S(2)}, u32[]{:S(2)}) collective-permute-start(bf16[64,4096]{1,0:T(8,128)(2,1)} %collective-permute-done.9.refs_6_), channel_id=1, source_target_pairs={{0,64},{64,0},{128,192},{192,128},{256,320},{320,256},{384,448},{4... | collective-permute-start | bytes 1572872 | tf_op jit(solution)/shard_map/ppermute | solution.py:50
  85.8 0.1 stack.57.from_ref
  85.9 0.1 stack.59.from_ref
  86.0 1.3 copy-done.2
  87.3 7.2 %shard_map.155 = (bf16[4,2,512,512]{3,2,1,0:T(8,128)(2,1)S(1)}, bf16[1024,128]{1,0:T(8,128)(2,1)S(1)}) custom-call(s32[1,8]{1,0:T(1,128)S(1)} %copy-done.11, s32[8]{0:T(128)S(1)} %stack.57.from_ref, bf16[2,128,1152]{2,1,0:T(8,128)(2,1)S(1)} %copy-done, bf16[2,128,1152]{2,1,0:T(8,128)(2,1)S(1)} %collective-permute-done.refs_1_, ...), custom_call_target="tpu_custom_call" | custom-call | tf_op jit(solution)/shard_map/pallas_call | solution.py:218
  94.5 2.0 %copy-done.5 = bf16[4,2,512,512]{3,2,1,0:T(8,128)(2,1)} copy-done((bf16[4,2,512,512]{3,2,1,0:T(8,128)(2,1)}, bf16[4,2,512,512]{3,2,1,0:T(8,128)(2,1)S(1)}, u32[]{:S(2)}) %copy-start.5) | copy-done | bytes 4194328
  96.5 0.0 collective-permute-done.4.refs_1_
  96.5 0.0 collective-permute-done.12.refs_9_
  96.5 0.0 collective-permute-done.8.refs_5_
  96.5 0.0 collective-permute-done.11.refs_8_
  96.5 0.0 collective-permute-done.6.refs_3_
  96.5 4.8 %shard_map.160 = bf16[4096,128]{1,0:T(8,128)(2,1)S(1)} custom-call(s32[8]{0:T(128)S(1)} %stack.59.from_ref, bf16[128,4096]{1,0:T(8,128)(2,1)} %bitcast.11.refs_0_, bf16[128,4096]{1,0:T(8,128)(2,1)} %collective-permute-done.4.refs_1_, bf16[128,4096]{1,0:T(8,128)(2,1)S(1)} %collective-permute-done.5.refs_2_, bf16[128,4096]{1,0:T(8,128)(2,1)} %collective-permute-done.6.refs_3_, ...), custom_call_target="tpu_custom_call" | custom-call | tf_op jit(solution)/shard_map/pallas_call | solution.py:279
  101.3 1.0 copy-done.4
  102.3 0.0 all-to-all-done
  102.4 16.8 %all-to-all-start.1 = ((bf16[64,64,128]{2,1,0:T(8,128)(2,1)}), bf16[64,64,128]{2,1,0:T(8,128)(2,1)}, u32[]{:S(2)}, u32[]{:S(2)}) async-start(bf16[64,64,128]{2,1,0:T(8,128)(2,1)} %bitcast.16), calls=%async_computation.1 | async-start | bytes 2097152 | tf_op jit(solution)/shard_map/all_to_all | solution.py:502
  119.1 5.6 %shard_map.156.refs_6_ = bf16[1024,128]{1,0:T(8,128)(2,1)S(1)} custom-call(s32[8]{0:T(128)S(1)} %stack.59.from_ref, bf16[128,4096]{1,0:T(8,128)(2,1)} %bitcast.11.refs_0_, bf16[128,4096]{1,0:T(8,128)(2,1)} %collective-permute-done.4.refs_1_, bf16[128,4096]{1,0:T(8,128)(2,1)S(1)} %collective-permute-done.5.refs_2_, ...), custom_call_target="tpu_custom_call" | custom-call | tf_op jit(solution)/shard_map/pallas_call | solution.py:293
  124.8 8.2 %shard_map.157 = (bf16[2,128,640]{2,1,0:T(8,128)(2,1)S(1)}, bf16[2,128,640]{2,1,0:T(8,128)(2,1)S(1)}, bf16[2,128,640]{2,1,0:T(8,128)(2,1)S(1)}, bf16[2,128,640]{2,1,0:T(8,128)(2,1)S(1)}) custom-call(s32[8]{0:T(128)S(1)} %stack.57.from_ref, s32[8]{0:T(128)S(1)} %copy-done.10, bf16[2,128,1152]{2,1,0:T(8,128)(2,1)S(1)} %copy-done, ...), custom_call_target="tpu_custom_call" | custom-call | tf_op jit(solution)/shard_map/pallas_call | solution.py:359
  133.0 0.0 copy-start.12
  133.0 0.0 copy-start.13
  133.0 1.9 %collective-permute-start.13 = (bf16[2,128,640]{2,1,0:T(8,128)(2,1)S(1)}, bf16[2,128,640]{2,1,0:T(8,128)(2,1)S(1)}, u32[]{:S(2)}, u32[]{:S(2)}) collective-permute-start(bf16[2,128,640]{2,1,0:T(8,128)(2,1)S(1)} %get-tuple-element.32), channel_id=1, source_target_pairs={{0,128},{64,192},{128,256},{192,320},{256,384},{320,448},{384,0},{... | collective-permute-start | bytes 983048 | tf_op jit(solution)/shard_map/ppermute | solution.py:50
  134.9 3.5 %collective-permute-start.14 = (bf16[2,128,640]{2,1,0:T(8,128)(2,1)S(1)}, bf16[2,128,640]{2,1,0:T(8,128)(2,1)S(1)}, u32[]{:S(2)}, u32[]{:S(2)}) collective-permute-start(bf16[2,128,640]{2,1,0:T(8,128)(2,1)S(1)} %get-tuple-element.33), channel_id=1, source_target_pairs={{0,256},{64,320},{128,384},{192,448},{256,0},{320,64},{384,128},{4... | collective-permute-start | bytes 983048 | tf_op jit(solution)/shard_map/ppermute | solution.py:50
  138.5 3.0 %collective-permute-start.15 = (bf16[2,128,640]{2,1,0:T(8,128)(2,1)S(1)}, bf16[2,128,640]{2,1,0:T(8,128)(2,1)S(1)}, u32[]{:S(2)}, u32[]{:S(2)}) collective-permute-start(bf16[2,128,640]{2,1,0:T(8,128)(2,1)S(1)} %get-tuple-element.34), channel_id=1, source_target_pairs={{0,384},{64,448},{128,0},{192,64},{256,128},{320,192},{384,256},{4... | collective-permute-start | bytes 983048 | tf_op jit(solution)/shard_map/ppermute | solution.py:50
  141.5 3.7 %collective-permute-done.13.refs_1_ = bf16[2,128,640]{2,1,0:T(8,128)(2,1)S(1)} collective-permute-done((bf16[2,128,640]{2,1,0:T(8,128)(2,1)S(1)}, bf16[2,128,640]{2,1,0:T(8,128)(2,1)S(1)}, u32[]{:S(2)}, u32[]{:S(2)}) %collective-permute-start.13) | collective-permute-done | bytes 327712 | tf_op jit(solution)/shard_map/ppermute | solution.py:50
  145.1 6.0 %collective-permute-done.14.refs_2_ = bf16[2,128,640]{2,1,0:T(8,128)(2,1)S(1)} collective-permute-done((bf16[2,128,640]{2,1,0:T(8,128)(2,1)S(1)}, bf16[2,128,640]{2,1,0:T(8,128)(2,1)S(1)}, u32[]{:S(2)}, u32[]{:S(2)}) %collective-permute-start.14) | collective-permute-done | bytes 327712 | tf_op jit(solution)/shard_map/ppermute | solution.py:50
  151.2 3.1 %collective-permute-done.15.refs_3_ = bf16[2,128,640]{2,1,0:T(8,128)(2,1)S(1)} collective-permute-done((bf16[2,128,640]{2,1,0:T(8,128)(2,1)S(1)}, bf16[2,128,640]{2,1,0:T(8,128)(2,1)S(1)}, u32[]{:S(2)}, u32[]{:S(2)}) %collective-permute-start.15) | collective-permute-done | bytes 327712 | tf_op jit(solution)/shard_map/ppermute | solution.py:50
  154.3 0.9 shard_map.158
  155.1 0.0 copy-start.8
  155.1 0.0 copy-start.9
  155.1 3.5 %collective-permute-start.16 = (bf16[4,128,640]{2,1,0:T(8,128)(2,1)S(1)}, bf16[4,128,640]{2,1,0:T(8,128)(2,1)S(1)}, u32[]{:S(2)}, u32[]{:S(2)}) collective-permute-start(bf16[4,128,640]{2,1,0:T(8,128)(2,1)S(1)} %shard_map.158), channel_id=1, source_target_pairs={{0,64},{64,0},{128,192},{192,128},{256,320},{320,256},{384,448},{4... | collective-permute-start | bytes 1966088 | tf_op jit(solution)/shard_map/ppermute | solution.py:50
  158.6 0.1 copy.17.ms_ref
  158.7 0.1 copy.18.vs_ref
  158.8 1.5 collective-permute-done.16.refs_4_
  160.3 1.7 %shard_map.159 = (bf16[128,4096]{1,0:T(8,128)(2,1)}, bf16[128,1024]{1,0:T(8,128)(2,1)}) custom-call(s32[8]{0:T(128)S(1)} %stack.57.from_ref, bf16[2,128,640]{2,1,0:T(8,128)(2,1)S(1)} %get-tuple-element.31.refs_0_, bf16[2,128,640]{2,1,0:T(8,128)(2,1)S(1)} %collective-permute-done.13.refs_1_, bf16[2,128,640]{2,1,0:T(8,128)(2,1)S(1)} %collective-permute-done.14.refs_2_, ...), custom_call_target="tpu_custom_call" | custom-call | tf_op jit(solution)/shard_map/pallas_call | solution.py:396
  162.0 0.0 all-to-all-done.1.parts_ref
  162.1 2.1 %shard_map.161 = (f32[64,128]{1,0:T(8,128)}, bf16[64,128]{1,0:T(8,128)(2,1)}, f32[32,1]{1,0:T(8,128)S(1)}, bf16[64,128]{1,0:T(8,128)(2,1)}, f32[32,1]{1,0:T(8,128)S(1)}) custom-call(bf16[64,64,128]{2,1,0:T(8,128)(2,1)} %all-to-all-done.1.parts_ref, f32[64,128]{1,0:T(8,128)S(1)} %copy-done.7, bf16[64,128]{1,0:T(8,128)(2,1)S(1)} %copy-done.8, ...), custom_call_target="tpu_custom_call" | custom-call | tf_op jit(solution)/shard_map/pallas_call | solution.py:466
  164.2 0.6 copy.19
  164.8 0.6 copy.20
  (22 shorter events, 0.1 us)
Async XLA Ops:
  0.6 57.3 %collective-permute-start.7 = (bf16[128,4096]{1,0:T(8,128)(2,1)}, bf16[128,4096]{1,0:T(8,128)(2,1)S(1)}, u32[]{:S(2)}, u32[]{:S(2)}) collective-permute-start(bf16[128,4096]{1,0:T(8,128)(2,1)} %bitcast.11.refs_0_), channel_id=1, source_target_pairs={{0,384},{64,448},{128,0},{192,64},{256,128},{320,192},{384,256},{4... | collective-permute-start | bytes 3145736 | tf_op jit(solution)/shard_map/ppermute | solution.py:50
  6.5 14.2 %copy-start.7 = (f32[64,128]{1,0:T(8,128)S(1)}, f32[64,128]{1,0:T(8,128)}, u32[]{:S(2)}) copy-start(f32[64,128]{1,0:T(8,128)} %master_ref.1) | copy-start | bytes 98308
  9.8 28.9 %collective-permute-start = (bf16[2,128,1152]{2,1,0:T(8,128)(2,1)}, bf16[2,128,1152]{2,1,0:T(8,128)(2,1)S(1)}, u32[]{:S(2)}, u32[]{:S(2)}) collective-permute-start(bf16[2,128,1152]{2,1,0:T(8,128)(2,1)} %get-tuple-element.26), channel_id=1, source_target_pairs={{0,128},{64,192},{128,256},{192,320},{256,384},{320,448},{384,0},{... | collective-permute-start | bytes 1769480 | tf_op jit(solution)/shard_map/ppermute | solution.py:50
  11.7 27.1 %collective-permute-start.1 = (bf16[2,128,1152]{2,1,0:T(8,128)(2,1)}, bf16[2,128,1152]{2,1,0:T(8,128)(2,1)}, u32[]{:S(2)}, u32[]{:S(2)}) collective-permute-start(bf16[2,128,1152]{2,1,0:T(8,128)(2,1)} %get-tuple-element.27), channel_id=1, source_target_pairs={{0,256},{64,320},{128,384},{192,448},{256,0},{320,64},{384,128},{4... | collective-permute-start | bytes 1769480 | tf_op jit(solution)/shard_map/ppermute | solution.py:50
  15.4 35.2 %collective-permute-start.2 = (bf16[2,128,1152]{2,1,0:T(8,128)(2,1)}, bf16[2,128,1152]{2,1,0:T(8,128)(2,1)}, u32[]{:S(2)}, u32[]{:S(2)}) collective-permute-start(bf16[2,128,1152]{2,1,0:T(8,128)(2,1)} %get-tuple-element.28), channel_id=1, source_target_pairs={{0,384},{64,448},{128,0},{192,64},{256,128},{320,192},{384,256},{4... | collective-permute-start | bytes 1769480 | tf_op jit(solution)/shard_map/ppermute | solution.py:50
  18.2 45.1 %collective-permute-start.5 = (bf16[128,4096]{1,0:T(8,128)(2,1)}, bf16[128,4096]{1,0:T(8,128)(2,1)S(1)}, u32[]{:S(2)}, u32[]{:S(2)}) collective-permute-start(bf16[128,4096]{1,0:T(8,128)(2,1)} %bitcast.11.refs_0_), channel_id=1, source_target_pairs={{0,128},{64,192},{128,256},{192,320},{256,384},{320,448},{384,0},{... | collective-permute-start | bytes 3145736 | tf_op jit(solution)/shard_map/ppermute | solution.py:50
  22.0 28.6 %copy-start = (bf16[2,128,1152]{2,1,0:T(8,128)(2,1)S(1)}, bf16[2,128,1152]{2,1,0:T(8,128)(2,1)}, u32[]{:S(2)}) copy-start(bf16[2,128,1152]{2,1,0:T(8,128)(2,1)} %get-tuple-element.25.refs_0_) | copy-start | bytes 1769476
  22.0 80.4 %all-to-all-start = ((bf16[64,64,128]{2,1,0:T(8,128)(2,1)}), bf16[64,64,128]{2,1,0:T(8,128)(2,1)}, u32[]{:S(2)}, u32[]{:S(2)}) async-start(bf16[64,64,128]{2,1,0:T(8,128)(2,1)} %broadcast_in_dim.12), calls=%async_computation | async-start | bytes 2097152 | tf_op jit(solution)/shard_map/all_to_all | solution.py:493
  51.8 34.2 %copy-start.11 = (s32[1,8]{1,0:T(1,128)S(1)}, s32[1,8]{1,0:T(1,128)}, u32[]{:S(2)}) copy-start(s32[1,8]{1,0:T(1,128)} %lens_ref.1) | copy-start | bytes 100
  51.8 31.0 %collective-permute-start.3 = (bf16[4,128,1152]{2,1,0:T(8,128)(2,1)S(1)}, bf16[4,128,1152]{2,1,0:T(8,128)(2,1)S(1)}, u32[]{:S(2)}, u32[]{:S(2)}) collective-permute-start(bf16[4,128,1152]{2,1,0:T(8,128)(2,1)S(1)} %shard_map.154), channel_id=1, source_target_pairs={{0,64},{64,0},{128,192},{192,128},{256,320},{320,256},{384,448},{4... | collective-permute-start | bytes 3538952 | tf_op jit(solution)/shard_map/ppermute | solution.py:50
  58.0 16.7 %collective-permute-start.10 = (bf16[64,4096]{1,0:T(8,128)(2,1)S(1)}, bf16[64,4096]{1,0:T(8,128)(2,1)}, u32[]{:S(2)}, u32[]{:S(2)}) collective-permute-start(bf16[64,4096]{1,0:T(8,128)(2,1)S(1)} %slice.9), channel_id=1, source_target_pairs={{0,384},{64,448},{128,0},{192,64},{256,128},{320,192},{384,256},{4... | collective-permute-start | bytes 1572872 | tf_op jit(solution)/shard_map/ppermute | solution.py:50
  63.4 16.1 %collective-permute-start.9 = (bf16[64,4096]{1,0:T(8,128)(2,1)S(1)}, bf16[64,4096]{1,0:T(8,128)(2,1)}, u32[]{:S(2)}, u32[]{:S(2)}) collective-permute-start(bf16[64,4096]{1,0:T(8,128)(2,1)S(1)} %slice.8), channel_id=1, source_target_pairs={{0,128},{64,192},{128,256},{192,320},{256,384},{320,448},{384,0},{... | collective-permute-start | bytes 1572872 | tf_op jit(solution)/shard_map/ppermute | solution.py:50
  65.3 31.2 %collective-permute-start.4 = (bf16[128,4096]{1,0:T(8,128)(2,1)}, bf16[128,4096]{1,0:T(8,128)(2,1)}, u32[]{:S(2)}, u32[]{:S(2)}) collective-permute-start(bf16[128,4096]{1,0:T(8,128)(2,1)} %bitcast.11.refs_0_), channel_id=1, source_target_pairs={{0,64},{64,0},{128,192},{192,128},{256,320},{320,256},{384,448},{4... | collective-permute-start | bytes 3145736 | tf_op jit(solution)/shard_map/ppermute | solution.py:50
  67.9 28.6 %collective-permute-start.8 = (bf16[128,4096]{1,0:T(8,128)(2,1)S(1)}, bf16[128,4096]{1,0:T(8,128)(2,1)}, u32[]{:S(2)}, u32[]{:S(2)}) collective-permute-start(bf16[128,4096]{1,0:T(8,128)(2,1)S(1)} %collective-permute-done.7.refs_4_), channel_id=1, source_target_pairs={{0,64},{64,0},{128,192},{192,128},{256,320},{320,256},{384,448},{4... | collective-permute-start | bytes 3145736 | tf_op jit(solution)/shard_map/ppermute | solution.py:50
  74.6 21.8 %collective-permute-start.6 = (bf16[128,4096]{1,0:T(8,128)(2,1)S(1)}, bf16[128,4096]{1,0:T(8,128)(2,1)}, u32[]{:S(2)}, u32[]{:S(2)}) collective-permute-start(bf16[128,4096]{1,0:T(8,128)(2,1)S(1)} %collective-permute-done.5.refs_2_), channel_id=1, source_target_pairs={{0,64},{64,0},{128,192},{192,128},{256,320},{320,256},{384,448},{4... | collective-permute-start | bytes 3145736 | tf_op jit(solution)/shard_map/ppermute | solution.py:50
  79.4 17.0 %collective-permute-start.12 = (bf16[64,4096]{1,0:T(8,128)(2,1)}, bf16[64,4096]{1,0:T(8,128)(2,1)}, u32[]{:S(2)}, u32[]{:S(2)}) collective-permute-start(bf16[64,4096]{1,0:T(8,128)(2,1)} %collective-permute-done.10.refs_7_), channel_id=1, source_target_pairs={{0,64},{64,0},{128,192},{192,128},{256,320},{320,256},{384,448},{4... | collective-permute-start | bytes 1572872 | tf_op jit(solution)/shard_map/ppermute | solution.py:50
  82.8 1.1 copy-start.1
  83.9 12.6 %collective-permute-start.11 = (bf16[64,4096]{1,0:T(8,128)(2,1)}, bf16[64,4096]{1,0:T(8,128)(2,1)}, u32[]{:S(2)}, u32[]{:S(2)}) collective-permute-start(bf16[64,4096]{1,0:T(8,128)(2,1)} %collective-permute-done.9.refs_6_), channel_id=1, source_target_pairs={{0,64},{64,0},{128,192},{192,128},{256,320},{320,256},{384,448},{4... | collective-permute-start | bytes 1572872 | tf_op jit(solution)/shard_map/ppermute | solution.py:50
  86.0 1.3 copy-start.2
  94.5 2.0 %copy-start.5 = (bf16[4,2,512,512]{3,2,1,0:T(8,128)(2,1)}, bf16[4,2,512,512]{3,2,1,0:T(8,128)(2,1)S(1)}, u32[]{:S(2)}) copy-start(bf16[4,2,512,512]{3,2,1,0:T(8,128)(2,1)S(1)} %get-tuple-element.29.refs_5_) | copy-start | bytes 12582916
  101.3 1.0 copy-start.4
  102.4 59.7 %all-to-all-start.1 = ((bf16[64,64,128]{2,1,0:T(8,128)(2,1)}), bf16[64,64,128]{2,1,0:T(8,128)(2,1)}, u32[]{:S(2)}, u32[]{:S(2)}) async-start(bf16[64,64,128]{2,1,0:T(8,128)(2,1)} %bitcast.16), calls=%async_computation.1 | async-start | bytes 2097152 | tf_op jit(solution)/shard_map/all_to_all | solution.py:502
  119.1 5.7 %copy-start.3 = (bf16[4,128,1152]{2,1,0:T(8,128)(2,1)S(1)}, bf16[4,128,1152]{2,1,0:T(8,128)(2,1)}, u32[]{:S(2)}) copy-start(bf16[4,128,1152]{2,1,0:T(8,128)(2,1)} %copy-done.1) | copy-start | bytes 3538948
  119.1 5.7 %copy-start.6 = (bf16[4,2,512,512]{3,2,1,0:T(8,128)(2,1)S(1)}, bf16[4,2,512,512]{3,2,1,0:T(8,128)(2,1)}, u32[]{:S(2)}) copy-start(bf16[4,2,512,512]{3,2,1,0:T(8,128)(2,1)} %copy-done.5) | copy-start | bytes 12582916
  119.1 5.7 %copy-start.10 = (s32[8]{0:T(128)S(1)}, s32[8]{0:T(128)}, u32[]{:S(2)}) copy-start(s32[8]{0:T(128)} %stack.58.to_ref) | copy-start | bytes 100
  133.0 25.6 %copy-start.12 = (f32[32,1]{0,1:T(1,128)S(1)}, f32[32,1]{0,1:T(1,128)}, u32[]{:S(2)}) copy-start(f32[32,1]{0,1:T(1,128)} %param.17) | copy-start | bytes 388
  133.0 25.7 %copy-start.13 = (f32[32,1]{0,1:T(1,128)S(1)}, f32[32,1]{0,1:T(1,128)}, u32[]{:S(2)}) copy-start(f32[32,1]{0,1:T(1,128)} %param.19) | copy-start | bytes 388
  133.0 12.1 %collective-permute-start.13 = (bf16[2,128,640]{2,1,0:T(8,128)(2,1)S(1)}, bf16[2,128,640]{2,1,0:T(8,128)(2,1)S(1)}, u32[]{:S(2)}, u32[]{:S(2)}) collective-permute-start(bf16[2,128,640]{2,1,0:T(8,128)(2,1)S(1)} %get-tuple-element.32), channel_id=1, source_target_pairs={{0,128},{64,192},{128,256},{192,320},{256,384},{320,448},{384,0},{... | collective-permute-start | bytes 983048 | tf_op jit(solution)/shard_map/ppermute | solution.py:50
  134.9 16.2 %collective-permute-start.14 = (bf16[2,128,640]{2,1,0:T(8,128)(2,1)S(1)}, bf16[2,128,640]{2,1,0:T(8,128)(2,1)S(1)}, u32[]{:S(2)}, u32[]{:S(2)}) collective-permute-start(bf16[2,128,640]{2,1,0:T(8,128)(2,1)S(1)} %get-tuple-element.33), channel_id=1, source_target_pairs={{0,256},{64,320},{128,384},{192,448},{256,0},{320,64},{384,128},{4... | collective-permute-start | bytes 983048 | tf_op jit(solution)/shard_map/ppermute | solution.py:50
  138.5 15.8 %collective-permute-start.15 = (bf16[2,128,640]{2,1,0:T(8,128)(2,1)S(1)}, bf16[2,128,640]{2,1,0:T(8,128)(2,1)S(1)}, u32[]{:S(2)}, u32[]{:S(2)}) collective-permute-start(bf16[2,128,640]{2,1,0:T(8,128)(2,1)S(1)} %get-tuple-element.34), channel_id=1, source_target_pairs={{0,384},{64,448},{128,0},{192,64},{256,128},{320,192},{384,256},{4... | collective-permute-start | bytes 983048 | tf_op jit(solution)/shard_map/ppermute | solution.py:50
  155.1 6.9 %copy-start.8 = (bf16[64,128]{1,0:T(8,128)(2,1)S(1)}, bf16[64,128]{1,0:T(8,128)(2,1)}, u32[]{:S(2)}) copy-start(bf16[64,128]{1,0:T(8,128)(2,1)} %mc_ref.1) | copy-start | bytes 49156
  155.1 6.9 %copy-start.9 = (bf16[64,128]{1,0:T(8,128)(2,1)S(1)}, bf16[64,128]{1,0:T(8,128)(2,1)}, u32[]{:S(2)}) copy-start(bf16[64,128]{1,0:T(8,128)(2,1)} %vc_ref.1) | copy-start | bytes 49156
  155.1 5.2 %collective-permute-start.16 = (bf16[4,128,640]{2,1,0:T(8,128)(2,1)S(1)}, bf16[4,128,640]{2,1,0:T(8,128)(2,1)S(1)}, u32[]{:S(2)}, u32[]{:S(2)}) collective-permute-start(bf16[4,128,640]{2,1,0:T(8,128)(2,1)S(1)} %shard_map.158), channel_id=1, source_target_pairs={{0,64},{64,0},{128,192},{192,128},{256,320},{320,256},{384,448},{4... | collective-permute-start | bytes 1966088 | tf_op jit(solution)/shard_map/ppermute | solution.py:50

commit v5 on v4

--- a/solution.py
+++ b/solution.py
@@ -6,6 +6,7 @@
 from jax import lax
 from jax.experimental import pallas as pl
 from jax.experimental.pallas import tpu as pltpu
+from jax.sharding import Mesh
 from jax.sharding import PartitionSpec as P
 
 D = 4096
@@ -35,6 +36,12 @@
 
 def params(mebibytes=24):
     return pltpu.CompilerParams(vmem_limit_bytes=mebibytes * 1024 * 1024)
+
+
+def cost(microseconds):
+    return pl.CostEstimate(
+        flops=int(microseconds * 1e9), bytes_accessed=int(microseconds * 1e6), transcendentals=0
+    )
 
 
 XS = 4
@@ -90,6 +97,7 @@
         out_specs=[ANYWHERE] * XS,
         out_shape=[jax.ShapeDtypeStruct((2, tokens, 2 * QW + HD), BF16)] * XS,
         scratch_shapes=[pltpu.SemaphoreType.DMA((24,))],
+        cost_estimate=cost(3),
         compiler_params=params(60),
     )(to, query, cot, key)
 
@@ -108,6 +116,7 @@
         out_specs=ANYWHERE,
         out_shape=jax.ShapeDtypeStruct((XS,) + pairs[0].shape[1:], BF16),
         scratch_shapes=[pltpu.SemaphoreType.DMA((XS,))],
+        cost_estimate=cost(1),
         compiler_params=params(4),
     )(*pairs)
 
@@ -221,7 +230,7 @@
         in_specs=[SCALARS, SCALARS] + [ANYWHERE] * 5,
         out_specs=[PROBS_SPEC, pl.BlockSpec((SEQ, HD), lambda i: (0, 0))],
         out_shape=[
-            jax.ShapeDtypeStruct(PROBS_SHAPE, BF16),
+            pltpu.HBM(PROBS_SHAPE, BF16),
             jax.ShapeDtypeStruct((SEQ, HD), BF16),
         ],
         scratch_shapes=[
@@ -229,6 +238,7 @@
             pltpu.VMEM((SEQ, HD), F32),
             pltpu.SemaphoreType.DMA((8,)),
         ],
+        cost_estimate=cost(8),
         compiler_params=params(),
     )(doc_lens, origin, *pieces)
 
@@ -250,8 +260,8 @@
     term_ref[...] = (term.T * INV_WIDTH).astype(BF16)
 
 
-def values_kernel(from_ref, *refs):
-    hidden_refs, (w_ref, val_ref, acc_ref) = refs[:10], refs[10:]
+def values_kernel(*refs):
+    hidden_refs, (w_ref, val_ref, acc_ref) = refs[:-3], refs[-3:]
     j = pl.program_id(0)
 
     @pl.when(j == 0)
@@ -262,10 +272,7 @@
 
     @pl.when(j == pl.num_programs(0) - 1)
     def _():
-        for r in range(8):
-            rows = pl.ds(pl.multiple_of(from_ref[r] * ROWS, ROWS), ROWS)
-            part = acc_ref[r * ROWS : (r + 1) * ROWS, :]
-            val_ref[rows, :] = (part * INV_WIDTH).astype(BF16)
+        val_ref[...] = (acc_ref[...] * INV_WIDTH).astype(BF16)
 
 
 STRIPE = 1024
@@ -285,22 +292,23 @@
         out_specs=pl.BlockSpec((STRIPE, HD), lambda j: (j, 0)),
         out_shape=jax.ShapeDtypeStruct((D, HD), BF16),
         scratch_shapes=[pltpu.VMEM((HD, SEQ), BF16)],
+        cost_estimate=cost(5),
         compiler_params=params(),
     )(origin, *pieces, grad_values)
 
 
-def values_call(origin, pieces, weight):
+def values_call(pieces, weight):
+    rows = sum(piece.shape[0] for piece in pieces)
     return pl.pallas_call(
         values_kernel,
         grid=(D // STRIPE,),
-        in_specs=[SCALARS]
-        + hidden_specs(pieces)
-        + [pl.BlockSpec((STRIPE, HD), lambda j: (j, 0))],
-        out_specs=pl.BlockSpec((SEQ, HD), lambda j: (0, 0)),
-        out_shape=jax.ShapeDtypeStruct((SEQ, HD), BF16),
-        scratch_shapes=[pltpu.VMEM((SEQ, HD), F32)],
+        in_specs=hidden_specs(pieces) + [pl.BlockSpec((STRIPE, HD), lambda j: (j, 0))],
+        out_specs=pl.BlockSpec((rows, HD), lambda j: (0, 0)),
+        out_shape=jax.ShapeDtypeStruct((rows, HD), BF16),
+        scratch_shapes=[pltpu.VMEM((rows, HD), F32)],
+        cost_estimate=cost(rows * 6 // SEQ),
         compiler_params=params(),
-    )(origin, *pieces, weight)
+    )(*pieces, weight)
 
 
 def block_grads(block, r_ref, pt_ref, val_ref, out_ref, acc_ref, kt_ref, vt_ref):
@@ -321,9 +329,9 @@
         out_ref[first : first + ROWS, a * HD : (a + 1) * HD] = grad[a * ROWS : (a + 1) * ROWS, :]
 
 
-def grads_kernel(from_ref, to_ref, *refs):
-    pieces, (pt_ref, val_ref), outs = refs[:5], refs[5:7], refs[7 : 7 + XS]
-    r_ref, out_ref, acc_ref, kt_ref, vt_ref, sems = refs[7 + XS :]
+def grads_kernel(from_ref, to_ref, around_ref, *refs):
+    pieces, (pt_ref, near_ref, far_ref), outs = refs[:5], refs[5:8], refs[8 : 8 + XS]
+    r_ref, val_ref, out_ref, acc_ref, kt_ref, vt_ref, sems = refs[8 + XS :]
     i = pl.program_id(0)
 
     @pl.when(i == 0)
@@ -331,6 +339,10 @@
         gather_pieces(from_ref, pieces, r_ref, sems)
         acc_ref[...] = jnp.zeros_like(acc_ref)
         kt_ref[...] = r_ref[:, 2 * QW :].T
+        for r in range(8):
+            rows = pl.ds(pl.multiple_of(around_ref[r] * ROWS, ROWS), ROWS)
+            held, at = (near_ref, r) if r < 6 else (far_ref, r - 6)
+            val_ref[rows, :] = held[at * ROWS : (at + 1) * ROWS, :]
         vt_ref[...] = val_ref[...].T
 
     def body(v):
@@ -354,26 +366,32 @@
         )
 
 
-def grads_call(origin, to, pieces, probs, values):
+def grads_call(origin, to, around, pieces, probs, near, far):
     width = 2 * QW + HD
     return pl.pallas_call(
         grads_kernel,
         grid=(BLOCKS // 2,),
-        in_specs=[SCALARS, SCALARS]
+        in_specs=[SCALARS, SCALARS, SCALARS]
         + [ANYWHERE] * 5
-        + [PROBS_SPEC, pl.BlockSpec((SEQ, HD), lambda i: (0, 0))],
+        + [
+            PROBS_SPEC,
+            pl.BlockSpec(near.shape, lambda i: (0, 0)),
+            pl.BlockSpec(far.shape, lambda i: (0, 0)),
+        ],
         out_specs=[ANYWHERE] * XS,
         out_shape=[jax.ShapeDtypeStruct((2, ROWS, QW + HD), BF16)] * XS,
         scratch_shapes=[
             pltpu.VMEM((SEQ, width), BF16),
+            pltpu.VMEM((SEQ, HD), BF16),
             pltpu.VMEM((SEQ, QW + HD), BF16),
             pltpu.VMEM((SEQ, HD), F32),
             pltpu.VMEM((HD, SEQ), BF16),
             pltpu.VMEM((HD, SEQ), BF16),
             pltpu.SemaphoreType.DMA((8,)),
         ],
+        cost_estimate=cost(9),
         compiler_params=params(),
-    )(origin, to, *pieces, probs, values)
+    )(origin, to, around, *pieces, probs, near, far)
 
 
 def unpack_kernel(from_ref, *refs):
@@ -402,8 +420,25 @@
             jax.ShapeDtypeStruct((ROWS, 8 * HD), BF16),
         ],
         scratch_shapes=[pltpu.SemaphoreType.DMA((16,))],
+        cost_estimate=cost(2),
         compiler_params=params(4),
     )(origin, *pieces)
+
+
+def add_kernel(parts_ref, out_ref):
+    total = parts_ref[0].astype(F32)
+    for g in range(1, parts_ref.shape[0]):
+        total = total + parts_ref[g].astype(F32)
+    out_ref[...] = total.astype(BF16)
+
+
+def add_parts(parts):
+    return pl.pallas_call(
+        add_kernel,
+        out_shape=jax.ShapeDtypeStruct(parts.shape[1:], BF16),
+        cost_estimate=cost(1),
+        compiler_params=params(8),
+    )(parts)
 
 
 def adam_kernel(
@@ -473,12 +508,13 @@
             jax.ShapeDtypeStruct(v_scale.shape, F32),
         ],
         scratch_shapes=[pltpu.VMEM(shape, F32) for _ in range(6)],
+        cost_estimate=cost(2),
         compiler_params=params(16),
     )(parts, master, m_code, m_scale, v_code, v_scale)
 
 
 def shards(hidden, query, key, grad_out, doc_lens, master, m_code, m_scale, v_code, v_scale):
-    n_dp = lax.axis_size("dp")
+    n_y, n_z = lax.axis_size("y"), lax.axis_size("z")
     me = lax.axis_index("seq")
     to = jnp.stack([place(me, r // 2, r % 2) for r in range(8)])
     origin = jnp.stack([place(me, (XS - r // 2) % XS, r % 2) for r in range(8)])
@@ -489,50 +525,38 @@
     pairs = pack(to, query[0], grad_out[0], key[0])
     pieces = exchange(pairs)
     master_bf, _ = lax.optimization_barrier((master.astype(BF16), pairs[0]))
-    copies = jnp.broadcast_to(master_bf[None], (n_dp,) + master.shape)
-    weight = lax.all_to_all(copies, "dp", split_axis=0, concat_axis=0, tiled=True)
-    weight = weight.reshape(D, HD)
+    copies = jnp.broadcast_to(master_bf[None], (n_y * n_z,) + master.shape)
+    weight = lax.all_to_all(copies, ("y", "z"), split_axis=0, concat_axis=0, tiled=True)
+    weight = weight.reshape(n_y * n_z * master.shape[0], HD)
     far_lo, far_hi = send(left[:half], 1, 0), send(right[half:], 3, 0)
     own_core, left_core, right_core = send(own, 0, 1), send(left, 0, 1), send(right, 0, 1)
     probs, grad_values = probs_call(doc_lens, origin, pieces)
-
-    far_core = [send(far_lo, 0, 1), send(far_hi, 0, 1)]
-    hiddens = [own, own_core, left, left_core, right, right_core, far_lo, far_hi] + far_core
-    term = term_call(around, hiddens, grad_values)
+    near = [own, own_core, left, left_core, right, right_core]
+    near_values = values_call(near, weight)
+    far_lo, far_hi, grad_values, near_values = lax.optimization_barrier(
+        (far_lo, far_hi, grad_values, near_values)
+    )
+    far = [far_lo, far_hi, send(far_lo, 0, 1), send(far_hi, 0, 1)]
+    term = term_call(around, near + far, grad_values)
     parts = lax.all_to_all(
-        term.reshape((n_dp,) + master.shape), "dp", split_axis=0, concat_axis=0, tiled=True
-    )
-    values = values_call(around, hiddens, weight)
-    grads = grads_call(origin, to, pieces, probs, values)
+        term.reshape((n_y, n_z) + master.shape), "y", split_axis=0, concat_axis=0, tiled=True
+    )
+    parts = lax.all_to_all(add_parts(parts), "z", split_axis=0, concat_axis=0, tiled=True)
+    far_values = values_call(far, weight)
+    grads = grads_call(origin, to, around, pieces, probs, near_values, far_values)
     grad_query, grad_key = unpack(origin, exchange(grads))
     state = adam_call(parts, master, m_code, m_scale, v_code, v_scale)
     return (grad_query[None], grad_key[None]) + tuple(state)
 
 
 def solution(mesh):
+    tokens, state = P(("y", "z"), "seq", None), P(("y", "z"), "seq")
+    rows = math.gcd(8, mesh.shape["dp"])
+    cut = mesh.devices.reshape(mesh.shape["seq"], rows, mesh.shape["dp"] // rows)
     return jax.shard_map(
         shards,
-        mesh=mesh,
-        in_specs=(
-            P("dp", "seq", None),
-            P("dp", "seq", None),
-            P("dp", "seq", None),
-            P("dp", "seq", None),
-            P("dp", None),
-            P("dp", "seq"),
-            P("dp", "seq"),
-            P("dp", "seq"),
-            P("dp", "seq"),
-            P("dp", "seq"),
-        ),
-        out_specs=(
-            P("dp", "seq", None),
-            P("dp", "seq", None),
-            P("dp", "seq"),
-            P("dp", "seq"),
-            P("dp", "seq"),
-            P("dp", "seq"),
-            P("dp", "seq"),
-        ),
+        mesh=Mesh(cut, ("seq", "y", "z")),
+        in_specs=(tokens,) * 4 + (P(("y", "z"), None),) + (state,) * 5,
+        out_specs=(tokens,) * 2 + (state,) * 5,
         check_vma=False,
     )

time: 166 us -> 183 us (1.10)
  Pallas kernels: 34.9 us -> 65.4 us
  waiting for transfers between devices: 33.2 us -> 19.9 us
  starting transfers between devices: 87.3 us -> 83.3 us
  local copies, waits for them, and re-layouts: 8.82 us -> 12 us
    pallas_call x2, Pallas kernels: 2.05 us -> 28.8 us  [merge(): pl.pallas_call(merge_kernel, in_specs=[ANYWHERE] * XS, out_specs=ANYWHERE...]
    ppermute x17, waiting for transfers between devices: 33.2 us -> 15.2 us  [send(): return lax.ppermute(array, 'seq', pairs)]
    all_to_all x2 -> x3, starting transfers between devices: 33.5 us -> 27.8 us  [the longest x1 16.3 us: shards(): lax.all_to_all(copies, ('y', 'z'), split_axis=0, concat_axis=0, tiled=True)]
    all_to_all x2 -> x3, waiting for transfers between devices: 0.01 us -> 4.65 us  [the longest x1 4.65 us: shards(): lax.all_to_all(add_parts(parts), 'z', split_axis=0, concat_axis=0, tiled=...]
    pallas_call x1 -> x3, Pallas kernels: 5.62 us -> 8.35 us  [the longest x2 7.56 us: values_call(): pl.pallas_call(values_kernel, grid=(D // STRIPE,), in_specs=hidden_specs(...]
    unnamed x32 -> x38, local copies, waits for them, and re-layouts: 6.74 us -> 8.22 us
  transfers between devices with their start and end apart: 19 -> 20, of which waited for: 8 -> 5; matrix products, arithmetic and copies ran while one was open for 1% -> 2% of each run, Pallas kernels for 20% -> 31%
where the time goes in v5:
time: 183 us; the launch traced here: 182 us
  starting transfers between devices  83.3 us (46%)
  Pallas kernels  65.4 us (36%)
  waiting for transfers between devices  19.9 us (11%)
  local copies, waits for them, and re-layouts  12 us (7%)
    ppermute x17, starting transfers between devices, send(): return lax.ppermute(array, 'seq', pairs)  55.5 us
    pallas_call x2, Pallas kernels, merge(): pl.pallas_call(merge_kernel, in_specs=[ANYWHERE] * XS, out_specs=ANYWHERE...  28.8 us
    all_to_all x1, starting transfers between devices, shards(): lax.all_to_all(copies, ('y', 'z'), split_axis=0, concat_axis=0, tiled=True)  16.3 us
    ppermute x17, waiting for transfers between devices, send(): return lax.ppermute(array, 'seq', pairs)  15.2 us
    pallas_call x1, Pallas kernels, grads_call(): pl.pallas_call(grads_kernel, grid=(BLOCKS // 2,), in_specs=[SCALARS, SCAL...  8.5 us
    pallas_call x1, Pallas kernels, probs_call(): pl.pallas_call(probs_kernel, grid=(BLOCKS // 2,), in_specs=[SCALARS, SCAL...  8.48 us
    unnamed x38, local copies, waits for them, and re-layouts  8.22 us
    all_to_all x1, starting transfers between devices, shards(): lax.all_to_all(add_parts(parts), 'z', split_axis=0, concat_axis=0, tiled=...  7.76 us
  transfers between devices with their start and end apart: 20, of which 5 were waited for; matrix products, arithmetic and copies ran while one was open for 2% of the time, Pallas kernels for 31%

profile of v5, /device:TPU:1, one launch (start us, length us, event | category | flops | bytes accessed | tf_op | source)
XLA Modules:
  0.0 181.8 jit_solution(1840269650149979125)
XLA Ops:
  0.7 0.7 stack.58.to_ref
  1.4 3.3 %shard_map.153 = (bf16[2,128,1152]{2,1,0:T(8,128)(2,1)}, bf16[2,128,1152]{2,1,0:T(8,128)(2,1)}, bf16[2,128,1152]{2,1,0:T(8,128)(2,1)}, bf16[2,128,1152]{2,1,0:T(8,128)(2,1)}) custom-call(s32[8]{0:T(128)} %stack.58.to_ref, bf16[128,4096]{1,0:T(8,128)(2,1)} %bitcast.18, bf16[128,4096]{1,0:T(8,128)(2,1)} %bitcast.19, bf16[128,1024]{1,0:T(8,128)(2,1)} %bitcast.20), custom_call_target="tpu_custom_call" | custom-call | flops 3000000000 | bytes 3000000 | tf_op jit(solution)/shard_map/pallas_call | solution.py:94
  4.6 4.0 %collective-permute-start = (bf16[2,128,1152]{2,1,0:T(8,128)(2,1)}, bf16[2,128,1152]{2,1,0:T(8,128)(2,1)}, u32[]{:S(2)}, u32[]{:S(2)}) collective-permute-start(bf16[2,128,1152]{2,1,0:T(8,128)(2,1)} %get-tuple-element.30), channel_id=1, source_target_pairs={{0,128},{64,192},{128,256},{192,320},{256,384},{320,448},{384,0},{... | collective-permute-start | bytes 1769480 | tf_op jit(solution)/shard_map/ppermute | solution.py:57
  8.6 4.4 %collective-permute-start.1 = (bf16[2,128,1152]{2,1,0:T(8,128)(2,1)}, bf16[2,128,1152]{2,1,0:T(8,128)(2,1)}, u32[]{:S(2)}, u32[]{:S(2)}) collective-permute-start(bf16[2,128,1152]{2,1,0:T(8,128)(2,1)} %get-tuple-element.31), channel_id=1, source_target_pairs={{0,256},{64,320},{128,384},{192,448},{256,0},{320,64},{384,128},{4... | collective-permute-start | bytes 1769480 | tf_op jit(solution)/shard_map/ppermute | solution.py:57
  12.9 3.1 %collective-permute-start.2 = (bf16[2,128,1152]{2,1,0:T(8,128)(2,1)}, bf16[2,128,1152]{2,1,0:T(8,128)(2,1)}, u32[]{:S(2)}, u32[]{:S(2)}) collective-permute-start(bf16[2,128,1152]{2,1,0:T(8,128)(2,1)} %get-tuple-element.32), channel_id=1, source_target_pairs={{0,384},{64,448},{128,0},{192,64},{256,128},{320,192},{384,256},{4... | collective-permute-start | bytes 1769480 | tf_op jit(solution)/shard_map/ppermute | solution.py:57
  16.0 2.2 %collective-permute-start.4 = (bf16[128,4096]{1,0:T(8,128)(2,1)}, bf16[128,4096]{1,0:T(8,128)(2,1)S(1)}, u32[]{:S(2)}, u32[]{:S(2)}) collective-permute-start(bf16[128,4096]{1,0:T(8,128)(2,1)} %bitcast.11.refs_0_), channel_id=1, source_target_pairs={{0,128},{64,192},{128,256},{192,320},{256,384},{320,448},{384,0},{... | collective-permute-start | bytes 3145736 | tf_op jit(solution)/shard_map/ppermute | solution.py:57
  18.2 4.3 %collective-permute-start.6 = (bf16[128,4096]{1,0:T(8,128)(2,1)}, bf16[128,4096]{1,0:T(8,128)(2,1)S(1)}, u32[]{:S(2)}, u32[]{:S(2)}) collective-permute-start(bf16[128,4096]{1,0:T(8,128)(2,1)} %bitcast.11.refs_0_), channel_id=1, source_target_pairs={{0,384},{64,448},{128,0},{192,64},{256,128},{320,192},{384,256},{4... | collective-permute-start | bytes 3145736 | tf_op jit(solution)/shard_map/ppermute | solution.py:57
  22.5 1.2 broadcast_in_dim.12
  23.8 16.3 %all-to-all-start = ((bf16[64,64,128]{2,1,0:T(8,128)(2,1)}), bf16[64,64,128]{2,1,0:T(8,128)(2,1)S(1)}, u32[]{:S(2)}, u32[]{:S(2)}) async-start(bf16[64,64,128]{2,1,0:T(8,128)(2,1)} %broadcast_in_dim.12), calls=%async_computation | async-start | bytes 2097152 | tf_op jit(solution)/shard_map/all_to_all | solution.py:529
  40.1 0.0 collective-permute-done.refs_1_
  40.1 0.0 collective-permute-done.2.refs_3_
  40.1 1.1 copy-done.7
  41.2 27.9 %shard_map.154 = bf16[4,128,1152]{2,1,0:T(8,128)(2,1)} custom-call(bf16[2,128,1152]{2,1,0:T(8,128)(2,1)S(1)} %copy-done.7, bf16[2,128,1152]{2,1,0:T(8,128)(2,1)} %collective-permute-done.refs_1_, bf16[2,128,1152]{2,1,0:T(8,128)(2,1)} %collective-permute-done.1.refs_2_, bf16[2,128,1152]{2,1,0:T(8,128)(2,1)} %collective-permute-done.2.refs_3_), custom_call_target="tpu_custom_call" | custom-call | flops 1000000000 | bytes 1000000 | tf_op jit(solution)/shard_map/pallas_call | solution.py:113
  69.1 0.0 copy-start.6
  69.1 8.4 %collective-permute-start.3 = (bf16[4,128,1152]{2,1,0:T(8,128)(2,1)}, bf16[4,128,1152]{2,1,0:T(8,128)(2,1)}, u32[]{:S(2)}, u32[]{:S(2)}) collective-permute-start(bf16[4,128,1152]{2,1,0:T(8,128)(2,1)} %shard_map.154), channel_id=1, source_target_pairs={{0,64},{64,0},{128,192},{192,128},{256,320},{320,256},{384,448},{4... | collective-permute-start | bytes 3538952 | tf_op jit(solution)/shard_map/ppermute | solution.py:57
  77.5 1.9 %collective-permute-start.8 = (bf16[128,4096]{1,0:T(8,128)(2,1)}, bf16[128,4096]{1,0:T(8,128)(2,1)}, u32[]{:S(2)}, u32[]{:S(2)}) collective-permute-start(bf16[128,4096]{1,0:T(8,128)(2,1)} %bitcast.11.refs_0_), channel_id=1, source_target_pairs={{0,64},{64,0},{128,192},{192,128},{256,320},{320,256},{384,448},{4... | collective-permute-start | bytes 3145736 | tf_op jit(solution)/shard_map/ppermute | solution.py:57
  79.5 2.4 %collective-permute-start.9 = (bf16[128,4096]{1,0:T(8,128)(2,1)S(1)}, bf16[128,4096]{1,0:T(8,128)(2,1)}, u32[]{:S(2)}, u32[]{:S(2)}) collective-permute-start(bf16[128,4096]{1,0:T(8,128)(2,1)S(1)} %collective-permute-done.4.refs_2_), channel_id=1, source_target_pairs={{0,64},{64,0},{128,192},{192,128},{256,320},{320,256},{384,448},{4... | collective-permute-start | bytes 3145736 | tf_op jit(solution)/shard_map/ppermute | solution.py:57
  81.9 0.0 collective-permute-done.6.refs_4_
  81.9 1.9 %collective-permute-start.10 = (bf16[128,4096]{1,0:T(8,128)(2,1)S(1)}, bf16[128,4096]{1,0:T(8,128)(2,1)}, u32[]{:S(2)}, u32[]{:S(2)}) collective-permute-start(bf16[128,4096]{1,0:T(8,128)(2,1)S(1)} %collective-permute-done.6.refs_4_), channel_id=1, source_target_pairs={{0,64},{64,0},{128,192},{192,128},{256,320},{320,256},{384,448},{4... | collective-permute-start | bytes 3145736 | tf_op jit(solution)/shard_map/ppermute | solution.py:57
  83.8 0.1 stack.57.from_ref
  83.9 0.9 slice.8
  84.8 1.9 %collective-permute-start.5 = (bf16[64,4096]{1,0:T(8,128)(2,1)}, bf16[64,4096]{1,0:T(8,128)(2,1)}, u32[]{:S(2)}, u32[]{:S(2)}) collective-permute-start(bf16[64,4096]{1,0:T(8,128)(2,1)} %slice.8), channel_id=1, source_target_pairs={{0,128},{64,192},{128,256},{192,320},{256,384},{320,448},{384,0},{... | collective-permute-start | bytes 1572872 | tf_op jit(solution)/shard_map/ppermute | solution.py:57
  86.7 0.9 slice.9
  87.6 4.6 %collective-permute-start.7 = (bf16[64,4096]{1,0:T(8,128)(2,1)}, bf16[64,4096]{1,0:T(8,128)(2,1)}, u32[]{:S(2)}, u32[]{:S(2)}) collective-permute-start(bf16[64,4096]{1,0:T(8,128)(2,1)} %slice.9), channel_id=1, source_target_pairs={{0,384},{64,448},{128,0},{192,64},{256,128},{320,192},{384,256},{4... | collective-permute-start | bytes 1572872 | tf_op jit(solution)/shard_map/ppermute | solution.py:57
  92.2 8.5 %shard_map.155 = (bf16[4,2,512,512]{3,2,1,0:T(8,128)(2,1)}, bf16[1024,128]{1,0:T(8,128)(2,1)S(1)}) custom-call(s32[1,8]{1,0:T(1,128)S(1)} %copy-done.6, s32[8]{0:T(128)S(1)} %stack.57.from_ref, bf16[2,128,1152]{2,1,0:T(8,128)(2,1)S(1)} %copy-done.8, bf16[2,128,1152]{2,1,0:T(8,128)(2,1)} %collective-permute-done.refs_1_, ...), custom_call_target="tpu_custom_call" | custom-call | flops 8000000000 | bytes 8000000 | tf_op jit(solution)/shard_map/pallas_call | solution.py:227
  100.6 0.0 copy-start.13
  100.7 0.7 copy-done.13
  101.4 0.0 collective-permute-done.9.refs_3_
  101.4 4.3 %shard_map.156.refs_6_ = bf16[768,128]{1,0:T(8,128)(2,1)S(1)} custom-call(bf16[128,4096]{1,0:T(8,128)(2,1)} %bitcast.11.refs_0_, bf16[128,4096]{1,0:T(8,128)(2,1)} %collective-permute-done.8.refs_1_, bf16[128,4096]{1,0:T(8,128)(2,1)S(1)} %collective-permute-done.4.refs_2_, bf16[128,4096]{1,0:T(8,128)(2,1)} %collective-permute-done.9.refs_3_, ...), custom_call_target="tpu_custom_call" | custom-call | flops 4000000000 | bytes 4000000 | tf_op jit(solution)/shard_map/pallas_call | solution.py:302
  105.7 0.0 collective-permute-done.5.refs_0_.refs_6_
  105.7 0.0 collective-permute-done.7.refs_1_.refs_7_
  105.8 3.0 %collective-permute-start.11 = (bf16[64,4096]{1,0:T(8,128)(2,1)}, bf16[64,4096]{1,0:T(8,128)(2,1)}, u32[]{:S(2)}, u32[]{:S(2)}) collective-permute-start(bf16[64,4096]{1,0:T(8,128)(2,1)} %collective-permute-done.5.refs_0_.refs_6_), channel_id=1, source_target_pairs={{0,64},{64,0},{128,192},{192,128},{256,320},{320,256},{384,448},{4... | collective-permute-start | bytes 1572872 | tf_op jit(solution)/shard_map/ppermute | solution.py:57
  108.7 1.9 %collective-permute-start.12 = (bf16[64,4096]{1,0:T(8,128)(2,1)}, bf16[64,4096]{1,0:T(8,128)(2,1)}, u32[]{:S(2)}, u32[]{:S(2)}) collective-permute-start(bf16[64,4096]{1,0:T(8,128)(2,1)} %collective-permute-done.7.refs_1_.refs_7_), channel_id=1, source_target_pairs={{0,64},{64,0},{128,192},{192,128},{256,320},{320,256},{384,448},{4... | collective-permute-start | bytes 1572872 | tf_op jit(solution)/shard_map/ppermute | solution.py:57
  110.7 0.1 stack.59.around_ref.from_ref
  110.7 0.0 collective-permute-done.11.refs_2_.refs_8_
  110.8 2.1 %collective-permute-done.12.refs_3_.refs_9_ = bf16[64,4096]{1,0:T(8,128)(2,1)} collective-permute-done((bf16[64,4096]{1,0:T(8,128)(2,1)}, bf16[64,4096]{1,0:T(8,128)(2,1)}, u32[]{:S(2)}, u32[]{:S(2)}) %collective-permute-start.12) | collective-permute-done | bytes 524320 | tf_op jit(solution)/shard_map/ppermute | solution.py:57
  112.9 0.9 copy-done.14
  113.8 5.5 %shard_map.161 = bf16[4096,128]{1,0:T(8,128)(2,1)} custom-call(s32[8]{0:T(128)S(1)} %stack.59.around_ref.from_ref, bf16[128,4096]{1,0:T(8,128)(2,1)} %bitcast.11.refs_0_, bf16[128,4096]{1,0:T(8,128)(2,1)} %collective-permute-done.8.refs_1_, bf16[128,4096]{1,0:T(8,128)(2,1)S(1)} %collective-permute-done.4.refs_2_, ...), custom_call_target="tpu_custom_call" | custom-call | flops 5000000000 | bytes 5000000 | tf_op jit(solution)/shard_map/pallas_call | solution.py:286
  119.4 3.7 %all-to-all-start.1 = ((bf16[8,8,64,128]{3,2,1,0:T(8,128)(2,1)}), bf16[8,8,64,128]{3,2,1,0:T(8,128)(2,1)S(1)}, u32[]{:S(2)}, u32[]{:S(2)}) async-start(bf16[8,8,64,128]{3,2,1,0:T(8,128)(2,1)} %bitcast.15), calls=%async_computation.1 | async-start | bytes 2097152 | tf_op jit(solution)/shard_map/all_to_all | solution.py:541
  123.1 3.2 %shard_map.157.refs_7_ = bf16[256,128]{1,0:T(8,128)(2,1)S(1)} custom-call(bf16[64,4096]{1,0:T(8,128)(2,1)} %collective-permute-done.5.refs_0_.refs_6_, bf16[64,4096]{1,0:T(8,128)(2,1)} %collective-permute-done.7.refs_1_.refs_7_, bf16[64,4096]{1,0:T(8,128)(2,1)} %collective-permute-done.11.refs_2_.refs_8_, ...), custom_call_target="tpu_custom_call" | custom-call | flops 1000000000 | bytes 1000000 | tf_op jit(solution)/shard_map/pallas_call | solution.py:302
  126.4 2.2 %copy-done.12 = bf16[4,2,512,512]{3,2,1,0:T(8,128)(2,1)S(1)} copy-done((bf16[4,2,512,512]{3,2,1,0:T(8,128)(2,1)S(1)}, bf16[4,2,512,512]{3,2,1,0:T(8,128)(2,1)}, u32[]{:S(2)}) %copy-start.12) | copy-done | bytes 4194328
  128.6 8.5 %shard_map.158 = (bf16[2,128,640]{2,1,0:T(8,128)(2,1)S(1)}, bf16[2,128,640]{2,1,0:T(8,128)(2,1)S(1)}, bf16[2,128,640]{2,1,0:T(8,128)(2,1)S(1)}, bf16[2,128,640]{2,1,0:T(8,128)(2,1)S(1)}) custom-call(s32[8]{0:T(128)S(1)} %stack.57.from_ref, s32[8]{0:T(128)S(1)} %copy-done.1, s32[8]{0:T(128)S(1)} %stack.59.around_ref.from_ref, ...), custom_call_target="tpu_custom_call" | custom-call | flops 8999999488 | bytes 9000000 | tf_op jit(solution)/shard_map/pallas_call | solution.py:371
  137.1 1.9 %collective-permute-start.13 = (bf16[2,128,640]{2,1,0:T(8,128)(2,1)S(1)}, bf16[2,128,640]{2,1,0:T(8,128)(2,1)S(1)}, u32[]{:S(2)}, u32[]{:S(2)}) collective-permute-start(bf16[2,128,640]{2,1,0:T(8,128)(2,1)S(1)} %get-tuple-element.40), channel_id=1, source_target_pairs={{0,128},{64,192},{128,256},{192,320},{256,384},{320,448},{384,0},{... | collective-permute-start | bytes 983048 | tf_op jit(solution)/shard_map/ppermute | solution.py:57
  139.0 4.2 %collective-permute-start.14 = (bf16[2,128,640]{2,1,0:T(8,128)(2,1)S(1)}, bf16[2,128,640]{2,1,0:T(8,128)(2,1)S(1)}, u32[]{:S(2)}, u32[]{:S(2)}) collective-permute-start(bf16[2,128,640]{2,1,0:T(8,128)(2,1)S(1)} %get-tuple-element.41), channel_id=1, source_target_pairs={{0,256},{64,320},{128,384},{192,448},{256,0},{320,64},{384,128},{4... | collective-permute-start | bytes 983048 | tf_op jit(solution)/shard_map/ppermute | solution.py:57
  143.3 2.3 %collective-permute-start.15 = (bf16[2,128,640]{2,1,0:T(8,128)(2,1)S(1)}, bf16[2,128,640]{2,1,0:T(8,128)(2,1)S(1)}, u32[]{:S(2)}, u32[]{:S(2)}) collective-permute-start(bf16[2,128,640]{2,1,0:T(8,128)(2,1)S(1)} %get-tuple-element.42), channel_id=1, source_target_pairs={{0,384},{64,448},{128,0},{192,64},{256,128},{320,192},{384,256},{4... | collective-permute-start | bytes 983048 | tf_op jit(solution)/shard_map/ppermute | solution.py:57
  145.5 4.2 %collective-permute-done.13.refs_1_ = bf16[2,128,640]{2,1,0:T(8,128)(2,1)S(1)} collective-permute-done((bf16[2,128,640]{2,1,0:T(8,128)(2,1)S(1)}, bf16[2,128,640]{2,1,0:T(8,128)(2,1)S(1)}, u32[]{:S(2)}, u32[]{:S(2)}) %collective-permute-start.13) | collective-permute-done | bytes 327712 | tf_op jit(solution)/shard_map/ppermute | solution.py:57
  149.7 6.4 %collective-permute-done.14.refs_2_ = bf16[2,128,640]{2,1,0:T(8,128)(2,1)S(1)} collective-permute-done((bf16[2,128,640]{2,1,0:T(8,128)(2,1)S(1)}, bf16[2,128,640]{2,1,0:T(8,128)(2,1)S(1)}, u32[]{:S(2)}, u32[]{:S(2)}) %collective-permute-start.14) | collective-permute-done | bytes 327712 | tf_op jit(solution)/shard_map/ppermute | solution.py:57
  156.1 2.5 %collective-permute-done.15.refs_3_ = bf16[2,128,640]{2,1,0:T(8,128)(2,1)S(1)} collective-permute-done((bf16[2,128,640]{2,1,0:T(8,128)(2,1)S(1)}, bf16[2,128,640]{2,1,0:T(8,128)(2,1)S(1)}, u32[]{:S(2)}, u32[]{:S(2)}) %collective-permute-start.15) | collective-permute-done | bytes 327712 | tf_op jit(solution)/shard_map/ppermute | solution.py:57
  158.6 0.9 shard_map.159
  159.5 0.0 copy-start.15
  159.5 0.0 copy-start.16
  159.5 3.2 %collective-permute-start.16 = (bf16[4,128,640]{2,1,0:T(8,128)(2,1)S(1)}, bf16[4,128,640]{2,1,0:T(8,128)(2,1)S(1)}, u32[]{:S(2)}, u32[]{:S(2)}) collective-permute-start(bf16[4,128,640]{2,1,0:T(8,128)(2,1)S(1)} %shard_map.159), channel_id=1, source_target_pairs={{0,64},{64,0},{128,192},{192,128},{256,320},{320,256},{384,448},{4... | collective-permute-start | bytes 1966088 | tf_op jit(solution)/shard_map/ppermute | solution.py:57
  162.7 0.0 all-to-all-done.1.parts_ref
  162.7 0.8 shard_map.162
  163.5 7.8 %all-to-all-start.2 = ((bf16[8,64,128]{2,1,0:T(8,128)(2,1)}), bf16[8,64,128]{2,1,0:T(8,128)(2,1)S(1)}, u32[]{:S(2)}, u32[]{:S(2)}) async-start(bf16[8,64,128]{2,1,0:T(8,128)(2,1)} %shard_map.162), calls=%async_computation.2 | async-start | bytes 262144 | tf_op jit(solution)/shard_map/all_to_all | solution.py:544
  171.3 0.1 copy.17.ms_ref
  171.4 0.1 copy.18.vs_ref
  171.5 1.0 copy-done.3
  172.4 1.0 copy-done.11
  173.4 1.7 shard_map.160
  175.1 4.6 %all-to-all-done.2.parts_ref = bf16[8,64,128]{2,1,0:T(8,128)(2,1)S(1)} async-done(((bf16[8,64,128]{2,1,0:T(8,128)(2,1)}), bf16[8,64,128]{2,1,0:T(8,128)(2,1)S(1)}, u32[]{:S(2)}, u32[]{:S(2)}) %all-to-all-start.2) | async-done | bytes 131104 | tf_op jit(solution)/shard_map/all_to_all | solution.py:544
  179.8 0.8 shard_map.163
  180.6 0.6 copy.19
  181.2 0.6 copy.20
  (32 shorter events, 0.1 us)
Async XLA Ops:
  1.3 21.2 %copy-start = (f32[64,128]{1,0:T(8,128)S(1)}, f32[64,128]{1,0:T(8,128)}, u32[]{:S(2)}) copy-start(f32[64,128]{1,0:T(8,128)} %master_ref.1) | copy-start | bytes 98308
  4.6 35.5 %collective-permute-start = (bf16[2,128,1152]{2,1,0:T(8,128)(2,1)}, bf16[2,128,1152]{2,1,0:T(8,128)(2,1)}, u32[]{:S(2)}, u32[]{:S(2)}) collective-permute-start(bf16[2,128,1152]{2,1,0:T(8,128)(2,1)} %get-tuple-element.30), channel_id=1, source_target_pairs={{0,128},{64,192},{128,256},{192,320},{256,384},{320,448},{384,0},{... | collective-permute-start | bytes 1769480 | tf_op jit(solution)/shard_map/ppermute | solution.py:57
  8.6 31.5 %collective-permute-start.1 = (bf16[2,128,1152]{2,1,0:T(8,128)(2,1)}, bf16[2,128,1152]{2,1,0:T(8,128)(2,1)}, u32[]{:S(2)}, u32[]{:S(2)}) collective-permute-start(bf16[2,128,1152]{2,1,0:T(8,128)(2,1)} %get-tuple-element.31), channel_id=1, source_target_pairs={{0,256},{64,320},{128,384},{192,448},{256,0},{320,64},{384,128},{4... | collective-permute-start | bytes 1769480 | tf_op jit(solution)/shard_map/ppermute | solution.py:57
  12.9 27.2 %collective-permute-start.2 = (bf16[2,128,1152]{2,1,0:T(8,128)(2,1)}, bf16[2,128,1152]{2,1,0:T(8,128)(2,1)}, u32[]{:S(2)}, u32[]{:S(2)}) collective-permute-start(bf16[2,128,1152]{2,1,0:T(8,128)(2,1)} %get-tuple-element.32), channel_id=1, source_target_pairs={{0,384},{64,448},{128,0},{192,64},{256,128},{320,192},{384,256},{4... | collective-permute-start | bytes 1769480 | tf_op jit(solution)/shard_map/ppermute | solution.py:57
  16.0 63.5 %collective-permute-start.4 = (bf16[128,4096]{1,0:T(8,128)(2,1)}, bf16[128,4096]{1,0:T(8,128)(2,1)S(1)}, u32[]{:S(2)}, u32[]{:S(2)}) collective-permute-start(bf16[128,4096]{1,0:T(8,128)(2,1)} %bitcast.11.refs_0_), channel_id=1, source_target_pairs={{0,128},{64,192},{128,256},{192,320},{256,384},{320,448},{384,0},{... | collective-permute-start | bytes 3145736 | tf_op jit(solution)/shard_map/ppermute | solution.py:57
  18.2 63.7 %collective-permute-start.6 = (bf16[128,4096]{1,0:T(8,128)(2,1)}, bf16[128,4096]{1,0:T(8,128)(2,1)S(1)}, u32[]{:S(2)}, u32[]{:S(2)}) collective-permute-start(bf16[128,4096]{1,0:T(8,128)(2,1)} %bitcast.11.refs_0_), channel_id=1, source_target_pairs={{0,384},{64,448},{128,0},{192,64},{256,128},{320,192},{384,256},{4... | collective-permute-start | bytes 3145736 | tf_op jit(solution)/shard_map/ppermute | solution.py:57
  23.8 77.6 %all-to-all-start = ((bf16[64,64,128]{2,1,0:T(8,128)(2,1)}), bf16[64,64,128]{2,1,0:T(8,128)(2,1)S(1)}, u32[]{:S(2)}, u32[]{:S(2)}) async-start(bf16[64,64,128]{2,1,0:T(8,128)(2,1)} %broadcast_in_dim.12), calls=%async_computation | async-start | bytes 2097152 | tf_op jit(solution)/shard_map/all_to_all | solution.py:529
  40.1 1.1 copy-start.7
  69.1 23.0 %copy-start.6 = (s32[1,8]{1,0:T(1,128)S(1)}, s32[1,8]{1,0:T(1,128)}, u32[]{:S(2)}) copy-start(s32[1,8]{1,0:T(1,128)} %lens_ref.1) | copy-start | bytes 100
  69.1 18.4 %collective-permute-start.3 = (bf16[4,128,1152]{2,1,0:T(8,128)(2,1)}, bf16[4,128,1152]{2,1,0:T(8,128)(2,1)}, u32[]{:S(2)}, u32[]{:S(2)}) collective-permute-start(bf16[4,128,1152]{2,1,0:T(8,128)(2,1)} %shard_map.154), channel_id=1, source_target_pairs={{0,64},{64,0},{128,192},{192,128},{256,320},{320,256},{384,448},{4... | collective-permute-start | bytes 3538952 | tf_op jit(solution)/shard_map/ppermute | solution.py:57
  77.5 23.8 %collective-permute-start.8 = (bf16[128,4096]{1,0:T(8,128)(2,1)}, bf16[128,4096]{1,0:T(8,128)(2,1)}, u32[]{:S(2)}, u32[]{:S(2)}) collective-permute-start(bf16[128,4096]{1,0:T(8,128)(2,1)} %bitcast.11.refs_0_), channel_id=1, source_target_pairs={{0,64},{64,0},{128,192},{192,128},{256,320},{320,256},{384,448},{4... | collective-permute-start | bytes 3145736 | tf_op jit(solution)/shard_map/ppermute | solution.py:57
  79.5 21.9 %collective-permute-start.9 = (bf16[128,4096]{1,0:T(8,128)(2,1)S(1)}, bf16[128,4096]{1,0:T(8,128)(2,1)}, u32[]{:S(2)}, u32[]{:S(2)}) collective-permute-start(bf16[128,4096]{1,0:T(8,128)(2,1)S(1)} %collective-permute-done.4.refs_2_), channel_id=1, source_target_pairs={{0,64},{64,0},{128,192},{192,128},{256,320},{320,256},{384,448},{4... | collective-permute-start | bytes 3145736 | tf_op jit(solution)/shard_map/ppermute | solution.py:57
  81.9 19.5 %collective-permute-start.10 = (bf16[128,4096]{1,0:T(8,128)(2,1)S(1)}, bf16[128,4096]{1,0:T(8,128)(2,1)}, u32[]{:S(2)}, u32[]{:S(2)}) collective-permute-start(bf16[128,4096]{1,0:T(8,128)(2,1)S(1)} %collective-permute-done.6.refs_4_), channel_id=1, source_target_pairs={{0,64},{64,0},{128,192},{192,128},{256,320},{320,256},{384,448},{4... | collective-permute-start | bytes 3145736 | tf_op jit(solution)/shard_map/ppermute | solution.py:57
  83.9 8.2 %copy-start.8 = (bf16[2,128,1152]{2,1,0:T(8,128)(2,1)S(1)}, bf16[2,128,1152]{2,1,0:T(8,128)(2,1)}, u32[]{:S(2)}) copy-start(bf16[2,128,1152]{2,1,0:T(8,128)(2,1)} %get-tuple-element.29.refs_0_) | copy-start | bytes 1769476
  84.8 21.0 %collective-permute-start.5 = (bf16[64,4096]{1,0:T(8,128)(2,1)}, bf16[64,4096]{1,0:T(8,128)(2,1)}, u32[]{:S(2)}, u32[]{:S(2)}) collective-permute-start(bf16[64,4096]{1,0:T(8,128)(2,1)} %slice.8), channel_id=1, source_target_pairs={{0,128},{64,192},{128,256},{192,320},{256,384},{320,448},{384,0},{... | collective-permute-start | bytes 1572872 | tf_op jit(solution)/shard_map/ppermute | solution.py:57
  87.6 18.2 %collective-permute-start.7 = (bf16[64,4096]{1,0:T(8,128)(2,1)}, bf16[64,4096]{1,0:T(8,128)(2,1)}, u32[]{:S(2)}, u32[]{:S(2)}) collective-permute-start(bf16[64,4096]{1,0:T(8,128)(2,1)} %slice.9), channel_id=1, source_target_pairs={{0,384},{64,448},{128,0},{192,64},{256,128},{320,192},{384,256},{4... | collective-permute-start | bytes 1572872 | tf_op jit(solution)/shard_map/ppermute | solution.py:57
  100.6 0.7 copy-start.13
  105.8 5.0 %collective-permute-start.11 = (bf16[64,4096]{1,0:T(8,128)(2,1)}, bf16[64,4096]{1,0:T(8,128)(2,1)}, u32[]{:S(2)}, u32[]{:S(2)}) collective-permute-start(bf16[64,4096]{1,0:T(8,128)(2,1)} %collective-permute-done.5.refs_0_.refs_6_), channel_id=1, source_target_pairs={{0,64},{64,0},{128,192},{192,128},{256,320},{320,256},{384,448},{4... | collective-permute-start | bytes 1572872 | tf_op jit(solution)/shard_map/ppermute | solution.py:57
  108.7 4.1 %collective-permute-start.12 = (bf16[64,4096]{1,0:T(8,128)(2,1)}, bf16[64,4096]{1,0:T(8,128)(2,1)}, u32[]{:S(2)}, u32[]{:S(2)}) collective-permute-start(bf16[64,4096]{1,0:T(8,128)(2,1)} %collective-permute-done.7.refs_1_.refs_7_), channel_id=1, source_target_pairs={{0,64},{64,0},{128,192},{192,128},{256,320},{320,256},{384,448},{4... | collective-permute-start | bytes 1572872 | tf_op jit(solution)/shard_map/ppermute | solution.py:57
  112.9 1.0 copy-start.14
  119.4 43.3 %all-to-all-start.1 = ((bf16[8,8,64,128]{3,2,1,0:T(8,128)(2,1)}), bf16[8,8,64,128]{3,2,1,0:T(8,128)(2,1)S(1)}, u32[]{:S(2)}, u32[]{:S(2)}) async-start(bf16[8,8,64,128]{3,2,1,0:T(8,128)(2,1)} %bitcast.15), calls=%async_computation.1 | async-start | bytes 2097152 | tf_op jit(solution)/shard_map/all_to_all | solution.py:541
  123.1 3.2 %copy-start.1 = (s32[8]{0:T(128)S(1)}, s32[8]{0:T(128)}, u32[]{:S(2)}) copy-start(s32[8]{0:T(128)} %stack.58.to_ref) | copy-start | bytes 100
  123.1 3.2 %copy-start.9 = (bf16[2,128,1152]{2,1,0:T(8,128)(2,1)S(1)}, bf16[2,128,1152]{2,1,0:T(8,128)(2,1)}, u32[]{:S(2)}) copy-start(bf16[2,128,1152]{2,1,0:T(8,128)(2,1)} %get-tuple-element.29.refs_0_) | copy-start | bytes 1769476
  126.4 2.2 %copy-start.12 = (bf16[4,2,512,512]{3,2,1,0:T(8,128)(2,1)S(1)}, bf16[4,2,512,512]{3,2,1,0:T(8,128)(2,1)}, u32[]{:S(2)}) copy-start(bf16[4,2,512,512]{3,2,1,0:T(8,128)(2,1)} %get-tuple-element.33.refs_5_) | copy-start | bytes 12582916
  137.1 22.4 %copy-start.10 = (bf16[2,128,640]{2,1,0:T(8,128)(2,1)}, bf16[2,128,640]{2,1,0:T(8,128)(2,1)S(1)}, u32[]{:S(2)}) copy-start(bf16[2,128,640]{2,1,0:T(8,128)(2,1)S(1)} %get-tuple-element.39.refs_0_) | copy-start | bytes 983044
  137.1 12.6 %collective-permute-start.13 = (bf16[2,128,640]{2,1,0:T(8,128)(2,1)S(1)}, bf16[2,128,640]{2,1,0:T(8,128)(2,1)S(1)}, u32[]{:S(2)}, u32[]{:S(2)}) collective-permute-start(bf16[2,128,640]{2,1,0:T(8,128)(2,1)S(1)} %get-tuple-element.40), channel_id=1, source_target_pairs={{0,128},{64,192},{128,256},{192,320},{256,384},{320,448},{384,0},{... | collective-permute-start | bytes 983048 | tf_op jit(solution)/shard_map/ppermute | solution.py:57
  139.0 17.1 %collective-permute-start.14 = (bf16[2,128,640]{2,1,0:T(8,128)(2,1)S(1)}, bf16[2,128,640]{2,1,0:T(8,128)(2,1)S(1)}, u32[]{:S(2)}, u32[]{:S(2)}) collective-permute-start(bf16[2,128,640]{2,1,0:T(8,128)(2,1)S(1)} %get-tuple-element.41), channel_id=1, source_target_pairs={{0,256},{64,320},{128,384},{192,448},{256,0},{320,64},{384,128},{4... | collective-permute-start | bytes 983048 | tf_op jit(solution)/shard_map/ppermute | solution.py:57
  143.3 15.3 %collective-permute-start.15 = (bf16[2,128,640]{2,1,0:T(8,128)(2,1)S(1)}, bf16[2,128,640]{2,1,0:T(8,128)(2,1)S(1)}, u32[]{:S(2)}, u32[]{:S(2)}) collective-permute-start(bf16[2,128,640]{2,1,0:T(8,128)(2,1)S(1)} %get-tuple-element.42), channel_id=1, source_target_pairs={{0,384},{64,448},{128,0},{192,64},{256,128},{320,192},{384,256},{4... | collective-permute-start | bytes 983048 | tf_op jit(solution)/shard_map/ppermute | solution.py:57
  158.6 0.9 copy-start.2
  159.5 11.8 %copy-start.15 = (f32[32,1]{0,1:T(1,128)S(1)}, f32[32,1]{0,1:T(1,128)}, u32[]{:S(2)}) copy-start(f32[32,1]{0,1:T(1,128)} %param.17) | copy-start | bytes 388
  159.5 11.9 %copy-start.16 = (f32[32,1]{0,1:T(1,128)S(1)}, f32[32,1]{0,1:T(1,128)}, u32[]{:S(2)}) copy-start(f32[32,1]{0,1:T(1,128)} %param.19) | copy-start | bytes 388
  159.5 11.9 %collective-permute-start.16 = (bf16[4,128,640]{2,1,0:T(8,128)(2,1)S(1)}, bf16[4,128,640]{2,1,0:T(8,128)(2,1)S(1)}, u32[]{:S(2)}, u32[]{:S(2)}) collective-permute-start(bf16[4,128,640]{2,1,0:T(8,128)(2,1)S(1)} %shard_map.159), channel_id=1, source_target_pairs={{0,64},{64,0},{128,192},{192,128},{256,320},{320,256},{384,448},{4... | collective-permute-start | bytes 1966088 | tf_op jit(solution)/shard_map/ppermute | solution.py:57
  163.5 16.3 %all-to-all-start.2 = ((bf16[8,64,128]{2,1,0:T(8,128)(2,1)}), bf16[8,64,128]{2,1,0:T(8,128)(2,1)S(1)}, u32[]{:S(2)}, u32[]{:S(2)}) async-start(bf16[8,64,128]{2,1,0:T(8,128)(2,1)} %shard_map.162), calls=%async_computation.2 | async-start | bytes 262144 | tf_op jit(solution)/shard_map/all_to_all | solution.py:544
  171.5 1.0 copy-start.3
  172.4 1.0 copy-start.11
  173.4 6.4 %copy-start.4 = (bf16[64,128]{1,0:T(8,128)(2,1)S(1)}, bf16[64,128]{1,0:T(8,128)(2,1)}, u32[]{:S(2)}) copy-start(bf16[64,128]{1,0:T(8,128)(2,1)} %mc_ref.1) | copy-start | bytes 49156
  173.4 6.4 %copy-start.5 = (bf16[64,128]{1,0:T(8,128)(2,1)S(1)}, bf16[64,128]{1,0:T(8,128)(2,1)}, u32[]{:S(2)}) copy-start(bf16[64,128]{1,0:T(8,128)(2,1)} %vc_ref.1) | copy-start | bytes 49156

commit v6 on v5

--- a/solution.py
+++ b/solution.py
@@ -54,6 +54,11 @@
 
 def send(array, dx, dc):
     pairs = [(s, ((s // 2 + dx) % XS) * 2 + ((s % 2) ^ dc)) for s in range(2 * XS)]
+    return lax.ppermute(array, "seq", pairs)
+
+
+def turn(array, dx):
+    pairs = [(s, ((s // 2 + (dx if s % 2 == 0 else -dx)) % XS) * 2 + s % 2) for s in range(2 * XS)]
     return lax.ppermute(array, "seq", pairs)
 
 
@@ -113,17 +118,19 @@
     return pl.pallas_call(
         merge_kernel,
         in_specs=[ANYWHERE] * XS,
-        out_specs=ANYWHERE,
+        out_specs=pl.BlockSpec(memory_space=pltpu.VMEM),
         out_shape=jax.ShapeDtypeStruct((XS,) + pairs[0].shape[1:], BF16),
         scratch_shapes=[pltpu.SemaphoreType.DMA((XS,))],
         cost_estimate=cost(1),
-        compiler_params=params(4),
+        compiler_params=params(8),
     )(*pairs)
 
 
-def exchange(pairs):
-    got = [pairs[0]] + [send(pairs[dx], dx, 0) for dx in (1, 3, 2)]
-    got = [got[0], got[1], got[3], got[2]]
+def along(pairs):
+    return [pairs[0]] + [send(pairs[dx], dx, 0) for dx in range(1, XS)]
+
+
+def across(got):
     return got + [send(merge(got), 0, 1)]
 
 
@@ -248,7 +255,7 @@
 
 
 def term_kernel(from_ref, *refs):
-    hidden_refs, (gv_ref, term_ref, gvt_ref) = refs[:10], refs[10:]
+    hidden_refs, (gv_ref, term_ref, gvt_ref) = refs[:8], refs[8:]
 
     @pl.when(pl.program_id(0) == 0)
     def _():
@@ -330,8 +337,8 @@
 
 
 def grads_kernel(from_ref, to_ref, around_ref, *refs):
-    pieces, (pt_ref, near_ref, far_ref), outs = refs[:5], refs[5:8], refs[8 : 8 + XS]
-    r_ref, val_ref, out_ref, acc_ref, kt_ref, vt_ref, sems = refs[8 + XS :]
+    pieces, (pt_ref, held_ref), outs = refs[:5], refs[5:7], refs[7 : 7 + XS]
+    r_ref, val_ref, out_ref, acc_ref, kt_ref, vt_ref, sems = refs[7 + XS :]
     i = pl.program_id(0)
 
     @pl.when(i == 0)
@@ -341,8 +348,7 @@
         kt_ref[...] = r_ref[:, 2 * QW :].T
         for r in range(8):
             rows = pl.ds(pl.multiple_of(around_ref[r] * ROWS, ROWS), ROWS)
-            held, at = (near_ref, r) if r < 6 else (far_ref, r - 6)
-            val_ref[rows, :] = held[at * ROWS : (at + 1) * ROWS, :]
+            val_ref[rows, :] = held_ref[r * ROWS : (r + 1) * ROWS, :]
         vt_ref[...] = val_ref[...].T
 
     def body(v):
@@ -366,7 +372,7 @@
         )
 
 
-def grads_call(origin, to, around, pieces, probs, near, far):
+def grads_call(origin, to, around, pieces, probs, values):
     width = 2 * QW + HD
     return pl.pallas_call(
         grads_kernel,
@@ -375,8 +381,7 @@
         + [ANYWHERE] * 5
         + [
             PROBS_SPEC,
-            pl.BlockSpec(near.shape, lambda i: (0, 0)),
-            pl.BlockSpec(far.shape, lambda i: (0, 0)),
+            pl.BlockSpec((SEQ, HD), lambda i: (0, 0)),
         ],
         out_specs=[ANYWHERE] * XS,
         out_shape=[jax.ShapeDtypeStruct((2, ROWS, QW + HD), BF16)] * XS,
@@ -391,7 +396,7 @@
         ],
         cost_estimate=cost(9),
         compiler_params=params(),
-    )(origin, to, around, *pieces, probs, near, far)
+    )(origin, to, around, *pieces, probs, values)
 
 
 def unpack_kernel(from_ref, *refs):
@@ -413,7 +418,7 @@
 def unpack(origin, pieces):
     return pl.pallas_call(
         unpack_kernel,
-        in_specs=[SCALARS] + [ANYWHERE] * 5,
+        in_specs=[SCALARS] + [pl.BlockSpec(memory_space=pltpu.VMEM)] * 5,
         out_specs=[ANYWHERE] * 2,
         out_shape=[
             jax.ShapeDtypeStruct((ROWS, 8 * QW), BF16),
@@ -421,7 +426,7 @@
         ],
         scratch_shapes=[pltpu.SemaphoreType.DMA((16,))],
         cost_estimate=cost(2),
-        compiler_params=params(4),
+        compiler_params=params(8),
     )(origin, *pieces)
 
 
@@ -485,8 +490,8 @@
         jnp.max(jnp.abs(news[0][1]), axis=1, keepdims=True),
         jnp.max(jnp.abs(news[1][1]), axis=1, keepdims=True),
     )
-    ms_out[...] = m_top
-    vs_out[...] = v_top
+    ms_out[...] = jnp.broadcast_to(m_top, (half, HD)).T[0:1, :]
+    vs_out[...] = jnp.broadcast_to(v_top, (half, HD)).T[0:1, :]
     for odd in range(2):
         rows = pl.ds(odd, half, stride=2)
         mcode_ref[rows, :] = news[odd][0] / (m_top + 1e-06)
@@ -503,9 +508,9 @@
         out_shape=[
             jax.ShapeDtypeStruct(shape, F32),
             jax.ShapeDtypeStruct(shape, BF16),
-            jax.ShapeDtypeStruct(m_scale.shape, F32),
+            jax.ShapeDtypeStruct(m_scale.shape[::-1], F32),
             jax.ShapeDtypeStruct(shape, BF16),
-            jax.ShapeDtypeStruct(v_scale.shape, F32),
+            jax.ShapeDtypeStruct(v_scale.shape[::-1], F32),
         ],
         scratch_shapes=[pltpu.VMEM(shape, F32) for _ in range(6)],
         cost_estimate=cost(2),
@@ -519,34 +524,51 @@
     to = jnp.stack([place(me, r // 2, r % 2) for r in range(8)])
     origin = jnp.stack([place(me, (XS - r // 2) % XS, r % 2) for r in range(8)])
     around = jnp.stack([place(me, dx, dc) for dx in (0, 3, 1, 2) for dc in (0, 1)])
+    core = lax.rem(me, 2)
+    ahead = jnp.where(core == 0, XS - 1, 1)
     own = hidden[0]
-    half = own.shape[0] // 2
-    left, right = send(own, 1, 0), send(own, 3, 0)
+    first, second = turn(own, 1), turn(own, -1)
+    around = jnp.stack(
+        [
+            me,
+            place(me, 0, 1),
+            place(me, ahead, 0),
+            place(me, XS - ahead, 1),
+            place(me, XS - ahead, 0),
+            place(me, ahead, 1),
+            place(me, 2, 0),
+            place(me, 2, 1),
+        ]
+    )
     pairs = pack(to, query[0], grad_out[0], key[0])
-    pieces = exchange(pairs)
+    pieces = across(along(pairs))
     master_bf, _ = lax.optimization_barrier((master.astype(BF16), pairs[0]))
     copies = jnp.broadcast_to(master_bf[None], (n_y * n_z,) + master.shape)
     weight = lax.all_to_all(copies, ("y", "z"), split_axis=0, concat_axis=0, tiled=True)
     weight = weight.reshape(n_y * n_z * master.shape[0], HD)
-    far_lo, far_hi = send(left[:half], 1, 0), send(right[half:], 3, 0)
-    own_core, left_core, right_core = send(own, 0, 1), send(left, 0, 1), send(right, 0, 1)
+    far = turn(first, 1)
+    near = [own, send(own, 0, 1), first, send(first, 0, 1), second, send(second, 0, 1)]
     probs, grad_values = probs_call(doc_lens, origin, pieces)
-    near = [own, own_core, left, left_core, right, right_core]
-    near_values = values_call(near, weight)
-    far_lo, far_hi, grad_values, near_values = lax.optimization_barrier(
-        (far_lo, far_hi, grad_values, near_values)
-    )
-    far = [far_lo, far_hi, send(far_lo, 0, 1), send(far_hi, 0, 1)]
-    term = term_call(around, near + far, grad_values)
+    far, grad_values, weight, near[1], near[3], near[5] = lax.optimization_barrier(
+        (far, grad_values, weight, near[1], near[3], near[5])
+    )
+    hiddens = near + [far, send(far, 0, 1)]
+    term = term_call(around, hiddens, grad_values)
     parts = lax.all_to_all(
         term.reshape((n_y, n_z) + master.shape), "y", split_axis=0, concat_axis=0, tiled=True
     )
-    parts = lax.all_to_all(add_parts(parts), "z", split_axis=0, concat_axis=0, tiled=True)
-    far_values = values_call(far, weight)
-    grads = grads_call(origin, to, around, pieces, probs, near_values, far_values)
-    grad_query, grad_key = unpack(origin, exchange(grads))
-    state = adam_call(parts, master, m_code, m_scale, v_code, v_scale)
-    return (grad_query[None], grad_key[None]) + tuple(state)
+    summed = add_parts(parts)
+    parts = lax.all_to_all(summed, "z", split_axis=0, concat_axis=0, tiled=True)
+    values = values_call(hiddens, weight)
+    probs = pltpu.with_memory_space_constraint(probs, pltpu.HBM)
+    grads = along(grads_call(origin, to, around, pieces, probs, values))
+    grads[1], parts = lax.optimization_barrier((grads[1], parts))
+    grad_query, grad_key = unpack(origin, across(grads))
+    master, m_code, m_scale, v_code, v_scale = adam_call(
+        parts, master, m_code, m_scale, v_code, v_scale
+    )
+    state = (master, m_code, m_scale.T, v_code, v_scale.T)
+    return (grad_query[None], grad_key[None]) + state
 
 
 def solution(mesh):

time: 183 us -> 159 us (0.87)
  Pallas kernels: 65.4 us -> 37.8 us
  starting transfers between devices: 83.3 us -> 88.3 us
    pallas_call x3, Pallas kernels: 30.5 us -> 4.82 us  [the longest x2 3.1 us: merge(): pl.pallas_call(merge_kernel, in_specs=[ANYWHERE] * XS, out_specs=pl.Block...]
    ppermute x17 -> x12, starting transfers between devices: 55.5 us -> 42.7 us  [send(): return lax.ppermute(array, 'seq', pairs)]
    ppermute x17 -> x12, waiting for transfers between devices: 15.2 us -> 3.57 us  [send(): return lax.ppermute(array, 'seq', pairs)]
    ppermute x0 -> x3, starting transfers between devices: none -> 10.7 us  [turn(): return lax.ppermute(array, 'seq', pairs)]
    all_to_all x1, starting transfers between devices: 3.74 us -> 8.49 us  [shards(): lax.all_to_all(term.reshape((n_y, n_z) + master.shape), 'y', split_axis=0...]
    all_to_all x1, waiting for transfers between devices: 0.01 us -> 3.68 us  [shards(): lax.all_to_all(term.reshape((n_y, n_z) + master.shape), 'y', split_axis=0...]
    ppermute x0 -> x3, waiting for transfers between devices: none -> 3.58 us  [turn(): return lax.ppermute(array, 'seq', pairs)]
    all_to_all x1, waiting for transfers between devices: 4.65 us -> 7.76 us  [shards(): parts = lax.all_to_all(summed, 'z', split_axis=0, concat_axis=0, tiled=True)]
  transfers between devices with their start and end apart: 20 -> 18, of which waited for: 5 -> 5; matrix products, arithmetic and copies ran while one was open for 2% -> 1% of each run, Pallas kernels for 31% -> 17%
where the time goes in v6:
time: 159 us; the launch traced here: 158 us
  starting transfers between devices  88.3 us (56%)
  Pallas kernels  37.8 us (24%)
  waiting for transfers between devices  18.6 us (12%)
  local copies, waits for them, and re-layouts  11.7 us (7%)
    ppermute x12, starting transfers between devices, send(): return lax.ppermute(array, 'seq', pairs)  42.7 us
    all_to_all x1, starting transfers between devices, shards(): lax.all_to_all(copies, ('y', 'z'), split_axis=0, concat_axis=0, tiled=True)  16.3 us
    ppermute x3, starting transfers between devices, turn(): return lax.ppermute(array, 'seq', pairs)  10.7 us
    all_to_all x1, starting transfers between devices, shards(): parts = lax.all_to_all(summed, 'z', split_axis=0, concat_axis=0, tiled=True)  10 us
    unnamed x46, local copies, waits for them, and re-layouts  9.68 us
    pallas_call x1, Pallas kernels, grads_call(): pl.pallas_call(grads_kernel, grid=(BLOCKS // 2,), in_specs=[SCALARS, SCAL...  8.65 us
    all_to_all x1, starting transfers between devices, shards(): lax.all_to_all(term.reshape((n_y, n_z) + master.shape), 'y', split_axis=0...  8.49 us
    pallas_call x1, Pallas kernels, probs_call(): pl.pallas_call(probs_kernel, grid=(BLOCKS // 2,), in_specs=[SCALARS, SCAL...  8.23 us
  transfers between devices with their start and end apart: 18, of which 5 were waited for; matrix products, arithmetic and copies ran while one was open for 1% of the time, Pallas kernels for 17%

profile of v6, /device:TPU:1, one launch (start us, length us, event | category | flops | bytes accessed | tf_op | source)
XLA Modules:
  0.0 157.8 jit_solution(7492881328648429596)
XLA Ops:
  0.7 0.7 stack.68.to_ref
  1.4 3.3 %shard_map.153 = (bf16[2,128,1152]{2,1,0:T(8,128)(2,1)}, bf16[2,128,1152]{2,1,0:T(8,128)(2,1)}, bf16[2,128,1152]{2,1,0:T(8,128)(2,1)}, bf16[2,128,1152]{2,1,0:T(8,128)(2,1)}) custom-call(s32[8]{0:T(128)} %stack.68.to_ref, bf16[128,4096]{1,0:T(8,128)(2,1)} %bitcast.29, bf16[128,4096]{1,0:T(8,128)(2,1)} %bitcast.30, bf16[128,1024]{1,0:T(8,128)(2,1)} %bitcast.31), custom_call_target="tpu_custom_call" | custom-call | flops 3000000000 | bytes 3000000 | tf_op jit(solution)/shard_map/pallas_call | solution.py:99
  4.7 3.9 %collective-permute-start = (bf16[2,128,1152]{2,1,0:T(8,128)(2,1)}, bf16[2,128,1152]{2,1,0:T(8,128)(2,1)S(1)}, u32[]{:S(2)}, u32[]{:S(2)}) collective-permute-start(bf16[2,128,1152]{2,1,0:T(8,128)(2,1)} %get-tuple-element.34), channel_id=1, source_target_pairs={{0,128},{64,192},{128,256},{192,320},{256,384},{320,448},{384,0},{... | collective-permute-start | bytes 1769480 | tf_op jit(solution)/shard_map/ppermute | solution.py:57
  8.6 4.4 %collective-permute-start.1 = (bf16[2,128,1152]{2,1,0:T(8,128)(2,1)}, bf16[2,128,1152]{2,1,0:T(8,128)(2,1)S(1)}, u32[]{:S(2)}, u32[]{:S(2)}) collective-permute-start(bf16[2,128,1152]{2,1,0:T(8,128)(2,1)} %get-tuple-element.35), channel_id=1, source_target_pairs={{0,256},{64,320},{128,384},{192,448},{256,0},{320,64},{384,128},{4... | collective-permute-start | bytes 1769480 | tf_op jit(solution)/shard_map/ppermute | solution.py:57
  13.0 3.1 %collective-permute-start.2 = (bf16[2,128,1152]{2,1,0:T(8,128)(2,1)}, bf16[2,128,1152]{2,1,0:T(8,128)(2,1)}, u32[]{:S(2)}, u32[]{:S(2)}) collective-permute-start(bf16[2,128,1152]{2,1,0:T(8,128)(2,1)} %get-tuple-element.36), channel_id=1, source_target_pairs={{0,384},{64,448},{128,0},{192,64},{256,128},{320,192},{384,256},{4... | collective-permute-start | bytes 1769480 | tf_op jit(solution)/shard_map/ppermute | solution.py:57
  16.1 1.9 %collective-permute-start.4 = (bf16[128,4096]{1,0:T(8,128)(2,1)S(1)}, bf16[128,4096]{1,0:T(8,128)(2,1)}, u32[]{:S(2)}, u32[]{:S(2)}) collective-permute-start(bf16[128,4096]{1,0:T(8,128)(2,1)S(1)} %bitcast.24), channel_id=1, source_target_pairs={{0,128},{64,448},{128,256},{192,64},{256,384},{320,192},{384,0},{4... | collective-permute-start | bytes 3145736 | tf_op jit(solution)/shard_map/ppermute | solution.py:62
  18.0 3.4 %collective-permute-start.8 = (bf16[128,4096]{1,0:T(8,128)(2,1)S(1)}, bf16[128,4096]{1,0:T(8,128)(2,1)}, u32[]{:S(2)}, u32[]{:S(2)}) collective-permute-start(bf16[128,4096]{1,0:T(8,128)(2,1)S(1)} %bitcast.25), channel_id=1, source_target_pairs={{0,384},{64,192},{128,0},{192,320},{256,128},{320,448},{384,256},{... | collective-permute-start | bytes 3145736 | tf_op jit(solution)/shard_map/ppermute | solution.py:62
  21.4 1.2 broadcast_in_dim.12
  22.6 16.3 %all-to-all-start = ((bf16[64,64,128]{2,1,0:T(8,128)(2,1)}), bf16[64,64,128]{2,1,0:T(8,128)(2,1)S(1)}, u32[]{:S(2)}, u32[]{:S(2)}) async-start(bf16[64,64,128]{2,1,0:T(8,128)(2,1)} %broadcast_in_dim.12), calls=%async_computation | async-start | bytes 2097152 | tf_op jit(solution)/shard_map/all_to_all | solution.py:547
  39.0 0.0 copy-start.12
  39.0 0.0 collective-permute-done.1.refs_2_
  39.0 0.0 collective-permute-done.2.refs_3_
  39.0 1.1 copy-done.13
  40.1 2.2 %shard_map.154 = bf16[4,128,1152]{2,1,0:T(8,128)(2,1)} custom-call(bf16[2,128,1152]{2,1,0:T(8,128)(2,1)S(1)} %copy-done.13, bf16[2,128,1152]{2,1,0:T(8,128)(2,1)S(1)} %collective-permute-done.refs_1_, bf16[2,128,1152]{2,1,0:T(8,128)(2,1)S(1)} %collective-permute-done.1.refs_2_, bf16[2,128,1152]{2,1,0:T(8,128)(2,1)} %collective-permute-done.2.refs_3_), custom_call_target="tpu_custom_call" | custom-call | flops 1000000000 | bytes 1000000 | tf_op jit(solution)/shard_map/pallas_call | solution.py:118
  42.3 0.8 copy-done.4
  43.1 0.8 copy-done.7
  43.9 9.6 %collective-permute-start.3 = (bf16[4,128,1152]{2,1,0:T(8,128)(2,1)}, bf16[4,128,1152]{2,1,0:T(8,128)(2,1)S(1)}, u32[]{:S(2)}, u32[]{:S(2)}) collective-permute-start(bf16[4,128,1152]{2,1,0:T(8,128)(2,1)} %shard_map.154), channel_id=1, source_target_pairs={{0,64},{64,0},{128,192},{192,128},{256,320},{320,256},{384,448},{4... | collective-permute-start | bytes 3538952 | tf_op jit(solution)/shard_map/ppermute | solution.py:57
  53.5 1.9 %collective-permute-start.6 = (bf16[128,4096]{1,0:T(8,128)(2,1)S(1)}, bf16[128,4096]{1,0:T(8,128)(2,1)}, u32[]{:S(2)}, u32[]{:S(2)}) collective-permute-start(bf16[128,4096]{1,0:T(8,128)(2,1)S(1)} %bitcast.26), channel_id=1, source_target_pairs={{0,64},{64,0},{128,192},{192,128},{256,320},{320,256},{384,448},{4... | collective-permute-start | bytes 3145736 | tf_op jit(solution)/shard_map/ppermute | solution.py:57
  55.4 3.6 %collective-permute-done.4.refs_2_ = bf16[128,4096]{1,0:T(8,128)(2,1)} collective-permute-done((bf16[128,4096]{1,0:T(8,128)(2,1)S(1)}, bf16[128,4096]{1,0:T(8,128)(2,1)}, u32[]{:S(2)}, u32[]{:S(2)}) %collective-permute-start.4) | collective-permute-done | bytes 1048608 | tf_op jit(solution)/shard_map/ppermute | solution.py:62
  59.0 5.4 %collective-permute-start.5 = (bf16[128,4096]{1,0:T(8,128)(2,1)}, bf16[128,4096]{1,0:T(8,128)(2,1)}, u32[]{:S(2)}, u32[]{:S(2)}) collective-permute-start(bf16[128,4096]{1,0:T(8,128)(2,1)} %collective-permute-done.4.refs_2_), channel_id=1, source_target_pairs={{0,128},{64,448},{128,256},{192,64},{256,384},{320,192},{384,0},{4... | collective-permute-start | bytes 3145736 | tf_op jit(solution)/shard_map/ppermute | solution.py:62
  64.4 1.9 %collective-permute-start.7 = (bf16[128,4096]{1,0:T(8,128)(2,1)}, bf16[128,4096]{1,0:T(8,128)(2,1)}, u32[]{:S(2)}, u32[]{:S(2)}) collective-permute-start(bf16[128,4096]{1,0:T(8,128)(2,1)} %collective-permute-done.4.refs_2_), channel_id=1, source_target_pairs={{0,64},{64,0},{128,192},{192,128},{256,320},{320,256},{384,448},{4... | collective-permute-start | bytes 3145736 | tf_op jit(solution)/shard_map/ppermute | solution.py:57
  66.4 2.4 %collective-permute-start.9 = (bf16[128,4096]{1,0:T(8,128)(2,1)}, bf16[128,4096]{1,0:T(8,128)(2,1)}, u32[]{:S(2)}, u32[]{:S(2)}) collective-permute-start(bf16[128,4096]{1,0:T(8,128)(2,1)} %collective-permute-done.8.refs_4_), channel_id=1, source_target_pairs={{0,64},{64,0},{128,192},{192,128},{256,320},{320,256},{384,448},{4... | collective-permute-start | bytes 3145736 | tf_op jit(solution)/shard_map/ppermute | solution.py:57
  68.8 0.1 stack.67.from_ref
  68.9 0.0 collective-permute-done.3.refs_4_
  68.9 1.1 copy-done.5
  70.0 1.1 copy-done.8
  71.0 1.1 copy-done.14
  72.1 8.2 %shard_map.155 = (bf16[4,2,512,512]{3,2,1,0:T(8,128)(2,1)}, bf16[1024,128]{1,0:T(8,128)(2,1)S(1)}) custom-call(s32[1,8]{1,0:T(1,128)S(1)} %copy-done.12, s32[8]{0:T(128)S(1)} %stack.67.from_ref, bf16[2,128,1152]{2,1,0:T(8,128)(2,1)S(1)} %copy-done.14, bf16[2,128,1152]{2,1,0:T(8,128)(2,1)S(1)} %copy-done.5, bf16[2,128,1152]{2,1,0:T(8,128)(2,1)S(1)} %copy-done.8, ...), custom_call_target="tpu_custom_call" | custom-call | flops 8000000000 | bytes 8000000 | tf_op jit(solution)/shard_map/pallas_call | solution.py:234
  80.3 0.0 copy-start.18
  80.3 0.7 copy-done.18
  81.0 0.0 collective-permute-done.6.refs_1_
  81.0 0.0 all-to-all-done
  81.0 0.0 collective-permute-done.5.refs_6_
  81.1 0.0 collective-permute-done.9.refs_5_
  81.1 1.9 %collective-permute-start.10 = (bf16[128,4096]{1,0:T(8,128)(2,1)}, bf16[128,4096]{1,0:T(8,128)(2,1)}, u32[]{:S(2)}, u32[]{:S(2)}) collective-permute-start(bf16[128,4096]{1,0:T(8,128)(2,1)} %collective-permute-done.5.refs_6_), channel_id=1, source_target_pairs={{0,64},{64,0},{128,192},{192,128},{256,320},{320,256},{384,448},{4... | collective-permute-start | bytes 3145736 | tf_op jit(solution)/shard_map/ppermute | solution.py:57
  83.0 0.1 stack.74.around_ref.from_ref
  83.1 2.8 %collective-permute-done.10.refs_7_ = bf16[128,4096]{1,0:T(8,128)(2,1)} collective-permute-done((bf16[128,4096]{1,0:T(8,128)(2,1)}, bf16[128,4096]{1,0:T(8,128)(2,1)}, u32[]{:S(2)}, u32[]{:S(2)}) %collective-permute-start.10) | collective-permute-done | bytes 1048608 | tf_op jit(solution)/shard_map/ppermute | solution.py:57
  86.0 0.9 copy-done.19
  86.9 5.8 %shard_map.158 = bf16[4096,128]{1,0:T(8,128)(2,1)} custom-call(s32[8]{0:T(128)S(1)} %stack.74.around_ref.from_ref, bf16[128,4096]{1,0:T(8,128)(2,1)S(1)} %bitcast.27, bf16[128,4096]{1,0:T(8,128)(2,1)} %collective-permute-done.6.refs_1_, bf16[128,4096]{1,0:T(8,128)(2,1)} %collective-permute-done.4.refs_2_, bf16[128,4096]{1,0:T(8,128)(2,1)} %collective-permute-done.7.refs_3_, ...), custom_call_target="tpu_custom_call" | custom-call | flops 5000000000 | bytes 5000000 | tf_op jit(solution)/shard_map/pallas_call | solution.py:293
  92.7 8.5 %all-to-all-start.1 = ((bf16[8,8,64,128]{3,2,1,0:T(8,128)(2,1)}), bf16[8,8,64,128]{3,2,1,0:T(8,128)(2,1)S(1)}, u32[]{:S(2)}, u32[]{:S(2)}) async-start(bf16[8,8,64,128]{3,2,1,0:T(8,128)(2,1)} %bitcast.18), calls=%async_computation.1 | async-start | bytes 2097152 | tf_op jit(solution)/shard_map/all_to_all | solution.py:557
  101.2 1.2 copy-done.3
  102.4 5.5 %shard_map.156.refs_6_ = bf16[1024,128]{1,0:T(8,128)(2,1)S(1)} custom-call(bf16[128,4096]{1,0:T(8,128)(2,1)S(1)} %bitcast.28, bf16[128,4096]{1,0:T(8,128)(2,1)} %collective-permute-done.6.refs_1_, bf16[128,4096]{1,0:T(8,128)(2,1)} %collective-permute-done.4.refs_2_, bf16[128,4096]{1,0:T(8,128)(2,1)} %collective-permute-done.7.refs_3_, ...), custom_call_target="tpu_custom_call" | custom-call | flops 6000000000 | bytes 6000000 | tf_op jit(solution)/shard_map/pallas_call | solution.py:309
  107.9 8.6 %shard_map.157 = (bf16[2,128,640]{2,1,0:T(8,128)(2,1)S(1)}, bf16[2,128,640]{2,1,0:T(8,128)(2,1)}, bf16[2,128,640]{2,1,0:T(8,128)(2,1)S(1)}, bf16[2,128,640]{2,1,0:T(8,128)(2,1)S(1)}) custom-call(s32[8]{0:T(128)S(1)} %stack.67.from_ref, s32[8]{0:T(128)S(1)} %copy-done.1, s32[8]{0:T(128)S(1)} %stack.74.around_ref.from_ref, ...), custom_call_target="tpu_custom_call" | custom-call | flops 8999999488 | bytes 9000000 | tf_op jit(solution)/shard_map/pallas_call | solution.py:377
  116.6 0.7 copy-done.16
  117.3 1.9 %collective-permute-start.11 = (bf16[2,128,640]{2,1,0:T(8,128)(2,1)}, bf16[2,128,640]{2,1,0:T(8,128)(2,1)S(1)}, u32[]{:S(2)}, u32[]{:S(2)}) collective-permute-start(bf16[2,128,640]{2,1,0:T(8,128)(2,1)} %get-tuple-element.46), channel_id=1, source_target_pairs={{0,128},{64,192},{128,256},{192,320},{256,384},{320,448},{384,0},{... | collective-permute-start | bytes 983048 | tf_op jit(solution)/shard_map/ppermute | solution.py:57
  119.2 3.5 %collective-permute-start.12 = (bf16[2,128,640]{2,1,0:T(8,128)(2,1)S(1)}, bf16[2,128,640]{2,1,0:T(8,128)(2,1)S(1)}, u32[]{:S(2)}, u32[]{:S(2)}) collective-permute-start(bf16[2,128,640]{2,1,0:T(8,128)(2,1)S(1)} %get-tuple-element.49), channel_id=1, source_target_pairs={{0,256},{64,320},{128,384},{192,448},{256,0},{320,64},{384,128},{4... | collective-permute-start | bytes 983048 | tf_op jit(solution)/shard_map/ppermute | solution.py:57
  122.7 4.1 %collective-permute-start.13 = (bf16[2,128,640]{2,1,0:T(8,128)(2,1)S(1)}, bf16[2,128,640]{2,1,0:T(8,128)(2,1)S(1)}, u32[]{:S(2)}, u32[]{:S(2)}) collective-permute-start(bf16[2,128,640]{2,1,0:T(8,128)(2,1)S(1)} %get-tuple-element.50), channel_id=1, source_target_pairs={{0,384},{64,448},{128,0},{192,64},{256,128},{320,192},{384,256},{4... | collective-permute-start | bytes 983048 | tf_op jit(solution)/shard_map/ppermute | solution.py:57
  126.8 3.7 %all-to-all-done.1.parts_ref = bf16[8,8,64,128]{3,2,1,0:T(8,128)(2,1)S(1)} async-done(((bf16[8,8,64,128]{3,2,1,0:T(8,128)(2,1)}), bf16[8,8,64,128]{3,2,1,0:T(8,128)(2,1)S(1)}, u32[]{:S(2)}, u32[]{:S(2)}) %all-to-all-start.1) | async-done | bytes 1048608 | tf_op jit(solution)/shard_map/all_to_all | solution.py:557
  130.4 0.8 shard_map.159
  131.2 10.0 %all-to-all-start.2 = ((bf16[8,64,128]{2,1,0:T(8,128)(2,1)}), bf16[8,64,128]{2,1,0:T(8,128)(2,1)S(1)}, u32[]{:S(2)}, u32[]{:S(2)}) async-start(bf16[8,64,128]{2,1,0:T(8,128)(2,1)} %shard_map.159), calls=%async_computation.2 | async-start | bytes 262144 | tf_op jit(solution)/shard_map/all_to_all | solution.py:561
  141.3 0.0 collective-permute-done.11.refs_1_
  141.3 7.8 %all-to-all-done.2.parts_ref = bf16[8,64,128]{2,1,0:T(8,128)(2,1)S(1)} async-done(((bf16[8,64,128]{2,1,0:T(8,128)(2,1)}), bf16[8,64,128]{2,1,0:T(8,128)(2,1)S(1)}, u32[]{:S(2)}, u32[]{:S(2)}) %all-to-all-start.2) | async-done | bytes 131104 | tf_op jit(solution)/shard_map/all_to_all | solution.py:561
  149.0 0.0 collective-permute-done.12.refs_2_
  149.1 0.0 copy-start.20
  149.1 0.0 copy-start.21
  149.1 0.0 copy-start.10
  149.1 0.0 copy-start.11
  149.1 0.9 shard_map.160
  150.0 4.2 %collective-permute-start.14 = (bf16[4,128,640]{2,1,0:T(8,128)(2,1)S(1)}, bf16[4,128,640]{2,1,0:T(8,128)(2,1)S(1)}, u32[]{:S(2)}, u32[]{:S(2)}) collective-permute-start(bf16[4,128,640]{2,1,0:T(8,128)(2,1)S(1)} %shard_map.160), channel_id=1, source_target_pairs={{0,64},{64,0},{128,192},{192,128},{256,320},{320,256},{384,448},{4... | collective-permute-start | bytes 1966088 | tf_op jit(solution)/shard_map/ppermute | solution.py:57
  154.2 0.1 copy.17.ms_ref
  154.3 0.1 copy.18.vs_ref
  154.4 0.8 shard_map.162
  155.2 0.7 collective-permute-done.14.refs_4_
  155.9 1.7 %shard_map.161 = (bf16[128,4096]{1,0:T(8,128)(2,1)}, bf16[128,1024]{1,0:T(8,128)(2,1)}) custom-call(s32[8]{0:T(128)S(1)} %stack.67.from_ref, bf16[2,128,640]{2,1,0:T(8,128)(2,1)S(1)} %copy-done.17, bf16[2,128,640]{2,1,0:T(8,128)(2,1)S(1)} %collective-permute-done.11.refs_1_, bf16[2,128,640]{2,1,0:T(8,128)(2,1)S(1)} %collective-permute-done.12.refs_2_, ...), custom_call_target="tpu_custom_call" | custom-call | flops 2000000000 | bytes 2000000 | tf_op jit(solution)/shard_map/pallas_call | solution.py:419
  (33 shorter events, 0.1 us)
Async XLA Ops:
  1.4 14.7 %copy-start.2 = (bf16[1,128,4096]{2,1,0:T(8,128)(2,1)S(1)}, bf16[1,128,4096]{2,1,0:T(8,128)(2,1)}, u32[]{:S(2)}) copy-start(bf16[1,128,4096]{2,1,0:T(8,128)(2,1)} %param.10) | copy-start | bytes 3145732
  1.4 20.0 %copy-start = (f32[64,128]{1,0:T(8,128)S(1)}, f32[64,128]{1,0:T(8,128)}, u32[]{:S(2)}) copy-start(f32[64,128]{1,0:T(8,128)} %master_ref.1) | copy-start | bytes 98308
  4.7 34.3 %collective-permute-start = (bf16[2,128,1152]{2,1,0:T(8,128)(2,1)}, bf16[2,128,1152]{2,1,0:T(8,128)(2,1)S(1)}, u32[]{:S(2)}, u32[]{:S(2)}) collective-permute-start(bf16[2,128,1152]{2,1,0:T(8,128)(2,1)} %get-tuple-element.34), channel_id=1, source_target_pairs={{0,128},{64,192},{128,256},{192,320},{256,384},{320,448},{384,0},{... | collective-permute-start | bytes 1769480 | tf_op jit(solution)/shard_map/ppermute | solution.py:57
  8.6 30.3 %collective-permute-start.1 = (bf16[2,128,1152]{2,1,0:T(8,128)(2,1)}, bf16[2,128,1152]{2,1,0:T(8,128)(2,1)S(1)}, u32[]{:S(2)}, u32[]{:S(2)}) collective-permute-start(bf16[2,128,1152]{2,1,0:T(8,128)(2,1)} %get-tuple-element.35), channel_id=1, source_target_pairs={{0,256},{64,320},{128,384},{192,448},{256,0},{320,64},{384,128},{4... | collective-permute-start | bytes 1769480 | tf_op jit(solution)/shard_map/ppermute | solution.py:57
  13.0 26.0 %collective-permute-start.2 = (bf16[2,128,1152]{2,1,0:T(8,128)(2,1)}, bf16[2,128,1152]{2,1,0:T(8,128)(2,1)}, u32[]{:S(2)}, u32[]{:S(2)}) collective-permute-start(bf16[2,128,1152]{2,1,0:T(8,128)(2,1)} %get-tuple-element.36), channel_id=1, source_target_pairs={{0,384},{64,448},{128,0},{192,64},{256,128},{320,192},{384,256},{4... | collective-permute-start | bytes 1769480 | tf_op jit(solution)/shard_map/ppermute | solution.py:57
  16.1 42.9 %collective-permute-start.4 = (bf16[128,4096]{1,0:T(8,128)(2,1)S(1)}, bf16[128,4096]{1,0:T(8,128)(2,1)}, u32[]{:S(2)}, u32[]{:S(2)}) collective-permute-start(bf16[128,4096]{1,0:T(8,128)(2,1)S(1)} %bitcast.24), channel_id=1, source_target_pairs={{0,128},{64,448},{128,256},{192,64},{256,384},{320,192},{384,0},{4... | collective-permute-start | bytes 3145736 | tf_op jit(solution)/shard_map/ppermute | solution.py:62
  18.0 48.3 %collective-permute-start.8 = (bf16[128,4096]{1,0:T(8,128)(2,1)S(1)}, bf16[128,4096]{1,0:T(8,128)(2,1)}, u32[]{:S(2)}, u32[]{:S(2)}) collective-permute-start(bf16[128,4096]{1,0:T(8,128)(2,1)S(1)} %bitcast.25), channel_id=1, source_target_pairs={{0,384},{64,192},{128,0},{192,320},{256,128},{320,448},{384,256},{... | collective-permute-start | bytes 3145736 | tf_op jit(solution)/shard_map/ppermute | solution.py:62
  22.6 58.4 %all-to-all-start = ((bf16[64,64,128]{2,1,0:T(8,128)(2,1)}), bf16[64,64,128]{2,1,0:T(8,128)(2,1)S(1)}, u32[]{:S(2)}, u32[]{:S(2)}) async-start(bf16[64,64,128]{2,1,0:T(8,128)(2,1)} %broadcast_in_dim.12), calls=%async_computation | async-start | bytes 2097152 | tf_op jit(solution)/shard_map/all_to_all | solution.py:547
  39.0 29.9 %copy-start.12 = (s32[1,8]{1,0:T(1,128)S(1)}, s32[1,8]{1,0:T(1,128)}, u32[]{:S(2)}) copy-start(s32[1,8]{1,0:T(1,128)} %lens_ref.1) | copy-start | bytes 100
  39.0 1.1 copy-start.13
  42.3 0.8 copy-start.4
  43.1 0.8 copy-start.7
  43.9 24.9 %collective-permute-start.3 = (bf16[4,128,1152]{2,1,0:T(8,128)(2,1)}, bf16[4,128,1152]{2,1,0:T(8,128)(2,1)S(1)}, u32[]{:S(2)}, u32[]{:S(2)}) collective-permute-start(bf16[4,128,1152]{2,1,0:T(8,128)(2,1)} %shard_map.154), channel_id=1, source_target_pairs={{0,64},{64,0},{128,192},{192,128},{256,320},{320,256},{384,448},{4... | collective-permute-start | bytes 3538952 | tf_op jit(solution)/shard_map/ppermute | solution.py:57
  53.5 27.5 %collective-permute-start.6 = (bf16[128,4096]{1,0:T(8,128)(2,1)S(1)}, bf16[128,4096]{1,0:T(8,128)(2,1)}, u32[]{:S(2)}, u32[]{:S(2)}) collective-permute-start(bf16[128,4096]{1,0:T(8,128)(2,1)S(1)} %bitcast.26), channel_id=1, source_target_pairs={{0,64},{64,0},{128,192},{192,128},{256,320},{320,256},{384,448},{4... | collective-permute-start | bytes 3145736 | tf_op jit(solution)/shard_map/ppermute | solution.py:57
  59.0 22.0 %collective-permute-start.5 = (bf16[128,4096]{1,0:T(8,128)(2,1)}, bf16[128,4096]{1,0:T(8,128)(2,1)}, u32[]{:S(2)}, u32[]{:S(2)}) collective-permute-start(bf16[128,4096]{1,0:T(8,128)(2,1)} %collective-permute-done.4.refs_2_), channel_id=1, source_target_pairs={{0,128},{64,448},{128,256},{192,64},{256,384},{320,192},{384,0},{4... | collective-permute-start | bytes 3145736 | tf_op jit(solution)/shard_map/ppermute | solution.py:62
  64.4 16.6 %collective-permute-start.7 = (bf16[128,4096]{1,0:T(8,128)(2,1)}, bf16[128,4096]{1,0:T(8,128)(2,1)}, u32[]{:S(2)}, u32[]{:S(2)}) collective-permute-start(bf16[128,4096]{1,0:T(8,128)(2,1)} %collective-permute-done.4.refs_2_), channel_id=1, source_target_pairs={{0,64},{64,0},{128,192},{192,128},{256,320},{320,256},{384,448},{4... | collective-permute-start | bytes 3145736 | tf_op jit(solution)/shard_map/ppermute | solution.py:57
  66.4 14.7 %collective-permute-start.9 = (bf16[128,4096]{1,0:T(8,128)(2,1)}, bf16[128,4096]{1,0:T(8,128)(2,1)}, u32[]{:S(2)}, u32[]{:S(2)}) collective-permute-start(bf16[128,4096]{1,0:T(8,128)(2,1)} %collective-permute-done.8.refs_4_), channel_id=1, source_target_pairs={{0,64},{64,0},{128,192},{192,128},{256,320},{320,256},{384,448},{4... | collective-permute-start | bytes 3145736 | tf_op jit(solution)/shard_map/ppermute | solution.py:57
  68.9 1.1 copy-start.5
  70.0 1.1 copy-start.8
  71.0 1.1 copy-start.14
  80.3 0.7 copy-start.18
  81.1 4.9 %collective-permute-start.10 = (bf16[128,4096]{1,0:T(8,128)(2,1)}, bf16[128,4096]{1,0:T(8,128)(2,1)}, u32[]{:S(2)}, u32[]{:S(2)}) collective-permute-start(bf16[128,4096]{1,0:T(8,128)(2,1)} %collective-permute-done.5.refs_6_), channel_id=1, source_target_pairs={{0,64},{64,0},{128,192},{192,128},{256,320},{320,256},{384,448},{4... | collective-permute-start | bytes 3145736 | tf_op jit(solution)/shard_map/ppermute | solution.py:57
  86.0 1.0 copy-start.19
  92.7 37.8 %all-to-all-start.1 = ((bf16[8,8,64,128]{3,2,1,0:T(8,128)(2,1)}), bf16[8,8,64,128]{3,2,1,0:T(8,128)(2,1)S(1)}, u32[]{:S(2)}, u32[]{:S(2)}) async-start(bf16[8,8,64,128]{3,2,1,0:T(8,128)(2,1)} %bitcast.18), calls=%async_computation.1 | async-start | bytes 2097152 | tf_op jit(solution)/shard_map/all_to_all | solution.py:557
  101.2 1.2 copy-start.3
  102.4 5.5 %copy-start.1 = (s32[8]{0:T(128)S(1)}, s32[8]{0:T(128)}, u32[]{:S(2)}) copy-start(s32[8]{0:T(128)} %stack.68.to_ref) | copy-start | bytes 100
  102.4 5.5 %copy-start.6 = (bf16[2,128,1152]{2,1,0:T(8,128)(2,1)S(1)}, bf16[2,128,1152]{2,1,0:T(8,128)(2,1)}, u32[]{:S(2)}) copy-start(bf16[2,128,1152]{2,1,0:T(8,128)(2,1)} %copy-done.4) | copy-start | bytes 1769476
  102.4 5.5 %copy-start.9 = (bf16[2,128,1152]{2,1,0:T(8,128)(2,1)S(1)}, bf16[2,128,1152]{2,1,0:T(8,128)(2,1)}, u32[]{:S(2)}) copy-start(bf16[2,128,1152]{2,1,0:T(8,128)(2,1)} %copy-done.7) | copy-start | bytes 1769476
  102.4 5.5 %copy-start.15 = (bf16[2,128,1152]{2,1,0:T(8,128)(2,1)S(1)}, bf16[2,128,1152]{2,1,0:T(8,128)(2,1)}, u32[]{:S(2)}) copy-start(bf16[2,128,1152]{2,1,0:T(8,128)(2,1)} %get-tuple-element.33.refs_0_) | copy-start | bytes 1769476
  116.6 0.7 copy-start.16
  117.3 24.0 %collective-permute-start.11 = (bf16[2,128,640]{2,1,0:T(8,128)(2,1)}, bf16[2,128,640]{2,1,0:T(8,128)(2,1)S(1)}, u32[]{:S(2)}, u32[]{:S(2)}) collective-permute-start(bf16[2,128,640]{2,1,0:T(8,128)(2,1)} %get-tuple-element.46), channel_id=1, source_target_pairs={{0,128},{64,192},{128,256},{192,320},{256,384},{320,448},{384,0},{... | collective-permute-start | bytes 983048 | tf_op jit(solution)/shard_map/ppermute | solution.py:57
  119.2 29.9 %collective-permute-start.12 = (bf16[2,128,640]{2,1,0:T(8,128)(2,1)S(1)}, bf16[2,128,640]{2,1,0:T(8,128)(2,1)S(1)}, u32[]{:S(2)}, u32[]{:S(2)}) collective-permute-start(bf16[2,128,640]{2,1,0:T(8,128)(2,1)S(1)} %get-tuple-element.49), channel_id=1, source_target_pairs={{0,256},{64,320},{128,384},{192,448},{256,0},{320,64},{384,128},{4... | collective-permute-start | bytes 983048 | tf_op jit(solution)/shard_map/ppermute | solution.py:57
  122.6 26.4 %copy-start.17 = (bf16[2,128,640]{2,1,0:T(8,128)(2,1)S(1)}, bf16[2,128,640]{2,1,0:T(8,128)(2,1)}, u32[]{:S(2)}) copy-start(bf16[2,128,640]{2,1,0:T(8,128)(2,1)} %copy-done.16) | copy-start | bytes 983044
  122.7 26.4 %collective-permute-start.13 = (bf16[2,128,640]{2,1,0:T(8,128)(2,1)S(1)}, bf16[2,128,640]{2,1,0:T(8,128)(2,1)S(1)}, u32[]{:S(2)}, u32[]{:S(2)}) collective-permute-start(bf16[2,128,640]{2,1,0:T(8,128)(2,1)S(1)} %get-tuple-element.50), channel_id=1, source_target_pairs={{0,384},{64,448},{128,0},{192,64},{256,128},{320,192},{384,256},{4... | collective-permute-start | bytes 983048 | tf_op jit(solution)/shard_map/ppermute | solution.py:57
  131.2 17.8 %all-to-all-start.2 = ((bf16[8,64,128]{2,1,0:T(8,128)(2,1)}), bf16[8,64,128]{2,1,0:T(8,128)(2,1)S(1)}, u32[]{:S(2)}, u32[]{:S(2)}) async-start(bf16[8,64,128]{2,1,0:T(8,128)(2,1)} %shard_map.159), calls=%async_computation.2 | async-start | bytes 262144 | tf_op jit(solution)/shard_map/all_to_all | solution.py:561
  149.1 5.1 %copy-start.20 = (f32[32,1]{0,1:T(1,128)S(1)}, f32[32,1]{0,1:T(1,128)}, u32[]{:S(2)}) copy-start(f32[32,1]{0,1:T(1,128)} %param.17) | copy-start | bytes 388
  149.1 5.2 %copy-start.21 = (f32[32,1]{0,1:T(1,128)S(1)}, f32[32,1]{0,1:T(1,128)}, u32[]{:S(2)}) copy-start(f32[32,1]{0,1:T(1,128)} %param.19) | copy-start | bytes 388
  149.1 5.3 %copy-start.10 = (bf16[64,128]{1,0:T(8,128)(2,1)S(1)}, bf16[64,128]{1,0:T(8,128)(2,1)}, u32[]{:S(2)}) copy-start(bf16[64,128]{1,0:T(8,128)(2,1)} %mc_ref.1) | copy-start | bytes 49156
  149.1 5.3 %copy-start.11 = (bf16[64,128]{1,0:T(8,128)(2,1)S(1)}, bf16[64,128]{1,0:T(8,128)(2,1)}, u32[]{:S(2)}) copy-start(bf16[64,128]{1,0:T(8,128)(2,1)} %vc_ref.1) | copy-start | bytes 49156
  150.0 5.9 %collective-permute-start.14 = (bf16[4,128,640]{2,1,0:T(8,128)(2,1)S(1)}, bf16[4,128,640]{2,1,0:T(8,128)(2,1)S(1)}, u32[]{:S(2)}, u32[]{:S(2)}) collective-permute-start(bf16[4,128,640]{2,1,0:T(8,128)(2,1)S(1)} %shard_map.160), channel_id=1, source_target_pairs={{0,64},{64,0},{128,192},{192,128},{256,320},{320,256},{384,448},{4... | collective-permute-start | bytes 1966088 | tf_op jit(solution)/shard_map/ppermute | solution.py:57

commit v7 on v6

--- a/solution.py
+++ b/solution.py
@@ -60,6 +60,10 @@
 def turn(array, dx):
     pairs = [(s, ((s // 2 + (dx if s % 2 == 0 else -dx)) % XS) * 2 + s % 2) for s in range(2 * XS)]
     return lax.ppermute(array, "seq", pairs)
+
+
+def in_hbm(array):
+    return pltpu.with_memory_space_constraint(array, pltpu.HBM)
 
 
 ANYWHERE = pl.BlockSpec(memory_space=pl.ANY)
@@ -100,7 +104,7 @@
         pack_kernel,
         in_specs=[SCALARS] + [pl.BlockSpec(memory_space=pltpu.VMEM)] * 3,
         out_specs=[ANYWHERE] * XS,
-        out_shape=[jax.ShapeDtypeStruct((2, tokens, 2 * QW + HD), BF16)] * XS,
+        out_shape=[pltpu.HBM((2, tokens, 2 * QW + HD), BF16)] * XS,
         scratch_shapes=[pltpu.SemaphoreType.DMA((24,))],
         cost_estimate=cost(3),
         compiler_params=params(60),
@@ -238,7 +242,7 @@
         out_specs=[PROBS_SPEC, pl.BlockSpec((SEQ, HD), lambda i: (0, 0))],
         out_shape=[
             pltpu.HBM(PROBS_SHAPE, BF16),
-            jax.ShapeDtypeStruct((SEQ, HD), BF16),
+            pltpu.HBM((SEQ, HD), BF16),
         ],
         scratch_shapes=[
             pltpu.VMEM((SEQ, width), BF16),
@@ -254,8 +258,8 @@
     return jnp.concatenate([ref[...] for ref in refs], axis=0)
 
 
-def term_kernel(from_ref, *refs):
-    hidden_refs, (gv_ref, term_ref, gvt_ref) = refs[:8], refs[8:]
+def term_kernel(from_ref, low_ref, *refs):
+    hidden_refs, (gv_ref, keep_ref, give_ref, gvt_ref) = refs[:8], refs[8:]
 
     @pl.when(pl.program_id(0) == 0)
     def _():
@@ -264,7 +268,11 @@
             gvt_ref[:, r * ROWS : (r + 1) * ROWS] = gv_ref[rows, :].T
 
     term = dot(gvt_ref[...], join(hidden_refs))
-    term_ref[...] = (term.T * INV_WIDTH).astype(BF16)
+    term = (term.T * INV_WIDTH).astype(BF16)
+    term = term.reshape(keep_ref.shape[0], -1, keep_ref.shape[1], HD)
+    even, odd = term[:, 0], term[:, -1]
+    keep_ref[...] = jnp.where(low_ref[0] == 0, even, odd)
+    give_ref[...] = jnp.where(low_ref[0] == 0, odd, even)
 
 
 def values_kernel(*refs):
@@ -289,19 +297,22 @@
     return [pl.BlockSpec((piece.shape[0], STRIPE), lambda j: (0, j)) for piece in pieces]
 
 
-def term_call(origin, pieces, grad_values):
+def term_call(origin, low, pieces, grad_values, rows, pairing):
+    count = D // rows // pairing
+    step = count * STRIPE // D
+    block = pl.BlockSpec((step, rows, HD), lambda j: (j, 0, 0))
     return pl.pallas_call(
         term_kernel,
         grid=(D // STRIPE,),
-        in_specs=[SCALARS]
+        in_specs=[SCALARS, SCALARS]
         + hidden_specs(pieces)
         + [pl.BlockSpec((SEQ, HD), lambda j: (0, 0))],
-        out_specs=pl.BlockSpec((STRIPE, HD), lambda j: (j, 0)),
-        out_shape=jax.ShapeDtypeStruct((D, HD), BF16),
+        out_specs=[block, block],
+        out_shape=[pltpu.HBM((count, rows, HD), BF16)] * 2,
         scratch_shapes=[pltpu.VMEM((HD, SEQ), BF16)],
         cost_estimate=cost(5),
         compiler_params=params(),
-    )(origin, *pieces, grad_values)
+    )(origin, low, *pieces, grad_values)
 
 
 def values_call(pieces, weight):
@@ -384,7 +395,7 @@
             pl.BlockSpec((SEQ, HD), lambda i: (0, 0)),
         ],
         out_specs=[ANYWHERE] * XS,
-        out_shape=[jax.ShapeDtypeStruct((2, ROWS, QW + HD), BF16)] * XS,
+        out_shape=[pltpu.HBM((2, ROWS, QW + HD), BF16)] * XS,
         scratch_shapes=[
             pltpu.VMEM((SEQ, width), BF16),
             pltpu.VMEM((SEQ, HD), BF16),
@@ -430,20 +441,21 @@
     )(origin, *pieces)
 
 
-def add_kernel(parts_ref, out_ref):
-    total = parts_ref[0].astype(F32)
-    for g in range(1, parts_ref.shape[0]):
-        total = total + parts_ref[g].astype(F32)
-    out_ref[...] = total.astype(BF16)
-
-
-def add_parts(parts):
+def add_kernel(one_ref, two_ref, out_ref):
+    out_ref[...] = (one_ref[...].astype(F32) + two_ref[...].astype(F32)).astype(BF16)
+
+
+def add_pair(one, two):
     return pl.pallas_call(
         add_kernel,
-        out_shape=jax.ShapeDtypeStruct(parts.shape[1:], BF16),
+        out_shape=jax.ShapeDtypeStruct(one.shape, BF16),
         cost_estimate=cost(1),
         compiler_params=params(8),
-    )(parts)
+    )(one, two)
+
+
+def swap_low(array):
+    return lax.ppermute(array, "zl", [(0, 1), (1, 0)])
 
 
 def adam_kernel(
@@ -519,14 +531,16 @@
 
 
 def shards(hidden, query, key, grad_out, doc_lens, master, m_code, m_scale, v_code, v_scale):
-    n_y, n_z = lax.axis_size("y"), lax.axis_size("z")
+    n_far = lax.axis_size("y") * lax.axis_size("zh")
+    low = lax.axis_index("zl")
+    rows = master.shape[0]
     me = lax.axis_index("seq")
     to = jnp.stack([place(me, r // 2, r % 2) for r in range(8)])
     origin = jnp.stack([place(me, (XS - r // 2) % XS, r % 2) for r in range(8)])
     around = jnp.stack([place(me, dx, dc) for dx in (0, 3, 1, 2) for dc in (0, 1)])
     core = lax.rem(me, 2)
     ahead = jnp.where(core == 0, XS - 1, 1)
-    own = hidden[0]
+    own = in_hbm(hidden[0])
     first, second = turn(own, 1), turn(own, -1)
     around = jnp.stack(
         [
@@ -542,27 +556,31 @@
     )
     pairs = pack(to, query[0], grad_out[0], key[0])
     pieces = across(along(pairs))
-    master_bf, _ = lax.optimization_barrier((master.astype(BF16), pairs[0]))
-    copies = jnp.broadcast_to(master_bf[None], (n_y * n_z,) + master.shape)
-    weight = lax.all_to_all(copies, ("y", "z"), split_axis=0, concat_axis=0, tiled=True)
-    weight = weight.reshape(n_y * n_z * master.shape[0], HD)
+    mine = master.astype(BF16)
+    theirs = swap_low(mine)
+    both = jnp.where(low == 0, jnp.stack([mine, theirs]), jnp.stack([theirs, mine]))
+    both, _ = lax.optimization_barrier((both, pairs[0]))
+    copies = jnp.broadcast_to(both[None], (n_far,) + both.shape)
+    weight = lax.all_to_all(copies, ("y", "zh"), split_axis=0, concat_axis=0, tiled=True)
+    weight = weight.reshape(D, HD)
     far = turn(first, 1)
     near = [own, send(own, 0, 1), first, send(first, 0, 1), second, send(second, 0, 1)]
+    pieces = [in_hbm(piece) for piece in pieces[:XS]] + pieces[XS:]
     probs, grad_values = probs_call(doc_lens, origin, pieces)
     far, grad_values, weight, near[1], near[3], near[5] = lax.optimization_barrier(
         (far, grad_values, weight, near[1], near[3], near[5])
     )
     hiddens = near + [far, send(far, 0, 1)]
-    term = term_call(around, hiddens, grad_values)
+    keep, give = term_call(around, low[None], hiddens, in_hbm(grad_values), rows, 2)
+    other = swap_low(give)
+    values = values_call(hiddens, weight)
+    probs = in_hbm(probs)
+    grads = list(grads_call(origin, to, around, pieces, probs, values))
+    other, keep, grads[1] = lax.optimization_barrier((other, keep, grads[1]))
+    grads = along(grads)
     parts = lax.all_to_all(
-        term.reshape((n_y, n_z) + master.shape), "y", split_axis=0, concat_axis=0, tiled=True
-    )
-    summed = add_parts(parts)
-    parts = lax.all_to_all(summed, "z", split_axis=0, concat_axis=0, tiled=True)
-    values = values_call(hiddens, weight)
-    probs = pltpu.with_memory_space_constraint(probs, pltpu.HBM)
-    grads = along(grads_call(origin, to, around, pieces, probs, values))
-    grads[1], parts = lax.optimization_barrier((grads[1], parts))
+        add_pair(keep, other), ("y", "zh"), split_axis=0, concat_axis=0, tiled=True
+    )
     grad_query, grad_key = unpack(origin, across(grads))
     master, m_code, m_scale, v_code, v_scale = adam_call(
         parts, master, m_code, m_scale, v_code, v_scale
@@ -572,13 +590,12 @@
 
 
 def solution(mesh):
-    tokens, state = P(("y", "z"), "seq", None), P(("y", "z"), "seq")
-    rows = math.gcd(8, mesh.shape["dp"])
-    cut = mesh.devices.reshape(mesh.shape["seq"], rows, mesh.shape["dp"] // rows)
+    tokens, state = P(("y", "zh", "zl"), "seq", None), P(("y", "zh", "zl"), "seq")
+    cut = mesh.devices.reshape(mesh.shape["seq"], 8, mesh.shape["dp"] // 16, 2)
     return jax.shard_map(
         shards,
-        mesh=Mesh(cut, ("seq", "y", "z")),
-        in_specs=(tokens,) * 4 + (P(("y", "z"), None),) + (state,) * 5,
+        mesh=Mesh(cut, ("seq", "y", "zh", "zl")),
+        in_specs=(tokens,) * 4 + (P(("y", "zh", "zl"), None),) + (state,) * 5,
         out_specs=(tokens,) * 2 + (state,) * 5,
         check_vma=False,
     )

time: 159 us -> 155 us (0.975)
  the two profiles are of different devices: /device:TPU:1 before, /device:TPU:14 now
where the time goes in v7:
time: 155 us; the launch traced here: 154 us
  starting transfers between devices  86.2 us (56%)
  Pallas kernels  36.1 us (23%)
  waiting for transfers between devices  22.5 us (15%)
  local copies, waits for them, and re-layouts  7.88 us (5%)
    ppermute x12, starting transfers between devices, send(): return lax.ppermute(array, 'seq', pairs)  36.8 us
    all_to_all x1, starting transfers between devices, shards(): lax.all_to_all(copies, ('y', 'zh'), split_axis=0, concat_axis=0, tiled=True)  15.9 us
    all_to_all x1, starting transfers between devices, shards(): lax.all_to_all(add_pair(keep, other), ('y', 'zh'), split_axis=0, concat_a...  15.3 us
    all_to_all x1, waiting for transfers between devices, shards(): lax.all_to_all(add_pair(keep, other), ('y', 'zh'), split_axis=0, concat_a...  12.4 us
    ppermute x3, starting transfers between devices, turn(): return lax.ppermute(array, 'seq', pairs)  9.44 us
    ppermute x2, starting transfers between devices, swap_low(): return lax.ppermute(array, 'zl', [(0, 1), (1, 0)])  8.76 us
    pallas_call x1, Pallas kernels, probs_call(): pl.pallas_call(probs_kernel, grid=(BLOCKS // 2,), in_specs=[SCALARS, SCAL...  8.33 us
    pallas_call x1, Pallas kernels, grads_call(): pl.pallas_call(grads_kernel, grid=(BLOCKS // 2,), in_specs=[SCALARS, SCAL...  8.19 us
  transfers between devices with their start and end apart: 19, of which 5 were waited for; matrix products, arithmetic and copies ran while one was open for 1% of the time, Pallas kernels for 17%

profile of v7, /device:TPU:14, one launch (start us, length us, event | category | flops | bytes accessed | tf_op | source)
XLA Modules:
  0.0 153.9 jit_solution(5667006425573734287)
XLA Ops:
  0.7 0.6 stack.82.to_ref
  1.3 3.2 %shard_map.153 = (bf16[2,128,1152]{2,1,0:T(8,128)(2,1)}, bf16[2,128,1152]{2,1,0:T(8,128)(2,1)}, bf16[2,128,1152]{2,1,0:T(8,128)(2,1)}, bf16[2,128,1152]{2,1,0:T(8,128)(2,1)}) custom-call(s32[8]{0:T(128)} %stack.82.to_ref, bf16[128,4096]{1,0:T(8,128)(2,1)} %bitcast.28, bf16[128,4096]{1,0:T(8,128)(2,1)} %bitcast.29, bf16[128,1024]{1,0:T(8,128)(2,1)} %bitcast.30), custom_call_target="tpu_custom_call" | custom-call | flops 3000000000 | bytes 3000000 | tf_op jit(solution)/shard_map/pallas_call | solution.py:103
  4.6 2.4 %collective-permute-start = (bf16[2,128,1152]{2,1,0:T(8,128)(2,1)}, bf16[2,128,1152]{2,1,0:T(8,128)(2,1)S(1)}, u32[]{:S(2)}, u32[]{:S(2)}) collective-permute-start(bf16[2,128,1152]{2,1,0:T(8,128)(2,1)} %get-tuple-element.37), channel_id=1, source_target_pairs={{0,128},{64,192},{128,256},{192,320},{256,384},{320,448},{384,0},{... | collective-permute-start | bytes 1769480 | tf_op jit(solution)/shard_map/ppermute | solution.py:57
  7.0 4.3 %collective-permute-start.1 = (bf16[2,128,1152]{2,1,0:T(8,128)(2,1)}, bf16[2,128,1152]{2,1,0:T(8,128)(2,1)S(1)}, u32[]{:S(2)}, u32[]{:S(2)}) collective-permute-start(bf16[2,128,1152]{2,1,0:T(8,128)(2,1)} %get-tuple-element.38), channel_id=1, source_target_pairs={{0,256},{64,320},{128,384},{192,448},{256,0},{320,64},{384,128},{4... | collective-permute-start | bytes 1769480 | tf_op jit(solution)/shard_map/ppermute | solution.py:57
  11.3 1.9 %collective-permute-start.2 = (bf16[2,128,1152]{2,1,0:T(8,128)(2,1)}, bf16[2,128,1152]{2,1,0:T(8,128)(2,1)S(1)}, u32[]{:S(2)}, u32[]{:S(2)}) collective-permute-start(bf16[2,128,1152]{2,1,0:T(8,128)(2,1)} %get-tuple-element.39), channel_id=1, source_target_pairs={{0,384},{64,448},{128,0},{192,64},{256,128},{320,192},{384,256},{4... | collective-permute-start | bytes 1769480 | tf_op jit(solution)/shard_map/ppermute | solution.py:57
  13.2 5.1 %collective-permute-start.4 = (bf16[128,4096]{1,0:T(8,128)(2,1)}, bf16[128,4096]{1,0:T(8,128)(2,1)}, u32[]{:S(2)}, u32[]{:S(2)}) collective-permute-start(bf16[128,4096]{1,0:T(8,128)(2,1)} %bitcast.16.refs_0_), channel_id=1, source_target_pairs={{0,128},{64,448},{128,256},{192,64},{256,384},{320,192},{384,0},{4... | collective-permute-start | bytes 3145736 | tf_op jit(solution)/shard_map/ppermute | solution.py:62
  18.4 4.3 %collective-permute-start.6 = (bf16[64,128]{1,0:T(8,128)(2,1)S(1)}, bf16[64,128]{1,0:T(8,128)(2,1)S(1)}, u32[]{:S(2)}, u32[]{:S(2)}) collective-permute-start(bf16[64,128]{1,0:T(8,128)(2,1)S(1)} %convert_element_type.3), channel_id=1, source_target_pairs={{0,1},{1,0},{2,3},{3,2},{4,5},{5,4},{6,7},{7,6},{8,9},{9,8},{10,11... | collective-permute-start | bytes 49160 | tf_op jit(solution)/shard_map/ppermute | solution.py:458
  22.7 1.7 %collective-permute-done.6 = bf16[64,128]{1,0:T(8,128)(2,1)S(1)} collective-permute-done((bf16[64,128]{1,0:T(8,128)(2,1)S(1)}, bf16[64,128]{1,0:T(8,128)(2,1)S(1)}, u32[]{:S(2)}, u32[]{:S(2)}) %collective-permute-start.6) | collective-permute-done | bytes 16416 | tf_op jit(solution)/shard_map/ppermute | solution.py:458
  24.4 1.9 %collective-permute-start.9 = (bf16[128,4096]{1,0:T(8,128)(2,1)}, bf16[128,4096]{1,0:T(8,128)(2,1)}, u32[]{:S(2)}, u32[]{:S(2)}) collective-permute-start(bf16[128,4096]{1,0:T(8,128)(2,1)} %bitcast.16.refs_0_), channel_id=1, source_target_pairs={{0,384},{64,192},{128,0},{192,320},{256,128},{320,448},{384,256},{... | collective-permute-start | bytes 3145736 | tf_op jit(solution)/shard_map/ppermute | solution.py:62
  26.3 1.2 broadcast_in_dim.15
  27.5 15.9 %all-to-all-start = ((bf16[32,2,64,128]{3,2,1,0:T(8,128)(2,1)}), bf16[32,2,64,128]{3,2,1,0:T(8,128)(2,1)S(1)}, u32[]{:S(2)}, u32[]{:S(2)}) async-start(bf16[32,2,64,128]{3,2,1,0:T(8,128)(2,1)} %broadcast_in_dim.15), calls=%async_computation | async-start | bytes 2097152 | tf_op jit(solution)/shard_map/all_to_all | solution.py:564
  43.5 0.0 collective-permute-done.refs_1_
  43.5 0.0 collective-permute-done.1.refs_2_
  43.5 0.0 collective-permute-done.2.refs_3_
  43.5 0.9 copy-done.4
  44.4 1.1 copy-done.5
  45.5 1.1 copy-done.9
  46.5 0.3 shard_map.154
  46.8 0.8 copy-done.2
  47.7 0.8 copy-done.3
  48.5 1.9 %collective-permute-start.3 = (bf16[4,128,1152]{2,1,0:T(8,128)(2,1)S(1)}, bf16[4,128,1152]{2,1,0:T(8,128)(2,1)S(1)}, u32[]{:S(2)}, u32[]{:S(2)}) collective-permute-start(bf16[4,128,1152]{2,1,0:T(8,128)(2,1)S(1)} %shard_map.154), channel_id=1, source_target_pairs={{0,64},{64,0},{128,192},{192,128},{256,320},{320,256},{384,448},{4... | collective-permute-start | bytes 3538952 | tf_op jit(solution)/shard_map/ppermute | solution.py:57
  50.4 2.4 %collective-permute-start.7 = (bf16[128,4096]{1,0:T(8,128)(2,1)}, bf16[128,4096]{1,0:T(8,128)(2,1)}, u32[]{:S(2)}, u32[]{:S(2)}) collective-permute-start(bf16[128,4096]{1,0:T(8,128)(2,1)} %bitcast.16.refs_0_), channel_id=1, source_target_pairs={{0,64},{64,0},{128,192},{192,128},{256,320},{320,256},{384,448},{4... | collective-permute-start | bytes 3145736 | tf_op jit(solution)/shard_map/ppermute | solution.py:57
  52.8 4.2 %collective-permute-done.4.refs_2_ = bf16[128,4096]{1,0:T(8,128)(2,1)} collective-permute-done((bf16[128,4096]{1,0:T(8,128)(2,1)}, bf16[128,4096]{1,0:T(8,128)(2,1)}, u32[]{:S(2)}, u32[]{:S(2)}) %collective-permute-start.4) | collective-permute-done | bytes 1048608 | tf_op jit(solution)/shard_map/ppermute | solution.py:62
  57.0 2.4 %collective-permute-start.5 = (bf16[128,4096]{1,0:T(8,128)(2,1)}, bf16[128,4096]{1,0:T(8,128)(2,1)}, u32[]{:S(2)}, u32[]{:S(2)}) collective-permute-start(bf16[128,4096]{1,0:T(8,128)(2,1)} %collective-permute-done.4.refs_2_), channel_id=1, source_target_pairs={{0,128},{64,448},{128,256},{192,64},{256,384},{320,192},{384,0},{4... | collective-permute-start | bytes 3145736 | tf_op jit(solution)/shard_map/ppermute | solution.py:62
  59.4 5.0 %collective-permute-start.8 = (bf16[128,4096]{1,0:T(8,128)(2,1)}, bf16[128,4096]{1,0:T(8,128)(2,1)}, u32[]{:S(2)}, u32[]{:S(2)}) collective-permute-start(bf16[128,4096]{1,0:T(8,128)(2,1)} %collective-permute-done.4.refs_2_), channel_id=1, source_target_pairs={{0,64},{64,0},{128,192},{192,128},{256,320},{320,256},{384,448},{4... | collective-permute-start | bytes 3145736 | tf_op jit(solution)/shard_map/ppermute | solution.py:57
  64.4 0.0 collective-permute-done.9.refs_4_
  64.4 1.9 %collective-permute-start.10 = (bf16[128,4096]{1,0:T(8,128)(2,1)}, bf16[128,4096]{1,0:T(8,128)(2,1)}, u32[]{:S(2)}, u32[]{:S(2)}) collective-permute-start(bf16[128,4096]{1,0:T(8,128)(2,1)} %collective-permute-done.9.refs_4_), channel_id=1, source_target_pairs={{0,64},{64,0},{128,192},{192,128},{256,320},{320,256},{384,448},{4... | collective-permute-start | bytes 3145736 | tf_op jit(solution)/shard_map/ppermute | solution.py:57
  66.4 0.1 stack.81.from_ref
  66.4 0.0 collective-permute-done.3.refs_4_
  66.5 8.3 %shard_map.155 = (bf16[4,2,512,512]{3,2,1,0:T(8,128)(2,1)}, bf16[1024,128]{1,0:T(8,128)(2,1)}) custom-call(s32[1,8]{1,0:T(1,128)S(1)} %copy-done.8, s32[8]{0:T(128)S(1)} %stack.81.from_ref, bf16[2,128,1152]{2,1,0:T(8,128)(2,1)} %get-tuple-element.36.refs_0_, bf16[2,128,1152]{2,1,0:T(8,128)(2,1)} %copy-done.2, bf16[2,128,1152]{2,1,0:T(8,128)(2,1)} %copy-done.3, ...), custom_call_target="tpu_custom_call" | custom-call | flops 8000000000 | bytes 8000000 | tf_op jit(solution)/shard_map/pallas_call | solution.py:238
  74.8 0.0 collective-permute-done.7.refs_1_
  74.8 0.0 all-to-all-done
  74.8 0.0 collective-permute-done.5.refs_6_
  74.8 0.0 collective-permute-done.8.refs_3_
  74.8 0.0 collective-permute-done.10.refs_5_
  74.8 4.7 %collective-permute-start.11 = (bf16[128,4096]{1,0:T(8,128)(2,1)}, bf16[128,4096]{1,0:T(8,128)(2,1)S(1)}, u32[]{:S(2)}, u32[]{:S(2)}) collective-permute-start(bf16[128,4096]{1,0:T(8,128)(2,1)} %collective-permute-done.5.refs_6_), channel_id=1, source_target_pairs={{0,64},{64,0},{128,192},{192,128},{256,320},{320,256},{384,448},{4... | collective-permute-start | bytes 3145736 | tf_op jit(solution)/shard_map/ppermute | solution.py:57
  79.6 0.1 stack.88.around_ref.from_ref
  79.7 2.4 %collective-permute-done.11.refs_7_ = bf16[128,4096]{1,0:T(8,128)(2,1)S(1)} collective-permute-done((bf16[128,4096]{1,0:T(8,128)(2,1)}, bf16[128,4096]{1,0:T(8,128)(2,1)S(1)}, u32[]{:S(2)}, u32[]{:S(2)}) %collective-permute-start.11) | collective-permute-done | bytes 1048608 | tf_op jit(solution)/shard_map/ppermute | solution.py:57
  82.0 1.0 copy-done.14
  83.0 6.3 %shard_map.158 = (bf16[32,64,128]{2,1,0:T(8,128)(2,1)}, bf16[32,64,128]{2,1,0:T(8,128)(2,1)}) custom-call(s32[8]{0:T(128)S(1)} %stack.88.around_ref.from_ref, s32[1]{0:T(128)} %bitcast.20.low_ref, bf16[128,4096]{1,0:T(8,128)(2,1)} %bitcast.16.refs_0_, bf16[128,4096]{1,0:T(8,128)(2,1)} %collective-permute-done.7.refs_1_, ...), custom_call_target="tpu_custom_call" | custom-call | flops 5000000000 | bytes 5000000 | tf_op jit(solution)/shard_map/pallas_call | solution.py:304
  89.3 4.5 %collective-permute-start.12 = (bf16[32,64,128]{2,1,0:T(8,128)(2,1)}, bf16[32,64,128]{2,1,0:T(8,128)(2,1)S(1)}, u32[]{:S(2)}, u32[]{:S(2)}) collective-permute-start(bf16[32,64,128]{2,1,0:T(8,128)(2,1)} %get-tuple-element.50), channel_id=1, source_target_pairs={{0,1},{1,0},{2,3},{3,2},{4,5},{5,4},{6,7},{7,6},{8,9},{9,8},{10,11... | collective-permute-start | bytes 1572872 | tf_op jit(solution)/shard_map/ppermute | solution.py:458
  93.8 5.5 %shard_map.156.refs_6_ = bf16[1024,128]{1,0:T(8,128)(2,1)S(1)} custom-call(bf16[128,4096]{1,0:T(8,128)(2,1)} %bitcast.16.refs_0_, bf16[128,4096]{1,0:T(8,128)(2,1)} %collective-permute-done.7.refs_1_, bf16[128,4096]{1,0:T(8,128)(2,1)} %collective-permute-done.4.refs_2_, bf16[128,4096]{1,0:T(8,128)(2,1)} %collective-permute-done.8.refs_3_, ...), custom_call_target="tpu_custom_call" | custom-call | flops 6000000000 | bytes 6000000 | tf_op jit(solution)/shard_map/pallas_call | solution.py:320
  99.3 0.0 copy-done.1
  99.3 8.2 %shard_map.157 = (bf16[2,128,640]{2,1,0:T(8,128)(2,1)}, bf16[2,128,640]{2,1,0:T(8,128)(2,1)}, bf16[2,128,640]{2,1,0:T(8,128)(2,1)}, bf16[2,128,640]{2,1,0:T(8,128)(2,1)}) custom-call(s32[8]{0:T(128)S(1)} %stack.81.from_ref, s32[8]{0:T(128)S(1)} %copy-done.1, s32[8]{0:T(128)S(1)} %stack.88.around_ref.from_ref, ...), custom_call_target="tpu_custom_call" | custom-call | flops 8999999488 | bytes 9000000 | tf_op jit(solution)/shard_map/pallas_call | solution.py:388
  107.5 3.1 %collective-permute-start.14 = (bf16[2,128,640]{2,1,0:T(8,128)(2,1)}, bf16[2,128,640]{2,1,0:T(8,128)(2,1)S(1)}, u32[]{:S(2)}, u32[]{:S(2)}) collective-permute-start(bf16[2,128,640]{2,1,0:T(8,128)(2,1)} %get-tuple-element.54), channel_id=1, source_target_pairs={{0,256},{64,320},{128,384},{192,448},{256,0},{320,64},{384,128},{4... | collective-permute-start | bytes 983048 | tf_op jit(solution)/shard_map/ppermute | solution.py:57
  110.6 2.2 %collective-permute-start.15 = (bf16[2,128,640]{2,1,0:T(8,128)(2,1)}, bf16[2,128,640]{2,1,0:T(8,128)(2,1)S(1)}, u32[]{:S(2)}, u32[]{:S(2)}) collective-permute-start(bf16[2,128,640]{2,1,0:T(8,128)(2,1)} %get-tuple-element.55), channel_id=1, source_target_pairs={{0,384},{64,448},{128,0},{192,64},{256,128},{320,192},{384,256},{4... | collective-permute-start | bytes 983048 | tf_op jit(solution)/shard_map/ppermute | solution.py:57
  112.8 0.0 collective-permute-done.12.two_ref
  112.8 0.0 copy-start.11
  112.8 5.0 %collective-permute-start.13 = (bf16[2,128,640]{2,1,0:T(8,128)(2,1)}, bf16[2,128,640]{2,1,0:T(8,128)(2,1)S(1)}, u32[]{:S(2)}, u32[]{:S(2)}) collective-permute-start(bf16[2,128,640]{2,1,0:T(8,128)(2,1)} %get-tuple-element.53), channel_id=1, source_target_pairs={{0,128},{64,192},{128,256},{192,320},{256,384},{320,448},{384,0},{... | collective-permute-start | bytes 983048 | tf_op jit(solution)/shard_map/ppermute | solution.py:57
  117.8 0.9 shard_map.161
  118.8 15.3 %all-to-all-start.1 = ((bf16[32,64,128]{2,1,0:T(8,128)(2,1)}), bf16[32,64,128]{2,1,0:T(8,128)(2,1)S(1)}, u32[]{:S(2)}, u32[]{:S(2)}) async-start(bf16[32,64,128]{2,1,0:T(8,128)(2,1)} %shard_map.161), calls=%async_computation.1 | async-start | bytes 1048576 | tf_op jit(solution)/shard_map/all_to_all | solution.py:581
  134.0 0.0 collective-permute-done.14.refs_2_
  134.0 0.0 collective-permute-done.15.refs_3_
  134.0 0.0 collective-permute-done.13.refs_1_
  134.1 0.0 copy-start.12
  134.1 0.0 copy-start.13
  134.1 0.9 shard_map.159
  135.0 1.9 %collective-permute-start.16 = (bf16[4,128,640]{2,1,0:T(8,128)(2,1)S(1)}, bf16[4,128,640]{2,1,0:T(8,128)(2,1)S(1)}, u32[]{:S(2)}, u32[]{:S(2)}) collective-permute-start(bf16[4,128,640]{2,1,0:T(8,128)(2,1)S(1)} %shard_map.159), channel_id=1, source_target_pairs={{0,64},{64,0},{128,192},{192,128},{256,320},{320,256},{384,448},{4... | collective-permute-start | bytes 1966088 | tf_op jit(solution)/shard_map/ppermute | solution.py:57
  136.9 0.1 copy.17.ms_ref
  137.0 0.1 copy.18.vs_ref
  137.1 1.9 %collective-permute-done.16.refs_4_ = bf16[4,128,640]{2,1,0:T(8,128)(2,1)S(1)} collective-permute-done((bf16[4,128,640]{2,1,0:T(8,128)(2,1)S(1)}, bf16[4,128,640]{2,1,0:T(8,128)(2,1)S(1)}, u32[]{:S(2)}, u32[]{:S(2)}) %collective-permute-start.16) | collective-permute-done | bytes 655392 | tf_op jit(solution)/shard_map/ppermute | solution.py:57
  139.0 1.7 %shard_map.160 = (bf16[128,4096]{1,0:T(8,128)(2,1)}, bf16[128,1024]{1,0:T(8,128)(2,1)}) custom-call(s32[8]{0:T(128)S(1)} %stack.81.from_ref, bf16[2,128,640]{2,1,0:T(8,128)(2,1)S(1)} %copy-done.11, bf16[2,128,640]{2,1,0:T(8,128)(2,1)S(1)} %collective-permute-done.13.refs_1_, bf16[2,128,640]{2,1,0:T(8,128)(2,1)S(1)} %collective-permute-done.14.refs_2_, ...), custom_call_target="tpu_custom_call" | custom-call | flops 2000000000 | bytes 2000000 | tf_op jit(solution)/shard_map/pallas_call | solution.py:430
  140.7 12.4 %all-to-all-done.1.parts_ref = bf16[32,64,128]{2,1,0:T(8,128)(2,1)S(1)} async-done(((bf16[32,64,128]{2,1,0:T(8,128)(2,1)}), bf16[32,64,128]{2,1,0:T(8,128)(2,1)S(1)}, u32[]{:S(2)}, u32[]{:S(2)}) %all-to-all-start.1) | async-done | bytes 524320 | tf_op jit(solution)/shard_map/all_to_all | solution.py:581
  153.1 0.8 shard_map.162
  (23 shorter events, 0.1 us)
Async XLA Ops:
  1.3 17.0 %copy-start = (f32[64,128]{1,0:T(8,128)S(1)}, f32[64,128]{1,0:T(8,128)}, u32[]{:S(2)}) copy-start(f32[64,128]{1,0:T(8,128)} %master_ref.1) | copy-start | bytes 98308
  4.6 38.9 %collective-permute-start = (bf16[2,128,1152]{2,1,0:T(8,128)(2,1)}, bf16[2,128,1152]{2,1,0:T(8,128)(2,1)S(1)}, u32[]{:S(2)}, u32[]{:S(2)}) collective-permute-start(bf16[2,128,1152]{2,1,0:T(8,128)(2,1)} %get-tuple-element.37), channel_id=1, source_target_pairs={{0,128},{64,192},{128,256},{192,320},{256,384},{320,448},{384,0},{... | collective-permute-start | bytes 1769480 | tf_op jit(solution)/shard_map/ppermute | solution.py:57
  7.0 36.5 %collective-permute-start.1 = (bf16[2,128,1152]{2,1,0:T(8,128)(2,1)}, bf16[2,128,1152]{2,1,0:T(8,128)(2,1)S(1)}, u32[]{:S(2)}, u32[]{:S(2)}) collective-permute-start(bf16[2,128,1152]{2,1,0:T(8,128)(2,1)} %get-tuple-element.38), channel_id=1, source_target_pairs={{0,256},{64,320},{128,384},{192,448},{256,0},{320,64},{384,128},{4... | collective-permute-start | bytes 1769480 | tf_op jit(solution)/shard_map/ppermute | solution.py:57
  11.3 32.2 %collective-permute-start.2 = (bf16[2,128,1152]{2,1,0:T(8,128)(2,1)}, bf16[2,128,1152]{2,1,0:T(8,128)(2,1)S(1)}, u32[]{:S(2)}, u32[]{:S(2)}) collective-permute-start(bf16[2,128,1152]{2,1,0:T(8,128)(2,1)} %get-tuple-element.39), channel_id=1, source_target_pairs={{0,384},{64,448},{128,0},{192,64},{256,128},{320,192},{384,256},{4... | collective-permute-start | bytes 1769480 | tf_op jit(solution)/shard_map/ppermute | solution.py:57
  13.2 43.8 %collective-permute-start.4 = (bf16[128,4096]{1,0:T(8,128)(2,1)}, bf16[128,4096]{1,0:T(8,128)(2,1)}, u32[]{:S(2)}, u32[]{:S(2)}) collective-permute-start(bf16[128,4096]{1,0:T(8,128)(2,1)} %bitcast.16.refs_0_), channel_id=1, source_target_pairs={{0,128},{64,448},{128,256},{192,64},{256,384},{320,192},{384,0},{4... | collective-permute-start | bytes 3145736 | tf_op jit(solution)/shard_map/ppermute | solution.py:62
  18.4 6.0 %collective-permute-start.6 = (bf16[64,128]{1,0:T(8,128)(2,1)S(1)}, bf16[64,128]{1,0:T(8,128)(2,1)S(1)}, u32[]{:S(2)}, u32[]{:S(2)}) collective-permute-start(bf16[64,128]{1,0:T(8,128)(2,1)S(1)} %convert_element_type.3), channel_id=1, source_target_pairs={{0,1},{1,0},{2,3},{3,2},{4,5},{5,4},{6,7},{7,6},{8,9},{9,8},{10,11... | collective-permute-start | bytes 49160 | tf_op jit(solution)/shard_map/ppermute | solution.py:458
  24.4 40.0 %collective-permute-start.9 = (bf16[128,4096]{1,0:T(8,128)(2,1)}, bf16[128,4096]{1,0:T(8,128)(2,1)}, u32[]{:S(2)}, u32[]{:S(2)}) collective-permute-start(bf16[128,4096]{1,0:T(8,128)(2,1)} %bitcast.16.refs_0_), channel_id=1, source_target_pairs={{0,384},{64,192},{128,0},{192,320},{256,128},{320,448},{384,256},{... | collective-permute-start | bytes 3145736 | tf_op jit(solution)/shard_map/ppermute | solution.py:62
  27.5 38.9 %copy-start.8 = (s32[1,8]{1,0:T(1,128)S(1)}, s32[1,8]{1,0:T(1,128)}, u32[]{:S(2)}) copy-start(s32[1,8]{1,0:T(1,128)} %lens_ref.1) | copy-start | bytes 100
  27.5 47.3 %all-to-all-start = ((bf16[32,2,64,128]{3,2,1,0:T(8,128)(2,1)}), bf16[32,2,64,128]{3,2,1,0:T(8,128)(2,1)S(1)}, u32[]{:S(2)}, u32[]{:S(2)}) async-start(bf16[32,2,64,128]{3,2,1,0:T(8,128)(2,1)} %broadcast_in_dim.15), calls=%async_computation | async-start | bytes 2097152 | tf_op jit(solution)/shard_map/all_to_all | solution.py:564
  43.5 0.9 copy-start.4
  44.4 1.1 copy-start.5
  45.5 1.1 copy-start.9
  46.8 0.8 copy-start.2
  47.7 0.8 copy-start.3
  48.5 18.0 %collective-permute-start.3 = (bf16[4,128,1152]{2,1,0:T(8,128)(2,1)S(1)}, bf16[4,128,1152]{2,1,0:T(8,128)(2,1)S(1)}, u32[]{:S(2)}, u32[]{:S(2)}) collective-permute-start(bf16[4,128,1152]{2,1,0:T(8,128)(2,1)S(1)} %shard_map.154), channel_id=1, source_target_pairs={{0,64},{64,0},{128,192},{192,128},{256,320},{320,256},{384,448},{4... | collective-permute-start | bytes 3538952 | tf_op jit(solution)/shard_map/ppermute | solution.py:57
  50.4 24.4 %collective-permute-start.7 = (bf16[128,4096]{1,0:T(8,128)(2,1)}, bf16[128,4096]{1,0:T(8,128)(2,1)}, u32[]{:S(2)}, u32[]{:S(2)}) collective-permute-start(bf16[128,4096]{1,0:T(8,128)(2,1)} %bitcast.16.refs_0_), channel_id=1, source_target_pairs={{0,64},{64,0},{128,192},{192,128},{256,320},{320,256},{384,448},{4... | collective-permute-start | bytes 3145736 | tf_op jit(solution)/shard_map/ppermute | solution.py:57
  57.0 17.8 %collective-permute-start.5 = (bf16[128,4096]{1,0:T(8,128)(2,1)}, bf16[128,4096]{1,0:T(8,128)(2,1)}, u32[]{:S(2)}, u32[]{:S(2)}) collective-permute-start(bf16[128,4096]{1,0:T(8,128)(2,1)} %collective-permute-done.4.refs_2_), channel_id=1, source_target_pairs={{0,128},{64,448},{128,256},{192,64},{256,384},{320,192},{384,0},{4... | collective-permute-start | bytes 3145736 | tf_op jit(solution)/shard_map/ppermute | solution.py:62
  59.4 15.4 %collective-permute-start.8 = (bf16[128,4096]{1,0:T(8,128)(2,1)}, bf16[128,4096]{1,0:T(8,128)(2,1)}, u32[]{:S(2)}, u32[]{:S(2)}) collective-permute-start(bf16[128,4096]{1,0:T(8,128)(2,1)} %collective-permute-done.4.refs_2_), channel_id=1, source_target_pairs={{0,64},{64,0},{128,192},{192,128},{256,320},{320,256},{384,448},{4... | collective-permute-start | bytes 3145736 | tf_op jit(solution)/shard_map/ppermute | solution.py:57
  64.4 10.4 %collective-permute-start.10 = (bf16[128,4096]{1,0:T(8,128)(2,1)}, bf16[128,4096]{1,0:T(8,128)(2,1)}, u32[]{:S(2)}, u32[]{:S(2)}) collective-permute-start(bf16[128,4096]{1,0:T(8,128)(2,1)} %collective-permute-done.9.refs_4_), channel_id=1, source_target_pairs={{0,64},{64,0},{128,192},{192,128},{256,320},{320,256},{384,448},{4... | collective-permute-start | bytes 3145736 | tf_op jit(solution)/shard_map/ppermute | solution.py:57
  74.8 7.2 %collective-permute-start.11 = (bf16[128,4096]{1,0:T(8,128)(2,1)}, bf16[128,4096]{1,0:T(8,128)(2,1)S(1)}, u32[]{:S(2)}, u32[]{:S(2)}) collective-permute-start(bf16[128,4096]{1,0:T(8,128)(2,1)} %collective-permute-done.5.refs_6_), channel_id=1, source_target_pairs={{0,64},{64,0},{128,192},{192,128},{256,320},{320,256},{384,448},{4... | collective-permute-start | bytes 3145736 | tf_op jit(solution)/shard_map/ppermute | solution.py:57
  82.0 1.0 copy-start.14
  89.3 10.0 %copy-start.1 = (s32[8]{0:T(128)S(1)}, s32[8]{0:T(128)}, u32[]{:S(2)}) copy-start(s32[8]{0:T(128)} %stack.82.to_ref) | copy-start | bytes 100
  89.3 23.5 %collective-permute-start.12 = (bf16[32,64,128]{2,1,0:T(8,128)(2,1)}, bf16[32,64,128]{2,1,0:T(8,128)(2,1)S(1)}, u32[]{:S(2)}, u32[]{:S(2)}) collective-permute-start(bf16[32,64,128]{2,1,0:T(8,128)(2,1)} %get-tuple-element.50), channel_id=1, source_target_pairs={{0,1},{1,0},{2,3},{3,2},{4,5},{5,4},{6,7},{7,6},{8,9},{9,8},{10,11... | collective-permute-start | bytes 1572872 | tf_op jit(solution)/shard_map/ppermute | solution.py:458
  99.3 18.6 %copy-start.10 = (bf16[32,64,128]{2,1,0:T(8,128)(2,1)S(1)}, bf16[32,64,128]{2,1,0:T(8,128)(2,1)}, u32[]{:S(2)}) copy-start(bf16[32,64,128]{2,1,0:T(8,128)(2,1)} %get-tuple-element.58.one_ref) | copy-start | bytes 1572868
  107.5 26.5 %collective-permute-start.14 = (bf16[2,128,640]{2,1,0:T(8,128)(2,1)}, bf16[2,128,640]{2,1,0:T(8,128)(2,1)S(1)}, u32[]{:S(2)}, u32[]{:S(2)}) collective-permute-start(bf16[2,128,640]{2,1,0:T(8,128)(2,1)} %get-tuple-element.54), channel_id=1, source_target_pairs={{0,256},{64,320},{128,384},{192,448},{256,0},{320,64},{384,128},{4... | collective-permute-start | bytes 983048 | tf_op jit(solution)/shard_map/ppermute | solution.py:57
  110.6 23.4 %collective-permute-start.15 = (bf16[2,128,640]{2,1,0:T(8,128)(2,1)}, bf16[2,128,640]{2,1,0:T(8,128)(2,1)S(1)}, u32[]{:S(2)}, u32[]{:S(2)}) collective-permute-start(bf16[2,128,640]{2,1,0:T(8,128)(2,1)} %get-tuple-element.55), channel_id=1, source_target_pairs={{0,384},{64,448},{128,0},{192,64},{256,128},{320,192},{384,256},{4... | collective-permute-start | bytes 983048 | tf_op jit(solution)/shard_map/ppermute | solution.py:57
  112.8 21.2 %copy-start.11 = (bf16[2,128,640]{2,1,0:T(8,128)(2,1)S(1)}, bf16[2,128,640]{2,1,0:T(8,128)(2,1)}, u32[]{:S(2)}) copy-start(bf16[2,128,640]{2,1,0:T(8,128)(2,1)} %get-tuple-element.48.refs_0_) | copy-start | bytes 983044
  112.8 21.2 %collective-permute-start.13 = (bf16[2,128,640]{2,1,0:T(8,128)(2,1)}, bf16[2,128,640]{2,1,0:T(8,128)(2,1)S(1)}, u32[]{:S(2)}, u32[]{:S(2)}) collective-permute-start(bf16[2,128,640]{2,1,0:T(8,128)(2,1)} %get-tuple-element.53), channel_id=1, source_target_pairs={{0,128},{64,192},{128,256},{192,320},{256,384},{320,448},{384,0},{... | collective-permute-start | bytes 983048 | tf_op jit(solution)/shard_map/ppermute | solution.py:57
  118.8 34.3 %all-to-all-start.1 = ((bf16[32,64,128]{2,1,0:T(8,128)(2,1)}), bf16[32,64,128]{2,1,0:T(8,128)(2,1)S(1)}, u32[]{:S(2)}, u32[]{:S(2)}) async-start(bf16[32,64,128]{2,1,0:T(8,128)(2,1)} %shard_map.161), calls=%async_computation.1 | async-start | bytes 1048576 | tf_op jit(solution)/shard_map/all_to_all | solution.py:581
  134.1 2.9 %copy-start.12 = (f32[32,1]{0,1:T(1,128)S(1)}, f32[32,1]{0,1:T(1,128)}, u32[]{:S(2)}) copy-start(f32[32,1]{0,1:T(1,128)} %param.17) | copy-start | bytes 388
  134.1 2.9 %copy-start.13 = (f32[32,1]{0,1:T(1,128)S(1)}, f32[32,1]{0,1:T(1,128)}, u32[]{:S(2)}) copy-start(f32[32,1]{0,1:T(1,128)} %param.19) | copy-start | bytes 388
  135.0 4.0 %collective-permute-start.16 = (bf16[4,128,640]{2,1,0:T(8,128)(2,1)S(1)}, bf16[4,128,640]{2,1,0:T(8,128)(2,1)S(1)}, u32[]{:S(2)}, u32[]{:S(2)}) collective-permute-start(bf16[4,128,640]{2,1,0:T(8,128)(2,1)S(1)} %shard_map.159), channel_id=1, source_target_pairs={{0,64},{64,0},{128,192},{192,128},{256,320},{320,256},{384,448},{4... | collective-permute-start | bytes 1966088 | tf_op jit(solution)/shard_map/ppermute | solution.py:57
  137.1 16.0 %copy-start.6 = (bf16[64,128]{1,0:T(8,128)(2,1)S(1)}, bf16[64,128]{1,0:T(8,128)(2,1)}, u32[]{:S(2)}) copy-start(bf16[64,128]{1,0:T(8,128)(2,1)} %mc_ref.1) | copy-start | bytes 49156
  137.1 16.0 %copy-start.7 = (bf16[64,128]{1,0:T(8,128)(2,1)S(1)}, bf16[64,128]{1,0:T(8,128)(2,1)}, u32[]{:S(2)}) copy-start(bf16[64,128]{1,0:T(8,128)(2,1)} %vc_ref.1) | copy-start | bytes 49156

commit v8 on v7

--- a/solution.py
+++ b/solution.py
@@ -441,6 +441,26 @@
     )(origin, *pieces)
 
 
+def split_kernel(low_ref, one_ref, two_ref, keep_ref, give_ref):
+    total = one_ref[...].astype(F32) + two_ref[...].astype(F32)
+    total = total.astype(BF16).reshape((keep_ref.shape[0], -1) + keep_ref.shape[1:])
+    even, odd = total[:, 0], total[:, -1]
+    keep_ref[...] = jnp.where(low_ref[0] == 0, even, odd)
+    give_ref[...] = jnp.where(low_ref[0] == 0, odd, even)
+
+
+def split_pair(low, one, two, outer):
+    shape = (outer, one.shape[0] // outer // 2 * one.shape[1], HD)
+    whole = pl.BlockSpec(memory_space=pltpu.VMEM)
+    return pl.pallas_call(
+        split_kernel,
+        in_specs=[SCALARS, whole, whole],
+        out_shape=[jax.ShapeDtypeStruct(shape, BF16)] * 2,
+        cost_estimate=cost(1),
+        compiler_params=params(8),
+    )(low, one, two)
+
+
 def add_kernel(one_ref, two_ref, out_ref):
     out_ref[...] = (one_ref[...].astype(F32) + two_ref[...].astype(F32)).astype(BF16)
 
@@ -454,8 +474,8 @@
     )(one, two)
 
 
-def swap_low(array):
-    return lax.ppermute(array, "zl", [(0, 1), (1, 0)])
+def swap_low(array, axis):
+    return lax.ppermute(array, axis, [(0, 1), (1, 0)])
 
 
 def adam_kernel(
@@ -531,8 +551,8 @@
 
 
 def shards(hidden, query, key, grad_out, doc_lens, master, m_code, m_scale, v_code, v_scale):
-    n_far = lax.axis_size("y") * lax.axis_size("zh")
-    low = lax.axis_index("zl")
+    n_far = lax.axis_size("yh") * lax.axis_size("yl") * lax.axis_size("zh")
+    low, low_y = lax.axis_index("zl"), lax.axis_index("yl")
     rows = master.shape[0]
     me = lax.axis_index("seq")
     to = jnp.stack([place(me, r // 2, r % 2) for r in range(8)])
@@ -557,11 +577,11 @@
     pairs = pack(to, query[0], grad_out[0], key[0])
     pieces = across(along(pairs))
     mine = master.astype(BF16)
-    theirs = swap_low(mine)
+    theirs = swap_low(mine, "zl")
     both = jnp.where(low == 0, jnp.stack([mine, theirs]), jnp.stack([theirs, mine]))
     both, _ = lax.optimization_barrier((both, pairs[0]))
     copies = jnp.broadcast_to(both[None], (n_far,) + both.shape)
-    weight = lax.all_to_all(copies, ("y", "zh"), split_axis=0, concat_axis=0, tiled=True)
+    weight = lax.all_to_all(copies, ("yh", "yl", "zh"), split_axis=0, concat_axis=0, tiled=True)
     weight = weight.reshape(D, HD)
     far = turn(first, 1)
     near = [own, send(own, 0, 1), first, send(first, 0, 1), second, send(second, 0, 1)]
@@ -572,16 +592,19 @@
     )
     hiddens = near + [far, send(far, 0, 1)]
     keep, give = term_call(around, low[None], hiddens, in_hbm(grad_values), rows, 2)
-    other = swap_low(give)
+    other = swap_low(give, "zl")
     values = values_call(hiddens, weight)
+    keep, give = split_pair(low_y[None], keep, other, lax.axis_size("yh"))
+    values, keep, give = lax.optimization_barrier((values, keep, give))
+    other = swap_low(give, "yl")
     probs = in_hbm(probs)
     grads = list(grads_call(origin, to, around, pieces, probs, values))
     other, keep, grads[1] = lax.optimization_barrier((other, keep, grads[1]))
     grads = along(grads)
-    parts = lax.all_to_all(
-        add_pair(keep, other), ("y", "zh"), split_axis=0, concat_axis=0, tiled=True
-    )
+    parts = add_pair(keep, other).reshape((-1,) + master.shape)
+    parts = lax.all_to_all(parts, ("yh", "zh"), split_axis=0, concat_axis=0, tiled=True)
     grad_query, grad_key = unpack(origin, across(grads))
+    parts, grad_query, grad_key = lax.optimization_barrier((parts, grad_query, grad_key))
     master, m_code, m_scale, v_code, v_scale = adam_call(
         parts, master, m_code, m_scale, v_code, v_scale
     )
@@ -589,13 +612,16 @@
     return (grad_query[None], grad_key[None]) + state
 
 
+DP = ("yh", "yl", "zh", "zl")
+
+
 def solution(mesh):
-    tokens, state = P(("y", "zh", "zl"), "seq", None), P(("y", "zh", "zl"), "seq")
-    cut = mesh.devices.reshape(mesh.shape["seq"], 8, mesh.shape["dp"] // 16, 2)
+    tokens, state = P(DP, "seq", None), P(DP, "seq")
+    cut = mesh.devices.reshape(mesh.shape["seq"], mesh.shape["dp"] // 16, 2, 4, 2)
     return jax.shard_map(
         shards,
-        mesh=Mesh(cut, ("seq", "y", "zh", "zl")),
-        in_specs=(tokens,) * 4 + (P(("y", "zh", "zl"), None),) + (state,) * 5,
+        mesh=Mesh(cut, ("seq",) + DP),
+        in_specs=(tokens,) * 4 + (P(DP, None),) + (state,) * 5,
         out_specs=(tokens,) * 2 + (state,) * 5,
         check_vma=False,
     )

time: 155 us -> 175 us (1.13)
  the two profiles are of different devices: /device:TPU:14 before, /device:TPU:1 now
where the time goes in v8:
time: 175 us; the launch traced here: 172 us
  starting transfers between devices  90.2 us (52%)
  Pallas kernels  36.1 us (21%)
  waiting for transfers between devices  36 us (21%)
  local copies, waits for them, and re-layouts  8.88 us (5%)
    ppermute x12, starting transfers between devices, send(): return lax.ppermute(array, 'seq', pairs)  38.9 us
    all_to_all x1, starting transfers between devices, shards(): lax.all_to_all(copies, ('yh', 'yl', 'zh'), split_axis=0, concat_axis=0, t...  15.2 us
    all_to_all x1, starting transfers between devices, shards(): lax.all_to_all(parts, ('yh', 'zh'), split_axis=0, concat_axis=0, tiled=True)  13.6 us
    ppermute x12, waiting for transfers between devices, send(): return lax.ppermute(array, 'seq', pairs)  13.1 us
    ppermute x3, starting transfers between devices, swap_low(): return lax.ppermute(array, axis, [(0, 1), (1, 0)])  11.9 us
    all_to_all x1, waiting for transfers between devices, shards(): lax.all_to_all(parts, ('yh', 'zh'), split_axis=0, concat_axis=0, tiled=True)  10.7 us
    ppermute x3, starting transfers between devices, turn(): return lax.ppermute(array, 'seq', pairs)  10.6 us
    pallas_call x1, Pallas kernels, probs_call(): pl.pallas_call(probs_kernel, grid=(BLOCKS // 2,), in_specs=[SCALARS, SCAL...  8.32 us
  transfers between devices with their start and end apart: 20, of which 9 were waited for; matrix products, arithmetic and copies ran while one was open for 1% of the time, Pallas kernels for 14%

profile of v8, /device:TPU:1, one launch (start us, length us, event | category | flops | bytes accessed | tf_op | source)
XLA Modules:
  0.0 172.3 jit_solution(9535855185761971678)
XLA Ops:
  0.7 0.7 stack.82.to_ref
  1.4 3.2 %shard_map.153 = (bf16[2,128,1152]{2,1,0:T(8,128)(2,1)}, bf16[2,128,1152]{2,1,0:T(8,128)(2,1)}, bf16[2,128,1152]{2,1,0:T(8,128)(2,1)}, bf16[2,128,1152]{2,1,0:T(8,128)(2,1)}) custom-call(s32[8]{0:T(128)} %stack.82.to_ref, bf16[128,4096]{1,0:T(8,128)(2,1)} %bitcast.30, bf16[128,4096]{1,0:T(8,128)(2,1)} %bitcast.31, bf16[128,1024]{1,0:T(8,128)(2,1)} %bitcast.32), custom_call_target="tpu_custom_call" | custom-call | flops 3000000000 | bytes 3000000 | tf_op jit(solution)/shard_map/pallas_call | solution.py:103
  4.6 3.9 %collective-permute-start.2 = (bf16[2,128,1152]{2,1,0:T(8,128)(2,1)}, bf16[2,128,1152]{2,1,0:T(8,128)(2,1)S(1)}, u32[]{:S(2)}, u32[]{:S(2)}) collective-permute-start(bf16[2,128,1152]{2,1,0:T(8,128)(2,1)} %get-tuple-element.45), channel_id=1, source_target_pairs={{0,128},{64,192},{128,256},{192,320},{256,384},{320,448},{384,0},{... | collective-permute-start | bytes 1769480 | tf_op jit(solution)/shard_map/ppermute | solution.py:57
  8.6 4.4 %collective-permute-start.3 = (bf16[2,128,1152]{2,1,0:T(8,128)(2,1)}, bf16[2,128,1152]{2,1,0:T(8,128)(2,1)S(1)}, u32[]{:S(2)}, u32[]{:S(2)}) collective-permute-start(bf16[2,128,1152]{2,1,0:T(8,128)(2,1)} %get-tuple-element.46), channel_id=1, source_target_pairs={{0,256},{64,320},{128,384},{192,448},{256,0},{320,64},{384,128},{4... | collective-permute-start | bytes 1769480 | tf_op jit(solution)/shard_map/ppermute | solution.py:57
  13.0 3.1 %collective-permute-start.4 = (bf16[2,128,1152]{2,1,0:T(8,128)(2,1)}, bf16[2,128,1152]{2,1,0:T(8,128)(2,1)S(1)}, u32[]{:S(2)}, u32[]{:S(2)}) collective-permute-start(bf16[2,128,1152]{2,1,0:T(8,128)(2,1)} %get-tuple-element.47), channel_id=1, source_target_pairs={{0,384},{64,448},{128,0},{192,64},{256,128},{320,192},{384,256},{4... | collective-permute-start | bytes 1769480 | tf_op jit(solution)/shard_map/ppermute | solution.py:57
  16.0 1.9 %collective-permute-start = (bf16[128,4096]{1,0:T(8,128)(2,1)}, bf16[128,4096]{1,0:T(8,128)(2,1)}, u32[]{:S(2)}, u32[]{:S(2)}) collective-permute-start(bf16[128,4096]{1,0:T(8,128)(2,1)} %bitcast.refs_0_), channel_id=1, source_target_pairs={{0,128},{64,448},{128,256},{192,64},{256,384},{320,192},{384,0},{4... | collective-permute-start | bytes 3145736 | tf_op jit(solution)/shard_map/ppermute | solution.py:62
  18.0 4.0 %collective-permute-start.6 = (bf16[64,128]{1,0:T(8,128)(2,1)S(1)}, bf16[64,128]{1,0:T(8,128)(2,1)S(1)}, u32[]{:S(2)}, u32[]{:S(2)}) collective-permute-start(bf16[64,128]{1,0:T(8,128)(2,1)S(1)} %convert_element_type.3), channel_id=1, source_target_pairs={{0,1},{1,0},{2,3},{3,2},{4,5},{5,4},{6,7},{7,6},{8,9},{9,8},{10,11... | collective-permute-start | bytes 49160 | tf_op jit(solution)/shard_map/ppermute | solution.py:478
  22.0 1.4 collective-permute-done.6
  23.4 3.4 %collective-permute-start.9 = (bf16[128,4096]{1,0:T(8,128)(2,1)}, bf16[128,4096]{1,0:T(8,128)(2,1)}, u32[]{:S(2)}, u32[]{:S(2)}) collective-permute-start(bf16[128,4096]{1,0:T(8,128)(2,1)} %bitcast.refs_0_), channel_id=1, source_target_pairs={{0,384},{64,192},{128,0},{192,320},{256,128},{320,448},{384,256},{... | collective-permute-start | bytes 3145736 | tf_op jit(solution)/shard_map/ppermute | solution.py:62
  26.8 1.2 broadcast_in_dim.18
  28.0 15.2 %all-to-all-start = ((bf16[32,2,64,128]{3,2,1,0:T(8,128)(2,1)}), bf16[32,2,64,128]{3,2,1,0:T(8,128)(2,1)S(1)}, u32[]{:S(2)}, u32[]{:S(2)}) async-start(bf16[32,2,64,128]{3,2,1,0:T(8,128)(2,1)} %broadcast_in_dim.18), calls=%async_computation | async-start | bytes 2097152 | tf_op jit(solution)/shard_map/all_to_all | solution.py:584
  43.2 0.0 collective-permute-done.2.refs_1_
  43.2 0.0 collective-permute-done.3.refs_2_
  43.2 0.0 collective-permute-done.4.refs_3_
  43.2 0.9 copy-done.4
  44.1 1.1 copy-done.5
  45.2 1.1 copy-done.9
  46.2 0.3 shard_map.154
  46.5 0.8 copy-done.2
  47.3 0.8 copy-done.3
  48.1 6.3 %collective-permute-start.5 = (bf16[4,128,1152]{2,1,0:T(8,128)(2,1)S(1)}, bf16[4,128,1152]{2,1,0:T(8,128)(2,1)S(1)}, u32[]{:S(2)}, u32[]{:S(2)}) collective-permute-start(bf16[4,128,1152]{2,1,0:T(8,128)(2,1)S(1)} %shard_map.154), channel_id=1, source_target_pairs={{0,64},{64,0},{128,192},{192,128},{256,320},{320,256},{384,448},{4... | collective-permute-start | bytes 3538952 | tf_op jit(solution)/shard_map/ppermute | solution.py:57
  54.5 1.9 %collective-permute-start.7 = (bf16[128,4096]{1,0:T(8,128)(2,1)}, bf16[128,4096]{1,0:T(8,128)(2,1)}, u32[]{:S(2)}, u32[]{:S(2)}) collective-permute-start(bf16[128,4096]{1,0:T(8,128)(2,1)} %bitcast.refs_0_), channel_id=1, source_target_pairs={{0,64},{64,0},{128,192},{192,128},{256,320},{320,256},{384,448},{4... | collective-permute-start | bytes 3145736 | tf_op jit(solution)/shard_map/ppermute | solution.py:57
  56.4 2.7 %collective-permute-done.refs_2_ = bf16[128,4096]{1,0:T(8,128)(2,1)} collective-permute-done((bf16[128,4096]{1,0:T(8,128)(2,1)}, bf16[128,4096]{1,0:T(8,128)(2,1)}, u32[]{:S(2)}, u32[]{:S(2)}) %collective-permute-start) | collective-permute-done | bytes 1048608 | tf_op jit(solution)/shard_map/ppermute | solution.py:62
  59.1 5.3 %collective-permute-start.1 = (bf16[128,4096]{1,0:T(8,128)(2,1)}, bf16[128,4096]{1,0:T(8,128)(2,1)}, u32[]{:S(2)}, u32[]{:S(2)}) collective-permute-start(bf16[128,4096]{1,0:T(8,128)(2,1)} %collective-permute-done.refs_2_), channel_id=1, source_target_pairs={{0,128},{64,448},{128,256},{192,64},{256,384},{320,192},{384,0},{4... | collective-permute-start | bytes 3145736 | tf_op jit(solution)/shard_map/ppermute | solution.py:62
  64.4 1.9 %collective-permute-start.8 = (bf16[128,4096]{1,0:T(8,128)(2,1)}, bf16[128,4096]{1,0:T(8,128)(2,1)}, u32[]{:S(2)}, u32[]{:S(2)}) collective-permute-start(bf16[128,4096]{1,0:T(8,128)(2,1)} %collective-permute-done.refs_2_), channel_id=1, source_target_pairs={{0,64},{64,0},{128,192},{192,128},{256,320},{320,256},{384,448},{4... | collective-permute-start | bytes 3145736 | tf_op jit(solution)/shard_map/ppermute | solution.py:57
  66.3 0.0 collective-permute-done.9.refs_4_
  66.3 2.4 %collective-permute-start.10 = (bf16[128,4096]{1,0:T(8,128)(2,1)}, bf16[128,4096]{1,0:T(8,128)(2,1)}, u32[]{:S(2)}, u32[]{:S(2)}) collective-permute-start(bf16[128,4096]{1,0:T(8,128)(2,1)} %collective-permute-done.9.refs_4_), channel_id=1, source_target_pairs={{0,64},{64,0},{128,192},{192,128},{256,320},{320,256},{384,448},{4... | collective-permute-start | bytes 3145736 | tf_op jit(solution)/shard_map/ppermute | solution.py:57
  68.7 0.1 stack.81.from_ref
  68.8 0.0 collective-permute-done.5.refs_4_
  68.8 8.3 %shard_map.155 = (bf16[4,2,512,512]{3,2,1,0:T(8,128)(2,1)}, bf16[1024,128]{1,0:T(8,128)(2,1)}) custom-call(s32[1,8]{1,0:T(1,128)S(1)} %copy-done.8, s32[8]{0:T(128)S(1)} %stack.81.from_ref, bf16[2,128,1152]{2,1,0:T(8,128)(2,1)} %get-tuple-element.44.refs_0_, bf16[2,128,1152]{2,1,0:T(8,128)(2,1)} %copy-done.2, bf16[2,128,1152]{2,1,0:T(8,128)(2,1)} %copy-done.3, ...), custom_call_target="tpu_custom_call" | custom-call | flops 8000000000 | bytes 8000000 | tf_op jit(solution)/shard_map/pallas_call | solution.py:238
  77.2 0.0 all-to-all-done
  77.2 1.3 collective-permute-done.1.refs_6_
  78.4 2.3 %collective-permute-start.11 = (bf16[128,4096]{1,0:T(8,128)(2,1)}, bf16[128,4096]{1,0:T(8,128)(2,1)S(1)}, u32[]{:S(2)}, u32[]{:S(2)}) collective-permute-start(bf16[128,4096]{1,0:T(8,128)(2,1)} %collective-permute-done.1.refs_6_), channel_id=1, source_target_pairs={{0,64},{64,0},{128,192},{192,128},{256,320},{320,256},{384,448},{4... | collective-permute-start | bytes 3145736 | tf_op jit(solution)/shard_map/ppermute | solution.py:57
  80.8 0.1 stack.92.from_ref.around_ref
  80.9 2.4 %collective-permute-done.11.refs_7_ = bf16[128,4096]{1,0:T(8,128)(2,1)S(1)} collective-permute-done((bf16[128,4096]{1,0:T(8,128)(2,1)}, bf16[128,4096]{1,0:T(8,128)(2,1)S(1)}, u32[]{:S(2)}, u32[]{:S(2)}) %collective-permute-start.11) | collective-permute-done | bytes 1048608 | tf_op jit(solution)/shard_map/ppermute | solution.py:57
  83.2 1.0 copy-done.15
  84.2 6.3 %shard_map.157 = (bf16[32,64,128]{2,1,0:T(8,128)(2,1)}, bf16[32,64,128]{2,1,0:T(8,128)(2,1)}) custom-call(s32[8]{0:T(128)S(1)} %stack.92.from_ref.around_ref, s32[1]{0:T(128)} %bitcast.21.low_ref, bf16[128,4096]{1,0:T(8,128)(2,1)} %bitcast.refs_0_, bf16[128,4096]{1,0:T(8,128)(2,1)} %collective-permute-done.7.refs_1_, ...), custom_call_target="tpu_custom_call" | custom-call | flops 5000000000 | bytes 5000000 | tf_op jit(solution)/shard_map/pallas_call | solution.py:304
  90.5 4.6 %collective-permute-start.12 = (bf16[32,64,128]{2,1,0:T(8,128)(2,1)}, bf16[32,64,128]{2,1,0:T(8,128)(2,1)S(1)}, u32[]{:S(2)}, u32[]{:S(2)}) collective-permute-start(bf16[32,64,128]{2,1,0:T(8,128)(2,1)} %get-tuple-element.57), channel_id=1, source_target_pairs={{0,1},{1,0},{2,3},{3,2},{4,5},{5,4},{6,7},{7,6},{8,9},{9,8},{10,11... | collective-permute-start | bytes 1572872 | tf_op jit(solution)/shard_map/ppermute | solution.py:478
  95.1 5.5 %shard_map.156.refs_6_ = bf16[1024,128]{1,0:T(8,128)(2,1)S(1)} custom-call(bf16[128,4096]{1,0:T(8,128)(2,1)} %bitcast.refs_0_, bf16[128,4096]{1,0:T(8,128)(2,1)} %collective-permute-done.7.refs_1_, bf16[128,4096]{1,0:T(8,128)(2,1)} %collective-permute-done.refs_2_, bf16[128,4096]{1,0:T(8,128)(2,1)} %collective-permute-done.8.refs_3_, ...), custom_call_target="tpu_custom_call" | custom-call | flops 6000000000 | bytes 6000000 | tf_op jit(solution)/shard_map/pallas_call | solution.py:320
  100.5 6.9 %collective-permute-done.12.two_ref = bf16[32,64,128]{2,1,0:T(8,128)(2,1)S(1)} collective-permute-done((bf16[32,64,128]{2,1,0:T(8,128)(2,1)}, bf16[32,64,128]{2,1,0:T(8,128)(2,1)S(1)}, u32[]{:S(2)}, u32[]{:S(2)}) %collective-permute-start.12) | collective-permute-done | bytes 524320 | tf_op jit(solution)/shard_map/ppermute | solution.py:478
  107.4 0.2 shard_map.158
  107.6 3.4 %collective-permute-start.13 = (bf16[4,256,128]{2,1,0:T(8,128)(2,1)S(1)}, bf16[4,256,128]{2,1,0:T(8,128)(2,1)S(1)}, u32[]{:S(2)}, u32[]{:S(2)}) collective-permute-start(bf16[4,256,128]{2,1,0:T(8,128)(2,1)S(1)} %get-tuple-element.60), channel_id=1, source_target_pairs={{0,8},{8,0},{1,9},{9,1},{2,10},{10,2},{3,11},{11,3},{4,12},{12,4},... | collective-permute-start | bytes 786440 | tf_op jit(solution)/shard_map/ppermute | solution.py:478
  111.0 8.1 %shard_map.159 = (bf16[2,128,640]{2,1,0:T(8,128)(2,1)}, bf16[2,128,640]{2,1,0:T(8,128)(2,1)}, bf16[2,128,640]{2,1,0:T(8,128)(2,1)}, bf16[2,128,640]{2,1,0:T(8,128)(2,1)}) custom-call(s32[8]{0:T(128)S(1)} %stack.81.from_ref, s32[8]{0:T(128)S(1)} %copy-done.1, s32[8]{0:T(128)S(1)} %stack.92.from_ref.around_ref, ...), custom_call_target="tpu_custom_call" | custom-call | flops 8999999488 | bytes 9000000 | tf_op jit(solution)/shard_map/pallas_call | solution.py:388
  119.2 3.4 %collective-permute-start.15 = (bf16[2,128,640]{2,1,0:T(8,128)(2,1)}, bf16[2,128,640]{2,1,0:T(8,128)(2,1)S(1)}, u32[]{:S(2)}, u32[]{:S(2)}) collective-permute-start(bf16[2,128,640]{2,1,0:T(8,128)(2,1)} %get-tuple-element.69), channel_id=1, source_target_pairs={{0,256},{64,320},{128,384},{192,448},{256,0},{320,64},{384,128},{4... | collective-permute-start | bytes 983048 | tf_op jit(solution)/shard_map/ppermute | solution.py:57
  122.6 3.6 %collective-permute-start.16 = (bf16[2,128,640]{2,1,0:T(8,128)(2,1)}, bf16[2,128,640]{2,1,0:T(8,128)(2,1)S(1)}, u32[]{:S(2)}, u32[]{:S(2)}) collective-permute-start(bf16[2,128,640]{2,1,0:T(8,128)(2,1)} %get-tuple-element.70), channel_id=1, source_target_pairs={{0,384},{64,448},{128,0},{192,64},{256,128},{320,192},{384,256},{4... | collective-permute-start | bytes 983048 | tf_op jit(solution)/shard_map/ppermute | solution.py:57
  126.3 0.0 collective-permute-done.13.two_ref
  126.3 1.9 %collective-permute-start.14 = (bf16[2,128,640]{2,1,0:T(8,128)(2,1)}, bf16[2,128,640]{2,1,0:T(8,128)(2,1)S(1)}, u32[]{:S(2)}, u32[]{:S(2)}) collective-permute-start(bf16[2,128,640]{2,1,0:T(8,128)(2,1)} %get-tuple-element.68), channel_id=1, source_target_pairs={{0,128},{64,192},{128,256},{192,320},{256,384},{320,448},{384,0},{... | collective-permute-start | bytes 983048 | tf_op jit(solution)/shard_map/ppermute | solution.py:57
  128.2 2.8 %collective-permute-done.15.refs_2_ = bf16[2,128,640]{2,1,0:T(8,128)(2,1)S(1)} collective-permute-done((bf16[2,128,640]{2,1,0:T(8,128)(2,1)}, bf16[2,128,640]{2,1,0:T(8,128)(2,1)S(1)}, u32[]{:S(2)}, u32[]{:S(2)}) %collective-permute-start.15) | collective-permute-done | bytes 327712 | tf_op jit(solution)/shard_map/ppermute | solution.py:57
  131.0 7.4 %collective-permute-done.16.refs_3_ = bf16[2,128,640]{2,1,0:T(8,128)(2,1)S(1)} collective-permute-done((bf16[2,128,640]{2,1,0:T(8,128)(2,1)}, bf16[2,128,640]{2,1,0:T(8,128)(2,1)S(1)}, u32[]{:S(2)}, u32[]{:S(2)}) %collective-permute-start.16) | collective-permute-done | bytes 327712 | tf_op jit(solution)/shard_map/ppermute | solution.py:57
  138.4 0.4 collective-permute-done.14.refs_1_
  138.9 1.0 copy-done.10
  139.9 0.9 shard_map.161
  140.7 0.0 copy-start.13
  140.7 0.0 copy-start.14
  140.7 0.0 copy-start.11
  140.8 3.7 %collective-permute-start.17 = (bf16[4,128,640]{2,1,0:T(8,128)(2,1)S(1)}, bf16[4,128,640]{2,1,0:T(8,128)(2,1)S(1)}, u32[]{:S(2)}, u32[]{:S(2)}) collective-permute-start(bf16[4,128,640]{2,1,0:T(8,128)(2,1)S(1)} %shard_map.161), channel_id=1, source_target_pairs={{0,64},{64,0},{128,192},{192,128},{256,320},{320,256},{384,448},{4... | collective-permute-start | bytes 1966088 | tf_op jit(solution)/shard_map/ppermute | solution.py:57
  144.4 0.8 shard_map.160
  145.2 13.6 %all-to-all-start.1 = ((bf16[16,64,128]{2,1,0:T(8,128)(2,1)}), bf16[16,64,128]{2,1,0:T(8,128)(2,1)S(1)}, u32[]{:S(2)}, u32[]{:S(2)}) async-start(bf16[16,64,128]{2,1,0:T(8,128)(2,1)} %bitcast.22), calls=%async_computation.1 | async-start | bytes 524288 | tf_op jit(solution)/shard_map/all_to_all | solution.py:605
  158.8 0.1 copy.17.ms_ref
  158.9 0.1 copy.18.vs_ref
  159.0 0.0 collective-permute-done.17.refs_4_
  159.0 1.7 shard_map.162
  160.8 10.7 %all-to-all-done.1.parts_ref = bf16[16,64,128]{2,1,0:T(8,128)(2,1)S(1)} async-done(((bf16[16,64,128]{2,1,0:T(8,128)(2,1)}), bf16[16,64,128]{2,1,0:T(8,128)(2,1)S(1)}, u32[]{:S(2)}, u32[]{:S(2)}) %all-to-all-start.1) | async-done | bytes 262176 | tf_op jit(solution)/shard_map/all_to_all | solution.py:605
  171.5 0.8 shard_map.163
  (28 shorter events, 0.1 us)
Async XLA Ops:
  1.4 16.6 %copy-start = (f32[64,128]{1,0:T(8,128)S(1)}, f32[64,128]{1,0:T(8,128)}, u32[]{:S(2)}) copy-start(f32[64,128]{1,0:T(8,128)} %master_ref.1) | copy-start | bytes 98308
  4.6 38.5 %collective-permute-start.2 = (bf16[2,128,1152]{2,1,0:T(8,128)(2,1)}, bf16[2,128,1152]{2,1,0:T(8,128)(2,1)S(1)}, u32[]{:S(2)}, u32[]{:S(2)}) collective-permute-start(bf16[2,128,1152]{2,1,0:T(8,128)(2,1)} %get-tuple-element.45), channel_id=1, source_target_pairs={{0,128},{64,192},{128,256},{192,320},{256,384},{320,448},{384,0},{... | collective-permute-start | bytes 1769480 | tf_op jit(solution)/shard_map/ppermute | solution.py:57
  8.6 34.6 %collective-permute-start.3 = (bf16[2,128,1152]{2,1,0:T(8,128)(2,1)}, bf16[2,128,1152]{2,1,0:T(8,128)(2,1)S(1)}, u32[]{:S(2)}, u32[]{:S(2)}) collective-permute-start(bf16[2,128,1152]{2,1,0:T(8,128)(2,1)} %get-tuple-element.46), channel_id=1, source_target_pairs={{0,256},{64,320},{128,384},{192,448},{256,0},{320,64},{384,128},{4... | collective-permute-start | bytes 1769480 | tf_op jit(solution)/shard_map/ppermute | solution.py:57
  13.0 30.2 %collective-permute-start.4 = (bf16[2,128,1152]{2,1,0:T(8,128)(2,1)}, bf16[2,128,1152]{2,1,0:T(8,128)(2,1)S(1)}, u32[]{:S(2)}, u32[]{:S(2)}) collective-permute-start(bf16[2,128,1152]{2,1,0:T(8,128)(2,1)} %get-tuple-element.47), channel_id=1, source_target_pairs={{0,384},{64,448},{128,0},{192,64},{256,128},{320,192},{384,256},{4... | collective-permute-start | bytes 1769480 | tf_op jit(solution)/shard_map/ppermute | solution.py:57
  16.0 43.0 %collective-permute-start = (bf16[128,4096]{1,0:T(8,128)(2,1)}, bf16[128,4096]{1,0:T(8,128)(2,1)}, u32[]{:S(2)}, u32[]{:S(2)}) collective-permute-start(bf16[128,4096]{1,0:T(8,128)(2,1)} %bitcast.refs_0_), channel_id=1, source_target_pairs={{0,128},{64,448},{128,256},{192,64},{256,384},{320,192},{384,0},{4... | collective-permute-start | bytes 3145736 | tf_op jit(solution)/shard_map/ppermute | solution.py:62
  18.0 5.4 %collective-permute-start.6 = (bf16[64,128]{1,0:T(8,128)(2,1)S(1)}, bf16[64,128]{1,0:T(8,128)(2,1)S(1)}, u32[]{:S(2)}, u32[]{:S(2)}) collective-permute-start(bf16[64,128]{1,0:T(8,128)(2,1)S(1)} %convert_element_type.3), channel_id=1, source_target_pairs={{0,1},{1,0},{2,3},{3,2},{4,5},{5,4},{6,7},{7,6},{8,9},{9,8},{10,11... | collective-permute-start | bytes 49160 | tf_op jit(solution)/shard_map/ppermute | solution.py:478
  23.4 42.9 %collective-permute-start.9 = (bf16[128,4096]{1,0:T(8,128)(2,1)}, bf16[128,4096]{1,0:T(8,128)(2,1)}, u32[]{:S(2)}, u32[]{:S(2)}) collective-permute-start(bf16[128,4096]{1,0:T(8,128)(2,1)} %bitcast.refs_0_), channel_id=1, source_target_pairs={{0,384},{64,192},{128,0},{192,320},{256,128},{320,448},{384,256},{... | collective-permute-start | bytes 3145736 | tf_op jit(solution)/shard_map/ppermute | solution.py:62
  28.0 40.8 %copy-start.8 = (s32[1,8]{1,0:T(1,128)S(1)}, s32[1,8]{1,0:T(1,128)}, u32[]{:S(2)}) copy-start(s32[1,8]{1,0:T(1,128)} %lens_ref.1) | copy-start | bytes 100
  28.0 49.2 %all-to-all-start = ((bf16[32,2,64,128]{3,2,1,0:T(8,128)(2,1)}), bf16[32,2,64,128]{3,2,1,0:T(8,128)(2,1)S(1)}, u32[]{:S(2)}, u32[]{:S(2)}) async-start(bf16[32,2,64,128]{3,2,1,0:T(8,128)(2,1)} %broadcast_in_dim.18), calls=%async_computation | async-start | bytes 2097152 | tf_op jit(solution)/shard_map/all_to_all | solution.py:584
  43.2 0.9 copy-start.4
  44.1 1.1 copy-start.5
  45.1 1.1 copy-start.9
  46.5 0.8 copy-start.2
  47.3 0.8 copy-start.3
  48.1 20.7 %collective-permute-start.5 = (bf16[4,128,1152]{2,1,0:T(8,128)(2,1)S(1)}, bf16[4,128,1152]{2,1,0:T(8,128)(2,1)S(1)}, u32[]{:S(2)}, u32[]{:S(2)}) collective-permute-start(bf16[4,128,1152]{2,1,0:T(8,128)(2,1)S(1)} %shard_map.154), channel_id=1, source_target_pairs={{0,64},{64,0},{128,192},{192,128},{256,320},{320,256},{384,448},{4... | collective-permute-start | bytes 3538952 | tf_op jit(solution)/shard_map/ppermute | solution.py:57
  54.5 22.7 %collective-permute-start.7 = (bf16[128,4096]{1,0:T(8,128)(2,1)}, bf16[128,4096]{1,0:T(8,128)(2,1)}, u32[]{:S(2)}, u32[]{:S(2)}) collective-permute-start(bf16[128,4096]{1,0:T(8,128)(2,1)} %bitcast.refs_0_), channel_id=1, source_target_pairs={{0,64},{64,0},{128,192},{192,128},{256,320},{320,256},{384,448},{4... | collective-permute-start | bytes 3145736 | tf_op jit(solution)/shard_map/ppermute | solution.py:57
  59.1 19.4 %collective-permute-start.1 = (bf16[128,4096]{1,0:T(8,128)(2,1)}, bf16[128,4096]{1,0:T(8,128)(2,1)}, u32[]{:S(2)}, u32[]{:S(2)}) collective-permute-start(bf16[128,4096]{1,0:T(8,128)(2,1)} %collective-permute-done.refs_2_), channel_id=1, source_target_pairs={{0,128},{64,448},{128,256},{192,64},{256,384},{320,192},{384,0},{4... | collective-permute-start | bytes 3145736 | tf_op jit(solution)/shard_map/ppermute | solution.py:62
  64.4 14.1 %collective-permute-start.8 = (bf16[128,4096]{1,0:T(8,128)(2,1)}, bf16[128,4096]{1,0:T(8,128)(2,1)}, u32[]{:S(2)}, u32[]{:S(2)}) collective-permute-start(bf16[128,4096]{1,0:T(8,128)(2,1)} %collective-permute-done.refs_2_), channel_id=1, source_target_pairs={{0,64},{64,0},{128,192},{192,128},{256,320},{320,256},{384,448},{4... | collective-permute-start | bytes 3145736 | tf_op jit(solution)/shard_map/ppermute | solution.py:57
  66.3 12.1 %collective-permute-start.10 = (bf16[128,4096]{1,0:T(8,128)(2,1)}, bf16[128,4096]{1,0:T(8,128)(2,1)}, u32[]{:S(2)}, u32[]{:S(2)}) collective-permute-start(bf16[128,4096]{1,0:T(8,128)(2,1)} %collective-permute-done.9.refs_4_), channel_id=1, source_target_pairs={{0,64},{64,0},{128,192},{192,128},{256,320},{320,256},{384,448},{4... | collective-permute-start | bytes 3145736 | tf_op jit(solution)/shard_map/ppermute | solution.py:57
  78.4 4.8 %collective-permute-start.11 = (bf16[128,4096]{1,0:T(8,128)(2,1)}, bf16[128,4096]{1,0:T(8,128)(2,1)S(1)}, u32[]{:S(2)}, u32[]{:S(2)}) collective-permute-start(bf16[128,4096]{1,0:T(8,128)(2,1)} %collective-permute-done.1.refs_6_), channel_id=1, source_target_pairs={{0,64},{64,0},{128,192},{192,128},{256,320},{320,256},{384,448},{4... | collective-permute-start | bytes 3145736 | tf_op jit(solution)/shard_map/ppermute | solution.py:57
  83.2 1.0 copy-start.15
  90.5 16.9 %copy-start.12 = (bf16[32,64,128]{2,1,0:T(8,128)(2,1)S(1)}, bf16[32,64,128]{2,1,0:T(8,128)(2,1)}, u32[]{:S(2)}) copy-start(bf16[32,64,128]{2,1,0:T(8,128)(2,1)} %get-tuple-element.56.one_ref) | copy-start | bytes 1572868
  90.5 16.9 %collective-permute-start.12 = (bf16[32,64,128]{2,1,0:T(8,128)(2,1)}, bf16[32,64,128]{2,1,0:T(8,128)(2,1)S(1)}, u32[]{:S(2)}, u32[]{:S(2)}) collective-permute-start(bf16[32,64,128]{2,1,0:T(8,128)(2,1)} %get-tuple-element.57), channel_id=1, source_target_pairs={{0,1},{1,0},{2,3},{3,2},{4,5},{5,4},{6,7},{7,6},{8,9},{9,8},{10,11... | collective-permute-start | bytes 1572872 | tf_op jit(solution)/shard_map/ppermute | solution.py:478
  107.4 3.6 %copy-start.1 = (s32[8]{0:T(128)S(1)}, s32[8]{0:T(128)}, u32[]{:S(2)}) copy-start(s32[8]{0:T(128)} %stack.82.to_ref) | copy-start | bytes 100
  107.6 18.6 %collective-permute-start.13 = (bf16[4,256,128]{2,1,0:T(8,128)(2,1)S(1)}, bf16[4,256,128]{2,1,0:T(8,128)(2,1)S(1)}, u32[]{:S(2)}, u32[]{:S(2)}) collective-permute-start(bf16[4,256,128]{2,1,0:T(8,128)(2,1)S(1)} %get-tuple-element.60), channel_id=1, source_target_pairs={{0,8},{8,0},{1,9},{9,1},{2,10},{10,2},{3,11},{11,3},{4,12},{12,4},... | collective-permute-start | bytes 786440 | tf_op jit(solution)/shard_map/ppermute | solution.py:478
  119.2 11.8 %collective-permute-start.15 = (bf16[2,128,640]{2,1,0:T(8,128)(2,1)}, bf16[2,128,640]{2,1,0:T(8,128)(2,1)S(1)}, u32[]{:S(2)}, u32[]{:S(2)}) collective-permute-start(bf16[2,128,640]{2,1,0:T(8,128)(2,1)} %get-tuple-element.69), channel_id=1, source_target_pairs={{0,256},{64,320},{128,384},{192,448},{256,0},{320,64},{384,128},{4... | collective-permute-start | bytes 983048 | tf_op jit(solution)/shard_map/ppermute | solution.py:57
  122.6 15.8 %collective-permute-start.16 = (bf16[2,128,640]{2,1,0:T(8,128)(2,1)}, bf16[2,128,640]{2,1,0:T(8,128)(2,1)S(1)}, u32[]{:S(2)}, u32[]{:S(2)}) collective-permute-start(bf16[2,128,640]{2,1,0:T(8,128)(2,1)} %get-tuple-element.70), channel_id=1, source_target_pairs={{0,384},{64,448},{128,0},{192,64},{256,128},{320,192},{384,256},{4... | collective-permute-start | bytes 983048 | tf_op jit(solution)/shard_map/ppermute | solution.py:57
  126.3 12.6 %collective-permute-start.14 = (bf16[2,128,640]{2,1,0:T(8,128)(2,1)}, bf16[2,128,640]{2,1,0:T(8,128)(2,1)S(1)}, u32[]{:S(2)}, u32[]{:S(2)}) collective-permute-start(bf16[2,128,640]{2,1,0:T(8,128)(2,1)} %get-tuple-element.68), channel_id=1, source_target_pairs={{0,128},{64,192},{128,256},{192,320},{256,384},{320,448},{384,0},{... | collective-permute-start | bytes 983048 | tf_op jit(solution)/shard_map/ppermute | solution.py:57
  138.9 1.0 copy-start.10
  140.7 18.1 %copy-start.13 = (f32[32,1]{0,1:T(1,128)S(1)}, f32[32,1]{0,1:T(1,128)}, u32[]{:S(2)}) copy-start(f32[32,1]{0,1:T(1,128)} %param.17) | copy-start | bytes 388
  140.7 18.2 %copy-start.14 = (f32[32,1]{0,1:T(1,128)S(1)}, f32[32,1]{0,1:T(1,128)}, u32[]{:S(2)}) copy-start(f32[32,1]{0,1:T(1,128)} %param.19) | copy-start | bytes 388
  140.7 18.3 %copy-start.11 = (bf16[2,128,640]{2,1,0:T(8,128)(2,1)S(1)}, bf16[2,128,640]{2,1,0:T(8,128)(2,1)}, u32[]{:S(2)}) copy-start(bf16[2,128,640]{2,1,0:T(8,128)(2,1)} %get-tuple-element.67.refs_0_) | copy-start | bytes 983044
  140.8 18.3 %collective-permute-start.17 = (bf16[4,128,640]{2,1,0:T(8,128)(2,1)S(1)}, bf16[4,128,640]{2,1,0:T(8,128)(2,1)S(1)}, u32[]{:S(2)}, u32[]{:S(2)}) collective-permute-start(bf16[4,128,640]{2,1,0:T(8,128)(2,1)S(1)} %shard_map.161), channel_id=1, source_target_pairs={{0,64},{64,0},{128,192},{192,128},{256,320},{320,256},{384,448},{4... | collective-permute-start | bytes 1966088 | tf_op jit(solution)/shard_map/ppermute | solution.py:57
  145.2 26.3 %all-to-all-start.1 = ((bf16[16,64,128]{2,1,0:T(8,128)(2,1)}), bf16[16,64,128]{2,1,0:T(8,128)(2,1)S(1)}, u32[]{:S(2)}, u32[]{:S(2)}) async-start(bf16[16,64,128]{2,1,0:T(8,128)(2,1)} %bitcast.22), calls=%async_computation.1 | async-start | bytes 524288 | tf_op jit(solution)/shard_map/all_to_all | solution.py:605
  159.0 12.5 %copy-start.6 = (bf16[64,128]{1,0:T(8,128)(2,1)S(1)}, bf16[64,128]{1,0:T(8,128)(2,1)}, u32[]{:S(2)}) copy-start(bf16[64,128]{1,0:T(8,128)(2,1)} %mc_ref.1) | copy-start | bytes 49156
  159.0 12.5 %copy-start.7 = (bf16[64,128]{1,0:T(8,128)(2,1)S(1)}, bf16[64,128]{1,0:T(8,128)(2,1)}, u32[]{:S(2)}) copy-start(bf16[64,128]{1,0:T(8,128)(2,1)} %vc_ref.1) | copy-start | bytes 49156

commit v9 on v6

--- a/solution.py
+++ b/solution.py
@@ -6,7 +6,6 @@
 from jax import lax
 from jax.experimental import pallas as pl
 from jax.experimental.pallas import tpu as pltpu
-from jax.sharding import Mesh
 from jax.sharding import PartitionSpec as P
 
 D = 4096
@@ -60,6 +59,10 @@
 def turn(array, dx):
     pairs = [(s, ((s // 2 + (dx if s % 2 == 0 else -dx)) % XS) * 2 + s % 2) for s in range(2 * XS)]
     return lax.ppermute(array, "seq", pairs)
+
+
+def in_hbm(array):
+    return pltpu.with_memory_space_constraint(array, pltpu.HBM)
 
 
 ANYWHERE = pl.BlockSpec(memory_space=pl.ANY)
@@ -100,7 +103,7 @@
         pack_kernel,
         in_specs=[SCALARS] + [pl.BlockSpec(memory_space=pltpu.VMEM)] * 3,
         out_specs=[ANYWHERE] * XS,
-        out_shape=[jax.ShapeDtypeStruct((2, tokens, 2 * QW + HD), BF16)] * XS,
+        out_shape=[pltpu.HBM((2, tokens, 2 * QW + HD), BF16)] * XS,
         scratch_shapes=[pltpu.SemaphoreType.DMA((24,))],
         cost_estimate=cost(3),
         compiler_params=params(60),
@@ -238,7 +241,7 @@
         out_specs=[PROBS_SPEC, pl.BlockSpec((SEQ, HD), lambda i: (0, 0))],
         out_shape=[
             pltpu.HBM(PROBS_SHAPE, BF16),
-            jax.ShapeDtypeStruct((SEQ, HD), BF16),
+            pltpu.HBM((SEQ, HD), BF16),
         ],
         scratch_shapes=[
             pltpu.VMEM((SEQ, width), BF16),
@@ -297,7 +300,7 @@
         + hidden_specs(pieces)
         + [pl.BlockSpec((SEQ, HD), lambda j: (0, 0))],
         out_specs=pl.BlockSpec((STRIPE, HD), lambda j: (j, 0)),
-        out_shape=jax.ShapeDtypeStruct((D, HD), BF16),
+        out_shape=pltpu.HBM((D, HD), BF16),
         scratch_shapes=[pltpu.VMEM((HD, SEQ), BF16)],
         cost_estimate=cost(5),
         compiler_params=params(),
@@ -384,7 +387,7 @@
             pl.BlockSpec((SEQ, HD), lambda i: (0, 0)),
         ],
         out_specs=[ANYWHERE] * XS,
-        out_shape=[jax.ShapeDtypeStruct((2, ROWS, QW + HD), BF16)] * XS,
+        out_shape=[pltpu.HBM((2, ROWS, QW + HD), BF16)] * XS,
         scratch_shapes=[
             pltpu.VMEM((SEQ, width), BF16),
             pltpu.VMEM((SEQ, HD), BF16),
@@ -428,22 +431,6 @@
         cost_estimate=cost(2),
         compiler_params=params(8),
     )(origin, *pieces)
-
-
-def add_kernel(parts_ref, out_ref):
-    total = parts_ref[0].astype(F32)
-    for g in range(1, parts_ref.shape[0]):
-        total = total + parts_ref[g].astype(F32)
-    out_ref[...] = total.astype(BF16)
-
-
-def add_parts(parts):
-    return pl.pallas_call(
-        add_kernel,
-        out_shape=jax.ShapeDtypeStruct(parts.shape[1:], BF16),
-        cost_estimate=cost(1),
-        compiler_params=params(8),
-    )(parts)
 
 
 def adam_kernel(
@@ -519,14 +506,14 @@
 
 
 def shards(hidden, query, key, grad_out, doc_lens, master, m_code, m_scale, v_code, v_scale):
-    n_y, n_z = lax.axis_size("y"), lax.axis_size("z")
+    n_dp = lax.axis_size("dp")
     me = lax.axis_index("seq")
     to = jnp.stack([place(me, r // 2, r % 2) for r in range(8)])
     origin = jnp.stack([place(me, (XS - r // 2) % XS, r % 2) for r in range(8)])
     around = jnp.stack([place(me, dx, dc) for dx in (0, 3, 1, 2) for dc in (0, 1)])
     core = lax.rem(me, 2)
     ahead = jnp.where(core == 0, XS - 1, 1)
-    own = hidden[0]
+    own = in_hbm(hidden[0])
     first, second = turn(own, 1), turn(own, -1)
     around = jnp.stack(
         [
@@ -542,27 +529,25 @@
     )
     pairs = pack(to, query[0], grad_out[0], key[0])
     pieces = across(along(pairs))
-    master_bf, _ = lax.optimization_barrier((master.astype(BF16), pairs[0]))
-    copies = jnp.broadcast_to(master_bf[None], (n_y * n_z,) + master.shape)
-    weight = lax.all_to_all(copies, ("y", "z"), split_axis=0, concat_axis=0, tiled=True)
-    weight = weight.reshape(n_y * n_z * master.shape[0], HD)
+    mine, _ = lax.optimization_barrier((master.astype(BF16), pairs[0]))
+    copies = jnp.broadcast_to(mine[None], (n_dp,) + master.shape)
+    weight = lax.all_to_all(copies, "dp", split_axis=0, concat_axis=0, tiled=True)
+    weight = weight.reshape(D, HD)
     far = turn(first, 1)
     near = [own, send(own, 0, 1), first, send(first, 0, 1), second, send(second, 0, 1)]
+    pieces = [in_hbm(piece) for piece in pieces[:XS]] + pieces[XS:]
     probs, grad_values = probs_call(doc_lens, origin, pieces)
     far, grad_values, weight, near[1], near[3], near[5] = lax.optimization_barrier(
         (far, grad_values, weight, near[1], near[3], near[5])
     )
     hiddens = near + [far, send(far, 0, 1)]
-    term = term_call(around, hiddens, grad_values)
+    term = term_call(around, hiddens, in_hbm(grad_values))
     parts = lax.all_to_all(
-        term.reshape((n_y, n_z) + master.shape), "y", split_axis=0, concat_axis=0, tiled=True
-    )
-    summed = add_parts(parts)
-    parts = lax.all_to_all(summed, "z", split_axis=0, concat_axis=0, tiled=True)
+        term.reshape((n_dp,) + master.shape), "dp", split_axis=0, concat_axis=0, tiled=True
+    )
     values = values_call(hiddens, weight)
-    probs = pltpu.with_memory_space_constraint(probs, pltpu.HBM)
+    probs = in_hbm(probs)
     grads = along(grads_call(origin, to, around, pieces, probs, values))
-    grads[1], parts = lax.optimization_barrier((grads[1], parts))
     grad_query, grad_key = unpack(origin, across(grads))
     master, m_code, m_scale, v_code, v_scale = adam_call(
         parts, master, m_code, m_scale, v_code, v_scale
@@ -572,13 +557,11 @@
 
 
 def solution(mesh):
-    tokens, state = P(("y", "z"), "seq", None), P(("y", "z"), "seq")
-    rows = math.gcd(8, mesh.shape["dp"])
-    cut = mesh.devices.reshape(mesh.shape["seq"], rows, mesh.shape["dp"] // rows)
+    tokens, state = P("dp", "seq", None), P("dp", "seq")
     return jax.shard_map(
         shards,
-        mesh=Mesh(cut, ("seq", "y", "z")),
-        in_specs=(tokens,) * 4 + (P(("y", "z"), None),) + (state,) * 5,
+        mesh=mesh,
+        in_specs=(tokens,) * 4 + (P("dp", None),) + (state,) * 5,
         out_specs=(tokens,) * 2 + (state,) * 5,
         check_vma=False,
     )

time: 159 us -> 154 us (0.969)
  local copies, waits for them, and re-layouts: 11.7 us -> 8.1 us
  waiting for transfers between devices: 18.6 us -> 22.2 us
  starting transfers between devices: 88.3 us -> 85.5 us
    ppermute x12, waiting for transfers between devices: 3.57 us -> 16.4 us  [send(): return lax.ppermute(array, 'seq', pairs)]
    all_to_all x3 -> x2, waiting for transfers between devices: 11.4 us -> 0.01 us  [the longest x1 0.01 us: shards(): lax.all_to_all(copies, 'dp', split_axis=0, concat_axis=0, tiled=True)]
    unnamed x46 -> x30, local copies, waits for them, and re-layouts: 9.68 us -> 6.03 us
    ppermute x3, waiting for transfers between devices: 3.58 us -> 5.75 us  [turn(): return lax.ppermute(array, 'seq', pairs)]
    all_to_all x3 -> x2, starting transfers between devices: 34.8 us -> 33.4 us  [the longest x1 17.1 us: shards(): lax.all_to_all(term.reshape((n_dp,) + master.shape), 'dp', split_axis=0,...]
  transfers between devices with their start and end apart: 18 -> 17, of which waited for: 5 -> 7; matrix products, arithmetic and copies ran while one was open for 1% -> 1% of each run, Pallas kernels for 17% -> 17%
where the time goes in v9:
time: 154 us; the launch traced here: 153 us
  starting transfers between devices  85.5 us (56%)
  Pallas kernels  36.3 us (24%)
  waiting for transfers between devices  22.2 us (14%)
  local copies, waits for them, and re-layouts  8.1 us (5%)
    ppermute x12, starting transfers between devices, send(): return lax.ppermute(array, 'seq', pairs)  41.5 us
    all_to_all x1, starting transfers between devices, shards(): lax.all_to_all(term.reshape((n_dp,) + master.shape), 'dp', split_axis=0,...  17.1 us
    ppermute x12, waiting for transfers between devices, send(): return lax.ppermute(array, 'seq', pairs)  16.4 us
    all_to_all x1, starting transfers between devices, shards(): lax.all_to_all(copies, 'dp', split_axis=0, concat_axis=0, tiled=True)  16.3 us
    ppermute x3, starting transfers between devices, turn(): return lax.ppermute(array, 'seq', pairs)  10.6 us
    pallas_call x1, Pallas kernels, probs_call(): pl.pallas_call(probs_kernel, grid=(BLOCKS // 2,), in_specs=[SCALARS, SCAL...  8.32 us
    pallas_call x1, Pallas kernels, grads_call(): pl.pallas_call(grads_kernel, grid=(BLOCKS // 2,), in_specs=[SCALARS, SCAL...  8.14 us
    pallas_call x1, Pallas kernels, term_call(): pl.pallas_call(term_kernel, grid=(D // STRIPE,), in_specs=[SCALARS] + hid...  6.28 us
  transfers between devices with their start and end apart: 17, of which 7 were waited for; matrix products, arithmetic and copies ran while one was open for 1% of the time, Pallas kernels for 17%

profile of v9, /device:TPU:1, one launch (start us, length us, event | category | flops | bytes accessed | tf_op | source)
XLA Modules:
  0.0 153.1 jit_solution(4425877978824500804)
XLA Ops:
  0.7 0.7 stack.68.to_ref
  1.4 3.3 %shard_map.153 = (bf16[2,128,1152]{2,1,0:T(8,128)(2,1)}, bf16[2,128,1152]{2,1,0:T(8,128)(2,1)}, bf16[2,128,1152]{2,1,0:T(8,128)(2,1)}, bf16[2,128,1152]{2,1,0:T(8,128)(2,1)}) custom-call(s32[8]{0:T(128)} %stack.68.to_ref, bf16[128,4096]{1,0:T(8,128)(2,1)} %bitcast.25, bf16[128,4096]{1,0:T(8,128)(2,1)} %bitcast.26, bf16[128,1024]{1,0:T(8,128)(2,1)} %bitcast.27), custom_call_target="tpu_custom_call" | custom-call | flops 3000000000 | bytes 3000000 | tf_op jit(solution)/shard_map/pallas_call | solution.py:102
  4.6 3.9 %collective-permute-start = (bf16[2,128,1152]{2,1,0:T(8,128)(2,1)}, bf16[2,128,1152]{2,1,0:T(8,128)(2,1)S(1)}, u32[]{:S(2)}, u32[]{:S(2)}) collective-permute-start(bf16[2,128,1152]{2,1,0:T(8,128)(2,1)} %get-tuple-element.32), channel_id=1, source_target_pairs={{0,128},{64,192},{128,256},{192,320},{256,384},{320,448},{384,0},{... | collective-permute-start | bytes 1769480 | tf_op jit(solution)/shard_map/ppermute | solution.py:56
  8.6 4.4 %collective-permute-start.1 = (bf16[2,128,1152]{2,1,0:T(8,128)(2,1)}, bf16[2,128,1152]{2,1,0:T(8,128)(2,1)S(1)}, u32[]{:S(2)}, u32[]{:S(2)}) collective-permute-start(bf16[2,128,1152]{2,1,0:T(8,128)(2,1)} %get-tuple-element.33), channel_id=1, source_target_pairs={{0,256},{64,320},{128,384},{192,448},{256,0},{320,64},{384,128},{4... | collective-permute-start | bytes 1769480 | tf_op jit(solution)/shard_map/ppermute | solution.py:56
  13.0 3.1 %collective-permute-start.2 = (bf16[2,128,1152]{2,1,0:T(8,128)(2,1)}, bf16[2,128,1152]{2,1,0:T(8,128)(2,1)S(1)}, u32[]{:S(2)}, u32[]{:S(2)}) collective-permute-start(bf16[2,128,1152]{2,1,0:T(8,128)(2,1)} %get-tuple-element.34), channel_id=1, source_target_pairs={{0,384},{64,448},{128,0},{192,64},{256,128},{320,192},{384,256},{4... | collective-permute-start | bytes 1769480 | tf_op jit(solution)/shard_map/ppermute | solution.py:56
  16.0 1.9 %collective-permute-start.4 = (bf16[128,4096]{1,0:T(8,128)(2,1)}, bf16[128,4096]{1,0:T(8,128)(2,1)}, u32[]{:S(2)}, u32[]{:S(2)}) collective-permute-start(bf16[128,4096]{1,0:T(8,128)(2,1)} %bitcast.16.refs_0_), channel_id=1, source_target_pairs={{0,128},{64,448},{128,256},{192,64},{256,384},{320,192},{384,0},{4... | collective-permute-start | bytes 3145736 | tf_op jit(solution)/shard_map/ppermute | solution.py:61
  18.0 3.4 %collective-permute-start.8 = (bf16[128,4096]{1,0:T(8,128)(2,1)}, bf16[128,4096]{1,0:T(8,128)(2,1)}, u32[]{:S(2)}, u32[]{:S(2)}) collective-permute-start(bf16[128,4096]{1,0:T(8,128)(2,1)} %bitcast.16.refs_0_), channel_id=1, source_target_pairs={{0,384},{64,192},{128,0},{192,320},{256,128},{320,448},{384,256},{... | collective-permute-start | bytes 3145736 | tf_op jit(solution)/shard_map/ppermute | solution.py:61
  21.3 0.0 copy-done
  21.4 1.2 broadcast_in_dim.12
  22.6 16.3 %all-to-all-start = ((bf16[64,64,128]{2,1,0:T(8,128)(2,1)}), bf16[64,64,128]{2,1,0:T(8,128)(2,1)S(1)}, u32[]{:S(2)}, u32[]{:S(2)}) async-start(bf16[64,64,128]{2,1,0:T(8,128)(2,1)} %broadcast_in_dim.12), calls=%async_computation | async-start | bytes 2097152 | tf_op jit(solution)/shard_map/all_to_all | solution.py:534
  38.9 0.0 copy-start.7
  38.9 0.0 collective-permute-done.refs_1_
  38.9 0.0 copy-start.2
  38.9 0.0 collective-permute-done.1.refs_2_
  38.9 0.0 collective-permute-done.2.refs_3_
  38.9 0.0 copy-start.8
  39.0 1.3 copy-done.8
  40.2 1.3 shard_map.154
  41.5 0.0 copy-done.2
  41.5 0.0 copy-start.3
  41.6 0.8 copy-done.3
  42.4 0.8 copy-done.4
  43.2 9.3 %collective-permute-start.3 = (bf16[4,128,1152]{2,1,0:T(8,128)(2,1)}, bf16[4,128,1152]{2,1,0:T(8,128)(2,1)S(1)}, u32[]{:S(2)}, u32[]{:S(2)}) collective-permute-start(bf16[4,128,1152]{2,1,0:T(8,128)(2,1)} %shard_map.154), channel_id=1, source_target_pairs={{0,64},{64,0},{128,192},{192,128},{256,320},{320,256},{384,448},{4... | collective-permute-start | bytes 3538952 | tf_op jit(solution)/shard_map/ppermute | solution.py:56
  52.5 1.9 %collective-permute-start.6 = (bf16[128,4096]{1,0:T(8,128)(2,1)}, bf16[128,4096]{1,0:T(8,128)(2,1)}, u32[]{:S(2)}, u32[]{:S(2)}) collective-permute-start(bf16[128,4096]{1,0:T(8,128)(2,1)} %bitcast.16.refs_0_), channel_id=1, source_target_pairs={{0,64},{64,0},{128,192},{192,128},{256,320},{320,256},{384,448},{4... | collective-permute-start | bytes 3145736 | tf_op jit(solution)/shard_map/ppermute | solution.py:56
  54.4 4.7 %collective-permute-done.4.refs_2_ = bf16[128,4096]{1,0:T(8,128)(2,1)} collective-permute-done((bf16[128,4096]{1,0:T(8,128)(2,1)}, bf16[128,4096]{1,0:T(8,128)(2,1)}, u32[]{:S(2)}, u32[]{:S(2)}) %collective-permute-start.4) | collective-permute-done | bytes 1048608 | tf_op jit(solution)/shard_map/ppermute | solution.py:61
  59.1 5.3 %collective-permute-start.5 = (bf16[128,4096]{1,0:T(8,128)(2,1)}, bf16[128,4096]{1,0:T(8,128)(2,1)}, u32[]{:S(2)}, u32[]{:S(2)}) collective-permute-start(bf16[128,4096]{1,0:T(8,128)(2,1)} %collective-permute-done.4.refs_2_), channel_id=1, source_target_pairs={{0,128},{64,448},{128,256},{192,64},{256,384},{320,192},{384,0},{4... | collective-permute-start | bytes 3145736 | tf_op jit(solution)/shard_map/ppermute | solution.py:61
  64.4 1.9 %collective-permute-start.7 = (bf16[128,4096]{1,0:T(8,128)(2,1)}, bf16[128,4096]{1,0:T(8,128)(2,1)}, u32[]{:S(2)}, u32[]{:S(2)}) collective-permute-start(bf16[128,4096]{1,0:T(8,128)(2,1)} %collective-permute-done.4.refs_2_), channel_id=1, source_target_pairs={{0,64},{64,0},{128,192},{192,128},{256,320},{320,256},{384,448},{4... | collective-permute-start | bytes 3145736 | tf_op jit(solution)/shard_map/ppermute | solution.py:56
  66.3 0.0 collective-permute-done.8.refs_4_
  66.3 2.4 %collective-permute-start.9 = (bf16[128,4096]{1,0:T(8,128)(2,1)}, bf16[128,4096]{1,0:T(8,128)(2,1)}, u32[]{:S(2)}, u32[]{:S(2)}) collective-permute-start(bf16[128,4096]{1,0:T(8,128)(2,1)} %collective-permute-done.8.refs_4_), channel_id=1, source_target_pairs={{0,64},{64,0},{128,192},{192,128},{256,320},{320,256},{384,448},{4... | collective-permute-start | bytes 3145736 | tf_op jit(solution)/shard_map/ppermute | solution.py:56
  68.7 0.1 stack.67.from_ref
  68.8 0.0 collective-permute-done.3.refs_4_
  68.8 0.0 copy-done.7
  68.8 8.3 %shard_map.155 = (bf16[4,2,512,512]{3,2,1,0:T(8,128)(2,1)}, bf16[1024,128]{1,0:T(8,128)(2,1)}) custom-call(s32[1,8]{1,0:T(1,128)S(1)} %copy-done.7, s32[8]{0:T(128)S(1)} %stack.67.from_ref, bf16[2,128,1152]{2,1,0:T(8,128)(2,1)} %get-tuple-element.31.refs_0_, bf16[2,128,1152]{2,1,0:T(8,128)(2,1)} %copy-done.2, bf16[2,128,1152]{2,1,0:T(8,128)(2,1)} %copy-done.3, ...), custom_call_target="tpu_custom_call" | custom-call | flops 8000000000 | bytes 8000000 | tf_op jit(solution)/shard_map/pallas_call | solution.py:237
  77.2 0.0 collective-permute-done.6.refs_1_
  77.2 0.0 all-to-all-done
  77.2 1.1 collective-permute-done.5.refs_6_
  78.3 0.0 collective-permute-done.7.refs_3_
  78.3 0.0 collective-permute-done.9.refs_5_
  78.3 1.9 %collective-permute-start.10 = (bf16[128,4096]{1,0:T(8,128)(2,1)}, bf16[128,4096]{1,0:T(8,128)(2,1)S(1)}, u32[]{:S(2)}, u32[]{:S(2)}) collective-permute-start(bf16[128,4096]{1,0:T(8,128)(2,1)} %collective-permute-done.5.refs_6_), channel_id=1, source_target_pairs={{0,64},{64,0},{128,192},{192,128},{256,320},{320,256},{384,448},{4... | collective-permute-start | bytes 3145736 | tf_op jit(solution)/shard_map/ppermute | solution.py:56
  80.2 0.1 stack.74.around_ref.from_ref
  80.3 2.7 %collective-permute-done.10.refs_7_ = bf16[128,4096]{1,0:T(8,128)(2,1)S(1)} collective-permute-done((bf16[128,4096]{1,0:T(8,128)(2,1)}, bf16[128,4096]{1,0:T(8,128)(2,1)S(1)}, u32[]{:S(2)}, u32[]{:S(2)}) %collective-permute-start.10) | collective-permute-done | bytes 1048608 | tf_op jit(solution)/shard_map/ppermute | solution.py:56
  83.0 1.0 copy-done.13
  84.0 6.3 %shard_map.160 = bf16[4096,128]{1,0:T(8,128)(2,1)} custom-call(s32[8]{0:T(128)S(1)} %stack.74.around_ref.from_ref, bf16[128,4096]{1,0:T(8,128)(2,1)} %bitcast.16.refs_0_, bf16[128,4096]{1,0:T(8,128)(2,1)} %collective-permute-done.6.refs_1_, bf16[128,4096]{1,0:T(8,128)(2,1)} %collective-permute-done.4.refs_2_, ...), custom_call_target="tpu_custom_call" | custom-call | flops 5000000000 | bytes 5000000 | tf_op jit(solution)/shard_map/pallas_call | solution.py:296
  90.3 17.1 %all-to-all-start.1 = ((bf16[64,64,128]{2,1,0:T(8,128)(2,1)}), bf16[64,64,128]{2,1,0:T(8,128)(2,1)S(1)}, u32[]{:S(2)}, u32[]{:S(2)}) async-start(bf16[64,64,128]{2,1,0:T(8,128)(2,1)} %bitcast.24), calls=%async_computation.1 | async-start | bytes 2097152 | tf_op jit(solution)/shard_map/all_to_all | solution.py:545
  107.4 5.5 %shard_map.156.refs_6_ = bf16[1024,128]{1,0:T(8,128)(2,1)S(1)} custom-call(bf16[128,4096]{1,0:T(8,128)(2,1)} %bitcast.16.refs_0_, bf16[128,4096]{1,0:T(8,128)(2,1)} %collective-permute-done.6.refs_1_, bf16[128,4096]{1,0:T(8,128)(2,1)} %collective-permute-done.4.refs_2_, bf16[128,4096]{1,0:T(8,128)(2,1)} %collective-permute-done.7.refs_3_, ...), custom_call_target="tpu_custom_call" | custom-call | flops 6000000000 | bytes 6000000 | tf_op jit(solution)/shard_map/pallas_call | solution.py:312
  112.9 8.1 %shard_map.157 = (bf16[2,128,640]{2,1,0:T(8,128)(2,1)}, bf16[2,128,640]{2,1,0:T(8,128)(2,1)}, bf16[2,128,640]{2,1,0:T(8,128)(2,1)}, bf16[2,128,640]{2,1,0:T(8,128)(2,1)}) custom-call(s32[8]{0:T(128)S(1)} %stack.67.from_ref, s32[8]{0:T(128)S(1)} %copy-done.1, s32[8]{0:T(128)S(1)} %stack.74.around_ref.from_ref, ...), custom_call_target="tpu_custom_call" | custom-call | flops 8999999488 | bytes 9000000 | tf_op jit(solution)/shard_map/pallas_call | solution.py:380
  121.0 2.8 %collective-permute-start.11 = (bf16[2,128,640]{2,1,0:T(8,128)(2,1)}, bf16[2,128,640]{2,1,0:T(8,128)(2,1)S(1)}, u32[]{:S(2)}, u32[]{:S(2)}) collective-permute-start(bf16[2,128,640]{2,1,0:T(8,128)(2,1)} %get-tuple-element.44), channel_id=1, source_target_pairs={{0,128},{64,192},{128,256},{192,320},{256,384},{320,448},{384,0},{... | collective-permute-start | bytes 983048 | tf_op jit(solution)/shard_map/ppermute | solution.py:56
  123.8 4.6 %collective-permute-start.12 = (bf16[2,128,640]{2,1,0:T(8,128)(2,1)}, bf16[2,128,640]{2,1,0:T(8,128)(2,1)S(1)}, u32[]{:S(2)}, u32[]{:S(2)}) collective-permute-start(bf16[2,128,640]{2,1,0:T(8,128)(2,1)} %get-tuple-element.45), channel_id=1, source_target_pairs={{0,256},{64,320},{128,384},{192,448},{256,0},{320,64},{384,128},{4... | collective-permute-start | bytes 983048 | tf_op jit(solution)/shard_map/ppermute | solution.py:56
  128.3 2.0 %collective-permute-start.13 = (bf16[2,128,640]{2,1,0:T(8,128)(2,1)}, bf16[2,128,640]{2,1,0:T(8,128)(2,1)S(1)}, u32[]{:S(2)}, u32[]{:S(2)}) collective-permute-start(bf16[2,128,640]{2,1,0:T(8,128)(2,1)} %get-tuple-element.46), channel_id=1, source_target_pairs={{0,384},{64,448},{128,0},{192,64},{256,128},{320,192},{384,256},{4... | collective-permute-start | bytes 983048 | tf_op jit(solution)/shard_map/ppermute | solution.py:56
  130.4 2.8 %collective-permute-done.11.refs_1_ = bf16[2,128,640]{2,1,0:T(8,128)(2,1)S(1)} collective-permute-done((bf16[2,128,640]{2,1,0:T(8,128)(2,1)}, bf16[2,128,640]{2,1,0:T(8,128)(2,1)S(1)}, u32[]{:S(2)}, u32[]{:S(2)}) %collective-permute-start.11) | collective-permute-done | bytes 327712 | tf_op jit(solution)/shard_map/ppermute | solution.py:56
  133.2 7.9 %collective-permute-done.12.refs_2_ = bf16[2,128,640]{2,1,0:T(8,128)(2,1)S(1)} collective-permute-done((bf16[2,128,640]{2,1,0:T(8,128)(2,1)}, bf16[2,128,640]{2,1,0:T(8,128)(2,1)S(1)}, u32[]{:S(2)}, u32[]{:S(2)}) %collective-permute-start.12) | collective-permute-done | bytes 327712 | tf_op jit(solution)/shard_map/ppermute | solution.py:56
  141.0 1.5 %collective-permute-done.13.refs_3_ = bf16[2,128,640]{2,1,0:T(8,128)(2,1)S(1)} collective-permute-done((bf16[2,128,640]{2,1,0:T(8,128)(2,1)}, bf16[2,128,640]{2,1,0:T(8,128)(2,1)S(1)}, u32[]{:S(2)}, u32[]{:S(2)}) %collective-permute-start.13) | collective-permute-done | bytes 327712 | tf_op jit(solution)/shard_map/ppermute | solution.py:56
  142.6 1.0 copy-done.9
  143.5 0.9 shard_map.158
  144.4 3.4 %collective-permute-start.14 = (bf16[4,128,640]{2,1,0:T(8,128)(2,1)S(1)}, bf16[4,128,640]{2,1,0:T(8,128)(2,1)S(1)}, u32[]{:S(2)}, u32[]{:S(2)}) collective-permute-start(bf16[4,128,640]{2,1,0:T(8,128)(2,1)S(1)} %shard_map.158), channel_id=1, source_target_pairs={{0,64},{64,0},{128,192},{192,128},{256,320},{320,256},{384,448},{4... | collective-permute-start | bytes 1966088 | tf_op jit(solution)/shard_map/ppermute | solution.py:56
  147.8 0.1 copy.17.ms_ref
  147.9 0.1 copy.18.vs_ref
  148.0 1.5 collective-permute-done.14.refs_4_
  149.5 1.0 copy-done.10
  150.5 1.7 %shard_map.159 = (bf16[128,4096]{1,0:T(8,128)(2,1)}, bf16[128,1024]{1,0:T(8,128)(2,1)}) custom-call(s32[8]{0:T(128)S(1)} %stack.67.from_ref, bf16[2,128,640]{2,1,0:T(8,128)(2,1)S(1)} %copy-done.10, bf16[2,128,640]{2,1,0:T(8,128)(2,1)S(1)} %collective-permute-done.11.refs_1_, bf16[2,128,640]{2,1,0:T(8,128)(2,1)S(1)} %collective-permute-done.12.refs_2_, ...), custom_call_target="tpu_custom_call" | custom-call | flops 2000000000 | bytes 2000000 | tf_op jit(solution)/shard_map/pallas_call | solution.py:422
  152.2 0.0 all-to-all-done.1.parts_ref
  152.2 0.0 copy-done.5
  152.2 0.0 copy-done.6
  152.2 0.9 shard_map.161
  (14 shorter events, 0.0 us)
Async XLA Ops:
  1.4 20.0 %copy-start = (f32[64,128]{1,0:T(8,128)S(1)}, f32[64,128]{1,0:T(8,128)}, u32[]{:S(2)}) copy-start(f32[64,128]{1,0:T(8,128)} %master_ref.1) | copy-start | bytes 98308
  4.6 34.3 %collective-permute-start = (bf16[2,128,1152]{2,1,0:T(8,128)(2,1)}, bf16[2,128,1152]{2,1,0:T(8,128)(2,1)S(1)}, u32[]{:S(2)}, u32[]{:S(2)}) collective-permute-start(bf16[2,128,1152]{2,1,0:T(8,128)(2,1)} %get-tuple-element.32), channel_id=1, source_target_pairs={{0,128},{64,192},{128,256},{192,320},{256,384},{320,448},{384,0},{... | collective-permute-start | bytes 1769480 | tf_op jit(solution)/shard_map/ppermute | solution.py:56
  8.6 30.3 %collective-permute-start.1 = (bf16[2,128,1152]{2,1,0:T(8,128)(2,1)}, bf16[2,128,1152]{2,1,0:T(8,128)(2,1)S(1)}, u32[]{:S(2)}, u32[]{:S(2)}) collective-permute-start(bf16[2,128,1152]{2,1,0:T(8,128)(2,1)} %get-tuple-element.33), channel_id=1, source_target_pairs={{0,256},{64,320},{128,384},{192,448},{256,0},{320,64},{384,128},{4... | collective-permute-start | bytes 1769480 | tf_op jit(solution)/shard_map/ppermute | solution.py:56
  13.0 26.0 %collective-permute-start.2 = (bf16[2,128,1152]{2,1,0:T(8,128)(2,1)}, bf16[2,128,1152]{2,1,0:T(8,128)(2,1)S(1)}, u32[]{:S(2)}, u32[]{:S(2)}) collective-permute-start(bf16[2,128,1152]{2,1,0:T(8,128)(2,1)} %get-tuple-element.34), channel_id=1, source_target_pairs={{0,384},{64,448},{128,0},{192,64},{256,128},{320,192},{384,256},{4... | collective-permute-start | bytes 1769480 | tf_op jit(solution)/shard_map/ppermute | solution.py:56
  16.0 43.0 %collective-permute-start.4 = (bf16[128,4096]{1,0:T(8,128)(2,1)}, bf16[128,4096]{1,0:T(8,128)(2,1)}, u32[]{:S(2)}, u32[]{:S(2)}) collective-permute-start(bf16[128,4096]{1,0:T(8,128)(2,1)} %bitcast.16.refs_0_), channel_id=1, source_target_pairs={{0,128},{64,448},{128,256},{192,64},{256,384},{320,192},{384,0},{4... | collective-permute-start | bytes 3145736 | tf_op jit(solution)/shard_map/ppermute | solution.py:61
  18.0 48.3 %collective-permute-start.8 = (bf16[128,4096]{1,0:T(8,128)(2,1)}, bf16[128,4096]{1,0:T(8,128)(2,1)}, u32[]{:S(2)}, u32[]{:S(2)}) collective-permute-start(bf16[128,4096]{1,0:T(8,128)(2,1)} %bitcast.16.refs_0_), channel_id=1, source_target_pairs={{0,384},{64,192},{128,0},{192,320},{256,128},{320,448},{384,256},{... | collective-permute-start | bytes 3145736 | tf_op jit(solution)/shard_map/ppermute | solution.py:61
  22.6 54.6 %all-to-all-start = ((bf16[64,64,128]{2,1,0:T(8,128)(2,1)}), bf16[64,64,128]{2,1,0:T(8,128)(2,1)S(1)}, u32[]{:S(2)}, u32[]{:S(2)}) async-start(bf16[64,64,128]{2,1,0:T(8,128)(2,1)} %broadcast_in_dim.12), calls=%async_computation | async-start | bytes 2097152 | tf_op jit(solution)/shard_map/all_to_all | solution.py:534
  38.9 29.9 %copy-start.7 = (s32[1,8]{1,0:T(1,128)S(1)}, s32[1,8]{1,0:T(1,128)}, u32[]{:S(2)}) copy-start(s32[1,8]{1,0:T(1,128)} %lens_ref.1) | copy-start | bytes 100
  38.9 2.6 %copy-start.2 = (bf16[2,128,1152]{2,1,0:T(8,128)(2,1)}, bf16[2,128,1152]{2,1,0:T(8,128)(2,1)S(1)}, u32[]{:S(2)}) copy-start(bf16[2,128,1152]{2,1,0:T(8,128)(2,1)S(1)} %collective-permute-done.refs_1_) | copy-start | bytes 1769476
  38.9 1.3 copy-start.8
  41.5 0.8 copy-start.3
  42.4 0.8 copy-start.4
  43.2 25.6 %collective-permute-start.3 = (bf16[4,128,1152]{2,1,0:T(8,128)(2,1)}, bf16[4,128,1152]{2,1,0:T(8,128)(2,1)S(1)}, u32[]{:S(2)}, u32[]{:S(2)}) collective-permute-start(bf16[4,128,1152]{2,1,0:T(8,128)(2,1)} %shard_map.154), channel_id=1, source_target_pairs={{0,64},{64,0},{128,192},{192,128},{256,320},{320,256},{384,448},{4... | collective-permute-start | bytes 3538952 | tf_op jit(solution)/shard_map/ppermute | solution.py:56
  52.5 24.7 %collective-permute-start.6 = (bf16[128,4096]{1,0:T(8,128)(2,1)}, bf16[128,4096]{1,0:T(8,128)(2,1)}, u32[]{:S(2)}, u32[]{:S(2)}) collective-permute-start(bf16[128,4096]{1,0:T(8,128)(2,1)} %bitcast.16.refs_0_), channel_id=1, source_target_pairs={{0,64},{64,0},{128,192},{192,128},{256,320},{320,256},{384,448},{4... | collective-permute-start | bytes 3145736 | tf_op jit(solution)/shard_map/ppermute | solution.py:56
  59.1 19.2 %collective-permute-start.5 = (bf16[128,4096]{1,0:T(8,128)(2,1)}, bf16[128,4096]{1,0:T(8,128)(2,1)}, u32[]{:S(2)}, u32[]{:S(2)}) collective-permute-start(bf16[128,4096]{1,0:T(8,128)(2,1)} %collective-permute-done.4.refs_2_), channel_id=1, source_target_pairs={{0,128},{64,448},{128,256},{192,64},{256,384},{320,192},{384,0},{4... | collective-permute-start | bytes 3145736 | tf_op jit(solution)/shard_map/ppermute | solution.py:61
  64.4 13.9 %collective-permute-start.7 = (bf16[128,4096]{1,0:T(8,128)(2,1)}, bf16[128,4096]{1,0:T(8,128)(2,1)}, u32[]{:S(2)}, u32[]{:S(2)}) collective-permute-start(bf16[128,4096]{1,0:T(8,128)(2,1)} %collective-permute-done.4.refs_2_), channel_id=1, source_target_pairs={{0,64},{64,0},{128,192},{192,128},{256,320},{320,256},{384,448},{4... | collective-permute-start | bytes 3145736 | tf_op jit(solution)/shard_map/ppermute | solution.py:56
  66.3 12.0 %collective-permute-start.9 = (bf16[128,4096]{1,0:T(8,128)(2,1)}, bf16[128,4096]{1,0:T(8,128)(2,1)}, u32[]{:S(2)}, u32[]{:S(2)}) collective-permute-start(bf16[128,4096]{1,0:T(8,128)(2,1)} %collective-permute-done.8.refs_4_), channel_id=1, source_target_pairs={{0,64},{64,0},{128,192},{192,128},{256,320},{320,256},{384,448},{4... | collective-permute-start | bytes 3145736 | tf_op jit(solution)/shard_map/ppermute | solution.py:56
  78.3 4.8 %collective-permute-start.10 = (bf16[128,4096]{1,0:T(8,128)(2,1)}, bf16[128,4096]{1,0:T(8,128)(2,1)S(1)}, u32[]{:S(2)}, u32[]{:S(2)}) collective-permute-start(bf16[128,4096]{1,0:T(8,128)(2,1)} %collective-permute-done.5.refs_6_), channel_id=1, source_target_pairs={{0,64},{64,0},{128,192},{192,128},{256,320},{320,256},{384,448},{4... | collective-permute-start | bytes 3145736 | tf_op jit(solution)/shard_map/ppermute | solution.py:56
  83.0 1.0 copy-start.13
  90.3 61.9 %all-to-all-start.1 = ((bf16[64,64,128]{2,1,0:T(8,128)(2,1)}), bf16[64,64,128]{2,1,0:T(8,128)(2,1)S(1)}, u32[]{:S(2)}, u32[]{:S(2)}) async-start(bf16[64,64,128]{2,1,0:T(8,128)(2,1)} %bitcast.24), calls=%async_computation.1 | async-start | bytes 2097152 | tf_op jit(solution)/shard_map/all_to_all | solution.py:545
  107.4 5.5 %copy-start.1 = (s32[8]{0:T(128)S(1)}, s32[8]{0:T(128)}, u32[]{:S(2)}) copy-start(s32[8]{0:T(128)} %stack.68.to_ref) | copy-start | bytes 100
  121.0 12.2 %collective-permute-start.11 = (bf16[2,128,640]{2,1,0:T(8,128)(2,1)}, bf16[2,128,640]{2,1,0:T(8,128)(2,1)S(1)}, u32[]{:S(2)}, u32[]{:S(2)}) collective-permute-start(bf16[2,128,640]{2,1,0:T(8,128)(2,1)} %get-tuple-element.44), channel_id=1, source_target_pairs={{0,128},{64,192},{128,256},{192,320},{256,384},{320,448},{384,0},{... | collective-permute-start | bytes 983048 | tf_op jit(solution)/shard_map/ppermute | solution.py:56
  123.8 17.3 %collective-permute-start.12 = (bf16[2,128,640]{2,1,0:T(8,128)(2,1)}, bf16[2,128,640]{2,1,0:T(8,128)(2,1)S(1)}, u32[]{:S(2)}, u32[]{:S(2)}) collective-permute-start(bf16[2,128,640]{2,1,0:T(8,128)(2,1)} %get-tuple-element.45), channel_id=1, source_target_pairs={{0,256},{64,320},{128,384},{192,448},{256,0},{320,64},{384,128},{4... | collective-permute-start | bytes 983048 | tf_op jit(solution)/shard_map/ppermute | solution.py:56
  128.3 14.2 %collective-permute-start.13 = (bf16[2,128,640]{2,1,0:T(8,128)(2,1)}, bf16[2,128,640]{2,1,0:T(8,128)(2,1)S(1)}, u32[]{:S(2)}, u32[]{:S(2)}) collective-permute-start(bf16[2,128,640]{2,1,0:T(8,128)(2,1)} %get-tuple-element.46), channel_id=1, source_target_pairs={{0,384},{64,448},{128,0},{192,64},{256,128},{320,192},{384,256},{4... | collective-permute-start | bytes 983048 | tf_op jit(solution)/shard_map/ppermute | solution.py:56
  142.6 1.0 copy-start.9
  143.5 4.2 %copy-start.11 = (f32[32,1]{0,1:T(1,128)S(1)}, f32[32,1]{0,1:T(1,128)}, u32[]{:S(2)}) copy-start(f32[32,1]{0,1:T(1,128)} %param.17) | copy-start | bytes 388
  143.5 4.3 %copy-start.12 = (f32[32,1]{0,1:T(1,128)S(1)}, f32[32,1]{0,1:T(1,128)}, u32[]{:S(2)}) copy-start(f32[32,1]{0,1:T(1,128)} %param.19) | copy-start | bytes 388
  144.4 5.1 %collective-permute-start.14 = (bf16[4,128,640]{2,1,0:T(8,128)(2,1)S(1)}, bf16[4,128,640]{2,1,0:T(8,128)(2,1)S(1)}, u32[]{:S(2)}, u32[]{:S(2)}) collective-permute-start(bf16[4,128,640]{2,1,0:T(8,128)(2,1)S(1)} %shard_map.158), channel_id=1, source_target_pairs={{0,64},{64,0},{128,192},{192,128},{256,320},{320,256},{384,448},{4... | collective-permute-start | bytes 1966088 | tf_op jit(solution)/shard_map/ppermute | solution.py:56
  148.0 4.2 %copy-start.5 = (bf16[64,128]{1,0:T(8,128)(2,1)S(1)}, bf16[64,128]{1,0:T(8,128)(2,1)}, u32[]{:S(2)}) copy-start(bf16[64,128]{1,0:T(8,128)(2,1)} %mc_ref.1) | copy-start | bytes 49156
  148.0 4.2 %copy-start.6 = (bf16[64,128]{1,0:T(8,128)(2,1)S(1)}, bf16[64,128]{1,0:T(8,128)(2,1)}, u32[]{:S(2)}) copy-start(bf16[64,128]{1,0:T(8,128)(2,1)} %vc_ref.1) | copy-start | bytes 49156
  149.5 1.0 copy-start.10
